TPU v7x, 32 devices: a whole 2x2x4 slice. The times are simulated.
32 devices in a mesh: group: 8 (over z, core), blk: 4 (over y, x).
Axes of the slice: x: 2, y: 2, z: 4, core: 2. Of those that a mesh axis runs over, the one named last changes fastest.
Arguments:
- hamiltonian: bfloat16 [512, 6, 64, 256], P(('group', 'blk')), may hold values from -0.15625 to 0.15625
- block_columns: int32 [512, 6, 4], P(('group', 'blk')), may hold values from 0 to 15, as said below
- potential: float32 [32768], P(('group', 'blk')), may hold values from -1 to 1
- trial_slab: float32 [32768, 128], P(('group', 'blk')), may hold values from -40 to 40
Outputs:
- ortho_slab: float32 [32768, 128], P(('group', 'blk'))
- upper_factor: float32 [128, 128], replicated
Inputs may be any that keep to these rules, and one draw needn't show every extreme that they name: `block_columns`: for each row block and each source, the 4 entries are distinct.
All inputs are finite; a program needn't handle non-finite values.
Results may differ from a plain program's by a relative error of at most 0.0021.
Values may be sent and summed in bfloat16 or wider, within the bound.
No kernel may reach another device: no remote copies, remote signals or barrier semaphores. Data moves between devices by JAX's collectives and lax.ppermute only.
A program may use at most 64 MiB of HBM per device.

v0:
```python
import jax
import jax.numpy as jnp
from jax import lax
from jax.sharding import PartitionSpec as P

precise = lax.Precision.HIGHEST


def padded(block, sides, width):
    for axis, dim in sides:
        count = lax.axis_size(axis)
        forward = [(i, i + 1) for i in range(count - 1)]
        backward = [(target, source) for source, target in forward]
        low = lax.ppermute(
            lax.slice_in_dim(block, block.shape[dim] - width, None, axis=dim), axis, forward
        )
        high = lax.ppermute(lax.slice_in_dim(block, 0, width, axis=dim), axis, backward)
        block = jnp.concatenate([low, block, high], axis=dim)
    return block


def shifted(value, axis, steps):
    count = lax.axis_size(axis)
    pairs = [(source, (source + steps) % count) for source in range(count)]
    return lax.ppermute(value, axis, pairs)


def from_partner(block, axis, bit):
    count = lax.axis_size(axis)
    route = []
    for low in range(count):
        high = low | 1 << bit
        if high != low and high < count:
            route += [(low, high), (high, low)]
    return lax.ppermute(block, axis, route)


def couple_source(hamiltonian, block_columns, piece, source):
    coupling = lax.dynamic_index_in_dim(hamiltonian, source, 1, keepdims=False)
    columns = lax.dynamic_index_in_dim(block_columns, source, 1, keepdims=False)
    rows_here, per_source = columns.shape
    picked = piece[columns].reshape(rows_here, per_source * piece.shape[1], piece.shape[2])
    return jnp.einsum("rik,rkn->rin", coupling, picked, preferred_element_type=jnp.float32)


def couple_all(hamiltonian, block_columns, rounded):
    cycle_size = lax.axis_size("blk")
    shard_blocks = rounded.shape[0]
    with_rims = padded(rounded, (("group", 0),), shard_blocks)
    summed = couple_source(hamiltonian, block_columns, with_rims[:shard_blocks], cycle_size)
    summed = summed + couple_source(
        hamiltonian, block_columns, with_rims[2 * shard_blocks :], cycle_size + 1
    )
    held_piece = rounded
    own_index = lax.axis_index("blk")
    for turn_index in range(cycle_size):
        source = (own_index - turn_index) % cycle_size
        summed = summed + couple_source(hamiltonian, block_columns, held_piece, source)
        if turn_index + 1 < cycle_size:
            held_piece = shifted(held_piece, "blk", 1)
    return summed


def on_device(hamiltonian, block_columns, potential, trial_slab):
    shard_blocks = hamiltonian.shape[0]
    block_size = hamiltonian.shape[2]
    states = trial_slab.shape[1]
    start_slab = trial_slab.reshape(shard_blocks, block_size, states)
    weights = potential.reshape(shard_blocks, block_size, 1)
    coupled_start = couple_all(hamiltonian, block_columns, start_slab.astype(jnp.bfloat16))
    filtered_once = 0.5 * (coupled_start + weights * start_slab)
    coupled_next = couple_all(hamiltonian, block_columns, filtered_once.astype(jnp.bfloat16))
    filtered = coupled_next + weights * filtered_once - start_slab
    flat = filtered.reshape(shard_blocks * block_size, states)
    rows_total = flat.shape[0] * lax.axis_size("group") * lax.axis_size("blk")
    local_gram = jnp.dot(flat.T, flat, precision=precise) / rows_total
    lower = jnp.linalg.cholesky(local_gram)
    for level in range(lax.axis_size("blk").bit_length() - 1):
        partner = from_partner(lower.astype(jnp.bfloat16), "blk", level).astype(lower.dtype)
        lower = jnp.linalg.cholesky(
            jnp.dot(lower, lower.T, precision=precise)
            + jnp.dot(partner, partner.T, precision=precise)
        )
    for level in range(lax.axis_size("group").bit_length() - 1):
        partner = from_partner(lower, "group", level)
        lower = jnp.linalg.cholesky(
            jnp.dot(lower, lower.T, precision=precise)
            + jnp.dot(partner, partner.T, precision=precise)
        )
    ortho_slab = lax.linalg.triangular_solve(
        lower, flat, left_side=False, lower=True, transpose_a=True
    )
    return (ortho_slab, jnp.transpose(lower))


def solution(mesh):
    placed = (
        P(("group", "blk"), None, None, None),
        P(("group", "blk"), None, None),
        P(("group", "blk")),
        P(("group", "blk"), None),
    )
    return jax.shard_map(
        on_device,
        mesh=mesh,
        in_specs=placed,
        out_specs=(P(("group", "blk"), None), P()),
        check_vma=False,
    )
```

profile of v0, /device:TPU:0, one launch (start us, length us, event | category | flops | bytes accessed | tf_op | source)
XLA Modules:
  0.0 203.1 jit_solution(15965227129983009802)
XLA Ops:
  0.6 1.2 convert_element_type.14
  1.9 3.0 %collective-permute-start.2 = (bf16[16,64,128]{2,1,0:T(8,128)(2,1)S(1)}, bf16[16,64,128]{2,1,0:T(8,128)(2,1)}, u32[]{:S(2)}, u32[]{:S(2)}) collective-permute-start(bf16[16,64,128]{2,1,0:T(8,128)(2,1)S(1)} %convert_element_type.14), channel_id=1, source_target_pairs={{0,1},{1,2},{2,3},{3,0},{4,5},{5,6},{6,7},{7,4},{8,9},{9,10},{10,1... | collective-permute-start | bytes 786440 | tf_op jit(solution)/shard_map/ppermute | solution.py:25
  4.9 1.3 collective-permute-start.1
  6.2 3.7 %collective-permute-start = (bf16[16,64,128]{2,1,0:T(8,128)(2,1)S(1)}, bf16[16,64,128]{2,1,0:T(8,128)(2,1)}, u32[]{:S(2)}, u32[]{:S(2)}) collective-permute-start(bf16[16,64,128]{2,1,0:T(8,128)(2,1)S(1)} %convert_element_type.14), channel_id=1, source_target_pairs={{0,4},{4,8},{8,12},{12,16},{16,20},{20,24},{24,28},{1,5},{5,9},{9,... | collective-permute-start | bytes 786440 | tf_op jit(solution)/shard_map/ppermute | solution.py:14
  9.9 0.8 mul.28
  10.7 0.8 compare_select_fusion
  11.8 1.7 gather_fusion.2
  14.2 2.4 %fusion.26 = f32[16,64,128]{2,1,0:T(8,128)} fusion(bf16[16,256,128]{2,1,0:T(8,128)(2,1)} %bitcast.158, bf16[16,6,64,256]{3,2,1,0:T(8,128)(2,1)S(1)} %copy-done, s32[]{:T(128)S(6)} %select_n.135), kind=kOutput, calls=%fused_computation.50 | convolution fusion | flops 67108864 | bytes 2097156 | tf_op jit(solution)/shard_map/rik,rkn->rin/dot_general | solution.py:43
  16.6 2.6 %gather_fusion.1 = bf16[64,64,128]{2,1,0:T(8,128)(2,1)} fusion(bf16[16,64,128]{2,1,0:T(8,128)(2,1)} %collective-permute-done.1, s32[1024]{0:T(1024)S(1)} %pad_clamp_fusion.4), kind=kCustom, calls=%fused_computation.1 | custom fusion | bytes 2097408 | tf_op jit(solution)/shard_map/gather | solution.py:42
  19.2 2.4 %fusion.10 = f32[16,128,64]{1,2,0:T(8,128)} fusion(bf16[16,256,128]{2,1,0:T(8,128)(2,1)} %bitcast.165, bf16[16,6,64,256]{3,2,1,0:T(8,128)(2,1)S(1)} %copy-done), kind=kOutput, calls=%fused_computation.34 | convolution fusion | flops 67108864 | bytes 2097152 | tf_op jit(solution)/shard_map/rik,rkn->rin/dot_general | solution.py:43
  21.6 1.5 collective-permute-start.3
  23.1 2.7 %gather_fusion.3 = bf16[64,64,128]{2,1,0:T(8,128)(2,1)} fusion(bf16[16,64,128]{2,1,0:T(8,128)(2,1)} %collective-permute-done.2, s32[1024]{0:T(1024)S(1)} %pad_clamp_fusion.2), kind=kCustom, calls=%fused_computation.3 | custom fusion | bytes 2097408 | tf_op jit(solution)/shard_map/gather | solution.py:42
  25.7 2.3 %fusion.22 = f32[16,64,128]{2,1,0:T(8,128)} fusion(bf16[16,256,128]{2,1,0:T(8,128)(2,1)} %bitcast.161, bf16[16,6,64,256]{3,2,1,0:T(8,128)(2,1)S(1)} %copy-done, s32[]{:T(128)S(6)} %select_n.138), kind=kOutput, calls=%fused_computation.46 | convolution fusion | flops 67108864 | bytes 2097156 | tf_op jit(solution)/shard_map/rik,rkn->rin/dot_general | solution.py:43
  28.1 2.6 %gather_fusion = bf16[64,64,128]{2,1,0:T(8,128)(2,1)} fusion(bf16[16,64,128]{2,1,0:T(8,128)(2,1)} %collective-permute-done, s32[1024]{0:T(1024)S(1)} %pad_clamp_fusion.5), kind=kCustom, calls=%fused_computation | custom fusion | bytes 2097408 | tf_op jit(solution)/shard_map/gather | solution.py:42
  30.7 2.8 %fusion.7 = f32[16,64,128]{2,1,0:T(8,128)} fusion(f32[16,64,128]{2,1,0:T(8,128)} %fusion.22, f32[16,64,128]{2,1,0:T(8,128)} %fusion.26, f32[16,128,64]{1,2,0:T(8,128)} %fusion.10, bf16[16,256,128]{2,1,0:T(8,128)(2,1)} %bitcast.157, bf16[16,6,64,256]{3,2,1,0:T(8,128)(2,1)S(1)} %copy-done), kind=kOutput, calls=%fused_computation.25 | convolution fusion | flops 67502080 | bytes 3670016 | tf_op jit(solution)/shard_map/rik,rkn->rin/dot_general | solution.py:43
  33.5 1.5 collective-permute-start.4
  35.0 2.7 %gather_fusion.4 = bf16[64,64,128]{2,1,0:T(8,128)(2,1)} fusion(bf16[16,64,128]{2,1,0:T(8,128)(2,1)} %collective-permute-done.3, s32[1024]{0:T(1024)S(1)} %pad_clamp_fusion.1), kind=kCustom, calls=%fused_computation.4 | custom fusion | bytes 2097408 | tf_op jit(solution)/shard_map/gather | solution.py:42
  37.6 2.5 %convolution_add_fusion.5 = f32[16,64,128]{2,1,0:T(8,128)} fusion(f32[16,64,128]{2,1,0:T(8,128)} %fusion.7, bf16[16,256,128]{2,1,0:T(8,128)(2,1)} %bitcast.166, bf16[16,6,64,256]{3,2,1,0:T(8,128)(2,1)S(1)} %copy-done, s32[]{:T(128)S(6)} %select_n.141), kind=kOutput, calls=%fused_computation.19 | convolution fusion | flops 67239936 | bytes 2621444 | tf_op jit(solution)/shard_map/rik,rkn->rin/dot_general | solution.py:43
  40.1 3.0 %collective-permute-done.4 = bf16[16,64,128]{2,1,0:T(8,128)(2,1)S(1)} collective-permute-done((bf16[16,64,128]{2,1,0:T(8,128)(2,1)}, bf16[16,64,128]{2,1,0:T(8,128)(2,1)S(1)}, u32[]{:S(2)}, u32[]{:S(2)}) %collective-permute-start.4) | collective-permute-done | bytes 262176 | tf_op jit(solution)/shard_map/ppermute | solution.py:25
  43.1 1.7 gather_fusion.5
  44.8 2.6 %multiply_convert_fusion = (bf16[16,64,128]{2,1,0:T(8,128)(2,1)S(1)}, f32[16,64,128]{2,1,0:T(8,128)}) fusion(f32[16,64,128]{2,1,0:T(8,128)} %bitcast.154, f32[16,64]{1,0:T(8,128)S(1)} %mul.28, f32[16,64,128]{2,1,0:T(8,128)} %convolution_add_fusion.5, bf16[16,256,128]{2,1,0:T(8,128)(2,1)} %bitcast.163, bf16[16,6,64,256]{3,2,1,0:T(8,128)(2,1)S(1)} %copy-done, ...), kind=kOutput, calls=%fused_computation.52 | convolution fusion | flops 67764224 | bytes 3416068 | tf_op jit(solution)/shard_map/rik,rkn->rin/dot_general | solution.py:43
  48.0 1.7 gather_fusion.8
  49.7 1.3 collective-permute-start.6
  51.0 3.8 %collective-permute-start.5 = (bf16[16,64,128]{2,1,0:T(8,128)(2,1)S(1)}, bf16[16,64,128]{2,1,0:T(8,128)(2,1)}, u32[]{:S(2)}, u32[]{:S(2)}) collective-permute-start(bf16[16,64,128]{2,1,0:T(8,128)(2,1)S(1)} %get-tuple-element.15), channel_id=1, source_target_pairs={{0,4},{4,8},{8,12},{12,16},{16,20},{20,24},{24,28},{1,5},{5,9},{9,... | collective-permute-start | bytes 786440 | tf_op jit(solution)/shard_map/ppermute | solution.py:14
  54.7 2.4 %fusion.24 = f32[16,64,128]{2,1,0:T(8,128)} fusion(bf16[16,256,128]{2,1,0:T(8,128)(2,1)} %bitcast.159, bf16[16,6,64,256]{3,2,1,0:T(8,128)(2,1)S(1)} %copy-done, s32[]{:T(128)S(6)} %select_n.135), kind=kOutput, calls=%fused_computation.48 | convolution fusion | flops 67108864 | bytes 2097156 | tf_op jit(solution)/shard_map/rik,rkn->rin/dot_general | solution.py:43
  57.1 2.6 %gather_fusion.7 = bf16[64,64,128]{2,1,0:T(8,128)(2,1)} fusion(bf16[16,64,128]{2,1,0:T(8,128)(2,1)} %collective-permute-done.6, s32[1024]{0:T(1024)S(1)} %pad_clamp_fusion.4), kind=kCustom, calls=%fused_computation.7 | custom fusion | bytes 2097408 | tf_op jit(solution)/shard_map/gather | solution.py:42
  59.7 2.4 %fusion.12 = f32[16,128,64]{1,2,0:T(8,128)} fusion(bf16[16,256,128]{2,1,0:T(8,128)(2,1)} %bitcast.164, bf16[16,6,64,256]{3,2,1,0:T(8,128)(2,1)S(1)} %copy-done), kind=kOutput, calls=%fused_computation.36 | convolution fusion | flops 67108864 | bytes 2097152 | tf_op jit(solution)/shard_map/rik,rkn->rin/dot_general | solution.py:43
  62.1 2.6 %gather_fusion.9 = bf16[64,64,128]{2,1,0:T(8,128)(2,1)} fusion(bf16[16,64,128]{2,1,0:T(8,128)(2,1)} %collective-permute-done.7, s32[1024]{0:T(1024)S(1)} %pad_clamp_fusion.2), kind=kCustom, calls=%fused_computation.9 | custom fusion | bytes 2097408 | tf_op jit(solution)/shard_map/gather | solution.py:42
  64.7 1.4 collective-permute-start.8
  66.1 2.3 %fusion.20 = f32[16,64,128]{2,1,0:T(8,128)} fusion(bf16[16,256,128]{2,1,0:T(8,128)(2,1)} %bitcast.160, bf16[16,6,64,256]{3,2,1,0:T(8,128)(2,1)S(1)} %copy-done, s32[]{:T(128)S(6)} %select_n.138), kind=kOutput, calls=%fused_computation.44 | convolution fusion | flops 67108864 | bytes 2097156 | tf_op jit(solution)/shard_map/rik,rkn->rin/dot_general | solution.py:43
  68.4 2.6 %gather_fusion.6 = bf16[64,64,128]{2,1,0:T(8,128)(2,1)} fusion(bf16[16,64,128]{2,1,0:T(8,128)(2,1)} %collective-permute-done.5, s32[1024]{0:T(1024)S(1)} %pad_clamp_fusion.5), kind=kCustom, calls=%fused_computation.6 | custom fusion | bytes 2097408 | tf_op jit(solution)/shard_map/gather | solution.py:42
  71.0 2.8 %fusion.6 = f32[16,64,128]{2,1,0:T(8,128)} fusion(f32[16,64,128]{2,1,0:T(8,128)} %fusion.20, f32[16,64,128]{2,1,0:T(8,128)} %fusion.24, f32[16,128,64]{1,2,0:T(8,128)} %fusion.12, bf16[16,256,128]{2,1,0:T(8,128)(2,1)} %bitcast.156, bf16[16,6,64,256]{3,2,1,0:T(8,128)(2,1)S(1)} %copy-done), kind=kOutput, calls=%fused_computation.24 | convolution fusion | flops 67502080 | bytes 3670016 | tf_op jit(solution)/shard_map/rik,rkn->rin/dot_general | solution.py:43
  73.8 0.8 collective-permute-done.8
  74.6 2.6 %gather_fusion.10 = bf16[64,64,128]{2,1,0:T(8,128)(2,1)} fusion(bf16[16,64,128]{2,1,0:T(8,128)(2,1)} %collective-permute-done.8, s32[1024]{0:T(1024)S(1)} %pad_clamp_fusion.1), kind=kCustom, calls=%fused_computation.10 | custom fusion | bytes 2097408 | tf_op jit(solution)/shard_map/gather | solution.py:42
  77.7 2.5 %convolution_add_fusion.3 = f32[16,64,128]{2,1,0:T(8,128)} fusion(f32[16,64,128]{2,1,0:T(8,128)} %fusion.6, bf16[16,256,128]{2,1,0:T(8,128)(2,1)} %bitcast.162, bf16[16,6,64,256]{3,2,1,0:T(8,128)(2,1)S(1)} %copy-done, s32[]{:T(128)S(6)} %select_n.141), kind=kOutput, calls=%fused_computation.17 | convolution fusion | flops 67239936 | bytes 2621444 | tf_op jit(solution)/shard_map/rik,rkn->rin/dot_general | solution.py:43
  80.2 6.1 %collective-permute-done.9 = bf16[16,64,128]{2,1,0:T(8,128)(2,1)S(1)} collective-permute-done((bf16[16,64,128]{2,1,0:T(8,128)(2,1)}, bf16[16,64,128]{2,1,0:T(8,128)(2,1)S(1)}, u32[]{:S(2)}, u32[]{:S(2)}) %collective-permute-start.9) | collective-permute-done | bytes 262176 | tf_op jit(solution)/shard_map/ppermute | solution.py:25
  86.2 1.7 gather_fusion.11
  87.9 2.0 fusion.8
  89.9 0.8 copy-done.1
  90.7 1.0 fusion.9
  91.8 11.7 %cholesky.104 = f32[128,128]{1,0:T(8,128)S(1)} custom-call(f32[128,128]{1,0:T(8,128)S(1)} %fusion.47), custom_call_target="Cholesky" | custom-call | tf_op jit(solution)/shard_map/jit(cholesky)/cholesky | solution.py:77
  104.2 0.7 fusion.58
  105.0 0.9 fusion.59
  105.9 3.0 %collective-permute-done.10 = bf16[128,128]{1,0:T(8,128)(2,1)S(1)} collective-permute-done((bf16[128,128]{1,0:T(8,128)(2,1)S(1)}, bf16[128,128]{1,0:T(8,128)(2,1)S(1)}, u32[]{:S(2)}, u32[]{:S(2)}) %collective-permute-start.10) | collective-permute-done | bytes 32800 | tf_op jit(solution)/shard_map/ppermute | solution.py:35
  109.2 11.7 %cholesky.115 = f32[128,128]{1,0:T(8,128)S(1)} custom-call(f32[128,128]{1,0:T(8,128)S(1)} %fusion.46), custom_call_target="Cholesky" | custom-call | tf_op jit(solution)/shard_map/jit(cholesky)/cholesky | solution.py:80
  121.5 0.7 fusion.60
  122.2 1.3 collective-permute-start.11
  123.5 0.9 fusion.61
  124.4 1.7 collective-permute-done.11
  126.5 11.9 %cholesky.126 = f32[128,128]{1,0:T(8,128)S(1)} custom-call(f32[128,128]{1,0:T(8,128)S(1)} %fusion.45), custom_call_target="Cholesky" | custom-call | tf_op jit(solution)/shard_map/jit(cholesky)/cholesky | solution.py:80
  139.0 0.7 select_select_fusion.3
  140.0 1.0 collective-permute-done.12
  141.4 11.7 %cholesky.137 = f32[128,128]{1,0:T(8,128)S(1)} custom-call(f32[128,128]{1,0:T(8,128)S(1)} %fusion.44), custom_call_target="Cholesky" | custom-call | tf_op jit(solution)/shard_map/jit(cholesky)/cholesky | solution.py:86
  153.8 0.7 select_select_fusion.2
  154.5 1.6 collective-permute-start.13
  156.3 2.5 %collective-permute-done.13 = f32[128,128]{1,0:T(8,128)S(1)} collective-permute-done((f32[128,128]{1,0:T(8,128)S(1)}, f32[128,128]{1,0:T(8,128)S(1)}, u32[]{:S(2)}, u32[]{:S(2)}) %collective-permute-start.13) | collective-permute-done | bytes 65568 | tf_op jit(solution)/shard_map/ppermute | solution.py:35
  159.2 11.7 %cholesky.148 = f32[128,128]{1,0:T(8,128)S(1)} custom-call(f32[128,128]{1,0:T(8,128)S(1)} %fusion.43), custom_call_target="Cholesky" | custom-call | tf_op jit(solution)/shard_map/jit(cholesky)/cholesky | solution.py:86
  172.2 2.7 %collective-permute-start.14 = (f32[128,128]{1,0:T(8,128)S(1)}, f32[128,128]{1,0:T(8,128)S(1)}, u32[]{:S(2)}, u32[]{:S(2)}) collective-permute-start(f32[128,128]{1,0:T(8,128)S(1)} %select_select_fusion.1), channel_id=1, source_target_pairs={{0,16},{16,0},{4,20},{20,4},{8,24},{24,8},{12,28},{28,12},{1,17},{... | collective-permute-start | bytes 196616 | tf_op jit(solution)/shard_map/ppermute | solution.py:35
  175.1 2.3 %collective-permute-done.14 = f32[128,128]{1,0:T(8,128)S(1)} collective-permute-done((f32[128,128]{1,0:T(8,128)S(1)}, f32[128,128]{1,0:T(8,128)S(1)}, u32[]{:S(2)}, u32[]{:S(2)}) %collective-permute-start.14) | collective-permute-done | bytes 65568 | tf_op jit(solution)/shard_map/ppermute | solution.py:35
  177.8 12.0 %cholesky.159 = f32[128,128]{1,0:T(8,128)S(1)} custom-call(f32[128,128]{1,0:T(8,128)S(1)} %fusion.42), custom_call_target="Cholesky" | custom-call | tf_op jit(solution)/shard_map/jit(cholesky)/cholesky | solution.py:86
  190.5 0.7 fusion.62
  191.1 9.8 %custom-call.5 = f32[1,128,128]{1,2,0:T(8,128)S(1)} custom-call(f32[1,128,128]{2,1,0:T(8,128)S(1)} %get-tuple-element.8), custom_call_target="InvertDiagBlocksLowerTriangular" | custom-call | tf_op jit(solution)/shard_map/triangular_solve | solution.py:90
  201.0 0.7 copy.57
  201.7 1.4 fusion.40
  (68 shorter events, 9.6 us)
Async XLA Ops:
  0.6 13.6 %copy-start = (bf16[16,6,64,256]{3,2,1,0:T(8,128)(2,1)S(1)}, bf16[16,6,64,256]{3,2,1,0:T(8,128)(2,1)}, u32[]{:S(2)}) copy-start(bf16[16,6,64,256]{3,2,1,0:T(8,128)(2,1)} %param.5) | copy-start | bytes 9437188
  1.9 19.7 %collective-permute-start.2 = (bf16[16,64,128]{2,1,0:T(8,128)(2,1)S(1)}, bf16[16,64,128]{2,1,0:T(8,128)(2,1)}, u32[]{:S(2)}, u32[]{:S(2)}) collective-permute-start(bf16[16,64,128]{2,1,0:T(8,128)(2,1)S(1)} %convert_element_type.14), channel_id=1, source_target_pairs={{0,1},{1,2},{2,3},{3,0},{4,5},{5,6},{6,7},{7,4},{8,9},{9,10},{10,1... | collective-permute-start | bytes 786440 | tf_op jit(solution)/shard_map/ppermute | solution.py:25
  4.9 11.7 %collective-permute-start.1 = (bf16[16,64,128]{2,1,0:T(8,128)(2,1)S(1)}, bf16[16,64,128]{2,1,0:T(8,128)(2,1)}, u32[]{:S(2)}, u32[]{:S(2)}) collective-permute-start(bf16[16,64,128]{2,1,0:T(8,128)(2,1)S(1)} %convert_element_type.14), channel_id=1, source_target_pairs={{4,0},{8,4},{12,8},{16,12},{20,16},{24,20},{28,24},{5,1},{9,5},{13... | collective-permute-start | bytes 786440 | tf_op jit(solution)/shard_map/ppermute | solution.py:17
  6.2 21.9 %collective-permute-start = (bf16[16,64,128]{2,1,0:T(8,128)(2,1)S(1)}, bf16[16,64,128]{2,1,0:T(8,128)(2,1)}, u32[]{:S(2)}, u32[]{:S(2)}) collective-permute-start(bf16[16,64,128]{2,1,0:T(8,128)(2,1)S(1)} %convert_element_type.14), channel_id=1, source_target_pairs={{0,4},{4,8},{8,12},{12,16},{16,20},{20,24},{24,28},{1,5},{5,9},{9,... | collective-permute-start | bytes 786440 | tf_op jit(solution)/shard_map/ppermute | solution.py:14
  21.6 11.9 %collective-permute-start.3 = (bf16[16,64,128]{2,1,0:T(8,128)(2,1)}, bf16[16,64,128]{2,1,0:T(8,128)(2,1)}, u32[]{:S(2)}, u32[]{:S(2)}) collective-permute-start(bf16[16,64,128]{2,1,0:T(8,128)(2,1)} %collective-permute-done.2), channel_id=1, source_target_pairs={{0,1},{1,2},{2,3},{3,0},{4,5},{5,6},{6,7},{7,4},{8,9},{9,10},{10,1... | collective-permute-start | bytes 786440 | tf_op jit(solution)/shard_map/ppermute | solution.py:25
  33.5 9.6 %collective-permute-start.4 = (bf16[16,64,128]{2,1,0:T(8,128)(2,1)}, bf16[16,64,128]{2,1,0:T(8,128)(2,1)S(1)}, u32[]{:S(2)}, u32[]{:S(2)}) collective-permute-start(bf16[16,64,128]{2,1,0:T(8,128)(2,1)} %collective-permute-done.3), channel_id=1, source_target_pairs={{0,1},{1,2},{2,3},{3,0},{4,5},{5,6},{6,7},{7,4},{8,9},{9,10},{10,1... | collective-permute-start | bytes 786440 | tf_op jit(solution)/shard_map/ppermute | solution.py:25
  47.4 14.7 %collective-permute-start.7 = (bf16[16,64,128]{2,1,0:T(8,128)(2,1)S(1)}, bf16[16,64,128]{2,1,0:T(8,128)(2,1)}, u32[]{:S(2)}, u32[]{:S(2)}) collective-permute-start(bf16[16,64,128]{2,1,0:T(8,128)(2,1)S(1)} %get-tuple-element.15), channel_id=1, source_target_pairs={{0,1},{1,2},{2,3},{3,0},{4,5},{5,6},{6,7},{7,4},{8,9},{9,10},{10,1... | collective-permute-start | bytes 786440 | tf_op jit(solution)/shard_map/ppermute | solution.py:25
  49.7 7.4 %collective-permute-start.6 = (bf16[16,64,128]{2,1,0:T(8,128)(2,1)S(1)}, bf16[16,64,128]{2,1,0:T(8,128)(2,1)}, u32[]{:S(2)}, u32[]{:S(2)}) collective-permute-start(bf16[16,64,128]{2,1,0:T(8,128)(2,1)S(1)} %get-tuple-element.15), channel_id=1, source_target_pairs={{4,0},{8,4},{12,8},{16,12},{20,16},{24,20},{28,24},{5,1},{9,5},{13... | collective-permute-start | bytes 786440 | tf_op jit(solution)/shard_map/ppermute | solution.py:17
  51.0 17.4 %collective-permute-start.5 = (bf16[16,64,128]{2,1,0:T(8,128)(2,1)S(1)}, bf16[16,64,128]{2,1,0:T(8,128)(2,1)}, u32[]{:S(2)}, u32[]{:S(2)}) collective-permute-start(bf16[16,64,128]{2,1,0:T(8,128)(2,1)S(1)} %get-tuple-element.15), channel_id=1, source_target_pairs={{0,4},{4,8},{8,12},{12,16},{16,20},{20,24},{24,28},{1,5},{5,9},{9,... | collective-permute-start | bytes 786440 | tf_op jit(solution)/shard_map/ppermute | solution.py:14
  64.7 9.9 %collective-permute-start.8 = (bf16[16,64,128]{2,1,0:T(8,128)(2,1)}, bf16[16,64,128]{2,1,0:T(8,128)(2,1)}, u32[]{:S(2)}, u32[]{:S(2)}) collective-permute-start(bf16[16,64,128]{2,1,0:T(8,128)(2,1)} %collective-permute-done.7), channel_id=1, source_target_pairs={{0,1},{1,2},{2,3},{3,0},{4,5},{5,6},{6,7},{7,4},{8,9},{9,10},{10,1... | collective-permute-start | bytes 786440 | tf_op jit(solution)/shard_map/ppermute | solution.py:25
  77.2 9.0 %collective-permute-start.9 = (bf16[16,64,128]{2,1,0:T(8,128)(2,1)}, bf16[16,64,128]{2,1,0:T(8,128)(2,1)S(1)}, u32[]{:S(2)}, u32[]{:S(2)}) collective-permute-start(bf16[16,64,128]{2,1,0:T(8,128)(2,1)} %collective-permute-done.8), channel_id=1, source_target_pairs={{0,1},{1,2},{2,3},{3,0},{4,5},{5,6},{6,7},{7,4},{8,9},{9,10},{10,1... | collective-permute-start | bytes 786440 | tf_op jit(solution)/shard_map/ppermute | solution.py:25
  89.9 0.8 copy-start.1
  91.7 110.0 %copy-start.2 = (f32[16,64,128]{2,1,0:T(8,128)S(1)}, f32[16,64,128]{2,1,0:T(8,128)}, u32[]{:S(2)}) copy-start(f32[16,64,128]{2,1,0:T(8,128)} %copy-done.1) | copy-start | bytes 1572868
  104.9 4.0 %collective-permute-start.10 = (bf16[128,128]{1,0:T(8,128)(2,1)S(1)}, bf16[128,128]{1,0:T(8,128)(2,1)S(1)}, u32[]{:S(2)}, u32[]{:S(2)}) collective-permute-start(bf16[128,128]{1,0:T(8,128)(2,1)S(1)} %fusion.58), channel_id=1, source_target_pairs={{0,1},{1,0},{2,3},{3,2},{4,5},{5,4},{6,7},{7,6},{8,9},{9,8},{10,11... | collective-permute-start | bytes 98312 | tf_op jit(solution)/shard_map/ppermute | solution.py:35
  122.2 4.0 %collective-permute-start.11 = (bf16[128,128]{1,0:T(8,128)(2,1)S(1)}, bf16[128,128]{1,0:T(8,128)(2,1)S(1)}, u32[]{:S(2)}, u32[]{:S(2)}) collective-permute-start(bf16[128,128]{1,0:T(8,128)(2,1)S(1)} %fusion.60), channel_id=1, source_target_pairs={{0,2},{2,0},{1,3},{3,1},{4,6},{6,4},{5,7},{7,5},{8,10},{10,8},{9,1... | collective-permute-start | bytes 98312 | tf_op jit(solution)/shard_map/ppermute | solution.py:35
  139.7 1.3 collective-permute-start.12
  154.5 4.3 %collective-permute-start.13 = (f32[128,128]{1,0:T(8,128)S(1)}, f32[128,128]{1,0:T(8,128)S(1)}, u32[]{:S(2)}, u32[]{:S(2)}) collective-permute-start(f32[128,128]{1,0:T(8,128)S(1)} %select_select_fusion.2), channel_id=1, source_target_pairs={{0,8},{8,0},{4,12},{12,4},{16,24},{24,16},{20,28},{28,20},{1,9},{9... | collective-permute-start | bytes 196616 | tf_op jit(solution)/shard_map/ppermute | solution.py:35
  172.2 5.2 %collective-permute-start.14 = (f32[128,128]{1,0:T(8,128)S(1)}, f32[128,128]{1,0:T(8,128)S(1)}, u32[]{:S(2)}, u32[]{:S(2)}) collective-permute-start(f32[128,128]{1,0:T(8,128)S(1)} %select_select_fusion.1), channel_id=1, source_target_pairs={{0,16},{16,0},{4,20},{20,4},{8,24},{24,8},{12,28},{28,12},{1,17},{... | collective-permute-start | bytes 196616 | tf_op jit(solution)/shard_map/ppermute | solution.py:35
where the time goes:
time: 204 us; the launch traced here: 203 us
  other arithmetic  90.6 us (44%)
  matrix products  35.3 us (17%)
  local copies, waits for them, and re-layouts  31.6 us (15%)
  starting transfers between devices  24.2 us (12%)
  waiting for transfers between devices  20.4 us (10%)
    another operation x15, other arithmetic, on_device(): jnp.linalg.cholesky(jnp.dot(lower, lower.T, precision=precise) + jnp.dot(...  62.4 us
    dot_general x12, matrix products, couple_source(): jnp.einsum('rik,rkn->rin', coupling, picked, preferred_element_type=jnp.f...  29.3 us
    gather x12, local copies, waits for them, and re-layouts, couple_source(): piece[columns]  27.7 us
    another operation x3, other arithmetic, on_device(): lower = jnp.linalg.cholesky(local_gram)  12.4 us
    ppermute x5, waiting for transfers between devices, from_partner(): return lax.ppermute(block, axis, route)  10.5 us
    ppermute x6, waiting for transfers between devices, shifted(): return lax.ppermute(value, axis, pairs)  9.83 us
    another operation x1, other arithmetic, on_device(): lax.linalg.triangular_solve(lower, flat, left_side=False, lower=True, tra...  9.81 us
    ppermute x6, starting transfers between devices, shifted(): return lax.ppermute(value, axis, pairs)  8.43 us
  transfers between devices with their start and end apart: 15, of which 8 were waited for; matrix products, arithmetic and copies ran while one was open for 25% of the time, Pallas kernels for 0%

commit v1 on v0

v1 whole, which is shorter than its diff:
```python
import functools

import jax
import jax.numpy as jnp
from jax import lax
from jax.experimental import pallas as pl
from jax.experimental.pallas import tpu as pltpu
from jax.sharding import PartitionSpec as P

precise = lax.Precision.HIGHEST
LANES = 128
SUB = 8
VMEM_LIMIT = 40 * 1024 * 1024
vmem = pl.BlockSpec(memory_space=pltpu.VMEM)
smem = pl.BlockSpec(memory_space=pltpu.SMEM)


def pair_exchange(value, offset):
    count = lax.axis_size("group")
    route = []
    for low in range(offset, count - 1, 2):
        route += [(low, low + 1), (low + 1, low)]
    return lax.ppermute(value, "group", route)


def potential_columns(potential_ref):
    return jnp.transpose(potential_ref[...])


def couple_row(place_ref, columns_ref, hamiltonian_ref, pieces, row, total):
    sources, per_source = hamiltonian_ref.shape[1], hamiltonian_ref.shape[3] // hamiltonian_ref.shape[2]
    for source, block_of in pieces:
        first = (row * sources + source) * per_source
        picked = jnp.concatenate(
            [block_of(columns_ref[first + slot]) for slot in range(per_source)], axis=0
        )
        product = jnp.dot(
            hamiltonian_ref[row, source], picked, preferred_element_type=jnp.float32
        )
        total = product if total is None else total + product
    return total


def all_pieces(place_ref, gathered_ref, inner_ref, outer_ref):
    cycle_size = gathered_ref.shape[0]
    odd = place_ref[0]
    pieces = [
        (source, functools.partial(lambda source, block: gathered_ref[source, block], source))
        for source in range(cycle_size)
    ]
    pieces.append((cycle_size + 1 - odd, lambda block: inner_ref[block]))
    pieces.append((cycle_size + odd, lambda block: outer_ref[block]))
    return pieces


def first_kernel(
    place_ref, columns_ref, hamiltonian_ref, gathered_ref, inner_ref, outer_ref,
    potential_ref, trial_ref, once_ref, round_ref,
):
    shard_blocks, _, block_size, _ = hamiltonian_ref.shape
    weights = potential_columns(potential_ref)
    pieces = all_pieces(place_ref, gathered_ref, inner_ref, outer_ref)
    per_column = LANES // block_size
    for row in range(shard_blocks):
        column, part = divmod(row, per_column)
        weight = weights[part * block_size : (part + 1) * block_size, column : column + 1]
        rows = pl.ds(row * block_size, block_size)
        total = couple_row(place_ref, columns_ref, hamiltonian_ref, pieces, row, None)
        once = 0.5 * (total + weight * trial_ref[rows, :])
        once_ref[rows, :] = once
        round_ref[row] = once.astype(jnp.bfloat16)


def second_kernel(
    place_ref, columns_ref, hamiltonian_ref, gathered_ref, inner_ref, outer_ref,
    potential_ref, trial_ref, once_ref, filtered_ref, gram_ref,
):
    shard_blocks, _, block_size, _ = hamiltonian_ref.shape
    weights = potential_columns(potential_ref)
    pieces = all_pieces(place_ref, gathered_ref, inner_ref, outer_ref)
    per_column = LANES // block_size
    for row in range(shard_blocks):
        column, part = divmod(row, per_column)
        weight = weights[part * block_size : (part + 1) * block_size, column : column + 1]
        rows = pl.ds(row * block_size, block_size)
        total = couple_row(place_ref, columns_ref, hamiltonian_ref, pieces, row, None)
        filtered_ref[rows, :] = total + weight * once_ref[rows, :] - trial_ref[rows, :]
    flat = filtered_ref[...]
    gram_ref[...] = lax.dot_general(
        flat, flat, (((0,), (0,)), ((), ())), precision=precise,
        preferred_element_type=jnp.float32,
    )


def factor_kernel(rows_total, gram_ref, filtered_ref, ortho_ref, upper_ref, inverse_ref):
    size = gram_ref.shape[0]
    panels = size // SUB
    shape = (SUB, size)
    row_index = lax.broadcasted_iota(jnp.int32, shape, 0)
    lane_index = lax.broadcasted_iota(jnp.int32, shape, 1)

    def along_lanes(panel, lane):
        return jnp.broadcast_to(panel[:, lane : lane + 1], shape)

    def along_rows(panel, row):
        return jnp.broadcast_to(panel[row : row + 1, :], shape)

    matrix = [gram_ref[pl.ds(k * SUB, SUB), :] * (1.0 / rows_total) for k in range(panels)]
    inverse = [
        jnp.where(lane_index == row_index + k * SUB, 1.0, 0.0).astype(jnp.float32)
        for k in range(panels)
    ]
    for k in range(panels):
        block = [along_lanes(matrix[k], k * SUB + c) for c in range(SUB)]
        below = {
            p: [along_lanes(matrix[p], k * SUB + c) for c in range(SUB)]
            for p in range(k + 1, panels)
        }
        pivots = jnp.ones(shape, jnp.float32)
        for j in range(SUB):
            pivot = along_rows(block[j], j)
            reciprocal = 1.0 / pivot
            pivots = jnp.where(row_index == j, pivot, pivots)
            lower_part = jnp.where(row_index > j, block[j], 0.0)
            row = along_rows(matrix[k], j) * reciprocal
            inverse_row = along_rows(inverse[k], j) * reciprocal
            for c in range(j + 1, SUB):
                factor = along_rows(block[c], j) * reciprocal
                block[c] = block[c] - block[j] * factor
                for p in below:
                    below[p][c] = below[p][c] - below[p][j] * factor
            matrix[k] = matrix[k] - lower_part * row
            inverse[k] = inverse[k] - lower_part * inverse_row
            for p in below:
                matrix[p] = matrix[p] - below[p][j] * row
                inverse[p] = inverse[p] - below[p][j] * inverse_row
        scale = lax.rsqrt(pivots)
        upper = jnp.where(lane_index >= row_index + k * SUB, matrix[k] * scale, 0.0)
        upper_ref[pl.ds(k * SUB, SUB), :] = upper
        inverse_ref[pl.ds(k * SUB, SUB), :] = inverse[k] * scale
    ortho_ref[...] = lax.dot_general(
        filtered_ref[...], inverse_ref[...], (((1,), (1,)), ((), ())), precision=precise,
        preferred_element_type=jnp.float32,
    )


def call(kernel, out_shape, in_specs, scratch=()):
    return pl.pallas_call(
        kernel,
        out_shape=out_shape,
        in_specs=in_specs,
        out_specs=jax.tree.map(lambda _: vmem, out_shape),
        scratch_shapes=list(scratch),
        compiler_params=pltpu.CompilerParams(vmem_limit_bytes=VMEM_LIMIT),
    )


def on_device(hamiltonian, block_columns, potential, trial_slab):
    shard_blocks, _, block_size, _ = hamiltonian.shape
    flat_rows, states = trial_slab.shape
    columns = block_columns.reshape(-1)
    weights = potential.reshape(-1, LANES)
    rows_total = flat_rows * lax.axis_size("group") * lax.axis_size("blk")
    place = (lax.axis_index("group") % 2).reshape(1).astype(jnp.int32)
    flat = jax.ShapeDtypeStruct((flat_rows, states), jnp.float32)
    rounded = jax.ShapeDtypeStruct((shard_blocks, block_size, states), jnp.bfloat16)
    square = jax.ShapeDtypeStruct((states, states), jnp.float32)

    def exchanged(value):
        return lax.all_gather(value, "blk"), pair_exchange(value, 0), pair_exchange(value, 1)

    start = trial_slab.reshape(shard_blocks, block_size, states).astype(jnp.bfloat16)
    once, once_round = call(first_kernel, (flat, rounded), [smem, smem] + [vmem] * 6)(
        place, columns, hamiltonian, *exchanged(start), weights, trial_slab
    )
    filtered, gram = call(second_kernel, (flat, square), [smem, smem] + [vmem] * 7)(
        place, columns, hamiltonian, *exchanged(once_round), weights, trial_slab, once
    )
    gram = lax.psum(gram, ("group", "blk"))
    return call(
        functools.partial(factor_kernel, rows_total),
        (flat, square),
        [vmem, vmem],
        [pltpu.VMEM((states, states), jnp.float32)],
    )(gram, filtered)


def solution(mesh):
    placed = (
        P(("group", "blk"), None, None, None),
        P(("group", "blk"), None, None),
        P(("group", "blk")),
        P(("group", "blk"), None),
    )
    return jax.shard_map(
        on_device,
        mesh=mesh,
        in_specs=placed,
        out_specs=(P(("group", "blk"), None), P()),
        check_vma=False,
    )
```

time: 204 us -> 217 us (1.064)
  waiting for transfers between devices: 20.4 us -> 164 us
  other arithmetic: 90.6 us -> 1.77 us
  matrix products: 35.3 us -> 0 us
  starting transfers between devices: 24.2 us -> 8.81 us
  local copies, waits for them, and re-layouts: 31.6 us -> 16.6 us
  between operations: 0.97 us -> 13.8 us
  Pallas kernels: 0 us -> 10.2 us
    psum x0 -> x1, waiting for transfers between devices: none -> 118 us  [on_device(): gram = lax.psum(gram, ('group', 'blk'))]
    another operation x19 -> x0, other arithmetic: 84.6 us -> none  [the longest x15 62.4 us: on_device(): jnp.linalg.cholesky(jnp.dot(lower, lower.T, precision=precise) + jnp.dot(...]
    all_gather x0 -> x2, waiting for transfers between devices: none -> 44.6 us  [exchanged(): lax.all_gather(value, 'blk')]
    dot_general x23 -> x0, matrix products: 34 us -> none  [the longest x12 29.3 us: couple_source(): jnp.einsum('rik,rkn->rin', coupling, picked, preferred_element_type=jnp.f...]
    gather x12 -> x0, local copies, waits for them, and re-layouts: 27.7 us -> none  [couple_source(): piece[columns]]
    ppermute x15 -> x4, waiting for transfers between devices: 20.4 us -> 1.8 us  [pair_exchange(): return lax.ppermute(value, 'group', route)]
    ppermute x15 -> x4, starting transfers between devices: 24.2 us -> 8.69 us  [pair_exchange(): return lax.ppermute(value, 'group', route)]
    unnamed x7 -> x37, local copies, waits for them, and re-layouts: 1.53 us -> 16.5 us
  transfers between devices with their start and end apart: 15 -> 7, of which waited for: 8 -> 5; matrix products, arithmetic and copies ran while one was open for 25% -> 0% of each run, Pallas kernels for 0% -> 0%
where the time goes in v1:
time: 217 us; the launch traced here: 215 us
  waiting for transfers between devices  164 us (76%)
  local copies, waits for them, and re-layouts  16.6 us (8%)
  between operations  13.8 us (6%)
  Pallas kernels  10.2 us (5%)
  starting transfers between devices  8.81 us (4%)
    psum x1, waiting for transfers between devices, on_device(): gram = lax.psum(gram, ('group', 'blk'))  118 us
    all_gather x2, waiting for transfers between devices, exchanged(): lax.all_gather(value, 'blk')  44.6 us
    unnamed x37, local copies, waits for them, and re-layouts  16.5 us
    ppermute x4, starting transfers between devices, pair_exchange(): return lax.ppermute(value, 'group', route)  8.69 us
    pallas_call x1, Pallas kernels, on_device(): call(functools.partial(factor_kernel, rows_total), (flat, square), [vmem,...  5.38 us
  transfers between devices with their start and end apart: 7, of which 5 were waited for; matrix products, arithmetic and copies ran while one was open for 0% of the time, Pallas kernels for 0%

profile of v1, /device:TPU:0, one launch (start us, length us, event | category | flops | bytes accessed | tf_op | source)
XLA Modules:
  0.0 215.3 jit_solution(13607065345963047454)
XLA Ops:
  7.2 0.0 all-gather.4.cloned.1.call-start
  7.2 1.8 convert_element_type.16
  9.0 0.0 copy-start.17
  9.0 0.0 all-gather.4.cloned.1.call-update
  9.0 0.0 all-gather.6.cloned.1.call-start
  9.1 0.7 collective-permute-start.1
  9.7 4.4 %collective-permute-start = (bf16[16,64,128]{2,1,0:T(8,128)(2,1)}, bf16[16,64,128]{2,1,0:T(8,128)(2,1)S(1)}, u32[]{:S(2)}, u32[]{:S(2)}) collective-permute-start(bf16[16,64,128]{2,1,0:T(8,128)(2,1)} %bitcast.10), channel_id=1, source_target_pairs={{0,4},{4,0},{8,12},{12,8},{16,20},{20,16},{24,28},{28,24},{1,5},{5... | collective-permute-start | bytes 786440 | tf_op jit(solution)/shard_map/ppermute | solution.py:23
  14.2 0.8 copy.7
  15.0 0.1 reshape.27.columns_ref
  15.1 0.0 collective-permute-done.1.outer_ref
  15.1 0.4 collective-permute-done.inner_ref
  15.6 0.0 copy-start.10
  15.6 0.7 copy-done.10
  16.3 23.5 %all-gather.4.cloned.1.call-done.gathered_ref = bf16[4,16,64,128]{3,2,1,0:T(8,128)(2,1)} async-done(((bf16[1,16,64,128]{3,2,1,0:T(8,128)(2,1)}), bf16[4,16,64,128]{3,2,1,0:T(8,128)(2,1)}) %all-gather.4.cloned.1.call-update) | async-done | bytes 1048592 | tf_op jit(solution)/shard_map/all_gather | solution.py:170
  39.8 0.0 copy-start
  39.8 1.9 copy-done
  41.7 0.0 copy-start.2
  41.7 1.0 copy-done.2
  42.7 0.0 copy-start.5
  42.7 1.2 copy-done.5
  43.9 0.0 copy-start.11
  43.9 0.9 copy-done.11
  44.9 0.0 copy-start.16
  44.9 0.7 copy-done.16
  45.6 0.0 copy-start.1
  45.6 1.9 shard_map.59
  47.4 0.0 copy-start.6
  47.4 0.8 copy-done.6
  48.2 0.0 copy-start.14
  48.2 0.7 copy-done.14
  48.9 0.0 all-gather.6.cloned.1.call-update
  49.0 0.0 all-reduce.2.cloned.1.call-start
  49.0 0.7 collective-permute-start.3
  49.7 2.9 %collective-permute-start.2 = (bf16[16,64,128]{2,1,0:T(8,128)(2,1)}, bf16[16,64,128]{2,1,0:T(8,128)(2,1)S(1)}, u32[]{:S(2)}, u32[]{:S(2)}) collective-permute-start(bf16[16,64,128]{2,1,0:T(8,128)(2,1)} %copy-done.14), channel_id=1, source_target_pairs={{0,4},{4,0},{8,12},{12,8},{16,20},{20,16},{24,28},{28,24},{1,5},{5... | collective-permute-start | bytes 786440 | tf_op jit(solution)/shard_map/ppermute | solution.py:23
  52.6 0.0 collective-permute-done.3.outer_ref
  52.6 1.4 collective-permute-done.2.inner_ref
  54.0 0.0 copy-start.12
  54.0 0.7 copy-done.12
  54.7 21.1 %all-gather.6.cloned.1.call-done = bf16[64,64,128]{2,1,0:T(8,128)(2,1)} async-done(((bf16[16,64,128]{2,1,0:T(8,128)(2,1)}), bf16[64,64,128]{2,1,0:T(8,128)(2,1)}) %all-gather.6.cloned.1.call-update) | async-done | bytes 1048592 | tf_op jit(solution)/shard_map/all_gather | solution.py:170
  75.7 0.0 copy-done.17
  75.7 0.0 copy-done.1
  75.8 0.0 copy-start.3
  75.8 1.0 copy-done.3
  76.8 0.0 copy-start.4
  76.8 1.2 copy-done.4
  78.0 0.0 copy-start.7
  78.0 1.0 copy-done.7
  79.1 0.0 copy-start.13
  79.1 0.9 copy-done.13
  80.0 3.0 %shard_map.60 = (f32[1024,128]{1,0:T(8,128)S(1)}, f32[128,128]{1,0:T(8,128)}) custom-call(s32[1]{0:T(128)} %bitcast.place_ref, s32[384]{0:T(512)S(1)} %reshape.27.columns_ref, bf16[16,6,64,256]{3,2,1,0:T(8,128)(2,1)S(1)} %copy-done.1, bf16[4,16,64,128]{3,2,1,0:T(8,128)(2,1)S(1)} %bitcast.5, bf16[16,64,128]{2,1,0:T(8,128)(2,1)S(1)} %copy-done.13, ...), custom_call_target="tpu_custom_call" | custom-call | tf_op jit(solution)/shard_map/pallas_call | solution.py:176
  83.0 0.0 copy-start.8
  83.0 0.8 copy-done.8
  83.8 0.0 all-reduce.2.cloned.1.call-update
  83.8 117.7 %all-reduce.2.cloned.1.call-done.gram_ref = f32[128,128]{1,0:T(8,128)} async-done(((f32[128,128]{1,0:T(8,128)}), f32[128,128]{1,0:T(8,128)}) %all-reduce.2.cloned.1.call-update) | async-done | bytes 65552 | tf_op jit(solution)/shard_map/psum | solution.py:179
  201.5 0.0 copy-start.9
  201.5 1.0 copy-done.9
  202.5 0.0 copy-start.15
  202.5 0.8 copy-done.15
  203.4 5.4 %shard_map.61 = (f32[1024,128]{1,0:T(8,128)}, f32[128,128]{1,0:T(8,128)}) custom-call(f32[128,128]{1,0:T(8,128)S(1)} %copy-done.15, f32[1024,128]{1,0:T(8,128)S(1)} %copy-done.9), custom_call_target="tpu_custom_call" | custom-call | tf_op jit(solution)/shard_map/pallas_call | solution.py:180
Async XLA Ops:
  7.2 32.6 %all-gather.4.cloned.1.call-start = ((), (), s32[]{:S(2)}) async-start(), calls=%async_computation | async-start | bytes 1310720 | tf_op jit(solution)/shard_map/all_gather | solution.py:170
  9.0 66.8 %copy-start.17 = (f32[1024]{0:T(1024)S(1)}, f32[1024]{0:T(1024)}, u32[]{:S(2)}) copy-start(f32[1024]{0:T(1024)} %param.6) | copy-start | bytes 12292
  9.0 66.7 %all-gather.6.cloned.1.call-start = ((), (), s32[]{:S(2)}) async-start(), calls=%async_computation.2 | async-start | bytes 1310720 | tf_op jit(solution)/shard_map/all_gather | solution.py:170
  9.1 6.1 %collective-permute-start.1 = (bf16[16,64,128]{2,1,0:T(8,128)(2,1)}, bf16[16,64,128]{2,1,0:T(8,128)(2,1)S(1)}, u32[]{:S(2)}, u32[]{:S(2)}) collective-permute-start(bf16[16,64,128]{2,1,0:T(8,128)(2,1)} %bitcast.9), channel_id=1, source_target_pairs={{4,8},{8,4},{12,16},{16,12},{20,24},{24,20},{5,9},{9,5},{13,17},{1... | collective-permute-start | bytes 786440 | tf_op jit(solution)/shard_map/ppermute | solution.py:23
  9.7 5.8 %collective-permute-start = (bf16[16,64,128]{2,1,0:T(8,128)(2,1)}, bf16[16,64,128]{2,1,0:T(8,128)(2,1)S(1)}, u32[]{:S(2)}, u32[]{:S(2)}) collective-permute-start(bf16[16,64,128]{2,1,0:T(8,128)(2,1)} %bitcast.10), channel_id=1, source_target_pairs={{0,4},{4,0},{8,12},{12,8},{16,20},{20,16},{24,28},{28,24},{1,5},{5... | collective-permute-start | bytes 786440 | tf_op jit(solution)/shard_map/ppermute | solution.py:23
  15.6 0.7 copy-start.10
  39.8 1.9 copy-start
  41.7 1.0 copy-start.2
  42.7 1.2 copy-start.5
  43.9 0.9 copy-start.11
  44.9 0.7 copy-start.16
  45.6 30.2 %copy-start.1 = (bf16[16,6,64,256]{3,2,1,0:T(8,128)(2,1)S(1)}, bf16[16,6,64,256]{3,2,1,0:T(8,128)(2,1)}, u32[]{:S(2)}) copy-start(bf16[16,6,64,256]{3,2,1,0:T(8,128)(2,1)} %hamiltonian_ref.3) | copy-start | bytes 9437188
  47.4 0.8 copy-start.6
  48.2 0.7 copy-start.14
  49.0 152.5 %all-reduce.2.cloned.1.call-start = ((), (), s32[]{:S(2)}) async-start(), calls=%async_computation.1 | async-start | bytes 131072 | tf_op jit(solution)/shard_map/psum | solution.py:179
  49.0 3.6 %collective-permute-start.3 = (bf16[16,64,128]{2,1,0:T(8,128)(2,1)}, bf16[16,64,128]{2,1,0:T(8,128)(2,1)S(1)}, u32[]{:S(2)}, u32[]{:S(2)}) collective-permute-start(bf16[16,64,128]{2,1,0:T(8,128)(2,1)} %copy-done.14), channel_id=1, source_target_pairs={{4,8},{8,4},{12,16},{16,12},{20,24},{24,20},{5,9},{9,5},{13,17},{1... | collective-permute-start | bytes 786440 | tf_op jit(solution)/shard_map/ppermute | solution.py:23
  49.7 4.3 %collective-permute-start.2 = (bf16[16,64,128]{2,1,0:T(8,128)(2,1)}, bf16[16,64,128]{2,1,0:T(8,128)(2,1)S(1)}, u32[]{:S(2)}, u32[]{:S(2)}) collective-permute-start(bf16[16,64,128]{2,1,0:T(8,128)(2,1)} %copy-done.14), channel_id=1, source_target_pairs={{0,4},{4,0},{8,12},{12,8},{16,20},{20,16},{24,28},{28,24},{1,5},{5... | collective-permute-start | bytes 786440 | tf_op jit(solution)/shard_map/ppermute | solution.py:23
  54.0 0.7 copy-start.12
  75.8 1.0 copy-start.3
  76.8 1.2 copy-start.4
  78.0 1.0 copy-start.7
  79.1 0.9 copy-start.13
  83.0 0.8 copy-start.8
  201.5 1.0 copy-start.9
  202.5 0.8 copy-start.15
Sparse Core Ops, SparseCore 0:
  10.4 29.3 all-gather.3
  49.1 26.6 all-gather.5
  83.9 117.4 all-reduce.1

commit v2 on v1

--- a/solution.py
+++ b/solution.py
@@ -23,16 +23,48 @@
     return lax.ppermute(value, "group", route)
 
 
+def step_bits(group, level):
+    levels = lax.axis_size("blk").bit_length() - 1
+    return jnp.where(group % 2 == 1, levels - 1 - level, level)
+
+
+def cycle_exchange(value, level):
+    groups, cycle_size = lax.axis_size("group"), lax.axis_size("blk")
+    levels = cycle_size.bit_length() - 1
+    route = []
+    for group in range(groups):
+        bit = levels - 1 - level if group % 2 else level
+        route += [
+            (group * cycle_size + index, group * cycle_size + (index ^ 1 << bit))
+            for index in range(cycle_size)
+        ]
+    return lax.ppermute(value, ("group", "blk"), route)
+
+
+def from_partner(value, axis, bit):
+    count = lax.axis_size(axis)
+    return lax.ppermute(value, axis, [(index, index ^ 1 << bit) for index in range(count)])
+
+
+def summed(value):
+    for axis in ("group", "blk"):
+        for bit in range(lax.axis_size(axis).bit_length() - 1):
+            value = value + from_partner(value, axis, bit)
+    return value
+
+
 def potential_columns(potential_ref):
     return jnp.transpose(potential_ref[...])
 
 
-def couple_row(place_ref, columns_ref, hamiltonian_ref, pieces, row, total):
+def couple_row(sources_ref, columns_ref, hamiltonian_ref, pieces, row):
     sources, per_source = hamiltonian_ref.shape[1], hamiltonian_ref.shape[3] // hamiltonian_ref.shape[2]
-    for source, block_of in pieces:
+    total = None
+    for index, piece_ref in enumerate(pieces):
+        source = sources_ref[index]
         first = (row * sources + source) * per_source
         picked = jnp.concatenate(
-            [block_of(columns_ref[first + slot]) for slot in range(per_source)], axis=0
+            [piece_ref[columns_ref[first + slot]] for slot in range(per_source)], axis=0
         )
         product = jnp.dot(
             hamiltonian_ref[row, source], picked, preferred_element_type=jnp.float32
@@ -41,49 +73,33 @@
     return total
 
 
-def all_pieces(place_ref, gathered_ref, inner_ref, outer_ref):
-    cycle_size = gathered_ref.shape[0]
-    odd = place_ref[0]
-    pieces = [
-        (source, functools.partial(lambda source, block: gathered_ref[source, block], source))
-        for source in range(cycle_size)
-    ]
-    pieces.append((cycle_size + 1 - odd, lambda block: inner_ref[block]))
-    pieces.append((cycle_size + odd, lambda block: outer_ref[block]))
-    return pieces
-
-
-def first_kernel(
-    place_ref, columns_ref, hamiltonian_ref, gathered_ref, inner_ref, outer_ref,
-    potential_ref, trial_ref, once_ref, round_ref,
-):
+def first_kernel(count, sources_ref, columns_ref, hamiltonian_ref, potential_ref, trial_ref, *refs):
+    pieces, (once_ref, round_ref) = refs[:count], refs[count:]
     shard_blocks, _, block_size, _ = hamiltonian_ref.shape
     weights = potential_columns(potential_ref)
-    pieces = all_pieces(place_ref, gathered_ref, inner_ref, outer_ref)
     per_column = LANES // block_size
     for row in range(shard_blocks):
         column, part = divmod(row, per_column)
         weight = weights[part * block_size : (part + 1) * block_size, column : column + 1]
         rows = pl.ds(row * block_size, block_size)
-        total = couple_row(place_ref, columns_ref, hamiltonian_ref, pieces, row, None)
+        total = couple_row(sources_ref, columns_ref, hamiltonian_ref, pieces, row)
         once = 0.5 * (total + weight * trial_ref[rows, :])
         once_ref[rows, :] = once
         round_ref[row] = once.astype(jnp.bfloat16)
 
 
 def second_kernel(
-    place_ref, columns_ref, hamiltonian_ref, gathered_ref, inner_ref, outer_ref,
-    potential_ref, trial_ref, once_ref, filtered_ref, gram_ref,
+    count, sources_ref, columns_ref, hamiltonian_ref, potential_ref, trial_ref, once_ref, *refs
 ):
+    pieces, (filtered_ref, gram_ref) = refs[:count], refs[count:]
     shard_blocks, _, block_size, _ = hamiltonian_ref.shape
     weights = potential_columns(potential_ref)
-    pieces = all_pieces(place_ref, gathered_ref, inner_ref, outer_ref)
     per_column = LANES // block_size
     for row in range(shard_blocks):
         column, part = divmod(row, per_column)
         weight = weights[part * block_size : (part + 1) * block_size, column : column + 1]
         rows = pl.ds(row * block_size, block_size)
-        total = couple_row(place_ref, columns_ref, hamiltonian_ref, pieces, row, None)
+        total = couple_row(sources_ref, columns_ref, hamiltonian_ref, pieces, row)
         filtered_ref[rows, :] = total + weight * once_ref[rows, :] - trial_ref[rows, :]
     flat = filtered_ref[...]
     gram_ref[...] = lax.dot_general(
@@ -161,22 +177,35 @@
     columns = block_columns.reshape(-1)
     weights = potential.reshape(-1, LANES)
     rows_total = flat_rows * lax.axis_size("group") * lax.axis_size("blk")
-    place = (lax.axis_index("group") % 2).reshape(1).astype(jnp.int32)
+    group, index = lax.axis_index("group"), lax.axis_index("blk")
+    cycle_size = lax.axis_size("blk")
+    levels = cycle_size.bit_length() - 1
+    origins = [index]
+    for level in range(levels):
+        flip = jnp.left_shift(1, step_bits(group, level))
+        origins += [jnp.bitwise_xor(origin, flip) for origin in origins]
+    odd = group % 2
+    origins += [cycle_size + 1 - odd, cycle_size + odd]
+    sources = jnp.stack(origins).astype(jnp.int32)
     flat = jax.ShapeDtypeStruct((flat_rows, states), jnp.float32)
     rounded = jax.ShapeDtypeStruct((shard_blocks, block_size, states), jnp.bfloat16)
     square = jax.ShapeDtypeStruct((states, states), jnp.float32)
 
     def exchanged(value):
-        return lax.all_gather(value, "blk"), pair_exchange(value, 0), pair_exchange(value, 1)
-
+        pieces = [value]
+        for level in range(levels):
+            pieces += [cycle_exchange(piece, level) for piece in pieces]
+        return pieces + [pair_exchange(value, 0), pair_exchange(value, 1)]
+
+    count = cycle_size + 2
     start = trial_slab.reshape(shard_blocks, block_size, states).astype(jnp.bfloat16)
-    once, once_round = call(first_kernel, (flat, rounded), [smem, smem] + [vmem] * 6)(
-        place, columns, hamiltonian, *exchanged(start), weights, trial_slab
-    )
-    filtered, gram = call(second_kernel, (flat, square), [smem, smem] + [vmem] * 7)(
-        place, columns, hamiltonian, *exchanged(once_round), weights, trial_slab, once
-    )
-    gram = lax.psum(gram, ("group", "blk"))
+    once, once_round = call(
+        functools.partial(first_kernel, count), (flat, rounded), [smem] * 2 + [vmem] * (3 + count)
+    )(sources, columns, hamiltonian, weights, trial_slab, *exchanged(start))
+    filtered, gram = call(
+        functools.partial(second_kernel, count), (flat, square), [smem] * 2 + [vmem] * (4 + count)
+    )(sources, columns, hamiltonian, weights, trial_slab, once, *exchanged(once_round))
+    gram = summed(gram)
     return call(
         functools.partial(factor_kernel, rows_total),
         (flat, square),

time: 217 us -> 64.2 us (0.30)
  waiting for transfers between devices: 164 us -> 24 us
  starting transfers between devices: 8.81 us -> 23.7 us
  between operations: 13.8 us -> 0.71 us
  local copies, waits for them, and re-layouts: 16.6 us -> 4.63 us
    psum x1 -> x0, waiting for transfers between devices: 118 us -> none  [on_device(): gram = lax.psum(gram, ('group', 'blk'))]
    all_gather x2 -> x0, waiting for transfers between devices: 44.6 us -> none  [exchanged(): lax.all_gather(value, 'blk')]
    ppermute x0 -> x11, waiting for transfers between devices: none -> 24 us  [the longest x5 12.5 us: from_partner(): lax.ppermute(value, axis, [(index, index ^ 1 << bit) for index in range(c...]
    ppermute x0 -> x11, starting transfers between devices: none -> 16.4 us  [the longest x6 9.38 us: cycle_exchange(): return lax.ppermute(value, ('group', 'blk'), route)]
    unnamed x37 -> x7, local copies, waits for them, and re-layouts: 16.5 us -> 4.44 us
  transfers between devices with their start and end apart: 7 -> 15, of which waited for: 5 -> 10; matrix products, arithmetic and copies ran while one was open for 0% -> 2% of each run, Pallas kernels for 0% -> 0%
where the time goes in v2:
time: 64.2 us; the launch traced here: 63.8 us
  waiting for transfers between devices  24 us (37%)
  starting transfers between devices  23.7 us (37%)
  Pallas kernels  9.58 us (15%)
  local copies, waits for them, and re-layouts  4.63 us (7%)
  other arithmetic  1.12 us (2%)
  between operations  0.71 us (1%)
    ppermute x5, waiting for transfers between devices, from_partner(): lax.ppermute(value, axis, [(index, index ^ 1 << bit) for index in range(c...  12.5 us
    ppermute x6, waiting for transfers between devices, cycle_exchange(): return lax.ppermute(value, ('group', 'blk'), route)  11.5 us
    ppermute x6, starting transfers between devices, cycle_exchange(): return lax.ppermute(value, ('group', 'blk'), route)  9.38 us
    ppermute x4, starting transfers between devices, pair_exchange(): return lax.ppermute(value, 'group', route)  7.31 us
    ppermute x5, starting transfers between devices, from_partner(): lax.ppermute(value, axis, [(index, index ^ 1 << bit) for index in range(c...  7.06 us
    pallas_call x1, Pallas kernels, on_device(): call(functools.partial(factor_kernel, rows_total), (flat, square), [vmem,...  5.37 us
    unnamed x7, local copies, waits for them, and re-layouts  4.44 us
    pallas_call x1, Pallas kernels, on_device(): call(functools.partial(second_kernel, count), (flat, square), [smem] * 2...  2.32 us
  transfers between devices with their start and end apart: 15, of which 10 were waited for; matrix products, arithmetic and copies ran while one was open for 2% of the time, Pallas kernels for 0%

profile of v2, /device:TPU:0, one launch (start us, length us, event | category | flops | bytes accessed | tf_op | source)
XLA Modules:
  0.0 63.8 jit_solution(13861195906822551025)
XLA Ops:
  0.6 1.1 %convert_element_type.5 = bf16[1024,128]{1,0:T(8,128)(2,1)S(1)} convert(f32[1024,128]{1,0:T(8,128)} %trial_ref.3) | non-fusion elementwise | flops 131072 | bytes 786432 | tf_op jit(solution)/shard_map/convert_element_type | solution.py:201
  1.7 3.0 %collective-permute-start = (bf16[16,64,128]{2,1,0:T(8,128)(2,1)S(1)}, bf16[16,64,128]{2,1,0:T(8,128)(2,1)S(1)}, u32[]{:S(2)}, u32[]{:S(2)}) collective-permute-start(bf16[16,64,128]{2,1,0:T(8,128)(2,1)S(1)} %bitcast.8), channel_id=1, source_target_pairs={{0,1},{1,0},{2,3},{3,2},{4,6},{5,7},{6,4},{7,5},{8,9},{9,8},{10,11... | collective-permute-start | bytes 786440 | tf_op jit(solution)/shard_map/ppermute | solution.py:41
  4.7 0.7 %collective-permute-start.4 = (bf16[16,64,128]{2,1,0:T(8,128)(2,1)S(1)}, bf16[16,64,128]{2,1,0:T(8,128)(2,1)S(1)}, u32[]{:S(2)}, u32[]{:S(2)}) collective-permute-start(bf16[16,64,128]{2,1,0:T(8,128)(2,1)S(1)} %bitcast.9), channel_id=1, source_target_pairs={{4,8},{8,4},{12,16},{16,12},{20,24},{24,20},{5,9},{9,5},{13,17},{1... | collective-permute-start | bytes 786440 | tf_op jit(solution)/shard_map/ppermute | solution.py:23
  5.4 3.0 %collective-permute-start.3 = (bf16[16,64,128]{2,1,0:T(8,128)(2,1)S(1)}, bf16[16,64,128]{2,1,0:T(8,128)(2,1)S(1)}, u32[]{:S(2)}, u32[]{:S(2)}) collective-permute-start(bf16[16,64,128]{2,1,0:T(8,128)(2,1)S(1)} %bitcast.10), channel_id=1, source_target_pairs={{0,4},{4,0},{8,12},{12,8},{16,20},{20,16},{24,28},{28,24},{1,5},{5... | collective-permute-start | bytes 786440 | tf_op jit(solution)/shard_map/ppermute | solution.py:23
  8.4 1.5 %collective-permute-start.1 = (bf16[16,64,128]{2,1,0:T(8,128)(2,1)S(1)}, bf16[16,64,128]{2,1,0:T(8,128)(2,1)S(1)}, u32[]{:S(2)}, u32[]{:S(2)}) collective-permute-start(bf16[16,64,128]{2,1,0:T(8,128)(2,1)S(1)} %bitcast.11), channel_id=1, source_target_pairs={{0,2},{1,3},{2,0},{3,1},{4,5},{5,4},{6,7},{7,6},{8,10},{9,11},{10,... | collective-permute-start | bytes 786440 | tf_op jit(solution)/shard_map/ppermute | solution.py:41
  9.9 0.0 collective-permute-done.refs_1_
  9.9 1.2 %collective-permute-start.2 = (bf16[16,64,128]{2,1,0:T(8,128)(2,1)S(1)}, bf16[16,64,128]{2,1,0:T(8,128)(2,1)S(1)}, u32[]{:S(2)}, u32[]{:S(2)}) collective-permute-start(bf16[16,64,128]{2,1,0:T(8,128)(2,1)S(1)} %collective-permute-done.refs_1_), channel_id=1, source_target_pairs={{0,2},{1,3},{2,0},{3,1},{4,5},{5,4},{6,7},{7,6},{8,10},{9,11},{10,... | collective-permute-start | bytes 786440 | tf_op jit(solution)/shard_map/ppermute | solution.py:41
  11.1 0.8 %copy.6 = s32[16,6,4]{2,1,0:T(8,128)S(1)} copy(s32[16,6,4]{0,2,1:T(4,128)} %param.5) | data formatting | bytes 3072 | tf_op args[1]
  11.9 0.1 reshape.12.columns_ref
  12.0 0.1 stack.27.sources_ref
  12.1 0.0 collective-permute-done.4.refs_5_
  12.1 0.0 collective-permute-done.3.refs_4_
  12.1 2.6 %collective-permute-done.1.refs_2_ = bf16[16,64,128]{2,1,0:T(8,128)(2,1)S(1)} collective-permute-done((bf16[16,64,128]{2,1,0:T(8,128)(2,1)S(1)}, bf16[16,64,128]{2,1,0:T(8,128)(2,1)S(1)}, u32[]{:S(2)}, u32[]{:S(2)}) %collective-permute-start.1) | collective-permute-done | bytes 262176 | tf_op jit(solution)/shard_map/ppermute | solution.py:41
  14.7 2.8 %collective-permute-done.2.refs_3_ = bf16[16,64,128]{2,1,0:T(8,128)(2,1)S(1)} collective-permute-done((bf16[16,64,128]{2,1,0:T(8,128)(2,1)S(1)}, bf16[16,64,128]{2,1,0:T(8,128)(2,1)S(1)}, u32[]{:S(2)}, u32[]{:S(2)}) %collective-permute-start.2) | collective-permute-done | bytes 262176 | tf_op jit(solution)/shard_map/ppermute | solution.py:41
  17.6 0.0 copy-start
  17.6 1.9 %copy-done = bf16[16,6,64,256]{3,2,1,0:T(8,128)(2,1)S(1)} copy-done((bf16[16,6,64,256]{3,2,1,0:T(8,128)(2,1)S(1)}, bf16[16,6,64,256]{3,2,1,0:T(8,128)(2,1)}, u32[]{:S(2)}) %copy-start) | copy-done | bytes 3145752
  19.4 0.0 copy-start.1
  19.4 1.0 %copy-done.1 = f32[1024,128]{1,0:T(8,128)S(1)} copy-done((f32[1024,128]{1,0:T(8,128)S(1)}, f32[1024,128]{1,0:T(8,128)}, u32[]{:S(2)}) %copy-start.1) | copy-done | bytes 524312
  20.5 0.0 copy-start.2
  20.5 0.7 %copy-done.2 = f32[1024]{0:T(1024)S(1)} copy-done((f32[1024]{0:T(1024)S(1)}, f32[1024]{0:T(1024)}, u32[]{:S(2)}) %copy-start.2) | copy-done | bytes 4120
  21.2 1.9 %shard_map.59 = (f32[1024,128]{1,0:T(8,128)S(1)}, bf16[16,64,128]{2,1,0:T(8,128)(2,1)S(1)}) custom-call(s32[6]{0:T(128)S(1)} %stack.27.sources_ref, s32[384]{0:T(512)S(1)} %reshape.12.columns_ref, bf16[16,6,64,256]{3,2,1,0:T(8,128)(2,1)S(1)} %copy-done, f32[8,128]{1,0:T(8,128)S(1)} %bitcast.13, f32[1024,128]{1,0:T(8,128)S(1)} %copy-done.1, ...), custom_call_target="tpu_custom_call" | custom-call | tf_op jit(solution)/shard_map/pallas_call | solution.py:202
  23.1 0.6 collective-permute-start.5
  23.7 0.7 %collective-permute-start.9 = (bf16[16,64,128]{2,1,0:T(8,128)(2,1)S(1)}, bf16[16,64,128]{2,1,0:T(8,128)(2,1)S(1)}, u32[]{:S(2)}, u32[]{:S(2)}) collective-permute-start(bf16[16,64,128]{2,1,0:T(8,128)(2,1)S(1)} %get-tuple-element.7.refs_0_), channel_id=1, source_target_pairs={{4,8},{8,4},{12,16},{16,12},{20,24},{24,20},{5,9},{9,5},{13,17},{1... | collective-permute-start | bytes 786440 | tf_op jit(solution)/shard_map/ppermute | solution.py:23
  24.3 3.0 %collective-permute-start.8 = (bf16[16,64,128]{2,1,0:T(8,128)(2,1)S(1)}, bf16[16,64,128]{2,1,0:T(8,128)(2,1)S(1)}, u32[]{:S(2)}, u32[]{:S(2)}) collective-permute-start(bf16[16,64,128]{2,1,0:T(8,128)(2,1)S(1)} %get-tuple-element.7.refs_0_), channel_id=1, source_target_pairs={{0,4},{4,0},{8,12},{12,8},{16,20},{20,16},{24,28},{28,24},{1,5},{5... | collective-permute-start | bytes 786440 | tf_op jit(solution)/shard_map/ppermute | solution.py:23
  27.3 1.5 %collective-permute-start.6 = (bf16[16,64,128]{2,1,0:T(8,128)(2,1)S(1)}, bf16[16,64,128]{2,1,0:T(8,128)(2,1)S(1)}, u32[]{:S(2)}, u32[]{:S(2)}) collective-permute-start(bf16[16,64,128]{2,1,0:T(8,128)(2,1)S(1)} %get-tuple-element.7.refs_0_), channel_id=1, source_target_pairs={{0,2},{1,3},{2,0},{3,1},{4,5},{5,4},{6,7},{7,6},{8,10},{9,11},{10,... | collective-permute-start | bytes 786440 | tf_op jit(solution)/shard_map/ppermute | solution.py:41
  28.8 0.7 %collective-permute-done.5.refs_1_ = bf16[16,64,128]{2,1,0:T(8,128)(2,1)S(1)} collective-permute-done((bf16[16,64,128]{2,1,0:T(8,128)(2,1)S(1)}, bf16[16,64,128]{2,1,0:T(8,128)(2,1)S(1)}, u32[]{:S(2)}, u32[]{:S(2)}) %collective-permute-start.5) | collective-permute-done | bytes 262176 | tf_op jit(solution)/shard_map/ppermute | solution.py:41
  29.5 1.5 %collective-permute-start.7 = (bf16[16,64,128]{2,1,0:T(8,128)(2,1)S(1)}, bf16[16,64,128]{2,1,0:T(8,128)(2,1)S(1)}, u32[]{:S(2)}, u32[]{:S(2)}) collective-permute-start(bf16[16,64,128]{2,1,0:T(8,128)(2,1)S(1)} %collective-permute-done.5.refs_1_), channel_id=1, source_target_pairs={{0,2},{1,3},{2,0},{3,1},{4,5},{5,4},{6,7},{7,6},{8,10},{9,11},{10,... | collective-permute-start | bytes 786440 | tf_op jit(solution)/shard_map/ppermute | solution.py:41
  31.0 0.0 collective-permute-done.9.refs_5_
  31.0 0.0 collective-permute-done.8.refs_4_
  31.0 2.7 %collective-permute-done.6.refs_2_ = bf16[16,64,128]{2,1,0:T(8,128)(2,1)S(1)} collective-permute-done((bf16[16,64,128]{2,1,0:T(8,128)(2,1)S(1)}, bf16[16,64,128]{2,1,0:T(8,128)(2,1)S(1)}, u32[]{:S(2)}, u32[]{:S(2)}) %collective-permute-start.6) | collective-permute-done | bytes 262176 | tf_op jit(solution)/shard_map/ppermute | solution.py:41
  33.7 2.8 %collective-permute-done.7.refs_3_ = bf16[16,64,128]{2,1,0:T(8,128)(2,1)S(1)} collective-permute-done((bf16[16,64,128]{2,1,0:T(8,128)(2,1)S(1)}, bf16[16,64,128]{2,1,0:T(8,128)(2,1)S(1)}, u32[]{:S(2)}, u32[]{:S(2)}) %collective-permute-start.7) | collective-permute-done | bytes 262176 | tf_op jit(solution)/shard_map/ppermute | solution.py:41
  36.5 2.3 %shard_map.60 = (f32[1024,128]{1,0:T(8,128)S(1)}, f32[128,128]{1,0:T(8,128)S(1)}) custom-call(s32[6]{0:T(128)S(1)} %stack.27.sources_ref, s32[384]{0:T(512)S(1)} %reshape.12.columns_ref, bf16[16,6,64,256]{3,2,1,0:T(8,128)(2,1)S(1)} %copy-done, f32[8,128]{1,0:T(8,128)S(1)} %bitcast.14, f32[1024,128]{1,0:T(8,128)S(1)} %copy-done.1, ...), custom_call_target="tpu_custom_call" | custom-call | tf_op jit(solution)/shard_map/pallas_call | solution.py:205
  38.8 0.1 collective-permute-start.10
  38.9 1.2 %collective-permute-done.10 = f32[128,128]{1,0:T(8,128)S(1)} collective-permute-done((f32[128,128]{1,0:T(8,128)S(1)}, f32[128,128]{1,0:T(8,128)S(1)}, u32[]{:S(2)}, u32[]{:S(2)}) %collective-permute-start.10) | collective-permute-done | bytes 65568 | tf_op jit(solution)/shard_map/ppermute | solution.py:46
  40.2 1.6 %collective-permute-start.11 = (f32[128,128]{1,0:T(8,128)S(1)}, f32[128,128]{1,0:T(8,128)S(1)}, u32[]{:S(2)}, u32[]{:S(2)}) collective-permute-start(f32[128,128]{1,0:T(8,128)S(1)} %add.22), channel_id=1, source_target_pairs={{0,8},{4,12},{8,0},{12,4},{16,24},{20,28},{24,16},{28,20},{1,9},{5... | collective-permute-start | bytes 196616 | tf_op jit(solution)/shard_map/ppermute | solution.py:46
  41.8 2.7 %collective-permute-done.11 = f32[128,128]{1,0:T(8,128)S(1)} collective-permute-done((f32[128,128]{1,0:T(8,128)S(1)}, f32[128,128]{1,0:T(8,128)S(1)}, u32[]{:S(2)}, u32[]{:S(2)}) %collective-permute-start.11) | collective-permute-done | bytes 65568 | tf_op jit(solution)/shard_map/ppermute | solution.py:46
  44.5 2.2 %collective-permute-start.12 = (f32[128,128]{1,0:T(8,128)S(1)}, f32[128,128]{1,0:T(8,128)S(1)}, u32[]{:S(2)}, u32[]{:S(2)}) collective-permute-start(f32[128,128]{1,0:T(8,128)S(1)} %add.23), channel_id=1, source_target_pairs={{0,16},{4,20},{8,24},{12,28},{16,0},{20,4},{24,8},{28,12},{1,17},{... | collective-permute-start | bytes 196616 | tf_op jit(solution)/shard_map/ppermute | solution.py:46
  46.7 3.0 %collective-permute-done.12 = f32[128,128]{1,0:T(8,128)S(1)} collective-permute-done((f32[128,128]{1,0:T(8,128)S(1)}, f32[128,128]{1,0:T(8,128)S(1)}, u32[]{:S(2)}, u32[]{:S(2)}) %collective-permute-start.12) | collective-permute-done | bytes 65568 | tf_op jit(solution)/shard_map/ppermute | solution.py:46
  49.8 1.6 %collective-permute-start.13 = (f32[128,128]{1,0:T(8,128)S(1)}, f32[128,128]{1,0:T(8,128)S(1)}, u32[]{:S(2)}, u32[]{:S(2)}) collective-permute-start(f32[128,128]{1,0:T(8,128)S(1)} %add.24), channel_id=1, source_target_pairs={{0,1},{1,0},{2,3},{3,2},{4,5},{5,4},{6,7},{7,6},{8,9},{9,8},{10,11... | collective-permute-start | bytes 196616 | tf_op jit(solution)/shard_map/ppermute | solution.py:46
  51.3 2.8 %collective-permute-done.13 = f32[128,128]{1,0:T(8,128)S(1)} collective-permute-done((f32[128,128]{1,0:T(8,128)S(1)}, f32[128,128]{1,0:T(8,128)S(1)}, u32[]{:S(2)}, u32[]{:S(2)}) %collective-permute-start.13) | collective-permute-done | bytes 65568 | tf_op jit(solution)/shard_map/ppermute | solution.py:46
  54.1 1.6 %collective-permute-start.14 = (f32[128,128]{1,0:T(8,128)S(1)}, f32[128,128]{1,0:T(8,128)S(1)}, u32[]{:S(2)}, u32[]{:S(2)}) collective-permute-start(f32[128,128]{1,0:T(8,128)S(1)} %add.25), channel_id=1, source_target_pairs={{0,2},{1,3},{2,0},{3,1},{4,6},{5,7},{6,4},{7,5},{8,10},{9,11},{10,... | collective-permute-start | bytes 196616 | tf_op jit(solution)/shard_map/ppermute | solution.py:46
  55.7 2.7 %collective-permute-done.14 = f32[128,128]{1,0:T(8,128)S(1)} collective-permute-done((f32[128,128]{1,0:T(8,128)S(1)}, f32[128,128]{1,0:T(8,128)S(1)}, u32[]{:S(2)}, u32[]{:S(2)}) %collective-permute-start.14) | collective-permute-done | bytes 65568 | tf_op jit(solution)/shard_map/ppermute | solution.py:46
  58.4 5.4 %shard_map.61 = (f32[1024,128]{1,0:T(8,128)}, f32[128,128]{1,0:T(8,128)}) custom-call(f32[128,128]{1,0:T(8,128)S(1)} %add.26.gram_ref, f32[1024,128]{1,0:T(8,128)S(1)} %get-tuple-element.9.filtered_ref), custom_call_target="tpu_custom_call" | custom-call | tf_op jit(solution)/shard_map/pallas_call | solution.py:209
  (5 shorter events, 0.0 us)
Async XLA Ops:
  1.7 8.2 %collective-permute-start = (bf16[16,64,128]{2,1,0:T(8,128)(2,1)S(1)}, bf16[16,64,128]{2,1,0:T(8,128)(2,1)S(1)}, u32[]{:S(2)}, u32[]{:S(2)}) collective-permute-start(bf16[16,64,128]{2,1,0:T(8,128)(2,1)S(1)} %bitcast.8), channel_id=1, source_target_pairs={{0,1},{1,0},{2,3},{3,2},{4,6},{5,7},{6,4},{7,5},{8,9},{9,8},{10,11... | collective-permute-start | bytes 786440 | tf_op jit(solution)/shard_map/ppermute | solution.py:41
  4.7 7.4 %collective-permute-start.4 = (bf16[16,64,128]{2,1,0:T(8,128)(2,1)S(1)}, bf16[16,64,128]{2,1,0:T(8,128)(2,1)S(1)}, u32[]{:S(2)}, u32[]{:S(2)}) collective-permute-start(bf16[16,64,128]{2,1,0:T(8,128)(2,1)S(1)} %bitcast.9), channel_id=1, source_target_pairs={{4,8},{8,4},{12,16},{16,12},{20,24},{24,20},{5,9},{9,5},{13,17},{1... | collective-permute-start | bytes 786440 | tf_op jit(solution)/shard_map/ppermute | solution.py:23
  5.4 6.8 %collective-permute-start.3 = (bf16[16,64,128]{2,1,0:T(8,128)(2,1)S(1)}, bf16[16,64,128]{2,1,0:T(8,128)(2,1)S(1)}, u32[]{:S(2)}, u32[]{:S(2)}) collective-permute-start(bf16[16,64,128]{2,1,0:T(8,128)(2,1)S(1)} %bitcast.10), channel_id=1, source_target_pairs={{0,4},{4,0},{8,12},{12,8},{16,20},{20,16},{24,28},{28,24},{1,5},{5... | collective-permute-start | bytes 786440 | tf_op jit(solution)/shard_map/ppermute | solution.py:23
  8.4 6.4 %collective-permute-start.1 = (bf16[16,64,128]{2,1,0:T(8,128)(2,1)S(1)}, bf16[16,64,128]{2,1,0:T(8,128)(2,1)S(1)}, u32[]{:S(2)}, u32[]{:S(2)}) collective-permute-start(bf16[16,64,128]{2,1,0:T(8,128)(2,1)S(1)} %bitcast.11), channel_id=1, source_target_pairs={{0,2},{1,3},{2,0},{3,1},{4,5},{5,4},{6,7},{7,6},{8,10},{9,11},{10,... | collective-permute-start | bytes 786440 | tf_op jit(solution)/shard_map/ppermute | solution.py:41
  9.9 7.7 %collective-permute-start.2 = (bf16[16,64,128]{2,1,0:T(8,128)(2,1)S(1)}, bf16[16,64,128]{2,1,0:T(8,128)(2,1)S(1)}, u32[]{:S(2)}, u32[]{:S(2)}) collective-permute-start(bf16[16,64,128]{2,1,0:T(8,128)(2,1)S(1)} %collective-permute-done.refs_1_), channel_id=1, source_target_pairs={{0,2},{1,3},{2,0},{3,1},{4,5},{5,4},{6,7},{7,6},{8,10},{9,11},{10,... | collective-permute-start | bytes 786440 | tf_op jit(solution)/shard_map/ppermute | solution.py:41
  17.6 1.9 %copy-start = (bf16[16,6,64,256]{3,2,1,0:T(8,128)(2,1)S(1)}, bf16[16,6,64,256]{3,2,1,0:T(8,128)(2,1)}, u32[]{:S(2)}) copy-start(bf16[16,6,64,256]{3,2,1,0:T(8,128)(2,1)} %hamiltonian_ref.3) | copy-start | bytes 9437188
  19.4 1.0 %copy-start.1 = (f32[1024,128]{1,0:T(8,128)S(1)}, f32[1024,128]{1,0:T(8,128)}, u32[]{:S(2)}) copy-start(f32[1024,128]{1,0:T(8,128)} %trial_ref.3) | copy-start | bytes 1572868
  20.5 0.7 %copy-start.2 = (f32[1024]{0:T(1024)S(1)}, f32[1024]{0:T(1024)}, u32[]{:S(2)}) copy-start(f32[1024]{0:T(1024)} %param.6) | copy-start | bytes 12292
  23.1 6.4 %collective-permute-start.5 = (bf16[16,64,128]{2,1,0:T(8,128)(2,1)S(1)}, bf16[16,64,128]{2,1,0:T(8,128)(2,1)S(1)}, u32[]{:S(2)}, u32[]{:S(2)}) collective-permute-start(bf16[16,64,128]{2,1,0:T(8,128)(2,1)S(1)} %get-tuple-element.7.refs_0_), channel_id=1, source_target_pairs={{0,1},{1,0},{2,3},{3,2},{4,6},{5,7},{6,4},{7,5},{8,9},{9,8},{10,11... | collective-permute-start | bytes 786440 | tf_op jit(solution)/shard_map/ppermute | solution.py:41
  23.7 7.4 %collective-permute-start.9 = (bf16[16,64,128]{2,1,0:T(8,128)(2,1)S(1)}, bf16[16,64,128]{2,1,0:T(8,128)(2,1)S(1)}, u32[]{:S(2)}, u32[]{:S(2)}) collective-permute-start(bf16[16,64,128]{2,1,0:T(8,128)(2,1)S(1)} %get-tuple-element.7.refs_0_), channel_id=1, source_target_pairs={{4,8},{8,4},{12,16},{16,12},{20,24},{24,20},{5,9},{9,5},{13,17},{1... | collective-permute-start | bytes 786440 | tf_op jit(solution)/shard_map/ppermute | solution.py:23
  24.3 6.7 %collective-permute-start.8 = (bf16[16,64,128]{2,1,0:T(8,128)(2,1)S(1)}, bf16[16,64,128]{2,1,0:T(8,128)(2,1)S(1)}, u32[]{:S(2)}, u32[]{:S(2)}) collective-permute-start(bf16[16,64,128]{2,1,0:T(8,128)(2,1)S(1)} %get-tuple-element.7.refs_0_), channel_id=1, source_target_pairs={{0,4},{4,0},{8,12},{12,8},{16,20},{20,16},{24,28},{28,24},{1,5},{5... | collective-permute-start | bytes 786440 | tf_op jit(solution)/shard_map/ppermute | solution.py:23
  27.3 6.4 %collective-permute-start.6 = (bf16[16,64,128]{2,1,0:T(8,128)(2,1)S(1)}, bf16[16,64,128]{2,1,0:T(8,128)(2,1)S(1)}, u32[]{:S(2)}, u32[]{:S(2)}) collective-permute-start(bf16[16,64,128]{2,1,0:T(8,128)(2,1)S(1)} %get-tuple-element.7.refs_0_), channel_id=1, source_target_pairs={{0,2},{1,3},{2,0},{3,1},{4,5},{5,4},{6,7},{7,6},{8,10},{9,11},{10,... | collective-permute-start | bytes 786440 | tf_op jit(solution)/shard_map/ppermute | solution.py:41
  29.5 7.0 %collective-permute-start.7 = (bf16[16,64,128]{2,1,0:T(8,128)(2,1)S(1)}, bf16[16,64,128]{2,1,0:T(8,128)(2,1)S(1)}, u32[]{:S(2)}, u32[]{:S(2)}) collective-permute-start(bf16[16,64,128]{2,1,0:T(8,128)(2,1)S(1)} %collective-permute-done.5.refs_1_), channel_id=1, source_target_pairs={{0,2},{1,3},{2,0},{3,1},{4,5},{5,4},{6,7},{7,6},{8,10},{9,11},{10,... | collective-permute-start | bytes 786440 | tf_op jit(solution)/shard_map/ppermute | solution.py:41
  38.8 1.3 %collective-permute-start.10 = (f32[128,128]{1,0:T(8,128)S(1)}, f32[128,128]{1,0:T(8,128)S(1)}, u32[]{:S(2)}, u32[]{:S(2)}) collective-permute-start(f32[128,128]{1,0:T(8,128)S(1)} %get-tuple-element.8), channel_id=1, source_target_pairs={{0,4},{4,0},{8,12},{12,8},{16,20},{20,16},{24,28},{28,24},{1,5},{5... | collective-permute-start | bytes 196616 | tf_op jit(solution)/shard_map/ppermute | solution.py:46
  40.2 4.3 %collective-permute-start.11 = (f32[128,128]{1,0:T(8,128)S(1)}, f32[128,128]{1,0:T(8,128)S(1)}, u32[]{:S(2)}, u32[]{:S(2)}) collective-permute-start(f32[128,128]{1,0:T(8,128)S(1)} %add.22), channel_id=1, source_target_pairs={{0,8},{4,12},{8,0},{12,4},{16,24},{20,28},{24,16},{28,20},{1,9},{5... | collective-permute-start | bytes 196616 | tf_op jit(solution)/shard_map/ppermute | solution.py:46
  44.5 5.2 %collective-permute-start.12 = (f32[128,128]{1,0:T(8,128)S(1)}, f32[128,128]{1,0:T(8,128)S(1)}, u32[]{:S(2)}, u32[]{:S(2)}) collective-permute-start(f32[128,128]{1,0:T(8,128)S(1)} %add.23), channel_id=1, source_target_pairs={{0,16},{4,20},{8,24},{12,28},{16,0},{20,4},{24,8},{28,12},{1,17},{... | collective-permute-start | bytes 196616 | tf_op jit(solution)/shard_map/ppermute | solution.py:46
  49.8 4.3 %collective-permute-start.13 = (f32[128,128]{1,0:T(8,128)S(1)}, f32[128,128]{1,0:T(8,128)S(1)}, u32[]{:S(2)}, u32[]{:S(2)}) collective-permute-start(f32[128,128]{1,0:T(8,128)S(1)} %add.24), channel_id=1, source_target_pairs={{0,1},{1,0},{2,3},{3,2},{4,5},{5,4},{6,7},{7,6},{8,9},{9,8},{10,11... | collective-permute-start | bytes 196616 | tf_op jit(solution)/shard_map/ppermute | solution.py:46
  54.1 4.3 %collective-permute-start.14 = (f32[128,128]{1,0:T(8,128)S(1)}, f32[128,128]{1,0:T(8,128)S(1)}, u32[]{:S(2)}, u32[]{:S(2)}) collective-permute-start(f32[128,128]{1,0:T(8,128)S(1)} %add.25), channel_id=1, source_target_pairs={{0,2},{1,3},{2,0},{3,1},{4,6},{5,7},{6,4},{7,5},{8,10},{9,11},{10,... | collective-permute-start | bytes 196616 | tf_op jit(solution)/shard_map/ppermute | solution.py:46

commit v3 on v2

v3 whole, which is shorter than its diff:
```python
import functools

import jax
import jax.numpy as jnp
from jax import lax
from jax.experimental import pallas as pl
from jax.experimental.pallas import tpu as pltpu
from jax.sharding import PartitionSpec as P

precise = lax.Precision.HIGHEST
LANES = 128
SUB = 8
VMEM_LIMIT = 40 * 1024 * 1024
vmem = pl.BlockSpec(memory_space=pltpu.VMEM)
smem = pl.BlockSpec(memory_space=pltpu.SMEM)


def pair_exchange(value, offset):
    count = lax.axis_size("group")
    route = []
    for low in range(offset, count - 1, 2):
        route += [(low, low + 1), (low + 1, low)]
    return lax.ppermute(value, "group", route)


def step_bits(group, level):
    levels = lax.axis_size("blk").bit_length() - 1
    return jnp.where(group % 2 == 1, levels - 1 - level, level)


def cycle_exchange(value, level):
    groups, cycle_size = lax.axis_size("group"), lax.axis_size("blk")
    levels = cycle_size.bit_length() - 1
    route = []
    for group in range(groups):
        bit = levels - 1 - level if group % 2 else level
        route += [
            (group * cycle_size + index, group * cycle_size + (index ^ 1 << bit))
            for index in range(cycle_size)
        ]
    return lax.ppermute(value, ("group", "blk"), route)


def potential_columns(potential_ref):
    return jnp.transpose(potential_ref[...])


def couple_row(sources_ref, columns_ref, hamiltonian_ref, pieces, row):
    sources, per_source = hamiltonian_ref.shape[1], hamiltonian_ref.shape[3] // hamiltonian_ref.shape[2]
    total = None
    for index, piece_ref in pieces:
        source = sources_ref[index]
        first = (row * sources + source) * per_source
        picked = jnp.concatenate(
            [piece_ref[columns_ref[first + slot]] for slot in range(per_source)], axis=0
        )
        product = jnp.dot(
            hamiltonian_ref[row, source], picked, preferred_element_type=jnp.float32
        )
        total = product if total is None else total + product
    return total


def own_kernel(
    sources_ref, columns_ref, hamiltonian_ref, own_ref, potential_ref, scaled_ref, *refs
):
    less, partial_ref = refs[:-1], refs[-1]
    shard_blocks, _, block_size, _ = hamiltonian_ref.shape
    weights = potential_columns(potential_ref)
    per_column = LANES // block_size
    for row in range(shard_blocks):
        column, part = divmod(row, per_column)
        weight = weights[part * block_size : (part + 1) * block_size, column : column + 1]
        rows = pl.ds(row * block_size, block_size)
        total = weight * scaled_ref[rows, :]
        for less_ref in less:
            total = total - less_ref[rows, :]
        partial_ref[rows, :] = total + couple_row(
            sources_ref, columns_ref, hamiltonian_ref, [(0, own_ref)], row
        )


def middle_kernel(numbers, sources_ref, columns_ref, hamiltonian_ref, partial_ref, *refs):
    pieces, sum_ref = list(zip(numbers, refs[:-1])), refs[-1]
    shard_blocks, _, block_size, _ = hamiltonian_ref.shape
    for row in range(shard_blocks):
        rows = pl.ds(row * block_size, block_size)
        sum_ref[rows, :] = partial_ref[rows, :] + couple_row(
            sources_ref, columns_ref, hamiltonian_ref, pieces, row
        )


def first_kernel(
    number, sources_ref, columns_ref, hamiltonian_ref, partial_ref, piece_ref, once_ref, round_ref
):
    shard_blocks, _, block_size, _ = hamiltonian_ref.shape
    for row in range(shard_blocks):
        rows = pl.ds(row * block_size, block_size)
        once = 0.5 * (
            partial_ref[rows, :]
            + couple_row(sources_ref, columns_ref, hamiltonian_ref, [(number, piece_ref)], row)
        )
        once_ref[rows, :] = once
        round_ref[row] = once.astype(jnp.bfloat16)


def second_kernel(
    number, sources_ref, columns_ref, hamiltonian_ref, partial_ref, piece_ref,
    filtered_ref, packed_ref,
):
    shard_blocks, _, block_size, _ = hamiltonian_ref.shape
    for row in range(shard_blocks):
        rows = pl.ds(row * block_size, block_size)
        filtered_ref[rows, :] = partial_ref[rows, :] + couple_row(
            sources_ref, columns_ref, hamiltonian_ref, [(number, piece_ref)], row
        )
    flat = filtered_ref[...]
    gram = lax.dot_general(
        flat, flat, (((0,), (0,)), ((), ())), precision=precise,
        preferred_element_type=jnp.float32,
    )
    pack(gram, packed_ref)


def pack(gram, packed_ref):
    size = gram.shape[0]
    half = size // 2
    row = lax.broadcasted_iota(jnp.int32, (half, size), 0)
    lane = lax.broadcasted_iota(jnp.int32, (half, size), 1)
    lower = gram[half:, :]
    packed_ref[pl.ds(0, half), :] = jnp.where(lane < row, pltpu.roll(lower, half, 1), gram[:half, :])
    diagonal = jnp.sum(jnp.where(lane == row + half, lower, 0.0), axis=0, keepdims=True)
    packed_ref[pl.ds(half, SUB), :] = jnp.broadcast_to(diagonal, (SUB, size))


def unpack(packed_ref):
    size = packed_ref.shape[1]
    half = size // 2
    row = lax.broadcasted_iota(jnp.int32, (size, size), 0)
    lane = lax.broadcasted_iota(jnp.int32, (size, size), 1)
    upper = packed_ref[pl.ds(0, half), :]
    both = jnp.concatenate([upper, pltpu.roll(upper, half, 1)], axis=0)
    held = ((row < half) & (lane > row)) | ((row >= half) & (lane >= half) & (lane < row))
    off_diagonal = jnp.where(held, both, 0.0)
    diagonal = jnp.where(row < half, both, packed_ref[pl.ds(half, 1), :])
    return off_diagonal + jnp.transpose(off_diagonal) + jnp.where(row == lane, diagonal, 0.0)


def inverse_of(value):
    estimate = pl.reciprocal(value, approx=True)
    estimate = estimate * (2.0 - value * estimate)
    return estimate * (2.0 - value * estimate)


def factor_kernel(rows_total, packed_ref, filtered_ref, ortho_ref, upper_ref, inverse_ref):
    size = packed_ref.shape[1]
    panels = size // SUB
    shape = (SUB, size)
    row_index = lax.broadcasted_iota(jnp.int32, shape, 0)
    lane_index = lax.broadcasted_iota(jnp.int32, shape, 1)

    def along_lanes(panel, first):
        return [jnp.broadcast_to(panel[:, first + c : first + c + 1], shape) for c in range(SUB)]

    def along_rows(panel, row):
        return jnp.broadcast_to(panel[row : row + 1, :], shape)

    gram = unpack(packed_ref) * (1.0 / rows_total)
    matrix = [gram[k * SUB : (k + 1) * SUB, :] for k in range(panels)]
    inverse = [
        jnp.where(lane_index == row_index + k * SUB, 1.0, 0.0).astype(jnp.float32)
        for k in range(panels)
    ]
    block = along_lanes(matrix[0], 0)
    for k in range(panels):
        below = {p: along_lanes(matrix[p], k * SUB) for p in range(k + 1, panels)}
        following = along_lanes(matrix[k + 1], (k + 1) * SUB) if k + 1 < panels else None
        pivots = jnp.ones(shape, jnp.float32)
        for j in range(SUB):
            pivot = along_rows(block[j], j)
            reciprocal = inverse_of(pivot)
            pivots = jnp.where(row_index == j, pivot, pivots)
            factors = {c: along_rows(block[c], j) * reciprocal for c in range(j + 1, SUB)}
            for c in factors:
                block[c] = block[c] - block[j] * factors[c]
            if following is not None:
                column = below[k + 1][j]
                for c in factors:
                    below[k + 1][c] = below[k + 1][c] - column * factors[c]
                scaled = column * reciprocal
                for c in range(SUB):
                    following[c] = following[c] - column * along_rows(scaled, c)
            lower_part = jnp.where(row_index > j, block[j], 0.0)
            row = along_rows(matrix[k], j) * reciprocal
            inverse_row = along_rows(inverse[k], j) * reciprocal
            matrix[k] = matrix[k] - lower_part * row
            inverse[k] = inverse[k] - lower_part * inverse_row
            for p in below:
                if p > k + 1:
                    for c in factors:
                        below[p][c] = below[p][c] - below[p][j] * factors[c]
                matrix[p] = matrix[p] - below[p][j] * row
                inverse[p] = inverse[p] - below[p][j] * inverse_row
        block = following
        scale = lax.rsqrt(pivots)
        upper = jnp.where(lane_index >= row_index + k * SUB, matrix[k] * scale, 0.0)
        upper_ref[pl.ds(k * SUB, SUB), :] = upper
        inverse_ref[pl.ds(k * SUB, SUB), :] = inverse[k] * scale
    ortho_ref[...] = lax.dot_general(
        filtered_ref[...], inverse_ref[...], (((1,), (1,)), ((), ())), precision=precise,
        preferred_element_type=jnp.float32,
    )


def call(kernel, out_shape, in_specs, scratch=()):
    return pl.pallas_call(
        kernel,
        out_shape=out_shape,
        in_specs=in_specs,
        out_specs=jax.tree.map(lambda _: vmem, out_shape),
        scratch_shapes=list(scratch),
        compiler_params=pltpu.CompilerParams(vmem_limit_bytes=VMEM_LIMIT),
    )


def on_device(hamiltonian, block_columns, potential, trial_slab):
    shard_blocks, _, block_size, _ = hamiltonian.shape
    flat_rows, states = trial_slab.shape
    columns = block_columns.reshape(-1)
    weights = potential.reshape(-1, LANES)
    rows_total = flat_rows * lax.axis_size("group") * lax.axis_size("blk")
    group, index = lax.axis_index("group"), lax.axis_index("blk")
    cycle_size = lax.axis_size("blk")
    levels = cycle_size.bit_length() - 1
    origins = [index]
    for level in range(levels):
        flip = jnp.left_shift(1, step_bits(group, level))
        origins += [jnp.bitwise_xor(origin, flip) for origin in origins]
    odd = group % 2
    origins += [cycle_size + 1 - odd, cycle_size + odd]
    sources = jnp.stack(origins).astype(jnp.int32)
    last = cycle_size - 1
    middle = list(range(1, last)) + [cycle_size + 1, cycle_size]
    flat = jax.ShapeDtypeStruct((flat_rows, states), jnp.float32)
    rounded = jax.ShapeDtypeStruct((shard_blocks, block_size, states), jnp.bfloat16)
    packed = jax.ShapeDtypeStruct((states // 2 + SUB, states), jnp.float32)
    square = jax.ShapeDtypeStruct((states, states), jnp.float32)

    def exchanged(value):
        pairs = [pair_exchange(value, 0), pair_exchange(value, 1)]
        pieces = [value]
        for level in range(levels):
            pieces += [cycle_exchange(piece, level) for piece in pieces]
        return pieces + pairs

    def most(pieces, *terms):
        own = call(own_kernel, flat, [smem] * 2 + [vmem] * (3 + len(terms)))(
            sources, columns, hamiltonian, pieces[0], weights, *terms
        )
        return call(
            functools.partial(middle_kernel, middle), flat,
            [smem] * 2 + [vmem] * (2 + len(middle)),
        )(sources, columns, hamiltonian, own, *[pieces[number] for number in middle])

    pieces = exchanged(trial_slab.reshape(rounded.shape).astype(jnp.bfloat16))
    partial = most(pieces, trial_slab)
    once, once_round = call(
        functools.partial(first_kernel, last), (flat, rounded), [smem] * 2 + [vmem] * 3
    )(sources, columns, hamiltonian, partial, pieces[last])
    pieces = exchanged(once_round)
    partial = most(pieces, once, trial_slab)
    filtered, gram = call(
        functools.partial(second_kernel, last), (flat, packed), [smem] * 2 + [vmem] * 3
    )(sources, columns, hamiltonian, partial, pieces[last])
    gram = lax.psum(gram, ("group", "blk"))
    return call(
        functools.partial(factor_kernel, rows_total),
        (flat, square),
        [vmem, vmem],
        [pltpu.VMEM((states, states), jnp.float32)],
    )(gram, filtered)


def solution(mesh):
    placed = (
        P(("group", "blk"), None, None, None),
        P(("group", "blk"), None, None),
        P(("group", "blk")),
        P(("group", "blk"), None),
    )
    return jax.shard_map(
        on_device,
        mesh=mesh,
        in_specs=placed,
        out_specs=(P(("group", "blk"), None), P()),
        check_vma=False,
    )
```

time: 64.2 us -> 81.8 us (1.27)
  blocking collectives: 0 us -> 39.8 us
  waiting for transfers between devices: 24 us -> 5.16 us
  starting transfers between devices: 23.7 us -> 17.4 us
  Pallas kernels: 9.58 us -> 12.5 us
    psum x0 -> x1, blocking collectives: none -> 39.8 us  [on_device(): gram = lax.psum(gram, ('group', 'blk'))]
    ppermute x5 -> x0, waiting for transfers between devices: 12.5 us -> none  [from_partner(): lax.ppermute(value, axis, [(index, index ^ 1 << bit) for index in range(c...]
    ppermute x5 -> x0, starting transfers between devices: 7.06 us -> none  [from_partner(): lax.ppermute(value, axis, [(index, index ^ 1 << bit) for index in range(c...]
    ppermute x6, waiting for transfers between devices: 11.5 us -> 5.15 us  [cycle_exchange(): return lax.ppermute(value, ('group', 'blk'), route)]
    pallas_call x2 -> x6, Pallas kernels: 4.21 us -> 7.22 us  [the longest x2 2.96 us: most(): call(functools.partial(middle_kernel, middle), flat, [smem] * 2 + [vmem]...]
    unnamed x7 -> x9, local copies, waits for them, and re-layouts: 4.44 us -> 4.44 us
  transfers between devices with their start and end apart: 15 -> 10, of which waited for: 10 -> 3; matrix products, arithmetic and copies ran while one was open for 2% -> 1% of each run, Pallas kernels for 0% -> 6%
where the time goes in v3:
time: 81.8 us; the launch traced here: 81.4 us
  blocking collectives  39.8 us (49%)
  starting transfers between devices  17.4 us (21%)
  Pallas kernels  12.5 us (15%)
  waiting for transfers between devices  5.16 us (6%)
  local copies, waits for them, and re-layouts  4.64 us (6%)
  other arithmetic  1.07 us (1%)
    psum x1, blocking collectives, on_device(): gram = lax.psum(gram, ('group', 'blk'))  39.8 us
    ppermute x6, starting transfers between devices, cycle_exchange(): return lax.ppermute(value, ('group', 'blk'), route)  10.1 us
    ppermute x4, starting transfers between devices, pair_exchange(): return lax.ppermute(value, 'group', route)  7.31 us
    pallas_call x1, Pallas kernels, on_device(): call(functools.partial(factor_kernel, rows_total), (flat, square), [vmem,...  5.28 us
    ppermute x6, waiting for transfers between devices, cycle_exchange(): return lax.ppermute(value, ('group', 'blk'), route)  5.15 us
    unnamed x9, local copies, waits for them, and re-layouts  4.44 us
    pallas_call x2, Pallas kernels, most(): call(functools.partial(middle_kernel, middle), flat, [smem] * 2 + [vmem]...  2.96 us
    pallas_call x2, Pallas kernels, most(): call(own_kernel, flat, [smem] * 2 + [vmem] * (3 + len(terms)))  1.92 us
  transfers between devices with their start and end apart: 10, of which 3 were waited for; matrix products, arithmetic and copies ran while one was open for 1% of the time, Pallas kernels for 6%

profile of v3, /device:TPU:0, one launch (start us, length us, event | category | flops | bytes accessed | tf_op | source)
XLA Modules:
  0.0 81.4 jit_solution(11919298545175719467)
XLA Ops:
  0.6 1.1 %convert_element_type.5 = bf16[1024,128]{1,0:T(8,128)(2,1)S(1)} convert(f32[1024,128]{1,0:T(8,128)} %refs_0_.1) | non-fusion elementwise | flops 131072 | bytes 786432 | tf_op jit(solution)/shard_map/convert_element_type | solution.py:265
  1.7 3.0 %collective-permute-start = (bf16[16,64,128]{2,1,0:T(8,128)(2,1)S(1)}, bf16[16,64,128]{2,1,0:T(8,128)(2,1)S(1)}, u32[]{:S(2)}, u32[]{:S(2)}) collective-permute-start(bf16[16,64,128]{2,1,0:T(8,128)(2,1)S(1)} %bitcast.8), channel_id=1, source_target_pairs={{0,1},{1,0},{2,3},{3,2},{4,6},{5,7},{6,4},{7,5},{8,9},{9,8},{10,11... | collective-permute-start | bytes 786440 | tf_op jit(solution)/shard_map/ppermute | solution.py:41
  4.7 1.5 %collective-permute-start.1 = (bf16[16,64,128]{2,1,0:T(8,128)(2,1)S(1)}, bf16[16,64,128]{2,1,0:T(8,128)(2,1)S(1)}, u32[]{:S(2)}, u32[]{:S(2)}) collective-permute-start(bf16[16,64,128]{2,1,0:T(8,128)(2,1)S(1)} %bitcast.9), channel_id=1, source_target_pairs={{0,2},{1,3},{2,0},{3,1},{4,5},{5,4},{6,7},{7,6},{8,10},{9,11},{10,... | collective-permute-start | bytes 786440 | tf_op jit(solution)/shard_map/ppermute | solution.py:41
  6.2 0.7 collective-permute-start.2
  6.9 3.0 %collective-permute-start.3 = (bf16[16,64,128]{2,1,0:T(8,128)(2,1)S(1)}, bf16[16,64,128]{2,1,0:T(8,128)(2,1)S(1)}, u32[]{:S(2)}, u32[]{:S(2)}) collective-permute-start(bf16[16,64,128]{2,1,0:T(8,128)(2,1)S(1)} %bitcast.11), channel_id=1, source_target_pairs={{0,4},{4,0},{8,12},{12,8},{16,20},{20,16},{24,28},{28,24},{1,5},{5... | collective-permute-start | bytes 786440 | tf_op jit(solution)/shard_map/ppermute | solution.py:23
  9.9 1.4 %collective-permute-done.refs_0_ = bf16[16,64,128]{2,1,0:T(8,128)(2,1)S(1)} collective-permute-done((bf16[16,64,128]{2,1,0:T(8,128)(2,1)S(1)}, bf16[16,64,128]{2,1,0:T(8,128)(2,1)S(1)}, u32[]{:S(2)}, u32[]{:S(2)}) %collective-permute-start) | collective-permute-done | bytes 262176 | tf_op jit(solution)/shard_map/ppermute | solution.py:41
  11.3 1.6 %collective-permute-start.4 = (bf16[16,64,128]{2,1,0:T(8,128)(2,1)S(1)}, bf16[16,64,128]{2,1,0:T(8,128)(2,1)S(1)}, u32[]{:S(2)}, u32[]{:S(2)}) collective-permute-start(bf16[16,64,128]{2,1,0:T(8,128)(2,1)S(1)} %collective-permute-done.refs_0_), channel_id=1, source_target_pairs={{0,2},{1,3},{2,0},{3,1},{4,5},{5,4},{6,7},{7,6},{8,10},{9,11},{10,... | collective-permute-start | bytes 786440 | tf_op jit(solution)/shard_map/ppermute | solution.py:41
  12.9 0.8 %copy.6 = s32[16,6,4]{2,1,0:T(8,128)S(1)} copy(s32[16,6,4]{0,2,1:T(4,128)} %param.5) | data formatting | bytes 3072 | tf_op args[1]
  13.7 0.1 reshape.12.columns_ref
  13.8 0.1 stack.27.sources_ref
  13.9 0.0 copy-start
  13.9 1.9 %copy-done = bf16[16,6,64,256]{3,2,1,0:T(8,128)(2,1)S(1)} copy-done((bf16[16,6,64,256]{3,2,1,0:T(8,128)(2,1)S(1)}, bf16[16,6,64,256]{3,2,1,0:T(8,128)(2,1)}, u32[]{:S(2)}) %copy-start) | copy-done | bytes 3145752
  15.8 0.0 copy-start.1
  15.8 1.0 %copy-done.1 = f32[1024,128]{1,0:T(8,128)S(1)} copy-done((f32[1024,128]{1,0:T(8,128)S(1)}, f32[1024,128]{1,0:T(8,128)}, u32[]{:S(2)}) %copy-start.1) | copy-done | bytes 524312
  16.8 0.0 copy-start.3
  16.8 0.7 copy-done.3
  17.5 1.0 %shard_map.59.partial_ref = f32[1024,128]{1,0:T(8,128)S(1)} custom-call(s32[6]{0:T(128)S(1)} %stack.27.sources_ref, s32[384]{0:T(512)S(1)} %reshape.12.columns_ref, bf16[16,6,64,256]{3,2,1,0:T(8,128)(2,1)S(1)} %copy-done, bf16[16,64,128]{2,1,0:T(8,128)(2,1)S(1)} %bitcast.12, f32[8,128]{1,0:T(8,128)S(1)} %bitcast.13, f32[1024,128]{1,0:T(8,128)S(1)} %copy-done.1), custom_call_target="tpu_custom_call" | custom-call | tf_op jit(solution)/shard_map/pallas_call | solution.py:257
  18.5 0.0 collective-permute-done.1.refs_1_
  18.5 0.0 collective-permute-done.2.refs_2_
  18.5 0.0 collective-permute-done.3.refs_3_
  18.5 1.5 %shard_map.60.partial_ref = f32[1024,128]{1,0:T(8,128)S(1)} custom-call(s32[6]{0:T(128)S(1)} %stack.27.sources_ref, s32[384]{0:T(512)S(1)} %reshape.12.columns_ref, bf16[16,6,64,256]{3,2,1,0:T(8,128)(2,1)S(1)} %copy-done, f32[1024,128]{1,0:T(8,128)S(1)} %shard_map.59.partial_ref, bf16[16,64,128]{2,1,0:T(8,128)(2,1)S(1)} %collective-permute-done.refs_0_, ...), custom_call_target="tpu_custom_call" | custom-call | tf_op jit(solution)/shard_map/pallas_call | solution.py:260
  20.0 0.0 copy-start.2
  20.0 0.0 collective-permute-done.4.piece_ref
  20.0 0.9 %shard_map.61 = (f32[1024,128]{1,0:T(8,128)S(1)}, bf16[16,64,128]{2,1,0:T(8,128)(2,1)S(1)}) custom-call(s32[6]{0:T(128)S(1)} %stack.27.sources_ref, s32[384]{0:T(512)S(1)} %reshape.12.columns_ref, bf16[16,6,64,256]{3,2,1,0:T(8,128)(2,1)S(1)} %copy-done, f32[1024,128]{1,0:T(8,128)S(1)} %shard_map.60.partial_ref, ...), custom_call_target="tpu_custom_call" | custom-call | tf_op jit(solution)/shard_map/pallas_call | solution.py:267
  20.9 1.7 %collective-permute-start.5 = (bf16[16,64,128]{2,1,0:T(8,128)(2,1)S(1)}, bf16[16,64,128]{2,1,0:T(8,128)(2,1)S(1)}, u32[]{:S(2)}, u32[]{:S(2)}) collective-permute-start(bf16[16,64,128]{2,1,0:T(8,128)(2,1)S(1)} %get-tuple-element.6.own_ref), channel_id=1, source_target_pairs={{0,1},{1,0},{2,3},{3,2},{4,6},{5,7},{6,4},{7,5},{8,9},{9,8},{10,11... | collective-permute-start | bytes 786440 | tf_op jit(solution)/shard_map/ppermute | solution.py:41
  22.6 1.3 %collective-permute-start.6 = (bf16[16,64,128]{2,1,0:T(8,128)(2,1)S(1)}, bf16[16,64,128]{2,1,0:T(8,128)(2,1)S(1)}, u32[]{:S(2)}, u32[]{:S(2)}) collective-permute-start(bf16[16,64,128]{2,1,0:T(8,128)(2,1)S(1)} %get-tuple-element.6.own_ref), channel_id=1, source_target_pairs={{0,2},{1,3},{2,0},{3,1},{4,5},{5,4},{6,7},{7,6},{8,10},{9,11},{10,... | collective-permute-start | bytes 786440 | tf_op jit(solution)/shard_map/ppermute | solution.py:41
  23.9 0.7 collective-permute-start.7
  24.6 3.0 %collective-permute-start.8 = (bf16[16,64,128]{2,1,0:T(8,128)(2,1)S(1)}, bf16[16,64,128]{2,1,0:T(8,128)(2,1)S(1)}, u32[]{:S(2)}, u32[]{:S(2)}) collective-permute-start(bf16[16,64,128]{2,1,0:T(8,128)(2,1)S(1)} %get-tuple-element.6.own_ref), channel_id=1, source_target_pairs={{0,4},{4,0},{8,12},{12,8},{16,20},{20,16},{24,28},{28,24},{1,5},{5... | collective-permute-start | bytes 786440 | tf_op jit(solution)/shard_map/ppermute | solution.py:23
  27.6 0.8 %collective-permute-done.5.refs_0_ = bf16[16,64,128]{2,1,0:T(8,128)(2,1)S(1)} collective-permute-done((bf16[16,64,128]{2,1,0:T(8,128)(2,1)S(1)}, bf16[16,64,128]{2,1,0:T(8,128)(2,1)S(1)}, u32[]{:S(2)}, u32[]{:S(2)}) %collective-permute-start.5) | collective-permute-done | bytes 262176 | tf_op jit(solution)/shard_map/ppermute | solution.py:41
  28.4 1.0 %collective-permute-start.9 = (bf16[16,64,128]{2,1,0:T(8,128)(2,1)S(1)}, bf16[16,64,128]{2,1,0:T(8,128)(2,1)S(1)}, u32[]{:S(2)}, u32[]{:S(2)}) collective-permute-start(bf16[16,64,128]{2,1,0:T(8,128)(2,1)S(1)} %collective-permute-done.5.refs_0_), channel_id=1, source_target_pairs={{0,2},{1,3},{2,0},{3,1},{4,5},{5,4},{6,7},{7,6},{8,10},{9,11},{10,... | collective-permute-start | bytes 786440 | tf_op jit(solution)/shard_map/ppermute | solution.py:41
  29.4 0.0 copy-done.2
  29.4 1.0 %shard_map.62.partial_ref = f32[1024,128]{1,0:T(8,128)S(1)} custom-call(s32[6]{0:T(128)S(1)} %stack.27.sources_ref, s32[384]{0:T(512)S(1)} %reshape.12.columns_ref, bf16[16,6,64,256]{3,2,1,0:T(8,128)(2,1)S(1)} %copy-done, bf16[16,64,128]{2,1,0:T(8,128)(2,1)S(1)} %get-tuple-element.6.own_ref, f32[8,128]{1,0:T(8,128)S(1)} %bitcast.14, ...), custom_call_target="tpu_custom_call" | custom-call | tf_op jit(solution)/shard_map/pallas_call | solution.py:257
  30.4 0.0 collective-permute-done.6.refs_1_
  30.4 0.0 collective-permute-done.7.refs_2_
  30.4 0.0 collective-permute-done.8.refs_3_
  30.4 1.5 %shard_map.63.partial_ref = f32[1024,128]{1,0:T(8,128)S(1)} custom-call(s32[6]{0:T(128)S(1)} %stack.27.sources_ref, s32[384]{0:T(512)S(1)} %reshape.12.columns_ref, bf16[16,6,64,256]{3,2,1,0:T(8,128)(2,1)S(1)} %copy-done, f32[1024,128]{1,0:T(8,128)S(1)} %shard_map.62.partial_ref, bf16[16,64,128]{2,1,0:T(8,128)(2,1)S(1)} %collective-permute-done.5.refs_0_, ...), custom_call_target="tpu_custom_call" | custom-call | tf_op jit(solution)/shard_map/pallas_call | solution.py:260
  31.9 2.9 %collective-permute-done.9.piece_ref = bf16[16,64,128]{2,1,0:T(8,128)(2,1)S(1)} collective-permute-done((bf16[16,64,128]{2,1,0:T(8,128)(2,1)S(1)}, bf16[16,64,128]{2,1,0:T(8,128)(2,1)S(1)}, u32[]{:S(2)}, u32[]{:S(2)}) %collective-permute-start.9) | collective-permute-done | bytes 262176 | tf_op jit(solution)/shard_map/ppermute | solution.py:41
  34.8 1.5 %shard_map.64 = (f32[1024,128]{1,0:T(8,128)S(1)}, f32[72,128]{1,0:T(8,128)S(1)}) custom-call(s32[6]{0:T(128)S(1)} %stack.27.sources_ref, s32[384]{0:T(512)S(1)} %reshape.12.columns_ref, bf16[16,6,64,256]{3,2,1,0:T(8,128)(2,1)S(1)} %copy-done, f32[1024,128]{1,0:T(8,128)S(1)} %shard_map.63.partial_ref, bf16[16,64,128]{2,1,0:T(8,128)(2,1)S(1)} %collective-permute-done.9.piece_ref), custom_call_target="tpu_custom_call" | custom-call | tf_op jit(solution)/shard_map/pallas_call | solution.py:272
  36.3 39.8 %psum.7.packed_ref = f32[72,128]{1,0:T(8,128)S(1)} all-reduce(f32[72,128]{1,0:T(8,128)S(1)} %get-tuple-element.8), channel_id=1, replica_groups=mesh['group'=8,'blk'=4] {'group','blk'}, use_global_device_ids=true, to_apply=%region_0.1 | all-reduce | flops 9216 | bytes 73728 | tf_op jit(solution)/shard_map/psum | solution.py:275
  76.1 5.3 %shard_map.65 = (f32[1024,128]{1,0:T(8,128)}, f32[128,128]{1,0:T(8,128)}) custom-call(f32[72,128]{1,0:T(8,128)S(1)} %psum.7.packed_ref, f32[1024,128]{1,0:T(8,128)S(1)} %get-tuple-element.9.filtered_ref), custom_call_target="tpu_custom_call" | custom-call | tf_op jit(solution)/shard_map/pallas_call | solution.py:276
Async XLA Ops:
  1.7 9.6 %collective-permute-start = (bf16[16,64,128]{2,1,0:T(8,128)(2,1)S(1)}, bf16[16,64,128]{2,1,0:T(8,128)(2,1)S(1)}, u32[]{:S(2)}, u32[]{:S(2)}) collective-permute-start(bf16[16,64,128]{2,1,0:T(8,128)(2,1)S(1)} %bitcast.8), channel_id=1, source_target_pairs={{0,1},{1,0},{2,3},{3,2},{4,6},{5,7},{6,4},{7,5},{8,9},{9,8},{10,11... | collective-permute-start | bytes 786440 | tf_op jit(solution)/shard_map/ppermute | solution.py:41
  4.7 13.8 %collective-permute-start.1 = (bf16[16,64,128]{2,1,0:T(8,128)(2,1)S(1)}, bf16[16,64,128]{2,1,0:T(8,128)(2,1)S(1)}, u32[]{:S(2)}, u32[]{:S(2)}) collective-permute-start(bf16[16,64,128]{2,1,0:T(8,128)(2,1)S(1)} %bitcast.9), channel_id=1, source_target_pairs={{0,2},{1,3},{2,0},{3,1},{4,5},{5,4},{6,7},{7,6},{8,10},{9,11},{10,... | collective-permute-start | bytes 786440 | tf_op jit(solution)/shard_map/ppermute | solution.py:41
  6.2 12.3 %collective-permute-start.2 = (bf16[16,64,128]{2,1,0:T(8,128)(2,1)S(1)}, bf16[16,64,128]{2,1,0:T(8,128)(2,1)S(1)}, u32[]{:S(2)}, u32[]{:S(2)}) collective-permute-start(bf16[16,64,128]{2,1,0:T(8,128)(2,1)S(1)} %bitcast.10), channel_id=1, source_target_pairs={{4,8},{8,4},{12,16},{16,12},{20,24},{24,20},{5,9},{9,5},{13,17},{1... | collective-permute-start | bytes 786440 | tf_op jit(solution)/shard_map/ppermute | solution.py:23
  6.9 11.6 %collective-permute-start.3 = (bf16[16,64,128]{2,1,0:T(8,128)(2,1)S(1)}, bf16[16,64,128]{2,1,0:T(8,128)(2,1)S(1)}, u32[]{:S(2)}, u32[]{:S(2)}) collective-permute-start(bf16[16,64,128]{2,1,0:T(8,128)(2,1)S(1)} %bitcast.11), channel_id=1, source_target_pairs={{0,4},{4,0},{8,12},{12,8},{16,20},{20,16},{24,28},{28,24},{1,5},{5... | collective-permute-start | bytes 786440 | tf_op jit(solution)/shard_map/ppermute | solution.py:23
  11.3 8.7 %collective-permute-start.4 = (bf16[16,64,128]{2,1,0:T(8,128)(2,1)S(1)}, bf16[16,64,128]{2,1,0:T(8,128)(2,1)S(1)}, u32[]{:S(2)}, u32[]{:S(2)}) collective-permute-start(bf16[16,64,128]{2,1,0:T(8,128)(2,1)S(1)} %collective-permute-done.refs_0_), channel_id=1, source_target_pairs={{0,2},{1,3},{2,0},{3,1},{4,5},{5,4},{6,7},{7,6},{8,10},{9,11},{10,... | collective-permute-start | bytes 786440 | tf_op jit(solution)/shard_map/ppermute | solution.py:41
  13.9 1.9 %copy-start = (bf16[16,6,64,256]{3,2,1,0:T(8,128)(2,1)S(1)}, bf16[16,6,64,256]{3,2,1,0:T(8,128)(2,1)}, u32[]{:S(2)}) copy-start(bf16[16,6,64,256]{3,2,1,0:T(8,128)(2,1)} %hamiltonian_ref.11) | copy-start | bytes 9437188
  15.8 1.0 %copy-start.1 = (f32[1024,128]{1,0:T(8,128)S(1)}, f32[1024,128]{1,0:T(8,128)}, u32[]{:S(2)}) copy-start(f32[1024,128]{1,0:T(8,128)} %refs_0_.1) | copy-start | bytes 1572868
  16.8 0.7 copy-start.3
  20.0 9.4 %copy-start.2 = (f32[1024,128]{1,0:T(8,128)S(1)}, f32[1024,128]{1,0:T(8,128)}, u32[]{:S(2)}) copy-start(f32[1024,128]{1,0:T(8,128)} %refs_0_.1) | copy-start | bytes 1572868
  20.9 7.5 %collective-permute-start.5 = (bf16[16,64,128]{2,1,0:T(8,128)(2,1)S(1)}, bf16[16,64,128]{2,1,0:T(8,128)(2,1)S(1)}, u32[]{:S(2)}, u32[]{:S(2)}) collective-permute-start(bf16[16,64,128]{2,1,0:T(8,128)(2,1)S(1)} %get-tuple-element.6.own_ref), channel_id=1, source_target_pairs={{0,1},{1,0},{2,3},{3,2},{4,6},{5,7},{6,4},{7,5},{8,9},{9,8},{10,11... | collective-permute-start | bytes 786440 | tf_op jit(solution)/shard_map/ppermute | solution.py:41
  22.6 7.8 %collective-permute-start.6 = (bf16[16,64,128]{2,1,0:T(8,128)(2,1)S(1)}, bf16[16,64,128]{2,1,0:T(8,128)(2,1)S(1)}, u32[]{:S(2)}, u32[]{:S(2)}) collective-permute-start(bf16[16,64,128]{2,1,0:T(8,128)(2,1)S(1)} %get-tuple-element.6.own_ref), channel_id=1, source_target_pairs={{0,2},{1,3},{2,0},{3,1},{4,5},{5,4},{6,7},{7,6},{8,10},{9,11},{10,... | collective-permute-start | bytes 786440 | tf_op jit(solution)/shard_map/ppermute | solution.py:41
  23.9 6.5 %collective-permute-start.7 = (bf16[16,64,128]{2,1,0:T(8,128)(2,1)S(1)}, bf16[16,64,128]{2,1,0:T(8,128)(2,1)S(1)}, u32[]{:S(2)}, u32[]{:S(2)}) collective-permute-start(bf16[16,64,128]{2,1,0:T(8,128)(2,1)S(1)} %get-tuple-element.6.own_ref), channel_id=1, source_target_pairs={{4,8},{8,4},{12,16},{16,12},{20,24},{24,20},{5,9},{9,5},{13,17},{1... | collective-permute-start | bytes 786440 | tf_op jit(solution)/shard_map/ppermute | solution.py:23
  24.6 5.8 %collective-permute-start.8 = (bf16[16,64,128]{2,1,0:T(8,128)(2,1)S(1)}, bf16[16,64,128]{2,1,0:T(8,128)(2,1)S(1)}, u32[]{:S(2)}, u32[]{:S(2)}) collective-permute-start(bf16[16,64,128]{2,1,0:T(8,128)(2,1)S(1)} %get-tuple-element.6.own_ref), channel_id=1, source_target_pairs={{0,4},{4,0},{8,12},{12,8},{16,20},{20,16},{24,28},{28,24},{1,5},{5... | collective-permute-start | bytes 786440 | tf_op jit(solution)/shard_map/ppermute | solution.py:23
  28.4 6.4 %collective-permute-start.9 = (bf16[16,64,128]{2,1,0:T(8,128)(2,1)S(1)}, bf16[16,64,128]{2,1,0:T(8,128)(2,1)S(1)}, u32[]{:S(2)}, u32[]{:S(2)}) collective-permute-start(bf16[16,64,128]{2,1,0:T(8,128)(2,1)S(1)} %collective-permute-done.5.refs_0_), channel_id=1, source_target_pairs={{0,2},{1,3},{2,0},{3,1},{4,5},{5,4},{6,7},{7,6},{8,10},{9,11},{10,... | collective-permute-start | bytes 786440 | tf_op jit(solution)/shard_map/ppermute | solution.py:41

commit v4 on v3

--- a/solution.py
+++ b/solution.py
@@ -41,6 +41,16 @@
     return lax.ppermute(value, ("group", "blk"), route)
 
 
+def summed(value):
+    axes = ("group", "blk")
+    devices = lax.axis_size("group") * lax.axis_size("blk")
+    shape = value.shape
+    value = value.reshape((devices, -1) + ((shape[-1],) if shape[0] == devices else ()))
+    part = jnp.sum(lax.all_to_all(value, axes, 0, 0), axis=0)
+    shared = lax.all_to_all(jnp.broadcast_to(part, value.shape), axes, 0, 0)
+    return shared.reshape(-1, shape[-1])
+
+
 def potential_columns(potential_ref):
     return jnp.transpose(potential_ref[...])
 
@@ -106,7 +116,7 @@
 
 def second_kernel(
     number, sources_ref, columns_ref, hamiltonian_ref, partial_ref, piece_ref,
-    filtered_ref, packed_ref,
+    filtered_ref, gram_ref,
 ):
     shard_blocks, _, block_size, _ = hamiltonian_ref.shape
     for row in range(shard_blocks):
@@ -119,31 +129,9 @@
         flat, flat, (((0,), (0,)), ((), ())), precision=precise,
         preferred_element_type=jnp.float32,
     )
-    pack(gram, packed_ref)
-
-
-def pack(gram, packed_ref):
-    size = gram.shape[0]
-    half = size // 2
-    row = lax.broadcasted_iota(jnp.int32, (half, size), 0)
-    lane = lax.broadcasted_iota(jnp.int32, (half, size), 1)
-    lower = gram[half:, :]
-    packed_ref[pl.ds(0, half), :] = jnp.where(lane < row, pltpu.roll(lower, half, 1), gram[:half, :])
-    diagonal = jnp.sum(jnp.where(lane == row + half, lower, 0.0), axis=0, keepdims=True)
-    packed_ref[pl.ds(half, SUB), :] = jnp.broadcast_to(diagonal, (SUB, size))
-
-
-def unpack(packed_ref):
-    size = packed_ref.shape[1]
-    half = size // 2
-    row = lax.broadcasted_iota(jnp.int32, (size, size), 0)
-    lane = lax.broadcasted_iota(jnp.int32, (size, size), 1)
-    upper = packed_ref[pl.ds(0, half), :]
-    both = jnp.concatenate([upper, pltpu.roll(upper, half, 1)], axis=0)
-    held = ((row < half) & (lane > row)) | ((row >= half) & (lane >= half) & (lane < row))
-    off_diagonal = jnp.where(held, both, 0.0)
-    diagonal = jnp.where(row < half, both, packed_ref[pl.ds(half, 1), :])
-    return off_diagonal + jnp.transpose(off_diagonal) + jnp.where(row == lane, diagonal, 0.0)
+    per_part = gram_ref.shape[1]
+    for part in range(gram_ref.shape[0]):
+        gram_ref[part] = gram[part * per_part : (part + 1) * per_part, :]
 
 
 def inverse_of(value):
@@ -152,8 +140,8 @@
     return estimate * (2.0 - value * estimate)
 
 
-def factor_kernel(rows_total, packed_ref, filtered_ref, ortho_ref, upper_ref, inverse_ref):
-    size = packed_ref.shape[1]
+def factor_kernel(rows_total, gram_ref, filtered_ref, ortho_ref, upper_ref, inverse_ref):
+    size = gram_ref.shape[1]
     panels = size // SUB
     shape = (SUB, size)
     row_index = lax.broadcasted_iota(jnp.int32, shape, 0)
@@ -165,8 +153,7 @@
     def along_rows(panel, row):
         return jnp.broadcast_to(panel[row : row + 1, :], shape)
 
-    gram = unpack(packed_ref) * (1.0 / rows_total)
-    matrix = [gram[k * SUB : (k + 1) * SUB, :] for k in range(panels)]
+    matrix = [gram_ref[pl.ds(k * SUB, SUB), :] * (1.0 / rows_total) for k in range(panels)]
     inverse = [
         jnp.where(lane_index == row_index + k * SUB, 1.0, 0.0).astype(jnp.float32)
         for k in range(panels)
@@ -243,7 +230,9 @@
     middle = list(range(1, last)) + [cycle_size + 1, cycle_size]
     flat = jax.ShapeDtypeStruct((flat_rows, states), jnp.float32)
     rounded = jax.ShapeDtypeStruct((shard_blocks, block_size, states), jnp.bfloat16)
-    packed = jax.ShapeDtypeStruct((states // 2 + SUB, states), jnp.float32)
+    devices = lax.axis_size("group") * cycle_size
+    parts = min(devices, states)
+    parted = jax.ShapeDtypeStruct((parts, states // parts, states), jnp.float32)
     square = jax.ShapeDtypeStruct((states, states), jnp.float32)
 
     def exchanged(value):
@@ -270,9 +259,9 @@
     pieces = exchanged(once_round)
     partial = most(pieces, once, trial_slab)
     filtered, gram = call(
-        functools.partial(second_kernel, last), (flat, packed), [smem] * 2 + [vmem] * 3
+        functools.partial(second_kernel, last), (flat, parted), [smem] * 2 + [vmem] * 3
     )(sources, columns, hamiltonian, partial, pieces[last])
-    gram = lax.psum(gram, ("group", "blk"))
+    gram = summed(gram)
     return call(
         functools.partial(factor_kernel, rows_total),
         (flat, square),

time: 81.8 us -> 63 us (0.77)
  blocking collectives: 39.8 us -> 21.2 us
    psum x1 -> x0, blocking collectives: 39.8 us -> none  [on_device(): gram = lax.psum(gram, ('group', 'blk'))]
    all_to_all x0 -> x2, blocking collectives: none -> 21.2 us  [the longest x1 12 us: summed(): part = jnp.sum(lax.all_to_all(value, axes, 0, 0), axis=0)]
  transfers between devices with their start and end apart: 10 -> 10, of which waited for: 3 -> 3; matrix products, arithmetic and copies ran while one was open for 1% -> 2% of each run, Pallas kernels for 6% -> 8%
where the time goes in v4:
time: 63 us; the launch traced here: 62.6 us
  blocking collectives  21.2 us (34%)
  starting transfers between devices  17.4 us (28%)
  Pallas kernels  12.3 us (20%)
  waiting for transfers between devices  5.16 us (8%)
  local copies, waits for them, and re-layouts  4.65 us (7%)
  other arithmetic  1.11 us (2%)
  between operations  0.77 us (1%)
    all_to_all x1, blocking collectives, summed(): part = jnp.sum(lax.all_to_all(value, axes, 0, 0), axis=0)  12 us
    ppermute x6, starting transfers between devices, cycle_exchange(): return lax.ppermute(value, ('group', 'blk'), route)  10.1 us
    all_to_all x1, blocking collectives, summed(): shared = lax.all_to_all(jnp.broadcast_to(part, value.shape), axes, 0, 0)  9.19 us
    ppermute x4, starting transfers between devices, pair_exchange(): return lax.ppermute(value, 'group', route)  7.31 us
    ppermute x6, waiting for transfers between devices, cycle_exchange(): return lax.ppermute(value, ('group', 'blk'), route)  5.15 us
    pallas_call x1, Pallas kernels, on_device(): call(functools.partial(factor_kernel, rows_total), (flat, square), [vmem,...  5.15 us
    unnamed x9, local copies, waits for them, and re-layouts  4.44 us
    pallas_call x2, Pallas kernels, most(): call(functools.partial(middle_kernel, middle), flat, [smem] * 2 + [vmem]...  2.96 us
  transfers between devices with their start and end apart: 10, of which 3 were waited for; matrix products, arithmetic and copies ran while one was open for 2% of the time, Pallas kernels for 8%

profile of v4, /device:TPU:0, one launch (start us, length us, event | category | flops | bytes accessed | tf_op | source)
XLA Modules:
  0.0 62.6 jit_solution(15417581860589480567)
XLA Ops:
  0.6 1.1 %convert_element_type.5 = bf16[1024,128]{1,0:T(8,128)(2,1)S(1)} convert(f32[1024,128]{1,0:T(8,128)} %refs_0_.1) | non-fusion elementwise | flops 131072 | bytes 786432 | tf_op jit(solution)/shard_map/convert_element_type | solution.py:254
  1.7 3.0 %collective-permute-start = (bf16[16,64,128]{2,1,0:T(8,128)(2,1)S(1)}, bf16[16,64,128]{2,1,0:T(8,128)(2,1)S(1)}, u32[]{:S(2)}, u32[]{:S(2)}) collective-permute-start(bf16[16,64,128]{2,1,0:T(8,128)(2,1)S(1)} %bitcast.9), channel_id=1, source_target_pairs={{0,1},{1,0},{2,3},{3,2},{4,6},{5,7},{6,4},{7,5},{8,9},{9,8},{10,11... | collective-permute-start | bytes 786440 | tf_op jit(solution)/shard_map/ppermute | solution.py:41
  4.7 1.5 %collective-permute-start.1 = (bf16[16,64,128]{2,1,0:T(8,128)(2,1)S(1)}, bf16[16,64,128]{2,1,0:T(8,128)(2,1)S(1)}, u32[]{:S(2)}, u32[]{:S(2)}) collective-permute-start(bf16[16,64,128]{2,1,0:T(8,128)(2,1)S(1)} %bitcast.10), channel_id=1, source_target_pairs={{0,2},{1,3},{2,0},{3,1},{4,5},{5,4},{6,7},{7,6},{8,10},{9,11},{10,... | collective-permute-start | bytes 786440 | tf_op jit(solution)/shard_map/ppermute | solution.py:41
  6.2 0.7 %collective-permute-start.2 = (bf16[16,64,128]{2,1,0:T(8,128)(2,1)S(1)}, bf16[16,64,128]{2,1,0:T(8,128)(2,1)S(1)}, u32[]{:S(2)}, u32[]{:S(2)}) collective-permute-start(bf16[16,64,128]{2,1,0:T(8,128)(2,1)S(1)} %bitcast.11), channel_id=1, source_target_pairs={{4,8},{8,4},{12,16},{16,12},{20,24},{24,20},{5,9},{9,5},{13,17},{1... | collective-permute-start | bytes 786440 | tf_op jit(solution)/shard_map/ppermute | solution.py:23
  6.9 3.0 %collective-permute-start.3 = (bf16[16,64,128]{2,1,0:T(8,128)(2,1)S(1)}, bf16[16,64,128]{2,1,0:T(8,128)(2,1)S(1)}, u32[]{:S(2)}, u32[]{:S(2)}) collective-permute-start(bf16[16,64,128]{2,1,0:T(8,128)(2,1)S(1)} %bitcast.12), channel_id=1, source_target_pairs={{0,4},{4,0},{8,12},{12,8},{16,20},{20,16},{24,28},{28,24},{1,5},{5... | collective-permute-start | bytes 786440 | tf_op jit(solution)/shard_map/ppermute | solution.py:23
  9.9 1.4 %collective-permute-done.refs_0_ = bf16[16,64,128]{2,1,0:T(8,128)(2,1)S(1)} collective-permute-done((bf16[16,64,128]{2,1,0:T(8,128)(2,1)S(1)}, bf16[16,64,128]{2,1,0:T(8,128)(2,1)S(1)}, u32[]{:S(2)}, u32[]{:S(2)}) %collective-permute-start) | collective-permute-done | bytes 262176 | tf_op jit(solution)/shard_map/ppermute | solution.py:41
  11.3 1.6 %collective-permute-start.4 = (bf16[16,64,128]{2,1,0:T(8,128)(2,1)S(1)}, bf16[16,64,128]{2,1,0:T(8,128)(2,1)S(1)}, u32[]{:S(2)}, u32[]{:S(2)}) collective-permute-start(bf16[16,64,128]{2,1,0:T(8,128)(2,1)S(1)} %collective-permute-done.refs_0_), channel_id=1, source_target_pairs={{0,2},{1,3},{2,0},{3,1},{4,5},{5,4},{6,7},{7,6},{8,10},{9,11},{10,... | collective-permute-start | bytes 786440 | tf_op jit(solution)/shard_map/ppermute | solution.py:41
  12.9 0.8 %copy.6 = s32[16,6,4]{2,1,0:T(8,128)S(1)} copy(s32[16,6,4]{0,2,1:T(4,128)} %param.5) | data formatting | bytes 3072 | tf_op args[1]
  13.7 0.1 reshape.15.columns_ref
  13.8 0.1 stack.27.sources_ref
  13.9 0.0 copy-start
  13.9 1.9 %copy-done = bf16[16,6,64,256]{3,2,1,0:T(8,128)(2,1)S(1)} copy-done((bf16[16,6,64,256]{3,2,1,0:T(8,128)(2,1)S(1)}, bf16[16,6,64,256]{3,2,1,0:T(8,128)(2,1)}, u32[]{:S(2)}) %copy-start) | copy-done | bytes 3145752
  15.8 0.0 copy-start.1
  15.8 1.0 %copy-done.1 = f32[1024,128]{1,0:T(8,128)S(1)} copy-done((f32[1024,128]{1,0:T(8,128)S(1)}, f32[1024,128]{1,0:T(8,128)}, u32[]{:S(2)}) %copy-start.1) | copy-done | bytes 524312
  16.8 0.0 copy-start.3
  16.8 0.7 %copy-done.3 = f32[1024]{0:T(1024)S(1)} copy-done((f32[1024]{0:T(1024)S(1)}, f32[1024]{0:T(1024)}, u32[]{:S(2)}) %copy-start.3) | copy-done | bytes 4120
  17.5 1.0 %shard_map.59.partial_ref = f32[1024,128]{1,0:T(8,128)S(1)} custom-call(s32[6]{0:T(128)S(1)} %stack.27.sources_ref, s32[384]{0:T(512)S(1)} %reshape.15.columns_ref, bf16[16,6,64,256]{3,2,1,0:T(8,128)(2,1)S(1)} %copy-done, bf16[16,64,128]{2,1,0:T(8,128)(2,1)S(1)} %bitcast.13, f32[8,128]{1,0:T(8,128)S(1)} %bitcast.15, f32[1024,128]{1,0:T(8,128)S(1)} %copy-done.1), custom_call_target="tpu_custom_call" | custom-call | tf_op jit(solution)/shard_map/pallas_call | solution.py:246
  18.5 0.0 collective-permute-done.1.refs_1_
  18.5 0.0 collective-permute-done.2.refs_2_
  18.5 0.0 collective-permute-done.3.refs_3_
  18.5 1.5 %shard_map.60.partial_ref = f32[1024,128]{1,0:T(8,128)S(1)} custom-call(s32[6]{0:T(128)S(1)} %stack.27.sources_ref, s32[384]{0:T(512)S(1)} %reshape.15.columns_ref, bf16[16,6,64,256]{3,2,1,0:T(8,128)(2,1)S(1)} %copy-done, f32[1024,128]{1,0:T(8,128)S(1)} %shard_map.59.partial_ref, bf16[16,64,128]{2,1,0:T(8,128)(2,1)S(1)} %collective-permute-done.refs_0_, ...), custom_call_target="tpu_custom_call" | custom-call | tf_op jit(solution)/shard_map/pallas_call | solution.py:249
  20.0 0.0 copy-start.2
  20.0 0.0 collective-permute-done.4.piece_ref
  20.0 0.9 %shard_map.61 = (f32[1024,128]{1,0:T(8,128)S(1)}, bf16[16,64,128]{2,1,0:T(8,128)(2,1)S(1)}) custom-call(s32[6]{0:T(128)S(1)} %stack.27.sources_ref, s32[384]{0:T(512)S(1)} %reshape.15.columns_ref, bf16[16,6,64,256]{3,2,1,0:T(8,128)(2,1)S(1)} %copy-done, f32[1024,128]{1,0:T(8,128)S(1)} %shard_map.60.partial_ref, ...), custom_call_target="tpu_custom_call" | custom-call | tf_op jit(solution)/shard_map/pallas_call | solution.py:256
  20.9 1.7 %collective-permute-start.5 = (bf16[16,64,128]{2,1,0:T(8,128)(2,1)S(1)}, bf16[16,64,128]{2,1,0:T(8,128)(2,1)S(1)}, u32[]{:S(2)}, u32[]{:S(2)}) collective-permute-start(bf16[16,64,128]{2,1,0:T(8,128)(2,1)S(1)} %get-tuple-element.6.own_ref), channel_id=1, source_target_pairs={{0,1},{1,0},{2,3},{3,2},{4,6},{5,7},{6,4},{7,5},{8,9},{9,8},{10,11... | collective-permute-start | bytes 786440 | tf_op jit(solution)/shard_map/ppermute | solution.py:41
  22.6 1.3 %collective-permute-start.6 = (bf16[16,64,128]{2,1,0:T(8,128)(2,1)S(1)}, bf16[16,64,128]{2,1,0:T(8,128)(2,1)S(1)}, u32[]{:S(2)}, u32[]{:S(2)}) collective-permute-start(bf16[16,64,128]{2,1,0:T(8,128)(2,1)S(1)} %get-tuple-element.6.own_ref), channel_id=1, source_target_pairs={{0,2},{1,3},{2,0},{3,1},{4,5},{5,4},{6,7},{7,6},{8,10},{9,11},{10,... | collective-permute-start | bytes 786440 | tf_op jit(solution)/shard_map/ppermute | solution.py:41
  23.9 0.7 %collective-permute-start.7 = (bf16[16,64,128]{2,1,0:T(8,128)(2,1)S(1)}, bf16[16,64,128]{2,1,0:T(8,128)(2,1)S(1)}, u32[]{:S(2)}, u32[]{:S(2)}) collective-permute-start(bf16[16,64,128]{2,1,0:T(8,128)(2,1)S(1)} %get-tuple-element.6.own_ref), channel_id=1, source_target_pairs={{4,8},{8,4},{12,16},{16,12},{20,24},{24,20},{5,9},{9,5},{13,17},{1... | collective-permute-start | bytes 786440 | tf_op jit(solution)/shard_map/ppermute | solution.py:23
  24.6 3.0 %collective-permute-start.8 = (bf16[16,64,128]{2,1,0:T(8,128)(2,1)S(1)}, bf16[16,64,128]{2,1,0:T(8,128)(2,1)S(1)}, u32[]{:S(2)}, u32[]{:S(2)}) collective-permute-start(bf16[16,64,128]{2,1,0:T(8,128)(2,1)S(1)} %get-tuple-element.6.own_ref), channel_id=1, source_target_pairs={{0,4},{4,0},{8,12},{12,8},{16,20},{20,16},{24,28},{28,24},{1,5},{5... | collective-permute-start | bytes 786440 | tf_op jit(solution)/shard_map/ppermute | solution.py:23
  27.6 0.8 %collective-permute-done.5.refs_0_ = bf16[16,64,128]{2,1,0:T(8,128)(2,1)S(1)} collective-permute-done((bf16[16,64,128]{2,1,0:T(8,128)(2,1)S(1)}, bf16[16,64,128]{2,1,0:T(8,128)(2,1)S(1)}, u32[]{:S(2)}, u32[]{:S(2)}) %collective-permute-start.5) | collective-permute-done | bytes 262176 | tf_op jit(solution)/shard_map/ppermute | solution.py:41
  28.4 1.0 %collective-permute-start.9 = (bf16[16,64,128]{2,1,0:T(8,128)(2,1)S(1)}, bf16[16,64,128]{2,1,0:T(8,128)(2,1)S(1)}, u32[]{:S(2)}, u32[]{:S(2)}) collective-permute-start(bf16[16,64,128]{2,1,0:T(8,128)(2,1)S(1)} %collective-permute-done.5.refs_0_), channel_id=1, source_target_pairs={{0,2},{1,3},{2,0},{3,1},{4,5},{5,4},{6,7},{7,6},{8,10},{9,11},{10,... | collective-permute-start | bytes 786440 | tf_op jit(solution)/shard_map/ppermute | solution.py:41
  29.4 0.0 copy-done.2
  29.4 1.0 %shard_map.62.partial_ref = f32[1024,128]{1,0:T(8,128)S(1)} custom-call(s32[6]{0:T(128)S(1)} %stack.27.sources_ref, s32[384]{0:T(512)S(1)} %reshape.15.columns_ref, bf16[16,6,64,256]{3,2,1,0:T(8,128)(2,1)S(1)} %copy-done, bf16[16,64,128]{2,1,0:T(8,128)(2,1)S(1)} %get-tuple-element.6.own_ref, f32[8,128]{1,0:T(8,128)S(1)} %bitcast.16, ...), custom_call_target="tpu_custom_call" | custom-call | tf_op jit(solution)/shard_map/pallas_call | solution.py:246
  30.4 0.0 collective-permute-done.6.refs_1_
  30.4 0.0 collective-permute-done.7.refs_2_
  30.4 0.0 collective-permute-done.8.refs_3_
  30.4 1.5 %shard_map.63.partial_ref = f32[1024,128]{1,0:T(8,128)S(1)} custom-call(s32[6]{0:T(128)S(1)} %stack.27.sources_ref, s32[384]{0:T(512)S(1)} %reshape.15.columns_ref, bf16[16,6,64,256]{3,2,1,0:T(8,128)(2,1)S(1)} %copy-done, f32[1024,128]{1,0:T(8,128)S(1)} %shard_map.62.partial_ref, bf16[16,64,128]{2,1,0:T(8,128)(2,1)S(1)} %collective-permute-done.5.refs_0_, ...), custom_call_target="tpu_custom_call" | custom-call | tf_op jit(solution)/shard_map/pallas_call | solution.py:249
  31.9 2.9 %collective-permute-done.9.piece_ref = bf16[16,64,128]{2,1,0:T(8,128)(2,1)S(1)} collective-permute-done((bf16[16,64,128]{2,1,0:T(8,128)(2,1)S(1)}, bf16[16,64,128]{2,1,0:T(8,128)(2,1)S(1)}, u32[]{:S(2)}, u32[]{:S(2)}) %collective-permute-start.9) | collective-permute-done | bytes 262176 | tf_op jit(solution)/shard_map/ppermute | solution.py:41
  34.8 1.4 %shard_map.64 = (f32[1024,128]{1,0:T(8,128)S(1)}, f32[32,4,128]{2,1,0:T(4,128)S(1)}) custom-call(s32[6]{0:T(128)S(1)} %stack.27.sources_ref, s32[384]{0:T(512)S(1)} %reshape.15.columns_ref, bf16[16,6,64,256]{3,2,1,0:T(8,128)(2,1)S(1)} %copy-done, f32[1024,128]{1,0:T(8,128)S(1)} %shard_map.63.partial_ref, ...), custom_call_target="tpu_custom_call" | custom-call | tf_op jit(solution)/shard_map/pallas_call | solution.py:261
  36.2 12.0 %all_to_all.10 = f32[32,4,128]{2,1,0:T(4,128)S(1)} all-to-all(f32[32,4,128]{2,1,0:T(4,128)S(1)} %get-tuple-element.8), channel_id=1, replica_groups=mesh['group'=8,'blk'=4] {'group','blk'}, dimensions={0} | all-to-all | bytes 131072 | tf_op jit(solution)/shard_map/all_to_all | solution.py:49
  48.3 9.2 %all_to_all.11 = f32[32,4,128]{2,1,0:T(4,128)S(1)} all-to-all(f32[32,4,128]{2,1,0:T(4,128)S(1)} %broadcast_in_dim.3), channel_id=1, replica_groups=mesh['group'=8,'blk'=4] {'group','blk'}, dimensions={0} | all-to-all | bytes 131072 | tf_op jit(solution)/shard_map/all_to_all | solution.py:50
  57.5 5.1 %shard_map.65 = (f32[1024,128]{1,0:T(8,128)}, f32[128,128]{1,0:T(8,128)}) custom-call(f32[128,128]{1,0:T(8,128)S(1)} %bitcast.14, f32[1024,128]{1,0:T(8,128)S(1)} %get-tuple-element.9.filtered_ref), custom_call_target="tpu_custom_call" | custom-call | tf_op jit(solution)/shard_map/pallas_call | solution.py:265
  (2 shorter events, 0.1 us)
Async XLA Ops:
  1.7 9.6 %collective-permute-start = (bf16[16,64,128]{2,1,0:T(8,128)(2,1)S(1)}, bf16[16,64,128]{2,1,0:T(8,128)(2,1)S(1)}, u32[]{:S(2)}, u32[]{:S(2)}) collective-permute-start(bf16[16,64,128]{2,1,0:T(8,128)(2,1)S(1)} %bitcast.9), channel_id=1, source_target_pairs={{0,1},{1,0},{2,3},{3,2},{4,6},{5,7},{6,4},{7,5},{8,9},{9,8},{10,11... | collective-permute-start | bytes 786440 | tf_op jit(solution)/shard_map/ppermute | solution.py:41
  4.7 13.8 %collective-permute-start.1 = (bf16[16,64,128]{2,1,0:T(8,128)(2,1)S(1)}, bf16[16,64,128]{2,1,0:T(8,128)(2,1)S(1)}, u32[]{:S(2)}, u32[]{:S(2)}) collective-permute-start(bf16[16,64,128]{2,1,0:T(8,128)(2,1)S(1)} %bitcast.10), channel_id=1, source_target_pairs={{0,2},{1,3},{2,0},{3,1},{4,5},{5,4},{6,7},{7,6},{8,10},{9,11},{10,... | collective-permute-start | bytes 786440 | tf_op jit(solution)/shard_map/ppermute | solution.py:41
  6.2 12.3 %collective-permute-start.2 = (bf16[16,64,128]{2,1,0:T(8,128)(2,1)S(1)}, bf16[16,64,128]{2,1,0:T(8,128)(2,1)S(1)}, u32[]{:S(2)}, u32[]{:S(2)}) collective-permute-start(bf16[16,64,128]{2,1,0:T(8,128)(2,1)S(1)} %bitcast.11), channel_id=1, source_target_pairs={{4,8},{8,4},{12,16},{16,12},{20,24},{24,20},{5,9},{9,5},{13,17},{1... | collective-permute-start | bytes 786440 | tf_op jit(solution)/shard_map/ppermute | solution.py:23
  6.9 11.6 %collective-permute-start.3 = (bf16[16,64,128]{2,1,0:T(8,128)(2,1)S(1)}, bf16[16,64,128]{2,1,0:T(8,128)(2,1)S(1)}, u32[]{:S(2)}, u32[]{:S(2)}) collective-permute-start(bf16[16,64,128]{2,1,0:T(8,128)(2,1)S(1)} %bitcast.12), channel_id=1, source_target_pairs={{0,4},{4,0},{8,12},{12,8},{16,20},{20,16},{24,28},{28,24},{1,5},{5... | collective-permute-start | bytes 786440 | tf_op jit(solution)/shard_map/ppermute | solution.py:23
  11.3 8.7 %collective-permute-start.4 = (bf16[16,64,128]{2,1,0:T(8,128)(2,1)S(1)}, bf16[16,64,128]{2,1,0:T(8,128)(2,1)S(1)}, u32[]{:S(2)}, u32[]{:S(2)}) collective-permute-start(bf16[16,64,128]{2,1,0:T(8,128)(2,1)S(1)} %collective-permute-done.refs_0_), channel_id=1, source_target_pairs={{0,2},{1,3},{2,0},{3,1},{4,5},{5,4},{6,7},{7,6},{8,10},{9,11},{10,... | collective-permute-start | bytes 786440 | tf_op jit(solution)/shard_map/ppermute | solution.py:41
  13.9 1.9 %copy-start = (bf16[16,6,64,256]{3,2,1,0:T(8,128)(2,1)S(1)}, bf16[16,6,64,256]{3,2,1,0:T(8,128)(2,1)}, u32[]{:S(2)}) copy-start(bf16[16,6,64,256]{3,2,1,0:T(8,128)(2,1)} %hamiltonian_ref.11) | copy-start | bytes 9437188
  15.8 1.0 %copy-start.1 = (f32[1024,128]{1,0:T(8,128)S(1)}, f32[1024,128]{1,0:T(8,128)}, u32[]{:S(2)}) copy-start(f32[1024,128]{1,0:T(8,128)} %refs_0_.1) | copy-start | bytes 1572868
  16.8 0.7 %copy-start.3 = (f32[1024]{0:T(1024)S(1)}, f32[1024]{0:T(1024)}, u32[]{:S(2)}) copy-start(f32[1024]{0:T(1024)} %param.6) | copy-start | bytes 12292
  20.0 9.4 %copy-start.2 = (f32[1024,128]{1,0:T(8,128)S(1)}, f32[1024,128]{1,0:T(8,128)}, u32[]{:S(2)}) copy-start(f32[1024,128]{1,0:T(8,128)} %refs_0_.1) | copy-start | bytes 1572868
  20.9 7.5 %collective-permute-start.5 = (bf16[16,64,128]{2,1,0:T(8,128)(2,1)S(1)}, bf16[16,64,128]{2,1,0:T(8,128)(2,1)S(1)}, u32[]{:S(2)}, u32[]{:S(2)}) collective-permute-start(bf16[16,64,128]{2,1,0:T(8,128)(2,1)S(1)} %get-tuple-element.6.own_ref), channel_id=1, source_target_pairs={{0,1},{1,0},{2,3},{3,2},{4,6},{5,7},{6,4},{7,5},{8,9},{9,8},{10,11... | collective-permute-start | bytes 786440 | tf_op jit(solution)/shard_map/ppermute | solution.py:41
  22.6 7.8 %collective-permute-start.6 = (bf16[16,64,128]{2,1,0:T(8,128)(2,1)S(1)}, bf16[16,64,128]{2,1,0:T(8,128)(2,1)S(1)}, u32[]{:S(2)}, u32[]{:S(2)}) collective-permute-start(bf16[16,64,128]{2,1,0:T(8,128)(2,1)S(1)} %get-tuple-element.6.own_ref), channel_id=1, source_target_pairs={{0,2},{1,3},{2,0},{3,1},{4,5},{5,4},{6,7},{7,6},{8,10},{9,11},{10,... | collective-permute-start | bytes 786440 | tf_op jit(solution)/shard_map/ppermute | solution.py:41
  23.9 6.5 %collective-permute-start.7 = (bf16[16,64,128]{2,1,0:T(8,128)(2,1)S(1)}, bf16[16,64,128]{2,1,0:T(8,128)(2,1)S(1)}, u32[]{:S(2)}, u32[]{:S(2)}) collective-permute-start(bf16[16,64,128]{2,1,0:T(8,128)(2,1)S(1)} %get-tuple-element.6.own_ref), channel_id=1, source_target_pairs={{4,8},{8,4},{12,16},{16,12},{20,24},{24,20},{5,9},{9,5},{13,17},{1... | collective-permute-start | bytes 786440 | tf_op jit(solution)/shard_map/ppermute | solution.py:23
  24.6 5.8 %collective-permute-start.8 = (bf16[16,64,128]{2,1,0:T(8,128)(2,1)S(1)}, bf16[16,64,128]{2,1,0:T(8,128)(2,1)S(1)}, u32[]{:S(2)}, u32[]{:S(2)}) collective-permute-start(bf16[16,64,128]{2,1,0:T(8,128)(2,1)S(1)} %get-tuple-element.6.own_ref), channel_id=1, source_target_pairs={{0,4},{4,0},{8,12},{12,8},{16,20},{20,16},{24,28},{28,24},{1,5},{5... | collective-permute-start | bytes 786440 | tf_op jit(solution)/shard_map/ppermute | solution.py:23
  28.4 6.4 %collective-permute-start.9 = (bf16[16,64,128]{2,1,0:T(8,128)(2,1)S(1)}, bf16[16,64,128]{2,1,0:T(8,128)(2,1)S(1)}, u32[]{:S(2)}, u32[]{:S(2)}) collective-permute-start(bf16[16,64,128]{2,1,0:T(8,128)(2,1)S(1)} %collective-permute-done.5.refs_0_), channel_id=1, source_target_pairs={{0,2},{1,3},{2,0},{3,1},{4,5},{5,4},{6,7},{7,6},{8,10},{9,11},{10,... | collective-permute-start | bytes 786440 | tf_op jit(solution)/shard_map/ppermute | solution.py:41

commit v5 on v4

--- a/solution.py
+++ b/solution.py
@@ -41,14 +41,15 @@
     return lax.ppermute(value, ("group", "blk"), route)
 
 
+def handed_out(value, axis):
+    copies = jnp.broadcast_to(value, (lax.axis_size(axis),) + value.shape)
+    return lax.all_to_all(copies, axis, 0, 0)
+
+
 def summed(value):
-    axes = ("group", "blk")
-    devices = lax.axis_size("group") * lax.axis_size("blk")
-    shape = value.shape
-    value = value.reshape((devices, -1) + ((shape[-1],) if shape[0] == devices else ()))
-    part = jnp.sum(lax.all_to_all(value, axes, 0, 0), axis=0)
-    shared = lax.all_to_all(jnp.broadcast_to(part, value.shape), axes, 0, 0)
-    return shared.reshape(-1, shape[-1])
+    part = jnp.sum(lax.all_to_all(value, "blk", 0, 0), axis=0)
+    part = jnp.sum(handed_out(part, "group"), axis=0)
+    return handed_out(part, "blk").reshape(-1, value.shape[-1])
 
 
 def potential_columns(potential_ref):
@@ -230,9 +231,7 @@
     middle = list(range(1, last)) + [cycle_size + 1, cycle_size]
     flat = jax.ShapeDtypeStruct((flat_rows, states), jnp.float32)
     rounded = jax.ShapeDtypeStruct((shard_blocks, block_size, states), jnp.bfloat16)
-    devices = lax.axis_size("group") * cycle_size
-    parts = min(devices, states)
-    parted = jax.ShapeDtypeStruct((parts, states // parts, states), jnp.float32)
+    parted = jax.ShapeDtypeStruct((cycle_size, states // cycle_size, states), jnp.float32)
     square = jax.ShapeDtypeStruct((states, states), jnp.float32)
 
     def exchanged(value):

time: 63 us -> 67.8 us (1.076)
  blocking collectives: 21.2 us -> 25.9 us
    all_to_all x2 -> x3, blocking collectives: 21.2 us -> 25.9 us  [the longest x2 18.7 us: handed_out(): return lax.all_to_all(copies, axis, 0, 0)]
  transfers between devices with their start and end apart: 10 -> 10, of which waited for: 3 -> 3; matrix products, arithmetic and copies ran while one was open for 2% -> 2% of each run, Pallas kernels for 8% -> 7%
where the time goes in v5:
time: 67.8 us; the launch traced here: 67.3 us
  blocking collectives  25.9 us (38%)
  starting transfers between devices  17.4 us (26%)
  Pallas kernels  12.3 us (18%)
  waiting for transfers between devices  5.16 us (8%)
  local copies, waits for them, and re-layouts  4.66 us (7%)
  other arithmetic  1.09 us (2%)
  between operations  0.78 us (1%)
    all_to_all x2, blocking collectives, handed_out(): return lax.all_to_all(copies, axis, 0, 0)  18.7 us
    ppermute x6, starting transfers between devices, cycle_exchange(): return lax.ppermute(value, ('group', 'blk'), route)  10.1 us
    ppermute x4, starting transfers between devices, pair_exchange(): return lax.ppermute(value, 'group', route)  7.31 us
    all_to_all x1, blocking collectives, summed(): part = jnp.sum(lax.all_to_all(value, 'blk', 0, 0), axis=0)  7.23 us
    ppermute x6, waiting for transfers between devices, cycle_exchange(): return lax.ppermute(value, ('group', 'blk'), route)  5.15 us
    pallas_call x1, Pallas kernels, on_device(): call(functools.partial(factor_kernel, rows_total), (flat, square), [vmem,...  5.15 us
    unnamed x9, local copies, waits for them, and re-layouts  4.44 us
    pallas_call x2, Pallas kernels, most(): call(functools.partial(middle_kernel, middle), flat, [smem] * 2 + [vmem]...  2.96 us
  transfers between devices with their start and end apart: 10, of which 3 were waited for; matrix products, arithmetic and copies ran while one was open for 2% of the time, Pallas kernels for 7%

profile of v5, /device:TPU:0, one launch (start us, length us, event | category | flops | bytes accessed | tf_op | source)
XLA Modules:
  0.0 67.3 jit_solution(6543991598076768157)
XLA Ops:
  0.6 1.1 %convert_element_type.5 = bf16[1024,128]{1,0:T(8,128)(2,1)S(1)} convert(f32[1024,128]{1,0:T(8,128)} %refs_0_.1) | non-fusion elementwise | flops 131072 | bytes 786432 | tf_op jit(solution)/shard_map/convert_element_type | solution.py:253
  1.7 3.0 %collective-permute-start = (bf16[16,64,128]{2,1,0:T(8,128)(2,1)S(1)}, bf16[16,64,128]{2,1,0:T(8,128)(2,1)S(1)}, u32[]{:S(2)}, u32[]{:S(2)}) collective-permute-start(bf16[16,64,128]{2,1,0:T(8,128)(2,1)S(1)} %bitcast.9), channel_id=1, source_target_pairs={{0,1},{1,0},{2,3},{3,2},{4,6},{5,7},{6,4},{7,5},{8,9},{9,8},{10,11... | collective-permute-start | bytes 786440 | tf_op jit(solution)/shard_map/ppermute | solution.py:41
  4.7 1.5 %collective-permute-start.1 = (bf16[16,64,128]{2,1,0:T(8,128)(2,1)S(1)}, bf16[16,64,128]{2,1,0:T(8,128)(2,1)S(1)}, u32[]{:S(2)}, u32[]{:S(2)}) collective-permute-start(bf16[16,64,128]{2,1,0:T(8,128)(2,1)S(1)} %bitcast.10), channel_id=1, source_target_pairs={{0,2},{1,3},{2,0},{3,1},{4,5},{5,4},{6,7},{7,6},{8,10},{9,11},{10,... | collective-permute-start | bytes 786440 | tf_op jit(solution)/shard_map/ppermute | solution.py:41
  6.2 0.7 collective-permute-start.2
  6.9 3.0 %collective-permute-start.3 = (bf16[16,64,128]{2,1,0:T(8,128)(2,1)S(1)}, bf16[16,64,128]{2,1,0:T(8,128)(2,1)S(1)}, u32[]{:S(2)}, u32[]{:S(2)}) collective-permute-start(bf16[16,64,128]{2,1,0:T(8,128)(2,1)S(1)} %bitcast.12), channel_id=1, source_target_pairs={{0,4},{4,0},{8,12},{12,8},{16,20},{20,16},{24,28},{28,24},{1,5},{5... | collective-permute-start | bytes 786440 | tf_op jit(solution)/shard_map/ppermute | solution.py:23
  9.9 1.4 %collective-permute-done.refs_0_ = bf16[16,64,128]{2,1,0:T(8,128)(2,1)S(1)} collective-permute-done((bf16[16,64,128]{2,1,0:T(8,128)(2,1)S(1)}, bf16[16,64,128]{2,1,0:T(8,128)(2,1)S(1)}, u32[]{:S(2)}, u32[]{:S(2)}) %collective-permute-start) | collective-permute-done | bytes 262176 | tf_op jit(solution)/shard_map/ppermute | solution.py:41
  11.3 1.6 %collective-permute-start.4 = (bf16[16,64,128]{2,1,0:T(8,128)(2,1)S(1)}, bf16[16,64,128]{2,1,0:T(8,128)(2,1)S(1)}, u32[]{:S(2)}, u32[]{:S(2)}) collective-permute-start(bf16[16,64,128]{2,1,0:T(8,128)(2,1)S(1)} %collective-permute-done.refs_0_), channel_id=1, source_target_pairs={{0,2},{1,3},{2,0},{3,1},{4,5},{5,4},{6,7},{7,6},{8,10},{9,11},{10,... | collective-permute-start | bytes 786440 | tf_op jit(solution)/shard_map/ppermute | solution.py:41
  12.9 0.8 %copy.7 = s32[16,6,4]{2,1,0:T(8,128)S(1)} copy(s32[16,6,4]{0,2,1:T(4,128)} %param.5) | data formatting | bytes 3072 | tf_op args[1]
  13.7 0.1 reshape.15.columns_ref
  13.8 0.1 stack.27.sources_ref
  13.9 0.0 copy-start
  13.9 1.9 %copy-done = bf16[16,6,64,256]{3,2,1,0:T(8,128)(2,1)S(1)} copy-done((bf16[16,6,64,256]{3,2,1,0:T(8,128)(2,1)S(1)}, bf16[16,6,64,256]{3,2,1,0:T(8,128)(2,1)}, u32[]{:S(2)}) %copy-start) | copy-done | bytes 3145752
  15.8 0.0 copy-start.1
  15.8 1.0 %copy-done.1 = f32[1024,128]{1,0:T(8,128)S(1)} copy-done((f32[1024,128]{1,0:T(8,128)S(1)}, f32[1024,128]{1,0:T(8,128)}, u32[]{:S(2)}) %copy-start.1) | copy-done | bytes 524312
  16.8 0.0 copy-start.3
  16.8 0.7 %copy-done.3 = f32[1024]{0:T(1024)S(1)} copy-done((f32[1024]{0:T(1024)S(1)}, f32[1024]{0:T(1024)}, u32[]{:S(2)}) %copy-start.3) | copy-done | bytes 4120
  17.5 1.0 %shard_map.59.partial_ref = f32[1024,128]{1,0:T(8,128)S(1)} custom-call(s32[6]{0:T(128)S(1)} %stack.27.sources_ref, s32[384]{0:T(512)S(1)} %reshape.15.columns_ref, bf16[16,6,64,256]{3,2,1,0:T(8,128)(2,1)S(1)} %copy-done, bf16[16,64,128]{2,1,0:T(8,128)(2,1)S(1)} %bitcast.13, f32[8,128]{1,0:T(8,128)S(1)} %bitcast.15, f32[1024,128]{1,0:T(8,128)S(1)} %copy-done.1), custom_call_target="tpu_custom_call" | custom-call | tf_op jit(solution)/shard_map/pallas_call | solution.py:245
  18.5 0.0 collective-permute-done.1.refs_1_
  18.5 0.0 collective-permute-done.2.refs_2_
  18.5 0.0 collective-permute-done.3.refs_3_
  18.5 1.5 %shard_map.60.partial_ref = f32[1024,128]{1,0:T(8,128)S(1)} custom-call(s32[6]{0:T(128)S(1)} %stack.27.sources_ref, s32[384]{0:T(512)S(1)} %reshape.15.columns_ref, bf16[16,6,64,256]{3,2,1,0:T(8,128)(2,1)S(1)} %copy-done, f32[1024,128]{1,0:T(8,128)S(1)} %shard_map.59.partial_ref, bf16[16,64,128]{2,1,0:T(8,128)(2,1)S(1)} %collective-permute-done.refs_0_, ...), custom_call_target="tpu_custom_call" | custom-call | tf_op jit(solution)/shard_map/pallas_call | solution.py:248
  20.0 0.0 copy-start.2
  20.0 0.0 collective-permute-done.4.piece_ref
  20.0 0.9 %shard_map.61 = (f32[1024,128]{1,0:T(8,128)S(1)}, bf16[16,64,128]{2,1,0:T(8,128)(2,1)S(1)}) custom-call(s32[6]{0:T(128)S(1)} %stack.27.sources_ref, s32[384]{0:T(512)S(1)} %reshape.15.columns_ref, bf16[16,6,64,256]{3,2,1,0:T(8,128)(2,1)S(1)} %copy-done, f32[1024,128]{1,0:T(8,128)S(1)} %shard_map.60.partial_ref, ...), custom_call_target="tpu_custom_call" | custom-call | tf_op jit(solution)/shard_map/pallas_call | solution.py:255
  20.9 1.7 %collective-permute-start.5 = (bf16[16,64,128]{2,1,0:T(8,128)(2,1)S(1)}, bf16[16,64,128]{2,1,0:T(8,128)(2,1)S(1)}, u32[]{:S(2)}, u32[]{:S(2)}) collective-permute-start(bf16[16,64,128]{2,1,0:T(8,128)(2,1)S(1)} %get-tuple-element.6.own_ref), channel_id=1, source_target_pairs={{0,1},{1,0},{2,3},{3,2},{4,6},{5,7},{6,4},{7,5},{8,9},{9,8},{10,11... | collective-permute-start | bytes 786440 | tf_op jit(solution)/shard_map/ppermute | solution.py:41
  22.6 1.3 %collective-permute-start.6 = (bf16[16,64,128]{2,1,0:T(8,128)(2,1)S(1)}, bf16[16,64,128]{2,1,0:T(8,128)(2,1)S(1)}, u32[]{:S(2)}, u32[]{:S(2)}) collective-permute-start(bf16[16,64,128]{2,1,0:T(8,128)(2,1)S(1)} %get-tuple-element.6.own_ref), channel_id=1, source_target_pairs={{0,2},{1,3},{2,0},{3,1},{4,5},{5,4},{6,7},{7,6},{8,10},{9,11},{10,... | collective-permute-start | bytes 786440 | tf_op jit(solution)/shard_map/ppermute | solution.py:41
  23.9 0.7 collective-permute-start.7
  24.6 3.0 %collective-permute-start.8 = (bf16[16,64,128]{2,1,0:T(8,128)(2,1)S(1)}, bf16[16,64,128]{2,1,0:T(8,128)(2,1)S(1)}, u32[]{:S(2)}, u32[]{:S(2)}) collective-permute-start(bf16[16,64,128]{2,1,0:T(8,128)(2,1)S(1)} %get-tuple-element.6.own_ref), channel_id=1, source_target_pairs={{0,4},{4,0},{8,12},{12,8},{16,20},{20,16},{24,28},{28,24},{1,5},{5... | collective-permute-start | bytes 786440 | tf_op jit(solution)/shard_map/ppermute | solution.py:23
  27.6 0.8 %collective-permute-done.5.refs_0_ = bf16[16,64,128]{2,1,0:T(8,128)(2,1)S(1)} collective-permute-done((bf16[16,64,128]{2,1,0:T(8,128)(2,1)S(1)}, bf16[16,64,128]{2,1,0:T(8,128)(2,1)S(1)}, u32[]{:S(2)}, u32[]{:S(2)}) %collective-permute-start.5) | collective-permute-done | bytes 262176 | tf_op jit(solution)/shard_map/ppermute | solution.py:41
  28.4 1.0 %collective-permute-start.9 = (bf16[16,64,128]{2,1,0:T(8,128)(2,1)S(1)}, bf16[16,64,128]{2,1,0:T(8,128)(2,1)S(1)}, u32[]{:S(2)}, u32[]{:S(2)}) collective-permute-start(bf16[16,64,128]{2,1,0:T(8,128)(2,1)S(1)} %collective-permute-done.5.refs_0_), channel_id=1, source_target_pairs={{0,2},{1,3},{2,0},{3,1},{4,5},{5,4},{6,7},{7,6},{8,10},{9,11},{10,... | collective-permute-start | bytes 786440 | tf_op jit(solution)/shard_map/ppermute | solution.py:41
  29.4 0.0 copy-done.2
  29.4 1.0 %shard_map.62.partial_ref = f32[1024,128]{1,0:T(8,128)S(1)} custom-call(s32[6]{0:T(128)S(1)} %stack.27.sources_ref, s32[384]{0:T(512)S(1)} %reshape.15.columns_ref, bf16[16,6,64,256]{3,2,1,0:T(8,128)(2,1)S(1)} %copy-done, bf16[16,64,128]{2,1,0:T(8,128)(2,1)S(1)} %get-tuple-element.6.own_ref, f32[8,128]{1,0:T(8,128)S(1)} %bitcast.16, ...), custom_call_target="tpu_custom_call" | custom-call | tf_op jit(solution)/shard_map/pallas_call | solution.py:245
  30.4 0.0 collective-permute-done.6.refs_1_
  30.4 0.0 collective-permute-done.7.refs_2_
  30.4 0.0 collective-permute-done.8.refs_3_
  30.4 1.5 %shard_map.63.partial_ref = f32[1024,128]{1,0:T(8,128)S(1)} custom-call(s32[6]{0:T(128)S(1)} %stack.27.sources_ref, s32[384]{0:T(512)S(1)} %reshape.15.columns_ref, bf16[16,6,64,256]{3,2,1,0:T(8,128)(2,1)S(1)} %copy-done, f32[1024,128]{1,0:T(8,128)S(1)} %shard_map.62.partial_ref, bf16[16,64,128]{2,1,0:T(8,128)(2,1)S(1)} %collective-permute-done.5.refs_0_, ...), custom_call_target="tpu_custom_call" | custom-call | tf_op jit(solution)/shard_map/pallas_call | solution.py:248
  31.9 2.9 %collective-permute-done.9.piece_ref = bf16[16,64,128]{2,1,0:T(8,128)(2,1)S(1)} collective-permute-done((bf16[16,64,128]{2,1,0:T(8,128)(2,1)S(1)}, bf16[16,64,128]{2,1,0:T(8,128)(2,1)S(1)}, u32[]{:S(2)}, u32[]{:S(2)}) %collective-permute-start.9) | collective-permute-done | bytes 262176 | tf_op jit(solution)/shard_map/ppermute | solution.py:41
  34.8 1.4 %shard_map.64 = (f32[1024,128]{1,0:T(8,128)S(1)}, f32[4,32,128]{2,1,0:T(8,128)S(1)}) custom-call(s32[6]{0:T(128)S(1)} %stack.27.sources_ref, s32[384]{0:T(512)S(1)} %reshape.15.columns_ref, bf16[16,6,64,256]{3,2,1,0:T(8,128)(2,1)S(1)} %copy-done, f32[1024,128]{1,0:T(8,128)S(1)} %shard_map.63.partial_ref, ...), custom_call_target="tpu_custom_call" | custom-call | tf_op jit(solution)/shard_map/pallas_call | solution.py:260
  36.2 7.2 %all_to_all.15 = f32[4,32,128]{2,1,0:T(8,128)S(1)} all-to-all(f32[4,32,128]{2,1,0:T(8,128)S(1)} %get-tuple-element.8), channel_id=1, replica_groups=mesh['group'=8,'blk'=4] {'blk'}, dimensions={0} | all-to-all | bytes 131072 | tf_op jit(solution)/shard_map/all_to_all | solution.py:50
  43.5 11.5 %all_to_all.16 = f32[8,32,128]{2,1,0:T(8,128)S(1)} all-to-all(f32[8,32,128]{2,1,0:T(8,128)S(1)} %broadcast_in_dim.6), channel_id=1, replica_groups=mesh['group'=8,'blk'=4] {'group'}, dimensions={0} | all-to-all | bytes 262144 | tf_op jit(solution)/shard_map/all_to_all | solution.py:46
  54.9 7.2 %all_to_all.17 = f32[4,32,128]{2,1,0:T(8,128)S(1)} all-to-all(f32[4,32,128]{2,1,0:T(8,128)S(1)} %broadcast_in_dim.7), channel_id=1, replica_groups=mesh['group'=8,'blk'=4] {'blk'}, dimensions={0} | all-to-all | bytes 131072 | tf_op jit(solution)/shard_map/all_to_all | solution.py:46
  62.1 5.1 %shard_map.65 = (f32[1024,128]{1,0:T(8,128)}, f32[128,128]{1,0:T(8,128)}) custom-call(f32[128,128]{1,0:T(8,128)S(1)} %bitcast.14, f32[1024,128]{1,0:T(8,128)S(1)} %get-tuple-element.9.filtered_ref), custom_call_target="tpu_custom_call" | custom-call | tf_op jit(solution)/shard_map/pallas_call | solution.py:264
  (4 shorter events, 0.0 us)
Async XLA Ops:
  1.7 9.6 %collective-permute-start = (bf16[16,64,128]{2,1,0:T(8,128)(2,1)S(1)}, bf16[16,64,128]{2,1,0:T(8,128)(2,1)S(1)}, u32[]{:S(2)}, u32[]{:S(2)}) collective-permute-start(bf16[16,64,128]{2,1,0:T(8,128)(2,1)S(1)} %bitcast.9), channel_id=1, source_target_pairs={{0,1},{1,0},{2,3},{3,2},{4,6},{5,7},{6,4},{7,5},{8,9},{9,8},{10,11... | collective-permute-start | bytes 786440 | tf_op jit(solution)/shard_map/ppermute | solution.py:41
  4.7 13.8 %collective-permute-start.1 = (bf16[16,64,128]{2,1,0:T(8,128)(2,1)S(1)}, bf16[16,64,128]{2,1,0:T(8,128)(2,1)S(1)}, u32[]{:S(2)}, u32[]{:S(2)}) collective-permute-start(bf16[16,64,128]{2,1,0:T(8,128)(2,1)S(1)} %bitcast.10), channel_id=1, source_target_pairs={{0,2},{1,3},{2,0},{3,1},{4,5},{5,4},{6,7},{7,6},{8,10},{9,11},{10,... | collective-permute-start | bytes 786440 | tf_op jit(solution)/shard_map/ppermute | solution.py:41
  6.2 12.3 %collective-permute-start.2 = (bf16[16,64,128]{2,1,0:T(8,128)(2,1)S(1)}, bf16[16,64,128]{2,1,0:T(8,128)(2,1)S(1)}, u32[]{:S(2)}, u32[]{:S(2)}) collective-permute-start(bf16[16,64,128]{2,1,0:T(8,128)(2,1)S(1)} %bitcast.11), channel_id=1, source_target_pairs={{4,8},{8,4},{12,16},{16,12},{20,24},{24,20},{5,9},{9,5},{13,17},{1... | collective-permute-start | bytes 786440 | tf_op jit(solution)/shard_map/ppermute | solution.py:23
  6.9 11.6 %collective-permute-start.3 = (bf16[16,64,128]{2,1,0:T(8,128)(2,1)S(1)}, bf16[16,64,128]{2,1,0:T(8,128)(2,1)S(1)}, u32[]{:S(2)}, u32[]{:S(2)}) collective-permute-start(bf16[16,64,128]{2,1,0:T(8,128)(2,1)S(1)} %bitcast.12), channel_id=1, source_target_pairs={{0,4},{4,0},{8,12},{12,8},{16,20},{20,16},{24,28},{28,24},{1,5},{5... | collective-permute-start | bytes 786440 | tf_op jit(solution)/shard_map/ppermute | solution.py:23
  11.3 8.7 %collective-permute-start.4 = (bf16[16,64,128]{2,1,0:T(8,128)(2,1)S(1)}, bf16[16,64,128]{2,1,0:T(8,128)(2,1)S(1)}, u32[]{:S(2)}, u32[]{:S(2)}) collective-permute-start(bf16[16,64,128]{2,1,0:T(8,128)(2,1)S(1)} %collective-permute-done.refs_0_), channel_id=1, source_target_pairs={{0,2},{1,3},{2,0},{3,1},{4,5},{5,4},{6,7},{7,6},{8,10},{9,11},{10,... | collective-permute-start | bytes 786440 | tf_op jit(solution)/shard_map/ppermute | solution.py:41
  13.9 1.9 %copy-start = (bf16[16,6,64,256]{3,2,1,0:T(8,128)(2,1)S(1)}, bf16[16,6,64,256]{3,2,1,0:T(8,128)(2,1)}, u32[]{:S(2)}) copy-start(bf16[16,6,64,256]{3,2,1,0:T(8,128)(2,1)} %hamiltonian_ref.11) | copy-start | bytes 9437188
  15.8 1.0 %copy-start.1 = (f32[1024,128]{1,0:T(8,128)S(1)}, f32[1024,128]{1,0:T(8,128)}, u32[]{:S(2)}) copy-start(f32[1024,128]{1,0:T(8,128)} %refs_0_.1) | copy-start | bytes 1572868
  16.8 0.7 %copy-start.3 = (f32[1024]{0:T(1024)S(1)}, f32[1024]{0:T(1024)}, u32[]{:S(2)}) copy-start(f32[1024]{0:T(1024)} %param.6) | copy-start | bytes 12292
  20.0 9.4 %copy-start.2 = (f32[1024,128]{1,0:T(8,128)S(1)}, f32[1024,128]{1,0:T(8,128)}, u32[]{:S(2)}) copy-start(f32[1024,128]{1,0:T(8,128)} %refs_0_.1) | copy-start | bytes 1572868
  20.9 7.5 %collective-permute-start.5 = (bf16[16,64,128]{2,1,0:T(8,128)(2,1)S(1)}, bf16[16,64,128]{2,1,0:T(8,128)(2,1)S(1)}, u32[]{:S(2)}, u32[]{:S(2)}) collective-permute-start(bf16[16,64,128]{2,1,0:T(8,128)(2,1)S(1)} %get-tuple-element.6.own_ref), channel_id=1, source_target_pairs={{0,1},{1,0},{2,3},{3,2},{4,6},{5,7},{6,4},{7,5},{8,9},{9,8},{10,11... | collective-permute-start | bytes 786440 | tf_op jit(solution)/shard_map/ppermute | solution.py:41
  22.6 7.8 %collective-permute-start.6 = (bf16[16,64,128]{2,1,0:T(8,128)(2,1)S(1)}, bf16[16,64,128]{2,1,0:T(8,128)(2,1)S(1)}, u32[]{:S(2)}, u32[]{:S(2)}) collective-permute-start(bf16[16,64,128]{2,1,0:T(8,128)(2,1)S(1)} %get-tuple-element.6.own_ref), channel_id=1, source_target_pairs={{0,2},{1,3},{2,0},{3,1},{4,5},{5,4},{6,7},{7,6},{8,10},{9,11},{10,... | collective-permute-start | bytes 786440 | tf_op jit(solution)/shard_map/ppermute | solution.py:41
  23.9 6.5 %collective-permute-start.7 = (bf16[16,64,128]{2,1,0:T(8,128)(2,1)S(1)}, bf16[16,64,128]{2,1,0:T(8,128)(2,1)S(1)}, u32[]{:S(2)}, u32[]{:S(2)}) collective-permute-start(bf16[16,64,128]{2,1,0:T(8,128)(2,1)S(1)} %get-tuple-element.6.own_ref), channel_id=1, source_target_pairs={{4,8},{8,4},{12,16},{16,12},{20,24},{24,20},{5,9},{9,5},{13,17},{1... | collective-permute-start | bytes 786440 | tf_op jit(solution)/shard_map/ppermute | solution.py:23
  24.6 5.8 %collective-permute-start.8 = (bf16[16,64,128]{2,1,0:T(8,128)(2,1)S(1)}, bf16[16,64,128]{2,1,0:T(8,128)(2,1)S(1)}, u32[]{:S(2)}, u32[]{:S(2)}) collective-permute-start(bf16[16,64,128]{2,1,0:T(8,128)(2,1)S(1)} %get-tuple-element.6.own_ref), channel_id=1, source_target_pairs={{0,4},{4,0},{8,12},{12,8},{16,20},{20,16},{24,28},{28,24},{1,5},{5... | collective-permute-start | bytes 786440 | tf_op jit(solution)/shard_map/ppermute | solution.py:23
  28.4 6.4 %collective-permute-start.9 = (bf16[16,64,128]{2,1,0:T(8,128)(2,1)S(1)}, bf16[16,64,128]{2,1,0:T(8,128)(2,1)S(1)}, u32[]{:S(2)}, u32[]{:S(2)}) collective-permute-start(bf16[16,64,128]{2,1,0:T(8,128)(2,1)S(1)} %collective-permute-done.5.refs_0_), channel_id=1, source_target_pairs={{0,2},{1,3},{2,0},{3,1},{4,5},{5,4},{6,7},{7,6},{8,10},{9,11},{10,... | collective-permute-start | bytes 786440 | tf_op jit(solution)/shard_map/ppermute | solution.py:41

commit v6 on v3

--- a/solution.py
+++ b/solution.py
@@ -12,6 +12,7 @@
 SUB = 8
 VMEM_LIMIT = 40 * 1024 * 1024
 vmem = pl.BlockSpec(memory_space=pltpu.VMEM)
+hbm = pl.BlockSpec(memory_space=pl.ANY)
 smem = pl.BlockSpec(memory_space=pltpu.SMEM)
 
 
@@ -39,6 +40,37 @@
             for index in range(cycle_size)
         ]
     return lax.ppermute(value, ("group", "blk"), route)
+
+
+def on_odd_cores(value, axis, flip):
+    groups, cycle_size = lax.axis_size("group"), lax.axis_size("blk")
+    route = []
+    for group in range(1, groups, 2):
+        for index in range(cycle_size):
+            if axis == "group":
+                partner = (group ^ 2 * flip) * cycle_size + index
+            else:
+                partner = group * cycle_size + (index ^ flip)
+            route.append((group * cycle_size + index, partner))
+    return lax.ppermute(value, ("group", "blk"), route)
+
+
+def summed(value):
+    groups = lax.axis_size("group")
+    odd = lax.axis_index("group") % 2 == 1
+    up = [(group, group + 1) for group in range(0, groups - 1, 2)]
+    down = [(target, source) for source, target in up]
+    value = jnp.where(odd, value + lax.ppermute(value, "group", up), 0.0)
+    for axis, count in (("group", groups // 2), ("blk", lax.axis_size("blk"))):
+        step = 1
+        while step < count:
+            flips = [step, 2 * step, 3 * step] if 2 * step < count else [step]
+            others = [on_odd_cores(value, axis, flip) for flip in flips]
+            value = value + others[0]
+            if len(others) == 3:
+                value = value + (others[1] + others[2])
+            step *= len(flips) + 1
+    return value + lax.ppermute(value, "group", down)
 
 
 def potential_columns(potential_ref):
@@ -152,8 +184,8 @@
     return estimate * (2.0 - value * estimate)
 
 
-def factor_kernel(rows_total, packed_ref, filtered_ref, ortho_ref, upper_ref, inverse_ref):
-    size = packed_ref.shape[1]
+def factor(gram, upper_ref, inverse_ref):
+    size = gram.shape[1]
     panels = size // SUB
     shape = (SUB, size)
     row_index = lax.broadcasted_iota(jnp.int32, shape, 0)
@@ -165,59 +197,99 @@
     def along_rows(panel, row):
         return jnp.broadcast_to(panel[row : row + 1, :], shape)
 
-    gram = unpack(packed_ref) * (1.0 / rows_total)
-    matrix = [gram[k * SUB : (k + 1) * SUB, :] for k in range(panels)]
-    inverse = [
-        jnp.where(lane_index == row_index + k * SUB, 1.0, 0.0).astype(jnp.float32)
-        for k in range(panels)
-    ]
-    block = along_lanes(matrix[0], 0)
+    held = [gram[k * SUB : (k + 1) * SUB, :] for k in range(panels)]
+    block = along_lanes(held[0], 0)
     for k in range(panels):
-        below = {p: along_lanes(matrix[p], k * SUB) for p in range(k + 1, panels)}
-        following = along_lanes(matrix[k + 1], (k + 1) * SUB) if k + 1 < panels else None
+        first = k * SUB
+        below = {p: along_lanes(held[p], first) for p in range(k + 1, panels)}
+        after = list(below[k + 1]) if k + 1 < panels else None
+        following = along_lanes(held[k + 1], first + SUB) if k + 1 < panels else None
+        right = jnp.where(lane_index >= first, held[k], 0.0)
+        left = jnp.where(
+            lane_index < first, held[k], jnp.where(lane_index == row_index + first, 1.0, 0.0)
+        )
         pivots = jnp.ones(shape, jnp.float32)
-        for j in range(SUB):
-            pivot = along_rows(block[j], j)
-            reciprocal = inverse_of(pivot)
-            pivots = jnp.where(row_index == j, pivot, pivots)
-            factors = {c: along_rows(block[c], j) * reciprocal for c in range(j + 1, SUB)}
-            for c in factors:
-                block[c] = block[c] - block[j] * factors[c]
+        reciprocals = jnp.ones(shape, jnp.float32)
+        for j in range(0, SUB, 2):
+            a, b, c = along_rows(block[j], j), along_rows(block[j], j + 1), along_rows(block[j + 1], j + 1)
+            determinant = a * c - b * b
+            over = inverse_of(determinant)
+            over_a = inverse_of(a)
+            shift = b * over_a
+            pivots = jnp.where(row_index == j, a, pivots)
+            pivots = jnp.where(row_index == j + 1, determinant * over_a, pivots)
+            reciprocals = jnp.where(row_index == j, over_a, reciprocals)
+            reciprocals = jnp.where(row_index == j + 1, a * over, reciprocals)
+            x, y = block[j], block[j + 1]
+            one = jnp.where(row_index > j + 1, (x * c - y * b) * over, jnp.where(row_index == j + 1, shift, 0.0))
+            two = jnp.where(row_index > j + 1, (y * a - x * b) * over, 0.0)
+            upper = {n: (along_rows(block[n], j), along_rows(block[n], j + 1)) for n in range(j + 2, SUB)}
+            for n in upper:
+                block[n] = block[n] - one * upper[n][0] - two * upper[n][1]
             if following is not None:
-                column = below[k + 1][j]
-                for c in factors:
-                    below[k + 1][c] = below[k + 1][c] - column * factors[c]
-                scaled = column * reciprocal
-                for c in range(SUB):
-                    following[c] = following[c] - column * along_rows(scaled, c)
-            lower_part = jnp.where(row_index > j, block[j], 0.0)
-            row = along_rows(matrix[k], j) * reciprocal
-            inverse_row = along_rows(inverse[k], j) * reciprocal
-            matrix[k] = matrix[k] - lower_part * row
-            inverse[k] = inverse[k] - lower_part * inverse_row
+                x, y = after[j], after[j + 1]
+                next_one, next_two = (x * c - y * b) * over, (y * a - x * b) * over
+                for n in range(SUB):
+                    following[n] = following[n] - next_one * along_rows(x, n) - next_two * along_rows(y, n)
+                for n in upper:
+                    after[n] = after[n] - next_one * upper[n][0] - next_two * upper[n][1]
+            right = right - one * along_rows(right, j) - two * along_rows(right, j + 1)
+            left = left - one * along_rows(left, j) - two * along_rows(left, j + 1)
+        scale = lax.rsqrt(pivots)
+        upper_ref[pl.ds(first, SUB), :] = jnp.where(lane_index >= row_index + first, right * scale, 0.0)
+        inverse_ref[pl.ds(first, SUB), :] = left * scale
+        if k + 1 < panels:
+            reduced = jnp.where(lane_index >= first + SUB, right, left) * reciprocals
+            for n in range(SUB - 1, 0, -1):
+                column = jnp.where(row_index < n, block[n] * reciprocals, 0.0)
+                reduced = reduced - column * along_rows(reduced, n)
+            rows = [along_rows(reduced, n) for n in range(SUB)]
+            inside = (lane_index >= first) & (lane_index < first + SUB)
             for p in below:
-                if p > k + 1:
-                    for c in factors:
-                        below[p][c] = below[p][c] - below[p][j] * factors[c]
-                matrix[p] = matrix[p] - below[p][j] * row
-                inverse[p] = inverse[p] - below[p][j] * inverse_row
+                total = jnp.where(inside, 0.0, held[p])
+                for n in range(SUB):
+                    total = total - below[p][n] * rows[n]
+                held[p] = total
         block = following
-        scale = lax.rsqrt(pivots)
-        upper = jnp.where(lane_index >= row_index + k * SUB, matrix[k] * scale, 0.0)
-        upper_ref[pl.ds(k * SUB, SUB), :] = upper
-        inverse_ref[pl.ds(k * SUB, SUB), :] = inverse[k] * scale
-    ortho_ref[...] = lax.dot_general(
-        filtered_ref[...], inverse_ref[...], (((1,), (1,)), ((), ())), precision=precise,
-        preferred_element_type=jnp.float32,
-    )
-
-
-def call(kernel, out_shape, in_specs, scratch=()):
+
+
+def two_parts(value):
+    high = value.astype(jnp.bfloat16)
+    return high, (value - high.astype(jnp.float32)).astype(jnp.bfloat16)
+
+
+def factor_kernel(
+    rows_total, packed_ref, filtered_ref, ortho_hbm, upper_hbm,
+    upper_ref, inverse_ref, ortho_ref, sent, upper_sent,
+):
+    factor(unpack(packed_ref) * (1.0 / rows_total), upper_ref, inverse_ref)
+    copies = [pltpu.make_async_copy(upper_ref, upper_hbm, upper_sent)]
+    copies[0].start()
+    high, low = two_parts(inverse_ref[...])
+    right = jnp.concatenate([high, high, low], axis=1)
+    chunks = sent.shape[0]
+    per_chunk = filtered_ref.shape[0] // chunks
+    for chunk in range(chunks):
+        rows = pl.ds(chunk * per_chunk, per_chunk)
+        high, low = two_parts(filtered_ref[rows, :])
+        ortho_ref[rows, :] = lax.dot_general(
+            jnp.concatenate([high, low, high], axis=1), right, (((1,), (1,)), ((), ())),
+            preferred_element_type=jnp.float32,
+        )
+        copies.append(
+            pltpu.make_async_copy(ortho_ref.at[rows, :], ortho_hbm.at[rows, :], sent.at[chunk])
+        )
+        copies[-1].start()
+    for copy in copies:
+        copy.wait()
+
+
+def call(kernel, out_shape, in_specs, scratch=(), out_spec=vmem):
     return pl.pallas_call(
         kernel,
         out_shape=out_shape,
         in_specs=in_specs,
-        out_specs=jax.tree.map(lambda _: vmem, out_shape),
+        out_specs=jax.tree.map(lambda _: out_spec, out_shape),
         scratch_shapes=list(scratch),
         compiler_params=pltpu.CompilerParams(vmem_limit_bytes=VMEM_LIMIT),
     )
@@ -272,12 +344,19 @@
     filtered, gram = call(
         functools.partial(second_kernel, last), (flat, packed), [smem] * 2 + [vmem] * 3
     )(sources, columns, hamiltonian, partial, pieces[last])
-    gram = lax.psum(gram, ("group", "blk"))
+    gram = summed(gram)
     return call(
         functools.partial(factor_kernel, rows_total),
         (flat, square),
         [vmem, vmem],
-        [pltpu.VMEM((states, states), jnp.float32)],
+        [
+            pltpu.VMEM((states, states), jnp.float32),
+            pltpu.VMEM((states, states), jnp.float32),
+            pltpu.VMEM((flat_rows, states), jnp.float32),
+            pltpu.SemaphoreType.DMA((4,)),
+            pltpu.SemaphoreType.DMA,
+        ],
+        hbm,
     )(gram, filtered)
 
 

time: 81.8 us -> 71 us (0.87)
  blocking collectives: 39.8 us -> 0 us
  waiting for transfers between devices: 5.16 us -> 27.6 us
  starting transfers between devices: 17.4 us -> 24 us
    psum x1 -> x0, blocking collectives: 39.8 us -> none  [on_device(): gram = lax.psum(gram, ('group', 'blk'))]
    ppermute x0 -> x8, waiting for transfers between devices: none -> 22.5 us  [the longest x1 21.6 us: summed(): return value + lax.ppermute(value, 'group', down)]
    ppermute x0 -> x8, starting transfers between devices: none -> 6.55 us  [the longest x6 3.97 us: on_odd_cores(): return lax.ppermute(value, ('group', 'blk'), route)]
  transfers between devices with their start and end apart: 10 -> 18, of which waited for: 3 -> 5; matrix products, arithmetic and copies ran while one was open for 1% -> 1% of each run, Pallas kernels for 6% -> 7%
where the time goes in v6:
time: 71 us; the launch traced here: 70.4 us
  waiting for transfers between devices  27.6 us (39%)
  starting transfers between devices  24 us (34%)
  Pallas kernels  12.2 us (17%)
  local copies, waits for them, and re-layouts  4.64 us (7%)
  other arithmetic  1.11 us (2%)
  between operations  0.89 us (1%)
    ppermute x1, waiting for transfers between devices, summed(): return value + lax.ppermute(value, 'group', down)  21.6 us
    ppermute x6, starting transfers between devices, cycle_exchange(): return lax.ppermute(value, ('group', 'blk'), route)  10.1 us
    ppermute x4, starting transfers between devices, pair_exchange(): return lax.ppermute(value, 'group', route)  7.31 us
    ppermute x6, waiting for transfers between devices, cycle_exchange(): return lax.ppermute(value, ('group', 'blk'), route)  5.15 us
    pallas_call x1, Pallas kernels, on_device(): call(functools.partial(factor_kernel, rows_total), (flat, square), [vmem,...  4.97 us
    unnamed x9, local copies, waits for them, and re-layouts  4.44 us
    ppermute x6, starting transfers between devices, on_odd_cores(): return lax.ppermute(value, ('group', 'blk'), route)  3.97 us
    pallas_call x2, Pallas kernels, most(): call(functools.partial(middle_kernel, middle), flat, [smem] * 2 + [vmem]...  2.96 us
  transfers between devices with their start and end apart: 18, of which 5 were waited for; matrix products, arithmetic and copies ran while one was open for 1% of the time, Pallas kernels for 7%

profile of v6, /device:TPU:0, one launch (start us, length us, event | category | flops | bytes accessed | tf_op | source)
XLA Modules:
  0.0 70.4 jit_solution(400527357335363763)
XLA Ops:
  0.6 1.1 %convert_element_type.5 = bf16[1024,128]{1,0:T(8,128)(2,1)S(1)} convert(f32[1024,128]{1,0:T(8,128)} %refs_0_.1) | non-fusion elementwise | flops 131072 | bytes 786432 | tf_op jit(solution)/shard_map/convert_element_type | solution.py:337
  1.7 3.0 %collective-permute-start = (bf16[16,64,128]{2,1,0:T(8,128)(2,1)S(1)}, bf16[16,64,128]{2,1,0:T(8,128)(2,1)S(1)}, u32[]{:S(2)}, u32[]{:S(2)}) collective-permute-start(bf16[16,64,128]{2,1,0:T(8,128)(2,1)S(1)} %bitcast.8), channel_id=1, source_target_pairs={{0,1},{1,0},{2,3},{3,2},{4,6},{5,7},{6,4},{7,5},{8,9},{9,8},{10,11... | collective-permute-start | bytes 786440 | tf_op jit(solution)/shard_map/ppermute | solution.py:42
  4.7 1.5 %collective-permute-start.1 = (bf16[16,64,128]{2,1,0:T(8,128)(2,1)S(1)}, bf16[16,64,128]{2,1,0:T(8,128)(2,1)S(1)}, u32[]{:S(2)}, u32[]{:S(2)}) collective-permute-start(bf16[16,64,128]{2,1,0:T(8,128)(2,1)S(1)} %bitcast.9), channel_id=1, source_target_pairs={{0,2},{1,3},{2,0},{3,1},{4,5},{5,4},{6,7},{7,6},{8,10},{9,11},{10,... | collective-permute-start | bytes 786440 | tf_op jit(solution)/shard_map/ppermute | solution.py:42
  6.2 0.7 collective-permute-start.2
  6.9 3.0 %collective-permute-start.3 = (bf16[16,64,128]{2,1,0:T(8,128)(2,1)S(1)}, bf16[16,64,128]{2,1,0:T(8,128)(2,1)S(1)}, u32[]{:S(2)}, u32[]{:S(2)}) collective-permute-start(bf16[16,64,128]{2,1,0:T(8,128)(2,1)S(1)} %bitcast.11), channel_id=1, source_target_pairs={{0,4},{4,0},{8,12},{12,8},{16,20},{20,16},{24,28},{28,24},{1,5},{5... | collective-permute-start | bytes 786440 | tf_op jit(solution)/shard_map/ppermute | solution.py:24
  9.9 1.4 %collective-permute-done.refs_0_ = bf16[16,64,128]{2,1,0:T(8,128)(2,1)S(1)} collective-permute-done((bf16[16,64,128]{2,1,0:T(8,128)(2,1)S(1)}, bf16[16,64,128]{2,1,0:T(8,128)(2,1)S(1)}, u32[]{:S(2)}, u32[]{:S(2)}) %collective-permute-start) | collective-permute-done | bytes 262176 | tf_op jit(solution)/shard_map/ppermute | solution.py:42
  11.3 1.6 %collective-permute-start.4 = (bf16[16,64,128]{2,1,0:T(8,128)(2,1)S(1)}, bf16[16,64,128]{2,1,0:T(8,128)(2,1)S(1)}, u32[]{:S(2)}, u32[]{:S(2)}) collective-permute-start(bf16[16,64,128]{2,1,0:T(8,128)(2,1)S(1)} %collective-permute-done.refs_0_), channel_id=1, source_target_pairs={{0,2},{1,3},{2,0},{3,1},{4,5},{5,4},{6,7},{7,6},{8,10},{9,11},{10,... | collective-permute-start | bytes 786440 | tf_op jit(solution)/shard_map/ppermute | solution.py:42
  12.9 0.8 %copy.6 = s32[16,6,4]{2,1,0:T(8,128)S(1)} copy(s32[16,6,4]{0,2,1:T(4,128)} %param.5) | data formatting | bytes 3072 | tf_op args[1]
  13.7 0.1 reshape.12.columns_ref
  13.8 0.1 stack.27.sources_ref
  13.9 0.0 copy-start
  13.9 1.9 %copy-done = bf16[16,6,64,256]{3,2,1,0:T(8,128)(2,1)S(1)} copy-done((bf16[16,6,64,256]{3,2,1,0:T(8,128)(2,1)S(1)}, bf16[16,6,64,256]{3,2,1,0:T(8,128)(2,1)}, u32[]{:S(2)}) %copy-start) | copy-done | bytes 3145752
  15.8 0.0 copy-start.1
  15.8 1.0 %copy-done.1 = f32[1024,128]{1,0:T(8,128)S(1)} copy-done((f32[1024,128]{1,0:T(8,128)S(1)}, f32[1024,128]{1,0:T(8,128)}, u32[]{:S(2)}) %copy-start.1) | copy-done | bytes 524312
  16.8 0.0 copy-start.3
  16.8 0.7 copy-done.3
  17.5 1.0 %shard_map.59.partial_ref = f32[1024,128]{1,0:T(8,128)S(1)} custom-call(s32[6]{0:T(128)S(1)} %stack.27.sources_ref, s32[384]{0:T(512)S(1)} %reshape.12.columns_ref, bf16[16,6,64,256]{3,2,1,0:T(8,128)(2,1)S(1)} %copy-done, bf16[16,64,128]{2,1,0:T(8,128)(2,1)S(1)} %bitcast.12, f32[8,128]{1,0:T(8,128)S(1)} %bitcast.13, f32[1024,128]{1,0:T(8,128)S(1)} %copy-done.1), custom_call_target="tpu_custom_call" | custom-call | tf_op jit(solution)/shard_map/pallas_call | solution.py:329
  18.5 0.0 collective-permute-done.1.refs_1_
  18.5 0.0 collective-permute-done.2.refs_2_
  18.5 0.0 collective-permute-done.3.refs_3_
  18.5 1.5 %shard_map.60.partial_ref = f32[1024,128]{1,0:T(8,128)S(1)} custom-call(s32[6]{0:T(128)S(1)} %stack.27.sources_ref, s32[384]{0:T(512)S(1)} %reshape.12.columns_ref, bf16[16,6,64,256]{3,2,1,0:T(8,128)(2,1)S(1)} %copy-done, f32[1024,128]{1,0:T(8,128)S(1)} %shard_map.59.partial_ref, bf16[16,64,128]{2,1,0:T(8,128)(2,1)S(1)} %collective-permute-done.refs_0_, ...), custom_call_target="tpu_custom_call" | custom-call | tf_op jit(solution)/shard_map/pallas_call | solution.py:332
  20.0 0.0 copy-start.2
  20.0 0.0 collective-permute-done.4.piece_ref
  20.0 0.9 %shard_map.61 = (f32[1024,128]{1,0:T(8,128)S(1)}, bf16[16,64,128]{2,1,0:T(8,128)(2,1)S(1)}) custom-call(s32[6]{0:T(128)S(1)} %stack.27.sources_ref, s32[384]{0:T(512)S(1)} %reshape.12.columns_ref, bf16[16,6,64,256]{3,2,1,0:T(8,128)(2,1)S(1)} %copy-done, f32[1024,128]{1,0:T(8,128)S(1)} %shard_map.60.partial_ref, ...), custom_call_target="tpu_custom_call" | custom-call | tf_op jit(solution)/shard_map/pallas_call | solution.py:339
  20.9 1.7 %collective-permute-start.5 = (bf16[16,64,128]{2,1,0:T(8,128)(2,1)S(1)}, bf16[16,64,128]{2,1,0:T(8,128)(2,1)S(1)}, u32[]{:S(2)}, u32[]{:S(2)}) collective-permute-start(bf16[16,64,128]{2,1,0:T(8,128)(2,1)S(1)} %get-tuple-element.6.own_ref), channel_id=1, source_target_pairs={{0,1},{1,0},{2,3},{3,2},{4,6},{5,7},{6,4},{7,5},{8,9},{9,8},{10,11... | collective-permute-start | bytes 786440 | tf_op jit(solution)/shard_map/ppermute | solution.py:42
  22.6 1.3 %collective-permute-start.6 = (bf16[16,64,128]{2,1,0:T(8,128)(2,1)S(1)}, bf16[16,64,128]{2,1,0:T(8,128)(2,1)S(1)}, u32[]{:S(2)}, u32[]{:S(2)}) collective-permute-start(bf16[16,64,128]{2,1,0:T(8,128)(2,1)S(1)} %get-tuple-element.6.own_ref), channel_id=1, source_target_pairs={{0,2},{1,3},{2,0},{3,1},{4,5},{5,4},{6,7},{7,6},{8,10},{9,11},{10,... | collective-permute-start | bytes 786440 | tf_op jit(solution)/shard_map/ppermute | solution.py:42
  23.9 0.7 collective-permute-start.7
  24.6 3.0 %collective-permute-start.8 = (bf16[16,64,128]{2,1,0:T(8,128)(2,1)S(1)}, bf16[16,64,128]{2,1,0:T(8,128)(2,1)S(1)}, u32[]{:S(2)}, u32[]{:S(2)}) collective-permute-start(bf16[16,64,128]{2,1,0:T(8,128)(2,1)S(1)} %get-tuple-element.6.own_ref), channel_id=1, source_target_pairs={{0,4},{4,0},{8,12},{12,8},{16,20},{20,16},{24,28},{28,24},{1,5},{5... | collective-permute-start | bytes 786440 | tf_op jit(solution)/shard_map/ppermute | solution.py:24
  27.6 0.8 %collective-permute-done.5.refs_0_ = bf16[16,64,128]{2,1,0:T(8,128)(2,1)S(1)} collective-permute-done((bf16[16,64,128]{2,1,0:T(8,128)(2,1)S(1)}, bf16[16,64,128]{2,1,0:T(8,128)(2,1)S(1)}, u32[]{:S(2)}, u32[]{:S(2)}) %collective-permute-start.5) | collective-permute-done | bytes 262176 | tf_op jit(solution)/shard_map/ppermute | solution.py:42
  28.4 1.0 %collective-permute-start.9 = (bf16[16,64,128]{2,1,0:T(8,128)(2,1)S(1)}, bf16[16,64,128]{2,1,0:T(8,128)(2,1)S(1)}, u32[]{:S(2)}, u32[]{:S(2)}) collective-permute-start(bf16[16,64,128]{2,1,0:T(8,128)(2,1)S(1)} %collective-permute-done.5.refs_0_), channel_id=1, source_target_pairs={{0,2},{1,3},{2,0},{3,1},{4,5},{5,4},{6,7},{7,6},{8,10},{9,11},{10,... | collective-permute-start | bytes 786440 | tf_op jit(solution)/shard_map/ppermute | solution.py:42
  29.4 0.0 copy-done.2
  29.4 1.0 %shard_map.62.partial_ref = f32[1024,128]{1,0:T(8,128)S(1)} custom-call(s32[6]{0:T(128)S(1)} %stack.27.sources_ref, s32[384]{0:T(512)S(1)} %reshape.12.columns_ref, bf16[16,6,64,256]{3,2,1,0:T(8,128)(2,1)S(1)} %copy-done, bf16[16,64,128]{2,1,0:T(8,128)(2,1)S(1)} %get-tuple-element.6.own_ref, f32[8,128]{1,0:T(8,128)S(1)} %bitcast.14, ...), custom_call_target="tpu_custom_call" | custom-call | tf_op jit(solution)/shard_map/pallas_call | solution.py:329
  30.4 0.0 collective-permute-done.6.refs_1_
  30.4 0.0 collective-permute-done.7.refs_2_
  30.4 0.0 collective-permute-done.8.refs_3_
  30.4 1.5 %shard_map.63.partial_ref = f32[1024,128]{1,0:T(8,128)S(1)} custom-call(s32[6]{0:T(128)S(1)} %stack.27.sources_ref, s32[384]{0:T(512)S(1)} %reshape.12.columns_ref, bf16[16,6,64,256]{3,2,1,0:T(8,128)(2,1)S(1)} %copy-done, f32[1024,128]{1,0:T(8,128)S(1)} %shard_map.62.partial_ref, bf16[16,64,128]{2,1,0:T(8,128)(2,1)S(1)} %collective-permute-done.5.refs_0_, ...), custom_call_target="tpu_custom_call" | custom-call | tf_op jit(solution)/shard_map/pallas_call | solution.py:332
  31.9 2.9 %collective-permute-done.9.piece_ref = bf16[16,64,128]{2,1,0:T(8,128)(2,1)S(1)} collective-permute-done((bf16[16,64,128]{2,1,0:T(8,128)(2,1)S(1)}, bf16[16,64,128]{2,1,0:T(8,128)(2,1)S(1)}, u32[]{:S(2)}, u32[]{:S(2)}) %collective-permute-start.9) | collective-permute-done | bytes 262176 | tf_op jit(solution)/shard_map/ppermute | solution.py:42
  34.8 1.5 %shard_map.64 = (f32[1024,128]{1,0:T(8,128)S(1)}, f32[72,128]{1,0:T(8,128)S(1)}) custom-call(s32[6]{0:T(128)S(1)} %stack.27.sources_ref, s32[384]{0:T(512)S(1)} %reshape.12.columns_ref, bf16[16,6,64,256]{3,2,1,0:T(8,128)(2,1)S(1)} %copy-done, f32[1024,128]{1,0:T(8,128)S(1)} %shard_map.63.partial_ref, bf16[16,64,128]{2,1,0:T(8,128)(2,1)S(1)} %collective-permute-done.9.piece_ref), custom_call_target="tpu_custom_call" | custom-call | tf_op jit(solution)/shard_map/pallas_call | solution.py:344
  36.3 1.3 %collective-permute-start.10 = (f32[72,128]{1,0:T(8,128)S(1)}, f32[72,128]{1,0:T(8,128)S(1)}, u32[]{:S(2)}, u32[]{:S(2)}) collective-permute-start(f32[72,128]{1,0:T(8,128)S(1)} %get-tuple-element.8), channel_id=1, source_target_pairs={{0,4},{8,12},{16,20},{24,28},{1,5},{9,13},{17,21},{25,29},{2,6},{1... | collective-permute-start | bytes 110600 | tf_op jit(solution)/shard_map/ppermute | solution.py:63
  37.6 0.8 %collective-permute-done.10 = f32[72,128]{1,0:T(8,128)S(1)} collective-permute-done((f32[72,128]{1,0:T(8,128)S(1)}, f32[72,128]{1,0:T(8,128)S(1)}, u32[]{:S(2)}, u32[]{:S(2)}) %collective-permute-start.10) | collective-permute-done | bytes 36896 | tf_op jit(solution)/shard_map/ppermute | solution.py:63
  38.4 0.7 collective-permute-start.11
  39.1 0.7 collective-permute-start.12
  39.8 0.7 collective-permute-start.13
  40.4 0.0 collective-permute-done.11
  40.4 0.0 collective-permute-done.12
  40.4 0.0 collective-permute-done.13
  40.5 0.7 collective-permute-start.14
  41.1 0.7 collective-permute-start.15
  41.8 0.7 collective-permute-start.16
  42.5 0.0 collective-permute-done.14
  42.5 0.0 collective-permute-done.15
  42.5 0.0 collective-permute-done.16
  42.5 1.3 %collective-permute-start.17 = (f32[72,128]{1,0:T(8,128)S(1)}, f32[72,128]{1,0:T(8,128)S(1)}, u32[]{:S(2)}, u32[]{:S(2)}) collective-permute-start(f32[72,128]{1,0:T(8,128)S(1)} %add_add_fusion), channel_id=1, source_target_pairs={{4,0},{12,8},{20,16},{28,24},{5,1},{13,9},{21,17},{29,25},{6,2},{1... | collective-permute-start | bytes 110600 | tf_op jit(solution)/shard_map/ppermute | solution.py:73
  43.8 21.6 %collective-permute-done.17 = f32[72,128]{1,0:T(8,128)S(1)} collective-permute-done((f32[72,128]{1,0:T(8,128)S(1)}, f32[72,128]{1,0:T(8,128)S(1)}, u32[]{:S(2)}, u32[]{:S(2)}) %collective-permute-start.17) | collective-permute-done | bytes 36896 | tf_op jit(solution)/shard_map/ppermute | solution.py:73
  65.5 5.0 %shard_map.65 = (f32[1024,128]{1,0:T(8,128)}, f32[128,128]{1,0:T(8,128)}) custom-call(f32[72,128]{1,0:T(8,128)S(1)} %add.39.packed_ref, f32[1024,128]{1,0:T(8,128)S(1)} %get-tuple-element.9.filtered_ref), custom_call_target="tpu_custom_call" | custom-call | tf_op jit(solution)/shard_map/pallas_call | solution.py:348
  (4 shorter events, 0.0 us)
Async XLA Ops:
  1.7 9.6 %collective-permute-start = (bf16[16,64,128]{2,1,0:T(8,128)(2,1)S(1)}, bf16[16,64,128]{2,1,0:T(8,128)(2,1)S(1)}, u32[]{:S(2)}, u32[]{:S(2)}) collective-permute-start(bf16[16,64,128]{2,1,0:T(8,128)(2,1)S(1)} %bitcast.8), channel_id=1, source_target_pairs={{0,1},{1,0},{2,3},{3,2},{4,6},{5,7},{6,4},{7,5},{8,9},{9,8},{10,11... | collective-permute-start | bytes 786440 | tf_op jit(solution)/shard_map/ppermute | solution.py:42
  4.7 13.8 %collective-permute-start.1 = (bf16[16,64,128]{2,1,0:T(8,128)(2,1)S(1)}, bf16[16,64,128]{2,1,0:T(8,128)(2,1)S(1)}, u32[]{:S(2)}, u32[]{:S(2)}) collective-permute-start(bf16[16,64,128]{2,1,0:T(8,128)(2,1)S(1)} %bitcast.9), channel_id=1, source_target_pairs={{0,2},{1,3},{2,0},{3,1},{4,5},{5,4},{6,7},{7,6},{8,10},{9,11},{10,... | collective-permute-start | bytes 786440 | tf_op jit(solution)/shard_map/ppermute | solution.py:42
  6.2 12.3 %collective-permute-start.2 = (bf16[16,64,128]{2,1,0:T(8,128)(2,1)S(1)}, bf16[16,64,128]{2,1,0:T(8,128)(2,1)S(1)}, u32[]{:S(2)}, u32[]{:S(2)}) collective-permute-start(bf16[16,64,128]{2,1,0:T(8,128)(2,1)S(1)} %bitcast.10), channel_id=1, source_target_pairs={{4,8},{8,4},{12,16},{16,12},{20,24},{24,20},{5,9},{9,5},{13,17},{1... | collective-permute-start | bytes 786440 | tf_op jit(solution)/shard_map/ppermute | solution.py:24
  6.9 11.6 %collective-permute-start.3 = (bf16[16,64,128]{2,1,0:T(8,128)(2,1)S(1)}, bf16[16,64,128]{2,1,0:T(8,128)(2,1)S(1)}, u32[]{:S(2)}, u32[]{:S(2)}) collective-permute-start(bf16[16,64,128]{2,1,0:T(8,128)(2,1)S(1)} %bitcast.11), channel_id=1, source_target_pairs={{0,4},{4,0},{8,12},{12,8},{16,20},{20,16},{24,28},{28,24},{1,5},{5... | collective-permute-start | bytes 786440 | tf_op jit(solution)/shard_map/ppermute | solution.py:24
  11.3 8.7 %collective-permute-start.4 = (bf16[16,64,128]{2,1,0:T(8,128)(2,1)S(1)}, bf16[16,64,128]{2,1,0:T(8,128)(2,1)S(1)}, u32[]{:S(2)}, u32[]{:S(2)}) collective-permute-start(bf16[16,64,128]{2,1,0:T(8,128)(2,1)S(1)} %collective-permute-done.refs_0_), channel_id=1, source_target_pairs={{0,2},{1,3},{2,0},{3,1},{4,5},{5,4},{6,7},{7,6},{8,10},{9,11},{10,... | collective-permute-start | bytes 786440 | tf_op jit(solution)/shard_map/ppermute | solution.py:42
  13.9 1.9 %copy-start = (bf16[16,6,64,256]{3,2,1,0:T(8,128)(2,1)S(1)}, bf16[16,6,64,256]{3,2,1,0:T(8,128)(2,1)}, u32[]{:S(2)}) copy-start(bf16[16,6,64,256]{3,2,1,0:T(8,128)(2,1)} %hamiltonian_ref.11) | copy-start | bytes 9437188
  15.8 1.0 %copy-start.1 = (f32[1024,128]{1,0:T(8,128)S(1)}, f32[1024,128]{1,0:T(8,128)}, u32[]{:S(2)}) copy-start(f32[1024,128]{1,0:T(8,128)} %refs_0_.1) | copy-start | bytes 1572868
  16.8 0.7 copy-start.3
  20.0 9.4 %copy-start.2 = (f32[1024,128]{1,0:T(8,128)S(1)}, f32[1024,128]{1,0:T(8,128)}, u32[]{:S(2)}) copy-start(f32[1024,128]{1,0:T(8,128)} %refs_0_.1) | copy-start | bytes 1572868
  20.9 7.5 %collective-permute-start.5 = (bf16[16,64,128]{2,1,0:T(8,128)(2,1)S(1)}, bf16[16,64,128]{2,1,0:T(8,128)(2,1)S(1)}, u32[]{:S(2)}, u32[]{:S(2)}) collective-permute-start(bf16[16,64,128]{2,1,0:T(8,128)(2,1)S(1)} %get-tuple-element.6.own_ref), channel_id=1, source_target_pairs={{0,1},{1,0},{2,3},{3,2},{4,6},{5,7},{6,4},{7,5},{8,9},{9,8},{10,11... | collective-permute-start | bytes 786440 | tf_op jit(solution)/shard_map/ppermute | solution.py:42
  22.6 7.8 %collective-permute-start.6 = (bf16[16,64,128]{2,1,0:T(8,128)(2,1)S(1)}, bf16[16,64,128]{2,1,0:T(8,128)(2,1)S(1)}, u32[]{:S(2)}, u32[]{:S(2)}) collective-permute-start(bf16[16,64,128]{2,1,0:T(8,128)(2,1)S(1)} %get-tuple-element.6.own_ref), channel_id=1, source_target_pairs={{0,2},{1,3},{2,0},{3,1},{4,5},{5,4},{6,7},{7,6},{8,10},{9,11},{10,... | collective-permute-start | bytes 786440 | tf_op jit(solution)/shard_map/ppermute | solution.py:42
  23.9 6.5 %collective-permute-start.7 = (bf16[16,64,128]{2,1,0:T(8,128)(2,1)S(1)}, bf16[16,64,128]{2,1,0:T(8,128)(2,1)S(1)}, u32[]{:S(2)}, u32[]{:S(2)}) collective-permute-start(bf16[16,64,128]{2,1,0:T(8,128)(2,1)S(1)} %get-tuple-element.6.own_ref), channel_id=1, source_target_pairs={{4,8},{8,4},{12,16},{16,12},{20,24},{24,20},{5,9},{9,5},{13,17},{1... | collective-permute-start | bytes 786440 | tf_op jit(solution)/shard_map/ppermute | solution.py:24
  24.6 5.8 %collective-permute-start.8 = (bf16[16,64,128]{2,1,0:T(8,128)(2,1)S(1)}, bf16[16,64,128]{2,1,0:T(8,128)(2,1)S(1)}, u32[]{:S(2)}, u32[]{:S(2)}) collective-permute-start(bf16[16,64,128]{2,1,0:T(8,128)(2,1)S(1)} %get-tuple-element.6.own_ref), channel_id=1, source_target_pairs={{0,4},{4,0},{8,12},{12,8},{16,20},{20,16},{24,28},{28,24},{1,5},{5... | collective-permute-start | bytes 786440 | tf_op jit(solution)/shard_map/ppermute | solution.py:24
  28.4 6.4 %collective-permute-start.9 = (bf16[16,64,128]{2,1,0:T(8,128)(2,1)S(1)}, bf16[16,64,128]{2,1,0:T(8,128)(2,1)S(1)}, u32[]{:S(2)}, u32[]{:S(2)}) collective-permute-start(bf16[16,64,128]{2,1,0:T(8,128)(2,1)S(1)} %collective-permute-done.5.refs_0_), channel_id=1, source_target_pairs={{0,2},{1,3},{2,0},{3,1},{4,5},{5,4},{6,7},{7,6},{8,10},{9,11},{10,... | collective-permute-start | bytes 786440 | tf_op jit(solution)/shard_map/ppermute | solution.py:42
  36.3 2.1 %collective-permute-start.10 = (f32[72,128]{1,0:T(8,128)S(1)}, f32[72,128]{1,0:T(8,128)S(1)}, u32[]{:S(2)}, u32[]{:S(2)}) collective-permute-start(f32[72,128]{1,0:T(8,128)S(1)} %get-tuple-element.8), channel_id=1, source_target_pairs={{0,4},{8,12},{16,20},{24,28},{1,5},{9,13},{17,21},{25,29},{2,6},{1... | collective-permute-start | bytes 110600 | tf_op jit(solution)/shard_map/ppermute | solution.py:63
  38.4 2.0 %collective-permute-start.11 = (f32[72,128]{1,0:T(8,128)S(1)}, f32[72,128]{1,0:T(8,128)S(1)}, u32[]{:S(2)}, u32[]{:S(2)}) collective-permute-start(f32[72,128]{1,0:T(8,128)S(1)} %add_select_fusion), channel_id=1, source_target_pairs={{4,12},{5,13},{6,14},{7,15},{12,4},{13,5},{14,6},{15,7},{20,28},{2... | collective-permute-start | bytes 110600 | tf_op jit(solution)/shard_map/ppermute | solution.py:55
  39.1 1.4 %collective-permute-start.12 = (f32[72,128]{1,0:T(8,128)S(1)}, f32[72,128]{1,0:T(8,128)S(1)}, u32[]{:S(2)}, u32[]{:S(2)}) collective-permute-start(f32[72,128]{1,0:T(8,128)S(1)} %add_select_fusion), channel_id=1, source_target_pairs={{4,20},{5,21},{6,22},{7,23},{12,28},{13,29},{14,30},{15,31},{20,4}... | collective-permute-start | bytes 110600 | tf_op jit(solution)/shard_map/ppermute | solution.py:55
  39.8 0.7 collective-permute-start.13
  40.5 2.0 %collective-permute-start.14 = (f32[72,128]{1,0:T(8,128)S(1)}, f32[72,128]{1,0:T(8,128)S(1)}, u32[]{:S(2)}, u32[]{:S(2)}) collective-permute-start(f32[72,128]{1,0:T(8,128)S(1)} %add_add_fusion.1), channel_id=1, source_target_pairs={{4,5},{5,4},{6,7},{7,6},{12,13},{13,12},{14,15},{15,14},{20,21},{2... | collective-permute-start | bytes 110600 | tf_op jit(solution)/shard_map/ppermute | solution.py:55
  41.1 1.4 %collective-permute-start.15 = (f32[72,128]{1,0:T(8,128)S(1)}, f32[72,128]{1,0:T(8,128)S(1)}, u32[]{:S(2)}, u32[]{:S(2)}) collective-permute-start(f32[72,128]{1,0:T(8,128)S(1)} %add_add_fusion.1), channel_id=1, source_target_pairs={{4,6},{5,7},{6,4},{7,5},{12,14},{13,15},{14,12},{15,13},{20,22},{2... | collective-permute-start | bytes 110600 | tf_op jit(solution)/shard_map/ppermute | solution.py:55
  41.8 0.7 collective-permute-start.16
  42.5 22.9 %collective-permute-start.17 = (f32[72,128]{1,0:T(8,128)S(1)}, f32[72,128]{1,0:T(8,128)S(1)}, u32[]{:S(2)}, u32[]{:S(2)}) collective-permute-start(f32[72,128]{1,0:T(8,128)S(1)} %add_add_fusion), channel_id=1, source_target_pairs={{4,0},{12,8},{20,16},{28,24},{5,1},{13,9},{21,17},{29,25},{6,2},{1... | collective-permute-start | bytes 110600 | tf_op jit(solution)/shard_map/ppermute | solution.py:73

commit v7 on v6

--- a/solution.py
+++ b/solution.py
@@ -10,6 +10,7 @@
 precise = lax.Precision.HIGHEST
 LANES = 128
 SUB = 8
+OUTER = 4
 VMEM_LIMIT = 40 * 1024 * 1024
 vmem = pl.BlockSpec(memory_space=pltpu.VMEM)
 hbm = pl.BlockSpec(memory_space=pl.ANY)
@@ -18,10 +19,10 @@
 
 def pair_exchange(value, offset):
     count = lax.axis_size("group")
-    route = []
+    route = {group: group for group in range(count)}
     for low in range(offset, count - 1, 2):
-        route += [(low, low + 1), (low + 1, low)]
-    return lax.ppermute(value, "group", route)
+        route[low], route[low + 1] = low + 1, low
+    return lax.ppermute(value, "group", list(route.items()))
 
 
 def step_bits(group, level):
@@ -45,22 +46,18 @@
 def on_odd_cores(value, axis, flip):
     groups, cycle_size = lax.axis_size("group"), lax.axis_size("blk")
     route = []
-    for group in range(1, groups, 2):
+    for group in range(groups):
         for index in range(cycle_size):
-            if axis == "group":
-                partner = (group ^ 2 * flip) * cycle_size + index
-            else:
-                partner = group * cycle_size + (index ^ flip)
-            route.append((group * cycle_size + index, partner))
+            partner = (group, index)
+            if group % 2 == 1:
+                partner = (group ^ 2 * flip, index) if axis == "group" else (group, index ^ flip)
+            route.append((group * cycle_size + index, partner[0] * cycle_size + partner[1]))
     return lax.ppermute(value, ("group", "blk"), route)
 
 
 def summed(value):
     groups = lax.axis_size("group")
-    odd = lax.axis_index("group") % 2 == 1
-    up = [(group, group + 1) for group in range(0, groups - 1, 2)]
-    down = [(target, source) for source, target in up]
-    value = jnp.where(odd, value + lax.ppermute(value, "group", up), 0.0)
+    value = value + pair_exchange(value, 0)
     for axis, count in (("group", groups // 2), ("blk", lax.axis_size("blk"))):
         step = 1
         while step < count:
@@ -70,7 +67,7 @@
             if len(others) == 3:
                 value = value + (others[1] + others[2])
             step *= len(flips) + 1
-    return value + lax.ppermute(value, "group", down)
+    return jnp.where(lax.axis_index("group") % 2 == 1, value, pair_exchange(value, 0))
 
 
 def potential_columns(potential_ref):
@@ -89,6 +86,9 @@
         product = jnp.dot(
             hamiltonian_ref[row, source], picked, preferred_element_type=jnp.float32
         )
+        if index == sources - 1:
+            absent = sources_ref[sources] == index
+            product = jnp.where(absent, 0.0, product)
         total = product if total is None else total + product
     return total
 
@@ -197,60 +197,83 @@
     def along_rows(panel, row):
         return jnp.broadcast_to(panel[row : row + 1, :], shape)
 
+    def between(low, high):
+        return (lane_index >= low) & (lane_index < high)
+
     held = [gram[k * SUB : (k + 1) * SUB, :] for k in range(panels)]
-    block = along_lanes(held[0], 0)
-    for k in range(panels):
-        first = k * SUB
-        below = {p: along_lanes(held[p], first) for p in range(k + 1, panels)}
-        after = list(below[k + 1]) if k + 1 < panels else None
-        following = along_lanes(held[k + 1], first + SUB) if k + 1 < panels else None
-        right = jnp.where(lane_index >= first, held[k], 0.0)
-        left = jnp.where(
-            lane_index < first, held[k], jnp.where(lane_index == row_index + first, 1.0, 0.0)
-        )
-        pivots = jnp.ones(shape, jnp.float32)
-        reciprocals = jnp.ones(shape, jnp.float32)
-        for j in range(0, SUB, 2):
-            a, b, c = along_rows(block[j], j), along_rows(block[j], j + 1), along_rows(block[j + 1], j + 1)
-            determinant = a * c - b * b
-            over = inverse_of(determinant)
-            over_a = inverse_of(a)
-            shift = b * over_a
-            pivots = jnp.where(row_index == j, a, pivots)
-            pivots = jnp.where(row_index == j + 1, determinant * over_a, pivots)
-            reciprocals = jnp.where(row_index == j, over_a, reciprocals)
-            reciprocals = jnp.where(row_index == j + 1, a * over, reciprocals)
-            x, y = block[j], block[j + 1]
-            one = jnp.where(row_index > j + 1, (x * c - y * b) * over, jnp.where(row_index == j + 1, shift, 0.0))
-            two = jnp.where(row_index > j + 1, (y * a - x * b) * over, 0.0)
-            upper = {n: (along_rows(block[n], j), along_rows(block[n], j + 1)) for n in range(j + 2, SUB)}
-            for n in upper:
-                block[n] = block[n] - one * upper[n][0] - two * upper[n][1]
-            if following is not None:
-                x, y = after[j], after[j + 1]
-                next_one, next_two = (x * c - y * b) * over, (y * a - x * b) * over
-                for n in range(SUB):
-                    following[n] = following[n] - next_one * along_rows(x, n) - next_two * along_rows(y, n)
+    for outer in range(0, panels, OUTER):
+        end = outer + OUTER
+        rows_then, rows_reduced = [], []
+        block = along_lanes(held[outer], outer * SUB)
+        for k in range(outer, end):
+            first = k * SUB
+            below = {p: along_lanes(held[p], first) for p in range(k + 1, end)}
+            after = list(below[k + 1]) if k + 1 < end else None
+            following = along_lanes(held[k + 1], first + SUB) if k + 1 < end else None
+            right = held[k]
+            left = jnp.where(
+                lane_index < first, held[k], jnp.where(lane_index == row_index + first, 1.0, 0.0)
+            )
+            pivots = jnp.ones(shape, jnp.float32)
+            reciprocals = jnp.ones(shape, jnp.float32)
+            for j in range(0, SUB, 2):
+                a, b = along_rows(block[j], j), along_rows(block[j], j + 1)
+                c = along_rows(block[j + 1], j + 1)
+                determinant = a * c - b * b
+                over = inverse_of(determinant)
+                over_a = inverse_of(a)
+                pivots = jnp.where(row_index == j, a, pivots)
+                pivots = jnp.where(row_index == j + 1, determinant * over_a, pivots)
+                reciprocals = jnp.where(row_index == j, over_a, reciprocals)
+                reciprocals = jnp.where(row_index == j + 1, a * over, reciprocals)
+                x, y = block[j], block[j + 1]
+                one = jnp.where(row_index == j + 1, b * over_a, 0.0)
+                one = jnp.where(row_index > j + 1, (x * c - y * b) * over, one)
+                two = jnp.where(row_index > j + 1, (y * a - x * b) * over, 0.0)
+                upper = {
+                    n: (along_rows(block[n], j), along_rows(block[n], j + 1))
+                    for n in range(j + 2, SUB)
+                }
                 for n in upper:
-                    after[n] = after[n] - next_one * upper[n][0] - next_two * upper[n][1]
-            right = right - one * along_rows(right, j) - two * along_rows(right, j + 1)
-            left = left - one * along_rows(left, j) - two * along_rows(left, j + 1)
-        scale = lax.rsqrt(pivots)
-        upper_ref[pl.ds(first, SUB), :] = jnp.where(lane_index >= row_index + first, right * scale, 0.0)
-        inverse_ref[pl.ds(first, SUB), :] = left * scale
-        if k + 1 < panels:
-            reduced = jnp.where(lane_index >= first + SUB, right, left) * reciprocals
-            for n in range(SUB - 1, 0, -1):
-                column = jnp.where(row_index < n, block[n] * reciprocals, 0.0)
-                reduced = reduced - column * along_rows(reduced, n)
-            rows = [along_rows(reduced, n) for n in range(SUB)]
-            inside = (lane_index >= first) & (lane_index < first + SUB)
-            for p in below:
-                total = jnp.where(inside, 0.0, held[p])
-                for n in range(SUB):
-                    total = total - below[p][n] * rows[n]
-                held[p] = total
-        block = following
+                    block[n] = block[n] - one * upper[n][0] - two * upper[n][1]
+                if following is not None:
+                    x, y = after[j], after[j + 1]
+                    next_one, next_two = (x * c - y * b) * over, (y * a - x * b) * over
+                    for n in range(SUB):
+                        following[n] = (
+                            following[n] - next_one * along_rows(x, n) - next_two * along_rows(y, n)
+                        )
+                    for n in upper:
+                        after[n] = after[n] - next_one * upper[n][0] - next_two * upper[n][1]
+                right = right - one * along_rows(right, j) - two * along_rows(right, j + 1)
+                left = left - one * along_rows(left, j) - two * along_rows(left, j + 1)
+            scale = lax.rsqrt(pivots)
+            upper_ref[pl.ds(first, SUB), :] = jnp.where(
+                lane_index >= row_index + first, right * scale, 0.0
+            )
+            inverse_ref[pl.ds(first, SUB), :] = left * scale
+            if k + 1 < panels:
+                reduced = jnp.where(lane_index >= first + SUB, right, left) * reciprocals
+                for n in range(SUB - 1, 0, -1):
+                    column = jnp.where(row_index < n, block[n] * reciprocals, 0.0)
+                    reduced = reduced - column * along_rows(reduced, n)
+                rows_then.append(held[k])
+                rows_reduced.append(jnp.where(between(first + SUB, end * SUB), 0.0, reduced))
+                rows = [along_rows(reduced, n) for n in range(SUB)]
+                for p in below:
+                    total = jnp.where(between(first, first + SUB), 0.0, held[p])
+                    for n in range(SUB):
+                        total = total - below[p][n] * rows[n]
+                    held[p] = total
+            block = following
+        if end < panels:
+            change = lax.dot_general(
+                jnp.concatenate(rows_then, axis=0), jnp.concatenate(rows_reduced, axis=0),
+                (((0,), (0,)), ((), ())), precision=precise, preferred_element_type=jnp.float32,
+            )
+            for p in range(end, panels):
+                kept = jnp.where(between(outer * SUB, end * SUB), 0.0, held[p])
+                held[p] = kept - change[p * SUB : (p + 1) * SUB, :]
 
 
 def two_parts(value):
@@ -310,6 +333,8 @@
         origins += [jnp.bitwise_xor(origin, flip) for origin in origins]
     odd = group % 2
     origins += [cycle_size + 1 - odd, cycle_size + odd]
+    alone = (group == 0) | (group == lax.axis_size("group") - 1)
+    origins.append(jnp.where(alone, cycle_size + 1, -1))
     sources = jnp.stack(origins).astype(jnp.int32)
     last = cycle_size - 1
     middle = list(range(1, last)) + [cycle_size + 1, cycle_size]

time: 71 us -> 68.1 us (0.959)
  waiting for transfers between devices: 27.6 us -> 7.33 us
  starting transfers between devices: 24 us -> 42.2 us
  Pallas kernels: 12.2 us -> 11.4 us
    ppermute x6, waiting for transfers between devices: 22.5 us -> 2.08 us  [pair_exchange(): return lax.ppermute(value, 'group', list(route.items()))]
    ppermute x6, starting transfers between devices: 9.89 us -> 28.2 us  [pair_exchange(): return lax.ppermute(value, 'group', list(route.items()))]
  transfers between devices with their start and end apart: 18 -> 18, of which waited for: 5 -> 5; matrix products, arithmetic and copies ran while one was open for 1% -> 2% of each run, Pallas kernels for 7% -> 7%
where the time goes in v7:
time: 68.1 us; the launch traced here: 67.6 us
  starting transfers between devices  42.2 us (62%)
  Pallas kernels  11.4 us (17%)
  waiting for transfers between devices  7.33 us (11%)
  local copies, waits for them, and re-layouts  4.64 us (7%)
  other arithmetic  1.11 us (2%)
  between operations  0.89 us (1%)
    ppermute x6, starting transfers between devices, pair_exchange(): return lax.ppermute(value, 'group', list(route.items()))  28.2 us
    ppermute x6, starting transfers between devices, cycle_exchange(): return lax.ppermute(value, ('group', 'blk'), route)  10.1 us
    ppermute x6, waiting for transfers between devices, cycle_exchange(): return lax.ppermute(value, ('group', 'blk'), route)  5.24 us
    unnamed x9, local copies, waits for them, and re-layouts  4.44 us
    pallas_call x1, Pallas kernels, on_device(): call(functools.partial(factor_kernel, rows_total), (flat, square), [vmem,...  4.27 us
    ppermute x6, starting transfers between devices, on_odd_cores(): return lax.ppermute(value, ('group', 'blk'), route)  3.97 us
    pallas_call x2, Pallas kernels, most(): call(functools.partial(middle_kernel, middle), flat, [smem] * 2 + [vmem]...  2.81 us
    ppermute x6, waiting for transfers between devices, pair_exchange(): return lax.ppermute(value, 'group', list(route.items()))  2.08 us
  transfers between devices with their start and end apart: 18, of which 5 were waited for; matrix products, arithmetic and copies ran while one was open for 2% of the time, Pallas kernels for 7%

profile of v7, /device:TPU:0, one launch (start us, length us, event | category | flops | bytes accessed | tf_op | source)
XLA Modules:
  0.0 67.6 jit_solution(16701835643460585303)
XLA Ops:
  0.6 1.1 %convert_element_type.5 = bf16[1024,128]{1,0:T(8,128)(2,1)S(1)} convert(f32[1024,128]{1,0:T(8,128)} %refs_0_.1) | non-fusion elementwise | flops 131072 | bytes 786432 | tf_op jit(solution)/shard_map/convert_element_type | solution.py:362
  1.7 3.0 %collective-permute-start = (bf16[16,64,128]{2,1,0:T(8,128)(2,1)S(1)}, bf16[16,64,128]{2,1,0:T(8,128)(2,1)S(1)}, u32[]{:S(2)}, u32[]{:S(2)}) collective-permute-start(bf16[16,64,128]{2,1,0:T(8,128)(2,1)S(1)} %bitcast.9), channel_id=1, source_target_pairs={{0,1},{1,0},{2,3},{3,2},{4,6},{5,7},{6,4},{7,5},{8,9},{9,8},{10,11... | collective-permute-start | bytes 786440 | tf_op jit(solution)/shard_map/ppermute | solution.py:43
  4.7 1.5 %collective-permute-start.1 = (bf16[16,64,128]{2,1,0:T(8,128)(2,1)S(1)}, bf16[16,64,128]{2,1,0:T(8,128)(2,1)S(1)}, u32[]{:S(2)}, u32[]{:S(2)}) collective-permute-start(bf16[16,64,128]{2,1,0:T(8,128)(2,1)S(1)} %bitcast.10), channel_id=1, source_target_pairs={{0,2},{1,3},{2,0},{3,1},{4,5},{5,4},{6,7},{7,6},{8,10},{9,11},{10,... | collective-permute-start | bytes 786440 | tf_op jit(solution)/shard_map/ppermute | solution.py:43
  6.2 0.7 collective-permute-start.2
  6.9 3.0 %collective-permute-start.3 = (bf16[16,64,128]{2,1,0:T(8,128)(2,1)S(1)}, bf16[16,64,128]{2,1,0:T(8,128)(2,1)S(1)}, u32[]{:S(2)}, u32[]{:S(2)}) collective-permute-start(bf16[16,64,128]{2,1,0:T(8,128)(2,1)S(1)} %bitcast.12), channel_id=1, source_target_pairs={{0,4},{4,0},{8,12},{12,8},{16,20},{20,16},{24,28},{28,24},{1,5},{5... | collective-permute-start | bytes 786440 | tf_op jit(solution)/shard_map/ppermute | solution.py:25
  9.9 1.4 %collective-permute-done.refs_0_ = bf16[16,64,128]{2,1,0:T(8,128)(2,1)S(1)} collective-permute-done((bf16[16,64,128]{2,1,0:T(8,128)(2,1)S(1)}, bf16[16,64,128]{2,1,0:T(8,128)(2,1)S(1)}, u32[]{:S(2)}, u32[]{:S(2)}) %collective-permute-start) | collective-permute-done | bytes 262176 | tf_op jit(solution)/shard_map/ppermute | solution.py:43
  11.3 1.6 %collective-permute-start.4 = (bf16[16,64,128]{2,1,0:T(8,128)(2,1)S(1)}, bf16[16,64,128]{2,1,0:T(8,128)(2,1)S(1)}, u32[]{:S(2)}, u32[]{:S(2)}) collective-permute-start(bf16[16,64,128]{2,1,0:T(8,128)(2,1)S(1)} %collective-permute-done.refs_0_), channel_id=1, source_target_pairs={{0,2},{1,3},{2,0},{3,1},{4,5},{5,4},{6,7},{7,6},{8,10},{9,11},{10,... | collective-permute-start | bytes 786440 | tf_op jit(solution)/shard_map/ppermute | solution.py:43
  12.9 0.8 %copy.6 = s32[16,6,4]{2,1,0:T(8,128)S(1)} copy(s32[16,6,4]{0,2,1:T(4,128)} %param.5) | data formatting | bytes 3072 | tf_op args[1]
  13.7 0.1 reshape.12.columns_ref
  13.8 0.1 stack.31.sources_ref
  13.9 0.0 copy-start
  13.9 1.9 %copy-done = bf16[16,6,64,256]{3,2,1,0:T(8,128)(2,1)S(1)} copy-done((bf16[16,6,64,256]{3,2,1,0:T(8,128)(2,1)S(1)}, bf16[16,6,64,256]{3,2,1,0:T(8,128)(2,1)}, u32[]{:S(2)}) %copy-start) | copy-done | bytes 3145752
  15.8 0.0 copy-start.1
  15.8 1.0 %copy-done.1 = f32[1024,128]{1,0:T(8,128)S(1)} copy-done((f32[1024,128]{1,0:T(8,128)S(1)}, f32[1024,128]{1,0:T(8,128)}, u32[]{:S(2)}) %copy-start.1) | copy-done | bytes 524312
  16.8 0.0 copy-start.3
  16.8 0.7 %copy-done.3 = f32[1024]{0:T(1024)S(1)} copy-done((f32[1024]{0:T(1024)S(1)}, f32[1024]{0:T(1024)}, u32[]{:S(2)}) %copy-start.3) | copy-done | bytes 4120
  17.5 1.0 %shard_map.59.partial_ref = f32[1024,128]{1,0:T(8,128)S(1)} custom-call(s32[7]{0:T(128)S(1)} %stack.31.sources_ref, s32[384]{0:T(512)S(1)} %reshape.12.columns_ref, bf16[16,6,64,256]{3,2,1,0:T(8,128)(2,1)S(1)} %copy-done, bf16[16,64,128]{2,1,0:T(8,128)(2,1)S(1)} %bitcast.13, f32[8,128]{1,0:T(8,128)S(1)} %bitcast.14, f32[1024,128]{1,0:T(8,128)S(1)} %copy-done.1), custom_call_target="tpu_custom_call" | custom-call | tf_op jit(solution)/shard_map/pallas_call | solution.py:354
  18.5 0.0 collective-permute-done.1.refs_1_
  18.5 0.0 collective-permute-done.2.refs_2_
  18.5 0.0 collective-permute-done.3.refs_3_
  18.5 1.4 %shard_map.60.partial_ref = f32[1024,128]{1,0:T(8,128)S(1)} custom-call(s32[7]{0:T(128)S(1)} %stack.31.sources_ref, s32[384]{0:T(512)S(1)} %reshape.12.columns_ref, bf16[16,6,64,256]{3,2,1,0:T(8,128)(2,1)S(1)} %copy-done, f32[1024,128]{1,0:T(8,128)S(1)} %shard_map.59.partial_ref, bf16[16,64,128]{2,1,0:T(8,128)(2,1)S(1)} %collective-permute-done.refs_0_, ...), custom_call_target="tpu_custom_call" | custom-call | tf_op jit(solution)/shard_map/pallas_call | solution.py:357
  19.9 0.0 copy-start.2
  20.0 0.0 collective-permute-done.4.piece_ref
  20.0 0.9 %shard_map.61 = (f32[1024,128]{1,0:T(8,128)S(1)}, bf16[16,64,128]{2,1,0:T(8,128)(2,1)S(1)}) custom-call(s32[7]{0:T(128)S(1)} %stack.31.sources_ref, s32[384]{0:T(512)S(1)} %reshape.12.columns_ref, bf16[16,6,64,256]{3,2,1,0:T(8,128)(2,1)S(1)} %copy-done, f32[1024,128]{1,0:T(8,128)S(1)} %shard_map.60.partial_ref, ...), custom_call_target="tpu_custom_call" | custom-call | tf_op jit(solution)/shard_map/pallas_call | solution.py:364
  20.9 1.7 %collective-permute-start.5 = (bf16[16,64,128]{2,1,0:T(8,128)(2,1)S(1)}, bf16[16,64,128]{2,1,0:T(8,128)(2,1)S(1)}, u32[]{:S(2)}, u32[]{:S(2)}) collective-permute-start(bf16[16,64,128]{2,1,0:T(8,128)(2,1)S(1)} %get-tuple-element.6.own_ref), channel_id=1, source_target_pairs={{0,1},{1,0},{2,3},{3,2},{4,6},{5,7},{6,4},{7,5},{8,9},{9,8},{10,11... | collective-permute-start | bytes 786440 | tf_op jit(solution)/shard_map/ppermute | solution.py:43
  22.6 1.3 %collective-permute-start.6 = (bf16[16,64,128]{2,1,0:T(8,128)(2,1)S(1)}, bf16[16,64,128]{2,1,0:T(8,128)(2,1)S(1)}, u32[]{:S(2)}, u32[]{:S(2)}) collective-permute-start(bf16[16,64,128]{2,1,0:T(8,128)(2,1)S(1)} %get-tuple-element.6.own_ref), channel_id=1, source_target_pairs={{0,2},{1,3},{2,0},{3,1},{4,5},{5,4},{6,7},{7,6},{8,10},{9,11},{10,... | collective-permute-start | bytes 786440 | tf_op jit(solution)/shard_map/ppermute | solution.py:43
  23.9 0.7 collective-permute-start.7
  24.6 3.0 %collective-permute-start.8 = (bf16[16,64,128]{2,1,0:T(8,128)(2,1)S(1)}, bf16[16,64,128]{2,1,0:T(8,128)(2,1)S(1)}, u32[]{:S(2)}, u32[]{:S(2)}) collective-permute-start(bf16[16,64,128]{2,1,0:T(8,128)(2,1)S(1)} %get-tuple-element.6.own_ref), channel_id=1, source_target_pairs={{0,4},{4,0},{8,12},{12,8},{16,20},{20,16},{24,28},{28,24},{1,5},{5... | collective-permute-start | bytes 786440 | tf_op jit(solution)/shard_map/ppermute | solution.py:25
  27.5 0.8 %collective-permute-done.5.refs_0_ = bf16[16,64,128]{2,1,0:T(8,128)(2,1)S(1)} collective-permute-done((bf16[16,64,128]{2,1,0:T(8,128)(2,1)S(1)}, bf16[16,64,128]{2,1,0:T(8,128)(2,1)S(1)}, u32[]{:S(2)}, u32[]{:S(2)}) %collective-permute-start.5) | collective-permute-done | bytes 262176 | tf_op jit(solution)/shard_map/ppermute | solution.py:43
  28.4 1.0 %collective-permute-start.9 = (bf16[16,64,128]{2,1,0:T(8,128)(2,1)S(1)}, bf16[16,64,128]{2,1,0:T(8,128)(2,1)S(1)}, u32[]{:S(2)}, u32[]{:S(2)}) collective-permute-start(bf16[16,64,128]{2,1,0:T(8,128)(2,1)S(1)} %collective-permute-done.5.refs_0_), channel_id=1, source_target_pairs={{0,2},{1,3},{2,0},{3,1},{4,5},{5,4},{6,7},{7,6},{8,10},{9,11},{10,... | collective-permute-start | bytes 786440 | tf_op jit(solution)/shard_map/ppermute | solution.py:43
  29.4 0.0 copy-done.2
  29.4 1.0 %shard_map.62.partial_ref = f32[1024,128]{1,0:T(8,128)S(1)} custom-call(s32[7]{0:T(128)S(1)} %stack.31.sources_ref, s32[384]{0:T(512)S(1)} %reshape.12.columns_ref, bf16[16,6,64,256]{3,2,1,0:T(8,128)(2,1)S(1)} %copy-done, bf16[16,64,128]{2,1,0:T(8,128)(2,1)S(1)} %get-tuple-element.6.own_ref, f32[8,128]{1,0:T(8,128)S(1)} %bitcast.15, ...), custom_call_target="tpu_custom_call" | custom-call | tf_op jit(solution)/shard_map/pallas_call | solution.py:354
  30.3 0.0 collective-permute-done.6.refs_1_
  30.3 0.0 collective-permute-done.7.refs_2_
  30.4 0.0 collective-permute-done.8.refs_3_
  30.4 1.4 %shard_map.63.partial_ref = f32[1024,128]{1,0:T(8,128)S(1)} custom-call(s32[7]{0:T(128)S(1)} %stack.31.sources_ref, s32[384]{0:T(512)S(1)} %reshape.12.columns_ref, bf16[16,6,64,256]{3,2,1,0:T(8,128)(2,1)S(1)} %copy-done, f32[1024,128]{1,0:T(8,128)S(1)} %shard_map.62.partial_ref, bf16[16,64,128]{2,1,0:T(8,128)(2,1)S(1)} %collective-permute-done.5.refs_0_, ...), custom_call_target="tpu_custom_call" | custom-call | tf_op jit(solution)/shard_map/pallas_call | solution.py:357
  31.8 3.0 %collective-permute-done.9.piece_ref = bf16[16,64,128]{2,1,0:T(8,128)(2,1)S(1)} collective-permute-done((bf16[16,64,128]{2,1,0:T(8,128)(2,1)S(1)}, bf16[16,64,128]{2,1,0:T(8,128)(2,1)S(1)}, u32[]{:S(2)}, u32[]{:S(2)}) %collective-permute-start.9) | collective-permute-done | bytes 262176 | tf_op jit(solution)/shard_map/ppermute | solution.py:43
  34.7 1.5 %shard_map.64 = (f32[1024,128]{1,0:T(8,128)S(1)}, f32[72,128]{1,0:T(8,128)S(1)}) custom-call(s32[7]{0:T(128)S(1)} %stack.31.sources_ref, s32[384]{0:T(512)S(1)} %reshape.12.columns_ref, bf16[16,6,64,256]{3,2,1,0:T(8,128)(2,1)S(1)} %copy-done, f32[1024,128]{1,0:T(8,128)S(1)} %shard_map.63.partial_ref, bf16[16,64,128]{2,1,0:T(8,128)(2,1)S(1)} %collective-permute-done.9.piece_ref), custom_call_target="tpu_custom_call" | custom-call | tf_op jit(solution)/shard_map/pallas_call | solution.py:369
  36.2 0.1 collective-permute-start.10
  36.3 1.2 %collective-permute-done.10 = f32[72,128]{1,0:T(8,128)S(1)} collective-permute-done((f32[72,128]{1,0:T(8,128)S(1)}, f32[72,128]{1,0:T(8,128)S(1)}, u32[]{:S(2)}, u32[]{:S(2)}) %collective-permute-start.10) | collective-permute-done | bytes 36896 | tf_op jit(solution)/shard_map/ppermute | solution.py:25
  37.5 0.7 collective-permute-start.11
  38.2 0.7 collective-permute-start.12
  38.8 0.7 collective-permute-start.13
  39.5 0.0 collective-permute-done.11
  39.5 0.0 collective-permute-done.12
  39.5 0.0 collective-permute-done.13
  39.6 0.7 collective-permute-start.14
  40.2 0.7 collective-permute-start.15
  40.9 0.7 collective-permute-start.16
  41.6 0.0 collective-permute-done.14
  41.6 0.0 collective-permute-done.15
  41.6 0.0 collective-permute-done.16
  41.6 20.8 %collective-permute-start.17 = (f32[72,128]{1,0:T(8,128)S(1)}, f32[72,128]{1,0:T(8,128)S(1)}, u32[]{:S(2)}, u32[]{:S(2)}) collective-permute-start(f32[72,128]{1,0:T(8,128)S(1)} %add_add_fusion), channel_id=1, source_target_pairs={{0,4},{4,0},{8,12},{12,8},{16,20},{20,16},{24,28},{28,24},{1,5},{5... | collective-permute-start | bytes 110600 | tf_op jit(solution)/shard_map/ppermute | solution.py:25
  62.4 0.9 %collective-permute-done.17 = f32[72,128]{1,0:T(8,128)S(1)} collective-permute-done((f32[72,128]{1,0:T(8,128)S(1)}, f32[72,128]{1,0:T(8,128)S(1)}, u32[]{:S(2)}, u32[]{:S(2)}) %collective-permute-start.17) | collective-permute-done | bytes 36896 | tf_op jit(solution)/shard_map/ppermute | solution.py:25
  63.3 4.3 %shard_map.65 = (f32[1024,128]{1,0:T(8,128)}, f32[128,128]{1,0:T(8,128)}) custom-call(f32[72,128]{1,0:T(8,128)S(1)} %broadcast_select_fusion.packed_ref, f32[1024,128]{1,0:T(8,128)S(1)} %get-tuple-element.9.filtered_ref), custom_call_target="tpu_custom_call" | custom-call | tf_op jit(solution)/shard_map/pallas_call | solution.py:373
  (4 shorter events, 0.0 us)
Async XLA Ops:
  1.7 9.6 %collective-permute-start = (bf16[16,64,128]{2,1,0:T(8,128)(2,1)S(1)}, bf16[16,64,128]{2,1,0:T(8,128)(2,1)S(1)}, u32[]{:S(2)}, u32[]{:S(2)}) collective-permute-start(bf16[16,64,128]{2,1,0:T(8,128)(2,1)S(1)} %bitcast.9), channel_id=1, source_target_pairs={{0,1},{1,0},{2,3},{3,2},{4,6},{5,7},{6,4},{7,5},{8,9},{9,8},{10,11... | collective-permute-start | bytes 786440 | tf_op jit(solution)/shard_map/ppermute | solution.py:43
  4.7 13.8 %collective-permute-start.1 = (bf16[16,64,128]{2,1,0:T(8,128)(2,1)S(1)}, bf16[16,64,128]{2,1,0:T(8,128)(2,1)S(1)}, u32[]{:S(2)}, u32[]{:S(2)}) collective-permute-start(bf16[16,64,128]{2,1,0:T(8,128)(2,1)S(1)} %bitcast.10), channel_id=1, source_target_pairs={{0,2},{1,3},{2,0},{3,1},{4,5},{5,4},{6,7},{7,6},{8,10},{9,11},{10,... | collective-permute-start | bytes 786440 | tf_op jit(solution)/shard_map/ppermute | solution.py:43
  6.2 12.3 %collective-permute-start.2 = (bf16[16,64,128]{2,1,0:T(8,128)(2,1)S(1)}, bf16[16,64,128]{2,1,0:T(8,128)(2,1)S(1)}, u32[]{:S(2)}, u32[]{:S(2)}) collective-permute-start(bf16[16,64,128]{2,1,0:T(8,128)(2,1)S(1)} %bitcast.11), channel_id=1, source_target_pairs={{0,0},{4,8},{8,4},{12,16},{16,12},{20,24},{24,20},{28,28},{1,1},{5... | collective-permute-start | bytes 786440 | tf_op jit(solution)/shard_map/ppermute | solution.py:25
  6.9 11.6 %collective-permute-start.3 = (bf16[16,64,128]{2,1,0:T(8,128)(2,1)S(1)}, bf16[16,64,128]{2,1,0:T(8,128)(2,1)S(1)}, u32[]{:S(2)}, u32[]{:S(2)}) collective-permute-start(bf16[16,64,128]{2,1,0:T(8,128)(2,1)S(1)} %bitcast.12), channel_id=1, source_target_pairs={{0,4},{4,0},{8,12},{12,8},{16,20},{20,16},{24,28},{28,24},{1,5},{5... | collective-permute-start | bytes 786440 | tf_op jit(solution)/shard_map/ppermute | solution.py:25
  11.3 8.7 %collective-permute-start.4 = (bf16[16,64,128]{2,1,0:T(8,128)(2,1)S(1)}, bf16[16,64,128]{2,1,0:T(8,128)(2,1)S(1)}, u32[]{:S(2)}, u32[]{:S(2)}) collective-permute-start(bf16[16,64,128]{2,1,0:T(8,128)(2,1)S(1)} %collective-permute-done.refs_0_), channel_id=1, source_target_pairs={{0,2},{1,3},{2,0},{3,1},{4,5},{5,4},{6,7},{7,6},{8,10},{9,11},{10,... | collective-permute-start | bytes 786440 | tf_op jit(solution)/shard_map/ppermute | solution.py:43
  13.9 1.9 %copy-start = (bf16[16,6,64,256]{3,2,1,0:T(8,128)(2,1)S(1)}, bf16[16,6,64,256]{3,2,1,0:T(8,128)(2,1)}, u32[]{:S(2)}) copy-start(bf16[16,6,64,256]{3,2,1,0:T(8,128)(2,1)} %hamiltonian_ref.11) | copy-start | bytes 9437188
  15.8 1.0 %copy-start.1 = (f32[1024,128]{1,0:T(8,128)S(1)}, f32[1024,128]{1,0:T(8,128)}, u32[]{:S(2)}) copy-start(f32[1024,128]{1,0:T(8,128)} %refs_0_.1) | copy-start | bytes 1572868
  16.8 0.7 %copy-start.3 = (f32[1024]{0:T(1024)S(1)}, f32[1024]{0:T(1024)}, u32[]{:S(2)}) copy-start(f32[1024]{0:T(1024)} %param.6) | copy-start | bytes 12292
  19.9 9.4 %copy-start.2 = (f32[1024,128]{1,0:T(8,128)S(1)}, f32[1024,128]{1,0:T(8,128)}, u32[]{:S(2)}) copy-start(f32[1024,128]{1,0:T(8,128)} %refs_0_.1) | copy-start | bytes 1572868
  20.9 7.5 %collective-permute-start.5 = (bf16[16,64,128]{2,1,0:T(8,128)(2,1)S(1)}, bf16[16,64,128]{2,1,0:T(8,128)(2,1)S(1)}, u32[]{:S(2)}, u32[]{:S(2)}) collective-permute-start(bf16[16,64,128]{2,1,0:T(8,128)(2,1)S(1)} %get-tuple-element.6.own_ref), channel_id=1, source_target_pairs={{0,1},{1,0},{2,3},{3,2},{4,6},{5,7},{6,4},{7,5},{8,9},{9,8},{10,11... | collective-permute-start | bytes 786440 | tf_op jit(solution)/shard_map/ppermute | solution.py:43
  22.6 7.8 %collective-permute-start.6 = (bf16[16,64,128]{2,1,0:T(8,128)(2,1)S(1)}, bf16[16,64,128]{2,1,0:T(8,128)(2,1)S(1)}, u32[]{:S(2)}, u32[]{:S(2)}) collective-permute-start(bf16[16,64,128]{2,1,0:T(8,128)(2,1)S(1)} %get-tuple-element.6.own_ref), channel_id=1, source_target_pairs={{0,2},{1,3},{2,0},{3,1},{4,5},{5,4},{6,7},{7,6},{8,10},{9,11},{10,... | collective-permute-start | bytes 786440 | tf_op jit(solution)/shard_map/ppermute | solution.py:43
  23.9 6.5 %collective-permute-start.7 = (bf16[16,64,128]{2,1,0:T(8,128)(2,1)S(1)}, bf16[16,64,128]{2,1,0:T(8,128)(2,1)S(1)}, u32[]{:S(2)}, u32[]{:S(2)}) collective-permute-start(bf16[16,64,128]{2,1,0:T(8,128)(2,1)S(1)} %get-tuple-element.6.own_ref), channel_id=1, source_target_pairs={{0,0},{4,8},{8,4},{12,16},{16,12},{20,24},{24,20},{28,28},{1,1},{5... | collective-permute-start | bytes 786440 | tf_op jit(solution)/shard_map/ppermute | solution.py:25
  24.6 5.8 %collective-permute-start.8 = (bf16[16,64,128]{2,1,0:T(8,128)(2,1)S(1)}, bf16[16,64,128]{2,1,0:T(8,128)(2,1)S(1)}, u32[]{:S(2)}, u32[]{:S(2)}) collective-permute-start(bf16[16,64,128]{2,1,0:T(8,128)(2,1)S(1)} %get-tuple-element.6.own_ref), channel_id=1, source_target_pairs={{0,4},{4,0},{8,12},{12,8},{16,20},{20,16},{24,28},{28,24},{1,5},{5... | collective-permute-start | bytes 786440 | tf_op jit(solution)/shard_map/ppermute | solution.py:25
  28.4 6.4 %collective-permute-start.9 = (bf16[16,64,128]{2,1,0:T(8,128)(2,1)S(1)}, bf16[16,64,128]{2,1,0:T(8,128)(2,1)S(1)}, u32[]{:S(2)}, u32[]{:S(2)}) collective-permute-start(bf16[16,64,128]{2,1,0:T(8,128)(2,1)S(1)} %collective-permute-done.5.refs_0_), channel_id=1, source_target_pairs={{0,2},{1,3},{2,0},{3,1},{4,5},{5,4},{6,7},{7,6},{8,10},{9,11},{10,... | collective-permute-start | bytes 786440 | tf_op jit(solution)/shard_map/ppermute | solution.py:43
  36.2 1.3 %collective-permute-start.10 = (f32[72,128]{1,0:T(8,128)S(1)}, f32[72,128]{1,0:T(8,128)S(1)}, u32[]{:S(2)}, u32[]{:S(2)}) collective-permute-start(f32[72,128]{1,0:T(8,128)S(1)} %get-tuple-element.8), channel_id=1, source_target_pairs={{0,4},{4,0},{8,12},{12,8},{16,20},{20,16},{24,28},{28,24},{1,5},{5... | collective-permute-start | bytes 110600 | tf_op jit(solution)/shard_map/ppermute | solution.py:25
  37.5 2.0 %collective-permute-start.11 = (f32[72,128]{1,0:T(8,128)S(1)}, f32[72,128]{1,0:T(8,128)S(1)}, u32[]{:S(2)}, u32[]{:S(2)}) collective-permute-start(f32[72,128]{1,0:T(8,128)S(1)} %add.29), channel_id=1, source_target_pairs={{0,0},{1,1},{2,2},{3,3},{4,12},{5,13},{6,14},{7,15},{8,8},{9,9},{1... | collective-permute-start | bytes 110600 | tf_op jit(solution)/shard_map/ppermute | solution.py:55
  38.2 1.4 %collective-permute-start.12 = (f32[72,128]{1,0:T(8,128)S(1)}, f32[72,128]{1,0:T(8,128)S(1)}, u32[]{:S(2)}, u32[]{:S(2)}) collective-permute-start(f32[72,128]{1,0:T(8,128)S(1)} %add.29), channel_id=1, source_target_pairs={{0,0},{1,1},{2,2},{3,3},{4,20},{5,21},{6,22},{7,23},{8,8},{9,9},{1... | collective-permute-start | bytes 110600 | tf_op jit(solution)/shard_map/ppermute | solution.py:55
  38.8 0.7 %collective-permute-start.13 = (f32[72,128]{1,0:T(8,128)S(1)}, f32[72,128]{1,0:T(8,128)S(1)}, u32[]{:S(2)}, u32[]{:S(2)}) collective-permute-start(f32[72,128]{1,0:T(8,128)S(1)} %add.29), channel_id=1, source_target_pairs={{0,0},{1,1},{2,2},{3,3},{4,28},{5,29},{6,30},{7,31},{8,8},{9,9},{1... | collective-permute-start | bytes 110600 | tf_op jit(solution)/shard_map/ppermute | solution.py:55
  39.6 2.0 %collective-permute-start.14 = (f32[72,128]{1,0:T(8,128)S(1)}, f32[72,128]{1,0:T(8,128)S(1)}, u32[]{:S(2)}, u32[]{:S(2)}) collective-permute-start(f32[72,128]{1,0:T(8,128)S(1)} %add_add_fusion.1), channel_id=1, source_target_pairs={{0,0},{1,1},{2,2},{3,3},{4,5},{5,4},{6,7},{7,6},{8,8},{9,9},{10,10... | collective-permute-start | bytes 110600 | tf_op jit(solution)/shard_map/ppermute | solution.py:55
  40.2 1.4 %collective-permute-start.15 = (f32[72,128]{1,0:T(8,128)S(1)}, f32[72,128]{1,0:T(8,128)S(1)}, u32[]{:S(2)}, u32[]{:S(2)}) collective-permute-start(f32[72,128]{1,0:T(8,128)S(1)} %add_add_fusion.1), channel_id=1, source_target_pairs={{0,0},{1,1},{2,2},{3,3},{4,6},{5,7},{6,4},{7,5},{8,8},{9,9},{10,10... | collective-permute-start | bytes 110600 | tf_op jit(solution)/shard_map/ppermute | solution.py:55
  40.9 0.7 %collective-permute-start.16 = (f32[72,128]{1,0:T(8,128)S(1)}, f32[72,128]{1,0:T(8,128)S(1)}, u32[]{:S(2)}, u32[]{:S(2)}) collective-permute-start(f32[72,128]{1,0:T(8,128)S(1)} %add_add_fusion.1), channel_id=1, source_target_pairs={{0,0},{1,1},{2,2},{3,3},{4,7},{5,6},{6,5},{7,4},{8,8},{9,9},{10,10... | collective-permute-start | bytes 110600 | tf_op jit(solution)/shard_map/ppermute | solution.py:55
  41.6 21.7 %collective-permute-start.17 = (f32[72,128]{1,0:T(8,128)S(1)}, f32[72,128]{1,0:T(8,128)S(1)}, u32[]{:S(2)}, u32[]{:S(2)}) collective-permute-start(f32[72,128]{1,0:T(8,128)S(1)} %add_add_fusion), channel_id=1, source_target_pairs={{0,4},{4,0},{8,12},{12,8},{16,20},{20,16},{24,28},{28,24},{1,5},{5... | collective-permute-start | bytes 110600 | tf_op jit(solution)/shard_map/ppermute | solution.py:25

commit v8 on v7

--- a/solution.py
+++ b/solution.py
@@ -19,10 +19,11 @@
 
 def pair_exchange(value, offset):
     count = lax.axis_size("group")
-    route = {group: group for group in range(count)}
-    for low in range(offset, count - 1, 2):
-        route[low], route[low + 1] = low + 1, low
-    return lax.ppermute(value, "group", list(route.items()))
+    route = []
+    for low in range(offset, count + offset, 2):
+        first, second = low % count, (low + 1) % count
+        route += [(first, second), (second, first)]
+    return lax.ppermute(value, "group", route)
 
 
 def step_bits(group, level):
@@ -43,31 +44,22 @@
     return lax.ppermute(value, ("group", "blk"), route)
 
 
-def on_odd_cores(value, axis, flip):
-    groups, cycle_size = lax.axis_size("group"), lax.axis_size("blk")
-    route = []
-    for group in range(groups):
-        for index in range(cycle_size):
-            partner = (group, index)
-            if group % 2 == 1:
-                partner = (group ^ 2 * flip, index) if axis == "group" else (group, index ^ flip)
-            route.append((group * cycle_size + index, partner[0] * cycle_size + partner[1]))
-    return lax.ppermute(value, ("group", "blk"), route)
+def from_partner(value, axis, flip):
+    count = lax.axis_size(axis)
+    return lax.ppermute(value, axis, [(index, index ^ flip) for index in range(count)])
 
 
 def summed(value):
-    groups = lax.axis_size("group")
-    value = value + pair_exchange(value, 0)
-    for axis, count in (("group", groups // 2), ("blk", lax.axis_size("blk"))):
-        step = 1
+    for axis, step in (("group", 1), ("group", 2), ("blk", 1)):
+        count = 2 if (axis, step) == ("group", 1) else lax.axis_size(axis)
         while step < count:
             flips = [step, 2 * step, 3 * step] if 2 * step < count else [step]
-            others = [on_odd_cores(value, axis, flip) for flip in flips]
+            others = [from_partner(value, axis, flip) for flip in flips]
             value = value + others[0]
             if len(others) == 3:
                 value = value + (others[1] + others[2])
             step *= len(flips) + 1
-    return jnp.where(lax.axis_index("group") % 2 == 1, value, pair_exchange(value, 0))
+    return value
 
 
 def potential_columns(potential_ref):
@@ -93,20 +85,20 @@
     return total
 
 
-def own_kernel(
-    sources_ref, columns_ref, hamiltonian_ref, own_ref, potential_ref, scaled_ref, *refs
-):
-    less, partial_ref = refs[:-1], refs[-1]
+def own_kernel(sources_ref, columns_ref, hamiltonian_ref, own_ref, *refs):
+    terms, partial_ref = refs[:-1], refs[-1]
     shard_blocks, _, block_size, _ = hamiltonian_ref.shape
-    weights = potential_columns(potential_ref)
     per_column = LANES // block_size
+    if len(terms) == 3:
+        weights = potential_columns(terms[0])
     for row in range(shard_blocks):
-        column, part = divmod(row, per_column)
-        weight = weights[part * block_size : (part + 1) * block_size, column : column + 1]
         rows = pl.ds(row * block_size, block_size)
-        total = weight * scaled_ref[rows, :]
-        for less_ref in less:
-            total = total - less_ref[rows, :]
+        if len(terms) == 3:
+            column, part = divmod(row, per_column)
+            weight = weights[part * block_size : (part + 1) * block_size, column : column + 1]
+            total = weight * terms[1][rows, :] - terms[2][rows, :]
+        else:
+            total = terms[0][rows, :]
         partial_ref[rows, :] = total + couple_row(
             sources_ref, columns_ref, hamiltonian_ref, [(0, own_ref)], row
         )
@@ -337,38 +329,42 @@
     origins.append(jnp.where(alone, cycle_size + 1, -1))
     sources = jnp.stack(origins).astype(jnp.int32)
     last = cycle_size - 1
-    middle = list(range(1, last)) + [cycle_size + 1, cycle_size]
+    middle = [1, cycle_size, cycle_size + 1] + list(range(2, last))
     flat = jax.ShapeDtypeStruct((flat_rows, states), jnp.float32)
     rounded = jax.ShapeDtypeStruct((shard_blocks, block_size, states), jnp.bfloat16)
     packed = jax.ShapeDtypeStruct((states // 2 + SUB, states), jnp.float32)
     square = jax.ShapeDtypeStruct((states, states), jnp.float32)
 
-    def exchanged(value):
+    def own_part(value, *terms):
+        return call(own_kernel, flat, [smem] * 2 + [vmem] * (2 + len(terms)))(
+            sources, columns, hamiltonian, value, *terms
+        )
+
+    def coupled(value, *terms):
         pairs = [pair_exchange(value, 0), pair_exchange(value, 1)]
-        pieces = [value]
-        for level in range(levels):
-            pieces += [cycle_exchange(piece, level) for piece in pieces]
-        return pieces + pairs
-
-    def most(pieces, *terms):
-        own = call(own_kernel, flat, [smem] * 2 + [vmem] * (3 + len(terms)))(
-            sources, columns, hamiltonian, pieces[0], weights, *terms
-        )
-        return call(
+        pieces = [value, cycle_exchange(value, 0)]
+        partial = own_part(value, *terms)
+        for level in range(1, levels):
+            arrived = pieces[1:]
+            if level == 1:
+                arrived, partial = lax.optimization_barrier((arrived, partial))
+            pieces += [cycle_exchange(piece, level) for piece in [value] + arrived]
+        pieces += pairs
+        partial = call(
             functools.partial(middle_kernel, middle), flat,
             [smem] * 2 + [vmem] * (2 + len(middle)),
-        )(sources, columns, hamiltonian, own, *[pieces[number] for number in middle])
-
-    pieces = exchanged(trial_slab.reshape(rounded.shape).astype(jnp.bfloat16))
-    partial = most(pieces, trial_slab)
+        )(sources, columns, hamiltonian, partial, *[pieces[number] for number in middle])
+        return partial, pieces[last]
+
+    weighted = (weights.reshape(-1, 1) * trial_slab)
+    partial, piece = coupled(trial_slab.reshape(rounded.shape).astype(jnp.bfloat16), weighted)
     once, once_round = call(
         functools.partial(first_kernel, last), (flat, rounded), [smem] * 2 + [vmem] * 3
-    )(sources, columns, hamiltonian, partial, pieces[last])
-    pieces = exchanged(once_round)
-    partial = most(pieces, once, trial_slab)
+    )(sources, columns, hamiltonian, partial, piece)
+    partial, piece = coupled(once_round, weights, once, trial_slab)
     filtered, gram = call(
         functools.partial(second_kernel, last), (flat, packed), [smem] * 2 + [vmem] * 3
-    )(sources, columns, hamiltonian, partial, pieces[last])
+    )(sources, columns, hamiltonian, partial, piece)
     gram = summed(gram)
     return call(
         functools.partial(factor_kernel, rows_total),

time: 68.1 us -> 56.3 us (0.83)
  starting transfers between devices: 42.2 us -> 20.8 us
  waiting for transfers between devices: 7.33 us -> 18.9 us
  local copies, waits for them, and re-layouts: 4.64 us -> 2.92 us
    ppermute x12 -> x11, starting transfers between devices: 32.1 us -> 12.2 us  [the longest x7 8.01 us: from_partner(): lax.ppermute(value, axis, [(index, index ^ flip) for index in range(count)])]
    ppermute x12 -> x11, waiting for transfers between devices: 2.09 us -> 13.2 us  [the longest x7 7.54 us: from_partner(): lax.ppermute(value, axis, [(index, index ^ flip) for index in range(count)])]
    unnamed x9 -> x7, local copies, waits for them, and re-layouts: 4.44 us -> 2.72 us
    ppermute x6, starting transfers between devices: 10.1 us -> 8.64 us  [cycle_exchange(): return lax.ppermute(value, ('group', 'blk'), route)]
    mul x0 -> x1, other arithmetic: none -> 1.43 us  [on_device(): weighted = weights.reshape(-1, 1) * trial_slab]
    convert_element_type x1 -> x0, other arithmetic: 1.07 us -> none  [on_device(): pieces = exchanged(trial_slab.reshape(rounded.shape).astype(jnp.bfloat16))]
  transfers between devices with their start and end apart: 18 -> 17, of which waited for: 5 -> 11; matrix products, arithmetic and copies ran while one was open for 2% -> 2% of each run, Pallas kernels for 7% -> 8%
where the time goes in v8:
time: 56.3 us; the launch traced here: 56.1 us
  starting transfers between devices  20.8 us (37%)
  waiting for transfers between devices  18.9 us (34%)
  Pallas kernels  11.2 us (20%)
  local copies, waits for them, and re-layouts  2.92 us (5%)
  other arithmetic  1.46 us (3%)
  between operations  0.74 us (1%)
    ppermute x6, starting transfers between devices, cycle_exchange(): return lax.ppermute(value, ('group', 'blk'), route)  8.64 us
    ppermute x7, starting transfers between devices, from_partner(): lax.ppermute(value, axis, [(index, index ^ flip) for index in range(count)])  8.01 us
    ppermute x7, waiting for transfers between devices, from_partner(): lax.ppermute(value, axis, [(index, index ^ flip) for index in range(count)])  7.54 us
    ppermute x6, waiting for transfers between devices, cycle_exchange(): return lax.ppermute(value, ('group', 'blk'), route)  5.77 us
    ppermute x4, waiting for transfers between devices, pair_exchange(): return lax.ppermute(value, 'group', route)  5.62 us
    pallas_call x1, Pallas kernels, on_device(): call(functools.partial(factor_kernel, rows_total), (flat, square), [vmem,...  4.27 us
    ppermute x4, starting transfers between devices, pair_exchange(): return lax.ppermute(value, 'group', route)  4.18 us
    pallas_call x2, Pallas kernels, coupled(): call(functools.partial(middle_kernel, middle), flat, [smem] * 2 + [vmem]...  2.78 us
  transfers between devices with their start and end apart: 17, of which 11 were waited for; matrix products, arithmetic and copies ran while one was open for 2% of the time, Pallas kernels for 8%

profile of v8, /device:TPU:0, one launch (start us, length us, event | category | flops | bytes accessed | tf_op | source)
XLA Modules:
  0.0 56.1 jit_solution(15997431430594011334)
XLA Ops:
  0.6 1.4 %broadcast_multiply_fusion = (f32[1024,128]{1,0:T(8,128)S(1)}, bf16[1024,128]{1,0:T(8,128)(2,1)S(1)}) fusion(f32[1024,128]{1,0:T(8,128)} %refs_2_.1, f32[1024]{0:T(1024)} %param.6), kind=kLoop, calls=%fused_computation | loop fusion | flops 262144 | bytes 1314816 | tf_op jit(solution)/shard_map/mul | solution.py:359
  2.1 3.0 %collective-permute-start = (bf16[16,64,128]{2,1,0:T(8,128)(2,1)S(1)}, bf16[16,64,128]{2,1,0:T(8,128)(2,1)S(1)}, u32[]{:S(2)}, u32[]{:S(2)}) collective-permute-start(bf16[16,64,128]{2,1,0:T(8,128)(2,1)S(1)} %bitcast.9), channel_id=1, source_target_pairs={{0,1},{1,0},{2,3},{3,2},{4,6},{5,7},{6,4},{7,5},{8,9},{9,8},{10,11... | collective-permute-start | bytes 786440 | tf_op jit(solution)/shard_map/ppermute | solution.py:44
  5.1 1.5 %collective-permute-start.3 = (bf16[16,64,128]{2,1,0:T(8,128)(2,1)S(1)}, bf16[16,64,128]{2,1,0:T(8,128)(2,1)S(1)}, u32[]{:S(2)}, u32[]{:S(2)}) collective-permute-start(bf16[16,64,128]{2,1,0:T(8,128)(2,1)S(1)} %bitcast.10), channel_id=1, source_target_pairs={{0,2},{1,3},{2,0},{3,1},{4,5},{5,4},{6,7},{7,6},{8,10},{9,11},{10,... | collective-permute-start | bytes 786440 | tf_op jit(solution)/shard_map/ppermute | solution.py:44
  6.6 2.5 %collective-permute-start.2 = (bf16[16,64,128]{2,1,0:T(8,128)(2,1)S(1)}, bf16[16,64,128]{2,1,0:T(8,128)(2,1)S(1)}, u32[]{:S(2)}, u32[]{:S(2)}) collective-permute-start(bf16[16,64,128]{2,1,0:T(8,128)(2,1)S(1)} %bitcast.11), channel_id=1, source_target_pairs={{4,8},{8,4},{12,16},{16,12},{20,24},{24,20},{28,0},{0,28},{5,9},{9... | collective-permute-start | bytes 786440 | tf_op jit(solution)/shard_map/ppermute | solution.py:26
  9.1 0.0 collective-permute-start.1
  9.1 0.8 %copy.6 = s32[16,6,4]{2,1,0:T(8,128)S(1)} copy(s32[16,6,4]{0,2,1:T(4,128)} %param.5) | data formatting | bytes 3072 | tf_op args[1]
  9.9 0.1 reshape.13.columns_ref
  10.0 0.1 stack.31.sources_ref
  10.1 0.0 copy-start
  10.1 1.9 %copy-done = bf16[16,6,64,256]{3,2,1,0:T(8,128)(2,1)S(1)} copy-done((bf16[16,6,64,256]{3,2,1,0:T(8,128)(2,1)S(1)}, bf16[16,6,64,256]{3,2,1,0:T(8,128)(2,1)}, u32[]{:S(2)}) %copy-start) | copy-done | bytes 3145752
  12.0 0.9 %shard_map.59.partial_ref = f32[1024,128]{1,0:T(8,128)S(1)} custom-call(s32[7]{0:T(128)S(1)} %stack.31.sources_ref, s32[384]{0:T(512)S(1)} %reshape.13.columns_ref, bf16[16,6,64,256]{3,2,1,0:T(8,128)(2,1)S(1)} %copy-done, bf16[16,64,128]{2,1,0:T(8,128)(2,1)S(1)} %bitcast.13, f32[1024,128]{1,0:T(8,128)S(1)} %get-tuple-element.18.refs_0_), custom_call_target="tpu_custom_call" | custom-call | tf_op jit(solution)/shard_map/pallas_call | solution.py:339
  12.9 0.0 collective-permute-done.refs_0_
  12.9 0.6 %collective-permute-start.4 = (bf16[16,64,128]{2,1,0:T(8,128)(2,1)S(1)}, bf16[16,64,128]{2,1,0:T(8,128)(2,1)S(1)}, u32[]{:S(2)}, u32[]{:S(2)}) collective-permute-start(bf16[16,64,128]{2,1,0:T(8,128)(2,1)S(1)} %collective-permute-done.refs_0_), channel_id=1, source_target_pairs={{0,2},{1,3},{2,0},{3,1},{4,5},{5,4},{6,7},{7,6},{8,10},{9,11},{10,... | collective-permute-start | bytes 786440 | tf_op jit(solution)/shard_map/ppermute | solution.py:44
  13.5 0.0 collective-permute-done.3.refs_3_
  13.5 3.3 %collective-permute-done.2.refs_2_ = bf16[16,64,128]{2,1,0:T(8,128)(2,1)S(1)} collective-permute-done((bf16[16,64,128]{2,1,0:T(8,128)(2,1)S(1)}, bf16[16,64,128]{2,1,0:T(8,128)(2,1)S(1)}, u32[]{:S(2)}, u32[]{:S(2)}) %collective-permute-start.2) | collective-permute-done | bytes 262176 | tf_op jit(solution)/shard_map/ppermute | solution.py:26
  16.7 0.0 collective-permute-done.1.refs_1_
  16.7 1.4 %shard_map.60.partial_ref = f32[1024,128]{1,0:T(8,128)S(1)} custom-call(s32[7]{0:T(128)S(1)} %stack.31.sources_ref, s32[384]{0:T(512)S(1)} %reshape.13.columns_ref, bf16[16,6,64,256]{3,2,1,0:T(8,128)(2,1)S(1)} %copy-done, f32[1024,128]{1,0:T(8,128)S(1)} %shard_map.59.partial_ref, bf16[16,64,128]{2,1,0:T(8,128)(2,1)S(1)} %collective-permute-done.refs_0_, ...), custom_call_target="tpu_custom_call" | custom-call | tf_op jit(solution)/shard_map/pallas_call | solution.py:353
  18.2 0.0 copy-start.1
  18.2 0.0 copy-start.2
  18.2 1.1 %collective-permute-done.4.piece_ref = bf16[16,64,128]{2,1,0:T(8,128)(2,1)S(1)} collective-permute-done((bf16[16,64,128]{2,1,0:T(8,128)(2,1)S(1)}, bf16[16,64,128]{2,1,0:T(8,128)(2,1)S(1)}, u32[]{:S(2)}, u32[]{:S(2)}) %collective-permute-start.4) | collective-permute-done | bytes 262176 | tf_op jit(solution)/shard_map/ppermute | solution.py:44
  19.3 0.9 %shard_map.61 = (f32[1024,128]{1,0:T(8,128)S(1)}, bf16[16,64,128]{2,1,0:T(8,128)(2,1)S(1)}) custom-call(s32[7]{0:T(128)S(1)} %stack.31.sources_ref, s32[384]{0:T(512)S(1)} %reshape.13.columns_ref, bf16[16,6,64,256]{3,2,1,0:T(8,128)(2,1)S(1)} %copy-done, f32[1024,128]{1,0:T(8,128)S(1)} %shard_map.60.partial_ref, ...), custom_call_target="tpu_custom_call" | custom-call | tf_op jit(solution)/shard_map/pallas_call | solution.py:361
  20.2 1.2 %collective-permute-start.5 = (bf16[16,64,128]{2,1,0:T(8,128)(2,1)S(1)}, bf16[16,64,128]{2,1,0:T(8,128)(2,1)S(1)}, u32[]{:S(2)}, u32[]{:S(2)}) collective-permute-start(bf16[16,64,128]{2,1,0:T(8,128)(2,1)S(1)} %get-tuple-element.12.own_ref), channel_id=1, source_target_pairs={{0,1},{1,0},{2,3},{3,2},{4,6},{5,7},{6,4},{7,5},{8,9},{9,8},{10,11... | collective-permute-start | bytes 786440 | tf_op jit(solution)/shard_map/ppermute | solution.py:44
  21.5 0.7 %collective-permute-start.8 = (bf16[16,64,128]{2,1,0:T(8,128)(2,1)S(1)}, bf16[16,64,128]{2,1,0:T(8,128)(2,1)S(1)}, u32[]{:S(2)}, u32[]{:S(2)}) collective-permute-start(bf16[16,64,128]{2,1,0:T(8,128)(2,1)S(1)} %get-tuple-element.12.own_ref), channel_id=1, source_target_pairs={{0,2},{1,3},{2,0},{3,1},{4,5},{5,4},{6,7},{7,6},{8,10},{9,11},{10,... | collective-permute-start | bytes 786440 | tf_op jit(solution)/shard_map/ppermute | solution.py:44
  22.2 0.0 collective-permute-start.7
  22.2 1.7 %collective-permute-start.6 = (bf16[16,64,128]{2,1,0:T(8,128)(2,1)S(1)}, bf16[16,64,128]{2,1,0:T(8,128)(2,1)S(1)}, u32[]{:S(2)}, u32[]{:S(2)}) collective-permute-start(bf16[16,64,128]{2,1,0:T(8,128)(2,1)S(1)} %get-tuple-element.12.own_ref), channel_id=1, source_target_pairs={{0,4},{4,0},{8,12},{12,8},{16,20},{20,16},{24,28},{28,24},{1,5},{5... | collective-permute-start | bytes 786440 | tf_op jit(solution)/shard_map/ppermute | solution.py:26
  23.9 0.0 copy-done.1
  23.9 0.0 copy-done.2
  23.9 1.0 %shard_map.62.partial_ref = f32[1024,128]{1,0:T(8,128)S(1)} custom-call(s32[7]{0:T(128)S(1)} %stack.31.sources_ref, s32[384]{0:T(512)S(1)} %reshape.13.columns_ref, bf16[16,6,64,256]{3,2,1,0:T(8,128)(2,1)S(1)} %copy-done, bf16[16,64,128]{2,1,0:T(8,128)(2,1)S(1)} %get-tuple-element.12.own_ref, f32[8,128]{1,0:T(8,128)S(1)} %bitcast.14, ...), custom_call_target="tpu_custom_call" | custom-call | tf_op jit(solution)/shard_map/pallas_call | solution.py:339
  24.9 3.5 %collective-permute-done.5.refs_0_ = bf16[16,64,128]{2,1,0:T(8,128)(2,1)S(1)} collective-permute-done((bf16[16,64,128]{2,1,0:T(8,128)(2,1)S(1)}, bf16[16,64,128]{2,1,0:T(8,128)(2,1)S(1)}, u32[]{:S(2)}, u32[]{:S(2)}) %collective-permute-start.5) | collective-permute-done | bytes 262176 | tf_op jit(solution)/shard_map/ppermute | solution.py:44
  28.4 1.6 %collective-permute-start.9 = (bf16[16,64,128]{2,1,0:T(8,128)(2,1)S(1)}, bf16[16,64,128]{2,1,0:T(8,128)(2,1)S(1)}, u32[]{:S(2)}, u32[]{:S(2)}) collective-permute-start(bf16[16,64,128]{2,1,0:T(8,128)(2,1)S(1)} %collective-permute-done.5.refs_0_), channel_id=1, source_target_pairs={{0,2},{1,3},{2,0},{3,1},{4,5},{5,4},{6,7},{7,6},{8,10},{9,11},{10,... | collective-permute-start | bytes 786440 | tf_op jit(solution)/shard_map/ppermute | solution.py:44
  30.0 0.0 collective-permute-done.8.refs_3_
  30.0 2.4 %collective-permute-done.7.refs_2_ = bf16[16,64,128]{2,1,0:T(8,128)(2,1)S(1)} collective-permute-done((bf16[16,64,128]{2,1,0:T(8,128)(2,1)S(1)}, bf16[16,64,128]{2,1,0:T(8,128)(2,1)S(1)}, u32[]{:S(2)}, u32[]{:S(2)}) %collective-permute-start.7) | collective-permute-done | bytes 262176 | tf_op jit(solution)/shard_map/ppermute | solution.py:26
  32.3 0.0 collective-permute-done.6.refs_1_
  32.3 1.4 %shard_map.63.partial_ref = f32[1024,128]{1,0:T(8,128)S(1)} custom-call(s32[7]{0:T(128)S(1)} %stack.31.sources_ref, s32[384]{0:T(512)S(1)} %reshape.13.columns_ref, bf16[16,6,64,256]{3,2,1,0:T(8,128)(2,1)S(1)} %copy-done, f32[1024,128]{1,0:T(8,128)S(1)} %shard_map.62.partial_ref, bf16[16,64,128]{2,1,0:T(8,128)(2,1)S(1)} %collective-permute-done.5.refs_0_, ...), custom_call_target="tpu_custom_call" | custom-call | tf_op jit(solution)/shard_map/pallas_call | solution.py:353
  33.7 1.1 %collective-permute-done.9.piece_ref = bf16[16,64,128]{2,1,0:T(8,128)(2,1)S(1)} collective-permute-done((bf16[16,64,128]{2,1,0:T(8,128)(2,1)S(1)}, bf16[16,64,128]{2,1,0:T(8,128)(2,1)S(1)}, u32[]{:S(2)}, u32[]{:S(2)}) %collective-permute-start.9) | collective-permute-done | bytes 262176 | tf_op jit(solution)/shard_map/ppermute | solution.py:44
  34.8 1.4 %shard_map.64 = (f32[1024,128]{1,0:T(8,128)S(1)}, f32[72,128]{1,0:T(8,128)S(1)}) custom-call(s32[7]{0:T(128)S(1)} %stack.31.sources_ref, s32[384]{0:T(512)S(1)} %reshape.13.columns_ref, bf16[16,6,64,256]{3,2,1,0:T(8,128)(2,1)S(1)} %copy-done, f32[1024,128]{1,0:T(8,128)S(1)} %shard_map.63.partial_ref, bf16[16,64,128]{2,1,0:T(8,128)(2,1)S(1)} %collective-permute-done.9.piece_ref), custom_call_target="tpu_custom_call" | custom-call | tf_op jit(solution)/shard_map/pallas_call | solution.py:365
  36.2 0.1 collective-permute-start.10
  36.3 1.2 %collective-permute-done.10 = f32[72,128]{1,0:T(8,128)S(1)} collective-permute-done((f32[72,128]{1,0:T(8,128)S(1)}, f32[72,128]{1,0:T(8,128)S(1)}, u32[]{:S(2)}, u32[]{:S(2)}) %collective-permute-start.10) | collective-permute-done | bytes 36896 | tf_op jit(solution)/shard_map/ppermute | solution.py:49
  37.5 1.6 %collective-permute-start.13 = (f32[72,128]{1,0:T(8,128)S(1)}, f32[72,128]{1,0:T(8,128)S(1)}, u32[]{:S(2)}, u32[]{:S(2)}) collective-permute-start(f32[72,128]{1,0:T(8,128)S(1)} %add.28), channel_id=1, source_target_pairs={{0,24},{4,28},{8,16},{12,20},{16,8},{20,12},{24,0},{28,4},{1,25},{... | collective-permute-start | bytes 110600 | tf_op jit(solution)/shard_map/ppermute | solution.py:49
  39.1 0.2 collective-permute-start.12
  39.2 2.7 %collective-permute-start.11 = (f32[72,128]{1,0:T(8,128)S(1)}, f32[72,128]{1,0:T(8,128)S(1)}, u32[]{:S(2)}, u32[]{:S(2)}) collective-permute-start(f32[72,128]{1,0:T(8,128)S(1)} %add.28), channel_id=1, source_target_pairs={{0,8},{4,12},{8,0},{12,4},{16,24},{20,28},{24,16},{28,20},{1,9},{5... | collective-permute-start | bytes 110600 | tf_op jit(solution)/shard_map/ppermute | solution.py:49
  41.9 1.4 %collective-permute-done.13 = f32[72,128]{1,0:T(8,128)S(1)} collective-permute-done((f32[72,128]{1,0:T(8,128)S(1)}, f32[72,128]{1,0:T(8,128)S(1)}, u32[]{:S(2)}, u32[]{:S(2)}) %collective-permute-start.13) | collective-permute-done | bytes 36896 | tf_op jit(solution)/shard_map/ppermute | solution.py:49
  43.3 1.2 %collective-permute-done.12 = f32[72,128]{1,0:T(8,128)S(1)} collective-permute-done((f32[72,128]{1,0:T(8,128)S(1)}, f32[72,128]{1,0:T(8,128)S(1)}, u32[]{:S(2)}, u32[]{:S(2)}) %collective-permute-start.12) | collective-permute-done | bytes 36896 | tf_op jit(solution)/shard_map/ppermute | solution.py:49
  44.5 0.0 collective-permute-done.11
  44.5 2.2 %collective-permute-start.16 = (f32[72,128]{1,0:T(8,128)S(1)}, f32[72,128]{1,0:T(8,128)S(1)}, u32[]{:S(2)}, u32[]{:S(2)}) collective-permute-start(f32[72,128]{1,0:T(8,128)S(1)} %add_add_fusion.1), channel_id=1, source_target_pairs={{0,3},{1,2},{2,1},{3,0},{4,7},{5,6},{6,5},{7,4},{8,11},{9,10},{10,... | collective-permute-start | bytes 110600 | tf_op jit(solution)/shard_map/ppermute | solution.py:49
  46.7 1.1 %collective-permute-start.15 = (f32[72,128]{1,0:T(8,128)S(1)}, f32[72,128]{1,0:T(8,128)S(1)}, u32[]{:S(2)}, u32[]{:S(2)}) collective-permute-start(f32[72,128]{1,0:T(8,128)S(1)} %add_add_fusion.1), channel_id=1, source_target_pairs={{0,2},{1,3},{2,0},{3,1},{4,6},{5,7},{6,4},{7,5},{8,10},{9,11},{10,... | collective-permute-start | bytes 110600 | tf_op jit(solution)/shard_map/ppermute | solution.py:49
  47.9 0.2 collective-permute-start.14
  48.1 1.4 %collective-permute-done.16 = f32[72,128]{1,0:T(8,128)S(1)} collective-permute-done((f32[72,128]{1,0:T(8,128)S(1)}, f32[72,128]{1,0:T(8,128)S(1)}, u32[]{:S(2)}, u32[]{:S(2)}) %collective-permute-start.16) | collective-permute-done | bytes 36896 | tf_op jit(solution)/shard_map/ppermute | solution.py:49
  49.5 1.2 %collective-permute-done.15 = f32[72,128]{1,0:T(8,128)S(1)} collective-permute-done((f32[72,128]{1,0:T(8,128)S(1)}, f32[72,128]{1,0:T(8,128)S(1)}, u32[]{:S(2)}, u32[]{:S(2)}) %collective-permute-start.15) | collective-permute-done | bytes 36896 | tf_op jit(solution)/shard_map/ppermute | solution.py:49
  50.7 1.1 %collective-permute-done.14 = f32[72,128]{1,0:T(8,128)S(1)} collective-permute-done((f32[72,128]{1,0:T(8,128)S(1)}, f32[72,128]{1,0:T(8,128)S(1)}, u32[]{:S(2)}, u32[]{:S(2)}) %collective-permute-start.14) | collective-permute-done | bytes 36896 | tf_op jit(solution)/shard_map/ppermute | solution.py:49
  51.8 4.3 %shard_map.65 = (f32[1024,128]{1,0:T(8,128)}, f32[128,128]{1,0:T(8,128)}) custom-call(f32[72,128]{1,0:T(8,128)S(1)} %add_add_fusion.packed_ref, f32[1024,128]{1,0:T(8,128)S(1)} %get-tuple-element.17.filtered_ref), custom_call_target="tpu_custom_call" | custom-call | tf_op jit(solution)/shard_map/pallas_call | solution.py:369
  (3 shorter events, 0.0 us)
Async XLA Ops:
  2.1 10.8 %collective-permute-start = (bf16[16,64,128]{2,1,0:T(8,128)(2,1)S(1)}, bf16[16,64,128]{2,1,0:T(8,128)(2,1)S(1)}, u32[]{:S(2)}, u32[]{:S(2)}) collective-permute-start(bf16[16,64,128]{2,1,0:T(8,128)(2,1)S(1)} %bitcast.9), channel_id=1, source_target_pairs={{0,1},{1,0},{2,3},{3,2},{4,6},{5,7},{6,4},{7,5},{8,9},{9,8},{10,11... | collective-permute-start | bytes 786440 | tf_op jit(solution)/shard_map/ppermute | solution.py:44
  5.1 8.4 %collective-permute-start.3 = (bf16[16,64,128]{2,1,0:T(8,128)(2,1)S(1)}, bf16[16,64,128]{2,1,0:T(8,128)(2,1)S(1)}, u32[]{:S(2)}, u32[]{:S(2)}) collective-permute-start(bf16[16,64,128]{2,1,0:T(8,128)(2,1)S(1)} %bitcast.10), channel_id=1, source_target_pairs={{0,2},{1,3},{2,0},{3,1},{4,5},{5,4},{6,7},{7,6},{8,10},{9,11},{10,... | collective-permute-start | bytes 786440 | tf_op jit(solution)/shard_map/ppermute | solution.py:44
  6.6 10.1 %collective-permute-start.2 = (bf16[16,64,128]{2,1,0:T(8,128)(2,1)S(1)}, bf16[16,64,128]{2,1,0:T(8,128)(2,1)S(1)}, u32[]{:S(2)}, u32[]{:S(2)}) collective-permute-start(bf16[16,64,128]{2,1,0:T(8,128)(2,1)S(1)} %bitcast.11), channel_id=1, source_target_pairs={{4,8},{8,4},{12,16},{16,12},{20,24},{24,20},{28,0},{0,28},{5,9},{9... | collective-permute-start | bytes 786440 | tf_op jit(solution)/shard_map/ppermute | solution.py:26
  9.1 7.7 %collective-permute-start.1 = (bf16[16,64,128]{2,1,0:T(8,128)(2,1)S(1)}, bf16[16,64,128]{2,1,0:T(8,128)(2,1)S(1)}, u32[]{:S(2)}, u32[]{:S(2)}) collective-permute-start(bf16[16,64,128]{2,1,0:T(8,128)(2,1)S(1)} %bitcast.12), channel_id=1, source_target_pairs={{0,4},{4,0},{8,12},{12,8},{16,20},{20,16},{24,28},{28,24},{1,5},{5... | collective-permute-start | bytes 786440 | tf_op jit(solution)/shard_map/ppermute | solution.py:26
  10.1 1.9 %copy-start = (bf16[16,6,64,256]{3,2,1,0:T(8,128)(2,1)S(1)}, bf16[16,6,64,256]{3,2,1,0:T(8,128)(2,1)}, u32[]{:S(2)}) copy-start(bf16[16,6,64,256]{3,2,1,0:T(8,128)(2,1)} %hamiltonian_ref.11) | copy-start | bytes 9437188
  12.9 6.4 %collective-permute-start.4 = (bf16[16,64,128]{2,1,0:T(8,128)(2,1)S(1)}, bf16[16,64,128]{2,1,0:T(8,128)(2,1)S(1)}, u32[]{:S(2)}, u32[]{:S(2)}) collective-permute-start(bf16[16,64,128]{2,1,0:T(8,128)(2,1)S(1)} %collective-permute-done.refs_0_), channel_id=1, source_target_pairs={{0,2},{1,3},{2,0},{3,1},{4,5},{5,4},{6,7},{7,6},{8,10},{9,11},{10,... | collective-permute-start | bytes 786440 | tf_op jit(solution)/shard_map/ppermute | solution.py:44
  18.2 5.7 %copy-start.1 = (f32[1024,128]{1,0:T(8,128)S(1)}, f32[1024,128]{1,0:T(8,128)}, u32[]{:S(2)}) copy-start(f32[1024,128]{1,0:T(8,128)} %refs_2_.1) | copy-start | bytes 1572868
  18.2 5.7 %copy-start.2 = (f32[1024]{0:T(1024)S(1)}, f32[1024]{0:T(1024)}, u32[]{:S(2)}) copy-start(f32[1024]{0:T(1024)} %param.6) | copy-start | bytes 12292
  20.2 8.2 %collective-permute-start.5 = (bf16[16,64,128]{2,1,0:T(8,128)(2,1)S(1)}, bf16[16,64,128]{2,1,0:T(8,128)(2,1)S(1)}, u32[]{:S(2)}, u32[]{:S(2)}) collective-permute-start(bf16[16,64,128]{2,1,0:T(8,128)(2,1)S(1)} %get-tuple-element.12.own_ref), channel_id=1, source_target_pairs={{0,1},{1,0},{2,3},{3,2},{4,6},{5,7},{6,4},{7,5},{8,9},{9,8},{10,11... | collective-permute-start | bytes 786440 | tf_op jit(solution)/shard_map/ppermute | solution.py:44
  21.5 8.5 %collective-permute-start.8 = (bf16[16,64,128]{2,1,0:T(8,128)(2,1)S(1)}, bf16[16,64,128]{2,1,0:T(8,128)(2,1)S(1)}, u32[]{:S(2)}, u32[]{:S(2)}) collective-permute-start(bf16[16,64,128]{2,1,0:T(8,128)(2,1)S(1)} %get-tuple-element.12.own_ref), channel_id=1, source_target_pairs={{0,2},{1,3},{2,0},{3,1},{4,5},{5,4},{6,7},{7,6},{8,10},{9,11},{10,... | collective-permute-start | bytes 786440 | tf_op jit(solution)/shard_map/ppermute | solution.py:44
  22.2 10.1 %collective-permute-start.7 = (bf16[16,64,128]{2,1,0:T(8,128)(2,1)S(1)}, bf16[16,64,128]{2,1,0:T(8,128)(2,1)S(1)}, u32[]{:S(2)}, u32[]{:S(2)}) collective-permute-start(bf16[16,64,128]{2,1,0:T(8,128)(2,1)S(1)} %get-tuple-element.12.own_ref), channel_id=1, source_target_pairs={{4,8},{8,4},{12,16},{16,12},{20,24},{24,20},{28,0},{0,28},{5,9},{9... | collective-permute-start | bytes 786440 | tf_op jit(solution)/shard_map/ppermute | solution.py:26
  22.2 10.1 %collective-permute-start.6 = (bf16[16,64,128]{2,1,0:T(8,128)(2,1)S(1)}, bf16[16,64,128]{2,1,0:T(8,128)(2,1)S(1)}, u32[]{:S(2)}, u32[]{:S(2)}) collective-permute-start(bf16[16,64,128]{2,1,0:T(8,128)(2,1)S(1)} %get-tuple-element.12.own_ref), channel_id=1, source_target_pairs={{0,4},{4,0},{8,12},{12,8},{16,20},{20,16},{24,28},{28,24},{1,5},{5... | collective-permute-start | bytes 786440 | tf_op jit(solution)/shard_map/ppermute | solution.py:26
  28.4 6.4 %collective-permute-start.9 = (bf16[16,64,128]{2,1,0:T(8,128)(2,1)S(1)}, bf16[16,64,128]{2,1,0:T(8,128)(2,1)S(1)}, u32[]{:S(2)}, u32[]{:S(2)}) collective-permute-start(bf16[16,64,128]{2,1,0:T(8,128)(2,1)S(1)} %collective-permute-done.5.refs_0_), channel_id=1, source_target_pairs={{0,2},{1,3},{2,0},{3,1},{4,5},{5,4},{6,7},{7,6},{8,10},{9,11},{10,... | collective-permute-start | bytes 786440 | tf_op jit(solution)/shard_map/ppermute | solution.py:44
  36.2 1.3 %collective-permute-start.10 = (f32[72,128]{1,0:T(8,128)S(1)}, f32[72,128]{1,0:T(8,128)S(1)}, u32[]{:S(2)}, u32[]{:S(2)}) collective-permute-start(f32[72,128]{1,0:T(8,128)S(1)} %get-tuple-element.16), channel_id=1, source_target_pairs={{0,4},{4,0},{8,12},{12,8},{16,20},{20,16},{24,28},{28,24},{1,5},{5... | collective-permute-start | bytes 110600 | tf_op jit(solution)/shard_map/ppermute | solution.py:49
  37.5 5.8 %collective-permute-start.13 = (f32[72,128]{1,0:T(8,128)S(1)}, f32[72,128]{1,0:T(8,128)S(1)}, u32[]{:S(2)}, u32[]{:S(2)}) collective-permute-start(f32[72,128]{1,0:T(8,128)S(1)} %add.28), channel_id=1, source_target_pairs={{0,24},{4,28},{8,16},{12,20},{16,8},{20,12},{24,0},{28,4},{1,25},{... | collective-permute-start | bytes 110600 | tf_op jit(solution)/shard_map/ppermute | solution.py:49
  39.1 5.4 %collective-permute-start.12 = (f32[72,128]{1,0:T(8,128)S(1)}, f32[72,128]{1,0:T(8,128)S(1)}, u32[]{:S(2)}, u32[]{:S(2)}) collective-permute-start(f32[72,128]{1,0:T(8,128)S(1)} %add.28), channel_id=1, source_target_pairs={{0,16},{4,20},{8,24},{12,28},{16,0},{20,4},{24,8},{28,12},{1,17},{... | collective-permute-start | bytes 110600 | tf_op jit(solution)/shard_map/ppermute | solution.py:49
  39.2 5.3 %collective-permute-start.11 = (f32[72,128]{1,0:T(8,128)S(1)}, f32[72,128]{1,0:T(8,128)S(1)}, u32[]{:S(2)}, u32[]{:S(2)}) collective-permute-start(f32[72,128]{1,0:T(8,128)S(1)} %add.28), channel_id=1, source_target_pairs={{0,8},{4,12},{8,0},{12,4},{16,24},{20,28},{24,16},{28,20},{1,9},{5... | collective-permute-start | bytes 110600 | tf_op jit(solution)/shard_map/ppermute | solution.py:49
  44.5 4.9 %collective-permute-start.16 = (f32[72,128]{1,0:T(8,128)S(1)}, f32[72,128]{1,0:T(8,128)S(1)}, u32[]{:S(2)}, u32[]{:S(2)}) collective-permute-start(f32[72,128]{1,0:T(8,128)S(1)} %add_add_fusion.1), channel_id=1, source_target_pairs={{0,3},{1,2},{2,1},{3,0},{4,7},{5,6},{6,5},{7,4},{8,11},{9,10},{10,... | collective-permute-start | bytes 110600 | tf_op jit(solution)/shard_map/ppermute | solution.py:49
  46.7 4.0 %collective-permute-start.15 = (f32[72,128]{1,0:T(8,128)S(1)}, f32[72,128]{1,0:T(8,128)S(1)}, u32[]{:S(2)}, u32[]{:S(2)}) collective-permute-start(f32[72,128]{1,0:T(8,128)S(1)} %add_add_fusion.1), channel_id=1, source_target_pairs={{0,2},{1,3},{2,0},{3,1},{4,6},{5,7},{6,4},{7,5},{8,10},{9,11},{10,... | collective-permute-start | bytes 110600 | tf_op jit(solution)/shard_map/ppermute | solution.py:49
  47.9 4.0 %collective-permute-start.14 = (f32[72,128]{1,0:T(8,128)S(1)}, f32[72,128]{1,0:T(8,128)S(1)}, u32[]{:S(2)}, u32[]{:S(2)}) collective-permute-start(f32[72,128]{1,0:T(8,128)S(1)} %add_add_fusion.1), channel_id=1, source_target_pairs={{0,1},{1,0},{2,3},{3,2},{4,5},{5,4},{6,7},{7,6},{8,9},{9,8},{10,11... | collective-permute-start | bytes 110600 | tf_op jit(solution)/shard_map/ppermute | solution.py:49

commit v9 on v8

--- a/solution.py
+++ b/solution.py
@@ -20,9 +20,8 @@
 def pair_exchange(value, offset):
     count = lax.axis_size("group")
     route = []
-    for low in range(offset, count + offset, 2):
-        first, second = low % count, (low + 1) % count
-        route += [(first, second), (second, first)]
+    for low in range(offset, count - 1, 2):
+        route += [(low, low + 1), (low + 1, low)]
     return lax.ppermute(value, "group", route)
 
 
@@ -66,26 +65,24 @@
     return jnp.transpose(potential_ref[...])
 
 
-def couple_row(sources_ref, columns_ref, hamiltonian_ref, pieces, row):
-    sources, per_source = hamiltonian_ref.shape[1], hamiltonian_ref.shape[3] // hamiltonian_ref.shape[2]
+def couple_row(index_ref, hamiltonian_ref, pieces, row):
+    shard_blocks, sources, block_size, width = hamiltonian_ref.shape
+    per_source = width // block_size
     total = None
-    for index, piece_ref in pieces:
-        source = sources_ref[index]
+    for number, piece_ref in pieces:
+        source = index_ref[shard_blocks * sources * per_source + number]
         first = (row * sources + source) * per_source
         picked = jnp.concatenate(
-            [piece_ref[columns_ref[first + slot]] for slot in range(per_source)], axis=0
+            [piece_ref[index_ref[first + slot]] for slot in range(per_source)], axis=0
         )
         product = jnp.dot(
             hamiltonian_ref[row, source], picked, preferred_element_type=jnp.float32
         )
-        if index == sources - 1:
-            absent = sources_ref[sources] == index
-            product = jnp.where(absent, 0.0, product)
         total = product if total is None else total + product
     return total
 
 
-def own_kernel(sources_ref, columns_ref, hamiltonian_ref, own_ref, *refs):
+def own_kernel(index_ref, hamiltonian_ref, own_ref, *refs):
     terms, partial_ref = refs[:-1], refs[-1]
     shard_blocks, _, block_size, _ = hamiltonian_ref.shape
     per_column = LANES // block_size
@@ -100,50 +97,57 @@
         else:
             total = terms[0][rows, :]
         partial_ref[rows, :] = total + couple_row(
-            sources_ref, columns_ref, hamiltonian_ref, [(0, own_ref)], row
-        )
-
-
-def middle_kernel(numbers, sources_ref, columns_ref, hamiltonian_ref, partial_ref, *refs):
+            index_ref, hamiltonian_ref, [(0, own_ref)], row
+        )
+
+
+def middle_kernel(numbers, index_ref, hamiltonian_ref, partial_ref, *refs):
     pieces, sum_ref = list(zip(numbers, refs[:-1])), refs[-1]
     shard_blocks, _, block_size, _ = hamiltonian_ref.shape
     for row in range(shard_blocks):
         rows = pl.ds(row * block_size, block_size)
         sum_ref[rows, :] = partial_ref[rows, :] + couple_row(
-            sources_ref, columns_ref, hamiltonian_ref, pieces, row
+            index_ref, hamiltonian_ref, pieces, row
         )
 
 
 def first_kernel(
-    number, sources_ref, columns_ref, hamiltonian_ref, partial_ref, piece_ref, once_ref, round_ref
+    number, index_ref, hamiltonian_ref, partial_ref, piece_ref, once_ref, round_ref
 ):
     shard_blocks, _, block_size, _ = hamiltonian_ref.shape
     for row in range(shard_blocks):
         rows = pl.ds(row * block_size, block_size)
         once = 0.5 * (
             partial_ref[rows, :]
-            + couple_row(sources_ref, columns_ref, hamiltonian_ref, [(number, piece_ref)], row)
+            + couple_row(index_ref, hamiltonian_ref, [(number, piece_ref)], row)
         )
         once_ref[rows, :] = once
         round_ref[row] = once.astype(jnp.bfloat16)
 
 
 def second_kernel(
-    number, sources_ref, columns_ref, hamiltonian_ref, partial_ref, piece_ref,
+    number, index_ref, hamiltonian_ref, partial_ref, piece_ref,
     filtered_ref, packed_ref,
 ):
     shard_blocks, _, block_size, _ = hamiltonian_ref.shape
     for row in range(shard_blocks):
         rows = pl.ds(row * block_size, block_size)
         filtered_ref[rows, :] = partial_ref[rows, :] + couple_row(
-            sources_ref, columns_ref, hamiltonian_ref, [(number, piece_ref)], row
-        )
-    flat = filtered_ref[...]
-    gram = lax.dot_general(
-        flat, flat, (((0,), (0,)), ((), ())), precision=precise,
-        preferred_element_type=jnp.float32,
-    )
+            index_ref, hamiltonian_ref, [(number, piece_ref)], row
+        )
+    states = filtered_ref.shape[1]
+    both = jnp.concatenate(two_parts(filtered_ref[...]), axis=1)
+    products = lax.dot_general(
+        both, both, (((0,), (0,)), ((), ())), preferred_element_type=jnp.float32
+    )
+    high, low = products[:states, :], products[states:, :]
+    gram = high[:, :states] + (high[:, states:] + low[:, :states] + low[:, states:])
     pack(gram, packed_ref)
+
+
+def two_parts(value):
+    high = value.astype(jnp.bfloat16)
+    return high, (value - high.astype(jnp.float32)).astype(jnp.bfloat16)
 
 
 def pack(gram, packed_ref):
@@ -268,11 +272,6 @@
                 held[p] = kept - change[p * SUB : (p + 1) * SUB, :]
 
 
-def two_parts(value):
-    high = value.astype(jnp.bfloat16)
-    return high, (value - high.astype(jnp.float32)).astype(jnp.bfloat16)
-
-
 def factor_kernel(
     rows_total, packed_ref, filtered_ref, ortho_hbm, upper_hbm,
     upper_ref, inverse_ref, ortho_ref, sent, upper_sent,
@@ -313,7 +312,6 @@
 def on_device(hamiltonian, block_columns, potential, trial_slab):
     shard_blocks, _, block_size, _ = hamiltonian.shape
     flat_rows, states = trial_slab.shape
-    columns = block_columns.reshape(-1)
     weights = potential.reshape(-1, LANES)
     rows_total = flat_rows * lax.axis_size("group") * lax.axis_size("blk")
     group, index = lax.axis_index("group"), lax.axis_index("blk")
@@ -325,9 +323,9 @@
         origins += [jnp.bitwise_xor(origin, flip) for origin in origins]
     odd = group % 2
     origins += [cycle_size + 1 - odd, cycle_size + odd]
-    alone = (group == 0) | (group == lax.axis_size("group") - 1)
-    origins.append(jnp.where(alone, cycle_size + 1, -1))
-    sources = jnp.stack(origins).astype(jnp.int32)
+    index_array = jnp.concatenate(
+        [block_columns.reshape(-1)] + [origin.reshape(1).astype(jnp.int32) for origin in origins]
+    )
     last = cycle_size - 1
     middle = [1, cycle_size, cycle_size + 1] + list(range(2, last))
     flat = jax.ShapeDtypeStruct((flat_rows, states), jnp.float32)
@@ -336,8 +334,8 @@
     square = jax.ShapeDtypeStruct((states, states), jnp.float32)
 
     def own_part(value, *terms):
-        return call(own_kernel, flat, [smem] * 2 + [vmem] * (2 + len(terms)))(
-            sources, columns, hamiltonian, value, *terms
+        return call(own_kernel, flat, [smem] + [vmem] * (2 + len(terms)))(
+            index_array, hamiltonian, value, *terms
         )
 
     def coupled(value, *terms):
@@ -352,19 +350,19 @@
         pieces += pairs
         partial = call(
             functools.partial(middle_kernel, middle), flat,
-            [smem] * 2 + [vmem] * (2 + len(middle)),
-        )(sources, columns, hamiltonian, partial, *[pieces[number] for number in middle])
+            [smem] + [vmem] * (2 + len(middle)),
+        )(index_array, hamiltonian, partial, *[pieces[number] for number in middle])
         return partial, pieces[last]
 
     weighted = (weights.reshape(-1, 1) * trial_slab)
     partial, piece = coupled(trial_slab.reshape(rounded.shape).astype(jnp.bfloat16), weighted)
     once, once_round = call(
-        functools.partial(first_kernel, last), (flat, rounded), [smem] * 2 + [vmem] * 3
-    )(sources, columns, hamiltonian, partial, piece)
+        functools.partial(first_kernel, last), (flat, rounded), [smem] + [vmem] * 3
+    )(index_array, hamiltonian, partial, piece)
     partial, piece = coupled(once_round, weights, once, trial_slab)
     filtered, gram = call(
-        functools.partial(second_kernel, last), (flat, packed), [smem] * 2 + [vmem] * 3
-    )(sources, columns, hamiltonian, partial, piece)
+        functools.partial(second_kernel, last), (flat, packed), [smem] + [vmem] * 3
+    )(index_array, hamiltonian, partial, piece)
     gram = summed(gram)
     return call(
         functools.partial(factor_kernel, rows_total),

time: 56.3 us -> 56 us (level)
  waiting for transfers between devices: 18.9 us -> 16.4 us
  starting transfers between devices: 20.8 us -> 23.1 us
    ppermute x4, waiting for transfers between devices: 5.62 us -> 0.01 us  [pair_exchange(): return lax.ppermute(value, 'group', route)]
    ppermute x6, waiting for transfers between devices: 5.77 us -> 9.65 us  [cycle_exchange(): return lax.ppermute(value, ('group', 'blk'), route)]
    ppermute x4, starting transfers between devices: 4.18 us -> 7.31 us  [pair_exchange(): return lax.ppermute(value, 'group', route)]
    ppermute x6, starting transfers between devices: 8.64 us -> 7.73 us  [cycle_exchange(): return lax.ppermute(value, ('group', 'blk'), route)]
    ppermute x7, waiting for transfers between devices: 7.54 us -> 6.72 us  [from_partner(): lax.ppermute(value, axis, [(index, index ^ flip) for index in range(count)])]
  transfers between devices with their start and end apart: 17 -> 17, of which waited for: 11 -> 9; matrix products, arithmetic and copies ran while one was open for 2% -> 2% of each run, Pallas kernels for 8% -> 9%
where the time goes in v9:
time: 56 us; the launch traced here: 55.7 us
  starting transfers between devices  23.1 us (41%)
  waiting for transfers between devices  16.4 us (29%)
  Pallas kernels  11.2 us (20%)
  local copies, waits for them, and re-layouts  2.92 us (5%)
  other arithmetic  1.46 us (3%)
  between operations  0.76 us (1%)
    ppermute x6, waiting for transfers between devices, cycle_exchange(): return lax.ppermute(value, ('group', 'blk'), route)  9.65 us
    ppermute x7, starting transfers between devices, from_partner(): lax.ppermute(value, axis, [(index, index ^ flip) for index in range(count)])  8.01 us
    ppermute x6, starting transfers between devices, cycle_exchange(): return lax.ppermute(value, ('group', 'blk'), route)  7.73 us
    ppermute x4, starting transfers between devices, pair_exchange(): return lax.ppermute(value, 'group', route)  7.31 us
    ppermute x7, waiting for transfers between devices, from_partner(): lax.ppermute(value, axis, [(index, index ^ flip) for index in range(count)])  6.72 us
    pallas_call x1, Pallas kernels, on_device(): call(functools.partial(factor_kernel, rows_total), (flat, square), [vmem,...  4.27 us
    pallas_call x2, Pallas kernels, coupled(): call(functools.partial(middle_kernel, middle), flat, [smem] + [vmem] * (2...  2.94 us
    unnamed x7, local copies, waits for them, and re-layouts  2.72 us
  transfers between devices with their start and end apart: 17, of which 9 were waited for; matrix products, arithmetic and copies ran while one was open for 2% of the time, Pallas kernels for 9%

profile of v9, /device:TPU:0, one launch (start us, length us, event | category | flops | bytes accessed | tf_op | source)
XLA Modules:
  0.0 55.7 jit_solution(6187936247530628935)
XLA Ops:
  0.6 1.4 %broadcast_multiply_fusion = (f32[1024,128]{1,0:T(8,128)S(1)}, bf16[1024,128]{1,0:T(8,128)(2,1)S(1)}) fusion(f32[1024,128]{1,0:T(8,128)} %refs_2_.1, f32[1024]{0:T(1024)} %param.6), kind=kLoop, calls=%fused_computation | loop fusion | flops 262144 | bytes 1314816 | tf_op jit(solution)/shard_map/mul | solution.py:357
  2.1 3.0 %collective-permute-start = (bf16[16,64,128]{2,1,0:T(8,128)(2,1)S(1)}, bf16[16,64,128]{2,1,0:T(8,128)(2,1)S(1)}, u32[]{:S(2)}, u32[]{:S(2)}) collective-permute-start(bf16[16,64,128]{2,1,0:T(8,128)(2,1)S(1)} %bitcast.8), channel_id=1, source_target_pairs={{0,1},{1,0},{2,3},{3,2},{4,6},{5,7},{6,4},{7,5},{8,9},{9,8},{10,11... | collective-permute-start | bytes 786440 | tf_op jit(solution)/shard_map/ppermute | solution.py:43
  5.1 1.5 %collective-permute-start.3 = (bf16[16,64,128]{2,1,0:T(8,128)(2,1)S(1)}, bf16[16,64,128]{2,1,0:T(8,128)(2,1)S(1)}, u32[]{:S(2)}, u32[]{:S(2)}) collective-permute-start(bf16[16,64,128]{2,1,0:T(8,128)(2,1)S(1)} %bitcast.9), channel_id=1, source_target_pairs={{0,2},{1,3},{2,0},{3,1},{4,5},{5,4},{6,7},{7,6},{8,10},{9,11},{10,... | collective-permute-start | bytes 786440 | tf_op jit(solution)/shard_map/ppermute | solution.py:43
  6.6 0.7 %collective-permute-start.2 = (bf16[16,64,128]{2,1,0:T(8,128)(2,1)S(1)}, bf16[16,64,128]{2,1,0:T(8,128)(2,1)S(1)}, u32[]{:S(2)}, u32[]{:S(2)}) collective-permute-start(bf16[16,64,128]{2,1,0:T(8,128)(2,1)S(1)} %bitcast.10), channel_id=1, source_target_pairs={{4,8},{8,4},{12,16},{16,12},{20,24},{24,20},{5,9},{9,5},{13,17},{1... | collective-permute-start | bytes 786440 | tf_op jit(solution)/shard_map/ppermute | solution.py:25
  7.3 3.0 %collective-permute-start.1 = (bf16[16,64,128]{2,1,0:T(8,128)(2,1)S(1)}, bf16[16,64,128]{2,1,0:T(8,128)(2,1)S(1)}, u32[]{:S(2)}, u32[]{:S(2)}) collective-permute-start(bf16[16,64,128]{2,1,0:T(8,128)(2,1)S(1)} %bitcast.11), channel_id=1, source_target_pairs={{0,4},{4,0},{8,12},{12,8},{16,20},{20,16},{24,28},{28,24},{1,5},{5... | collective-permute-start | bytes 786440 | tf_op jit(solution)/shard_map/ppermute | solution.py:25
  10.2 0.8 %copy.6 = s32[16,6,4]{2,1,0:T(8,128)S(1)} copy(s32[16,6,4]{0,2,1:T(4,128)} %param.5) | data formatting | bytes 3072 | tf_op args[1]
  11.1 0.1 reshape.31
  11.2 0.1 concatenate.3.index_ref
  11.3 0.0 copy-start
  11.3 1.9 %copy-done = bf16[16,6,64,256]{3,2,1,0:T(8,128)(2,1)S(1)} copy-done((bf16[16,6,64,256]{3,2,1,0:T(8,128)(2,1)S(1)}, bf16[16,6,64,256]{3,2,1,0:T(8,128)(2,1)}, u32[]{:S(2)}) %copy-start) | copy-done | bytes 3145752
  13.2 0.9 %shard_map.59.partial_ref = f32[1024,128]{1,0:T(8,128)S(1)} custom-call(s32[390]{0:T(512)S(1)} %concatenate.3.index_ref, bf16[16,6,64,256]{3,2,1,0:T(8,128)(2,1)S(1)} %copy-done, bf16[16,64,128]{2,1,0:T(8,128)(2,1)S(1)} %bitcast.12, f32[1024,128]{1,0:T(8,128)S(1)} %get-tuple-element.18.refs_0_), custom_call_target="tpu_custom_call" | custom-call | tf_op jit(solution)/shard_map/pallas_call | solution.py:337
  14.1 0.0 collective-permute-done.refs_0_
  14.1 0.6 %collective-permute-start.4 = (bf16[16,64,128]{2,1,0:T(8,128)(2,1)S(1)}, bf16[16,64,128]{2,1,0:T(8,128)(2,1)S(1)}, u32[]{:S(2)}, u32[]{:S(2)}) collective-permute-start(bf16[16,64,128]{2,1,0:T(8,128)(2,1)S(1)} %collective-permute-done.refs_0_), channel_id=1, source_target_pairs={{0,2},{1,3},{2,0},{3,1},{4,5},{5,4},{6,7},{7,6},{8,10},{9,11},{10,... | collective-permute-start | bytes 786440 | tf_op jit(solution)/shard_map/ppermute | solution.py:43
  14.6 0.0 collective-permute-done.3.refs_3_
  14.6 0.0 collective-permute-done.2.refs_2_
  14.6 0.0 collective-permute-done.1.refs_1_
  14.7 1.5 %shard_map.60.partial_ref = f32[1024,128]{1,0:T(8,128)S(1)} custom-call(s32[390]{0:T(512)S(1)} %concatenate.3.index_ref, bf16[16,6,64,256]{3,2,1,0:T(8,128)(2,1)S(1)} %copy-done, f32[1024,128]{1,0:T(8,128)S(1)} %shard_map.59.partial_ref, bf16[16,64,128]{2,1,0:T(8,128)(2,1)S(1)} %collective-permute-done.refs_0_, ...), custom_call_target="tpu_custom_call" | custom-call | tf_op jit(solution)/shard_map/pallas_call | solution.py:351
  16.1 0.0 copy-start.1
  16.1 0.0 copy-start.2
  16.2 4.3 %collective-permute-done.4.piece_ref = bf16[16,64,128]{2,1,0:T(8,128)(2,1)S(1)} collective-permute-done((bf16[16,64,128]{2,1,0:T(8,128)(2,1)S(1)}, bf16[16,64,128]{2,1,0:T(8,128)(2,1)S(1)}, u32[]{:S(2)}, u32[]{:S(2)}) %collective-permute-start.4) | collective-permute-done | bytes 262176 | tf_op jit(solution)/shard_map/ppermute | solution.py:43
  20.5 0.9 %shard_map.61 = (f32[1024,128]{1,0:T(8,128)S(1)}, bf16[16,64,128]{2,1,0:T(8,128)(2,1)S(1)}) custom-call(s32[390]{0:T(512)S(1)} %concatenate.3.index_ref, bf16[16,6,64,256]{3,2,1,0:T(8,128)(2,1)S(1)} %copy-done, f32[1024,128]{1,0:T(8,128)S(1)} %shard_map.60.partial_ref, bf16[16,64,128]{2,1,0:T(8,128)(2,1)S(1)} %collective-permute-done.4.piece_ref), custom_call_target="tpu_custom_call" | custom-call | tf_op jit(solution)/shard_map/pallas_call | solution.py:359
  21.4 0.6 %collective-permute-start.5 = (bf16[16,64,128]{2,1,0:T(8,128)(2,1)S(1)}, bf16[16,64,128]{2,1,0:T(8,128)(2,1)S(1)}, u32[]{:S(2)}, u32[]{:S(2)}) collective-permute-start(bf16[16,64,128]{2,1,0:T(8,128)(2,1)S(1)} %get-tuple-element.12.own_ref), channel_id=1, source_target_pairs={{0,1},{1,0},{2,3},{3,2},{4,6},{5,7},{6,4},{7,5},{8,9},{9,8},{10,11... | collective-permute-start | bytes 786440 | tf_op jit(solution)/shard_map/ppermute | solution.py:43
  22.0 0.5 collective-permute-start.8
  22.5 0.7 %collective-permute-start.7 = (bf16[16,64,128]{2,1,0:T(8,128)(2,1)S(1)}, bf16[16,64,128]{2,1,0:T(8,128)(2,1)S(1)}, u32[]{:S(2)}, u32[]{:S(2)}) collective-permute-start(bf16[16,64,128]{2,1,0:T(8,128)(2,1)S(1)} %get-tuple-element.12.own_ref), channel_id=1, source_target_pairs={{4,8},{8,4},{12,16},{16,12},{20,24},{24,20},{5,9},{9,5},{13,17},{1... | collective-permute-start | bytes 786440 | tf_op jit(solution)/shard_map/ppermute | solution.py:25
  23.2 3.0 %collective-permute-start.6 = (bf16[16,64,128]{2,1,0:T(8,128)(2,1)S(1)}, bf16[16,64,128]{2,1,0:T(8,128)(2,1)S(1)}, u32[]{:S(2)}, u32[]{:S(2)}) collective-permute-start(bf16[16,64,128]{2,1,0:T(8,128)(2,1)S(1)} %get-tuple-element.12.own_ref), channel_id=1, source_target_pairs={{0,4},{4,0},{8,12},{12,8},{16,20},{20,16},{24,28},{28,24},{1,5},{5... | collective-permute-start | bytes 786440 | tf_op jit(solution)/shard_map/ppermute | solution.py:25
  26.2 0.0 copy-done.1
  26.2 0.0 copy-done.2
  26.2 1.0 %shard_map.62.partial_ref = f32[1024,128]{1,0:T(8,128)S(1)} custom-call(s32[390]{0:T(512)S(1)} %concatenate.3.index_ref, bf16[16,6,64,256]{3,2,1,0:T(8,128)(2,1)S(1)} %copy-done, bf16[16,64,128]{2,1,0:T(8,128)(2,1)S(1)} %get-tuple-element.12.own_ref, f32[8,128]{1,0:T(8,128)S(1)} %bitcast.13, f32[1024,128]{1,0:T(8,128)S(1)} %get-tuple-element.13.refs_1_, ...), custom_call_target="tpu_custom_call" | custom-call | tf_op jit(solution)/shard_map/pallas_call | solution.py:337
  27.1 1.9 %collective-permute-done.5.refs_0_ = bf16[16,64,128]{2,1,0:T(8,128)(2,1)S(1)} collective-permute-done((bf16[16,64,128]{2,1,0:T(8,128)(2,1)S(1)}, bf16[16,64,128]{2,1,0:T(8,128)(2,1)S(1)}, u32[]{:S(2)}, u32[]{:S(2)}) %collective-permute-start.5) | collective-permute-done | bytes 262176 | tf_op jit(solution)/shard_map/ppermute | solution.py:43
  29.1 1.5 %collective-permute-start.9 = (bf16[16,64,128]{2,1,0:T(8,128)(2,1)S(1)}, bf16[16,64,128]{2,1,0:T(8,128)(2,1)S(1)}, u32[]{:S(2)}, u32[]{:S(2)}) collective-permute-start(bf16[16,64,128]{2,1,0:T(8,128)(2,1)S(1)} %collective-permute-done.5.refs_0_), channel_id=1, source_target_pairs={{0,2},{1,3},{2,0},{3,1},{4,5},{5,4},{6,7},{7,6},{8,10},{9,11},{10,... | collective-permute-start | bytes 786440 | tf_op jit(solution)/shard_map/ppermute | solution.py:43
  30.6 0.0 collective-permute-done.8.refs_3_
  30.6 0.0 collective-permute-done.7.refs_2_
  30.6 0.0 collective-permute-done.6.refs_1_
  30.6 1.5 %shard_map.63.partial_ref = f32[1024,128]{1,0:T(8,128)S(1)} custom-call(s32[390]{0:T(512)S(1)} %concatenate.3.index_ref, bf16[16,6,64,256]{3,2,1,0:T(8,128)(2,1)S(1)} %copy-done, f32[1024,128]{1,0:T(8,128)S(1)} %shard_map.62.partial_ref, bf16[16,64,128]{2,1,0:T(8,128)(2,1)S(1)} %collective-permute-done.5.refs_0_, ...), custom_call_target="tpu_custom_call" | custom-call | tf_op jit(solution)/shard_map/pallas_call | solution.py:351
  32.1 3.4 %collective-permute-done.9.piece_ref = bf16[16,64,128]{2,1,0:T(8,128)(2,1)S(1)} collective-permute-done((bf16[16,64,128]{2,1,0:T(8,128)(2,1)S(1)}, bf16[16,64,128]{2,1,0:T(8,128)(2,1)S(1)}, u32[]{:S(2)}, u32[]{:S(2)}) %collective-permute-start.9) | collective-permute-done | bytes 262176 | tf_op jit(solution)/shard_map/ppermute | solution.py:43
  35.5 1.2 %shard_map.64 = (f32[1024,128]{1,0:T(8,128)S(1)}, f32[72,128]{1,0:T(8,128)S(1)}) custom-call(s32[390]{0:T(512)S(1)} %concatenate.3.index_ref, bf16[16,6,64,256]{3,2,1,0:T(8,128)(2,1)S(1)} %copy-done, f32[1024,128]{1,0:T(8,128)S(1)} %shard_map.63.partial_ref, bf16[16,64,128]{2,1,0:T(8,128)(2,1)S(1)} %collective-permute-done.9.piece_ref), custom_call_target="tpu_custom_call" | custom-call | tf_op jit(solution)/shard_map/pallas_call | solution.py:363
  36.7 0.1 collective-permute-start.10
  36.8 1.2 %collective-permute-done.10 = f32[72,128]{1,0:T(8,128)S(1)} collective-permute-done((f32[72,128]{1,0:T(8,128)S(1)}, f32[72,128]{1,0:T(8,128)S(1)}, u32[]{:S(2)}, u32[]{:S(2)}) %collective-permute-start.10) | collective-permute-done | bytes 36896 | tf_op jit(solution)/shard_map/ppermute | solution.py:48
  38.0 2.4 %collective-permute-start.13 = (f32[72,128]{1,0:T(8,128)S(1)}, f32[72,128]{1,0:T(8,128)S(1)}, u32[]{:S(2)}, u32[]{:S(2)}) collective-permute-start(f32[72,128]{1,0:T(8,128)S(1)} %add.28), channel_id=1, source_target_pairs={{0,24},{4,28},{8,16},{12,20},{16,8},{20,12},{24,0},{28,4},{1,25},{... | collective-permute-start | bytes 110600 | tf_op jit(solution)/shard_map/ppermute | solution.py:48
  40.4 0.6 %collective-permute-start.12 = (f32[72,128]{1,0:T(8,128)S(1)}, f32[72,128]{1,0:T(8,128)S(1)}, u32[]{:S(2)}, u32[]{:S(2)}) collective-permute-start(f32[72,128]{1,0:T(8,128)S(1)} %add.28), channel_id=1, source_target_pairs={{0,16},{4,20},{8,24},{12,28},{16,0},{20,4},{24,8},{28,12},{1,17},{... | collective-permute-start | bytes 110600 | tf_op jit(solution)/shard_map/ppermute | solution.py:48
  41.0 1.4 %collective-permute-start.11 = (f32[72,128]{1,0:T(8,128)S(1)}, f32[72,128]{1,0:T(8,128)S(1)}, u32[]{:S(2)}, u32[]{:S(2)}) collective-permute-start(f32[72,128]{1,0:T(8,128)S(1)} %add.28), channel_id=1, source_target_pairs={{0,8},{4,12},{8,0},{12,4},{16,24},{20,28},{24,16},{28,20},{1,9},{5... | collective-permute-start | bytes 110600 | tf_op jit(solution)/shard_map/ppermute | solution.py:48
  42.4 1.5 %collective-permute-done.13 = f32[72,128]{1,0:T(8,128)S(1)} collective-permute-done((f32[72,128]{1,0:T(8,128)S(1)}, f32[72,128]{1,0:T(8,128)S(1)}, u32[]{:S(2)}, u32[]{:S(2)}) %collective-permute-start.13) | collective-permute-done | bytes 36896 | tf_op jit(solution)/shard_map/ppermute | solution.py:48
  43.8 1.6 %collective-permute-done.12 = f32[72,128]{1,0:T(8,128)S(1)} collective-permute-done((f32[72,128]{1,0:T(8,128)S(1)}, f32[72,128]{1,0:T(8,128)S(1)}, u32[]{:S(2)}, u32[]{:S(2)}) %collective-permute-start.12) | collective-permute-done | bytes 36896 | tf_op jit(solution)/shard_map/ppermute | solution.py:48
  45.4 0.0 collective-permute-done.11
  45.4 1.5 %collective-permute-start.16 = (f32[72,128]{1,0:T(8,128)S(1)}, f32[72,128]{1,0:T(8,128)S(1)}, u32[]{:S(2)}, u32[]{:S(2)}) collective-permute-start(f32[72,128]{1,0:T(8,128)S(1)} %add_add_fusion.1), channel_id=1, source_target_pairs={{0,3},{1,2},{2,1},{3,0},{4,7},{5,6},{6,5},{7,4},{8,11},{9,10},{10,... | collective-permute-start | bytes 110600 | tf_op jit(solution)/shard_map/ppermute | solution.py:48
  47.0 0.5 collective-permute-start.15
  47.5 1.5 %collective-permute-start.14 = (f32[72,128]{1,0:T(8,128)S(1)}, f32[72,128]{1,0:T(8,128)S(1)}, u32[]{:S(2)}, u32[]{:S(2)}) collective-permute-start(f32[72,128]{1,0:T(8,128)S(1)} %add_add_fusion.1), channel_id=1, source_target_pairs={{0,1},{1,0},{2,3},{3,2},{4,5},{5,4},{6,7},{7,6},{8,9},{9,8},{10,11... | collective-permute-start | bytes 110600 | tf_op jit(solution)/shard_map/ppermute | solution.py:48
  49.0 1.4 %collective-permute-done.16 = f32[72,128]{1,0:T(8,128)S(1)} collective-permute-done((f32[72,128]{1,0:T(8,128)S(1)}, f32[72,128]{1,0:T(8,128)S(1)}, u32[]{:S(2)}, u32[]{:S(2)}) %collective-permute-start.16) | collective-permute-done | bytes 36896 | tf_op jit(solution)/shard_map/ppermute | solution.py:48
  50.4 0.6 %collective-permute-done.15 = f32[72,128]{1,0:T(8,128)S(1)} collective-permute-done((f32[72,128]{1,0:T(8,128)S(1)}, f32[72,128]{1,0:T(8,128)S(1)}, u32[]{:S(2)}, u32[]{:S(2)}) %collective-permute-start.15) | collective-permute-done | bytes 36896 | tf_op jit(solution)/shard_map/ppermute | solution.py:48
  50.9 0.5 collective-permute-done.14
  51.5 4.3 %shard_map.65 = (f32[1024,128]{1,0:T(8,128)}, f32[128,128]{1,0:T(8,128)}) custom-call(f32[72,128]{1,0:T(8,128)S(1)} %add_add_fusion.packed_ref, f32[1024,128]{1,0:T(8,128)S(1)} %get-tuple-element.17.filtered_ref), custom_call_target="tpu_custom_call" | custom-call | tf_op jit(solution)/shard_map/pallas_call | solution.py:367
  (3 shorter events, 0.0 us)
Async XLA Ops:
  2.1 12.0 %collective-permute-start = (bf16[16,64,128]{2,1,0:T(8,128)(2,1)S(1)}, bf16[16,64,128]{2,1,0:T(8,128)(2,1)S(1)}, u32[]{:S(2)}, u32[]{:S(2)}) collective-permute-start(bf16[16,64,128]{2,1,0:T(8,128)(2,1)S(1)} %bitcast.8), channel_id=1, source_target_pairs={{0,1},{1,0},{2,3},{3,2},{4,6},{5,7},{6,4},{7,5},{8,9},{9,8},{10,11... | collective-permute-start | bytes 786440 | tf_op jit(solution)/shard_map/ppermute | solution.py:43
  5.1 9.6 %collective-permute-start.3 = (bf16[16,64,128]{2,1,0:T(8,128)(2,1)S(1)}, bf16[16,64,128]{2,1,0:T(8,128)(2,1)S(1)}, u32[]{:S(2)}, u32[]{:S(2)}) collective-permute-start(bf16[16,64,128]{2,1,0:T(8,128)(2,1)S(1)} %bitcast.9), channel_id=1, source_target_pairs={{0,2},{1,3},{2,0},{3,1},{4,5},{5,4},{6,7},{7,6},{8,10},{9,11},{10,... | collective-permute-start | bytes 786440 | tf_op jit(solution)/shard_map/ppermute | solution.py:43
  6.6 8.1 %collective-permute-start.2 = (bf16[16,64,128]{2,1,0:T(8,128)(2,1)S(1)}, bf16[16,64,128]{2,1,0:T(8,128)(2,1)S(1)}, u32[]{:S(2)}, u32[]{:S(2)}) collective-permute-start(bf16[16,64,128]{2,1,0:T(8,128)(2,1)S(1)} %bitcast.10), channel_id=1, source_target_pairs={{4,8},{8,4},{12,16},{16,12},{20,24},{24,20},{5,9},{9,5},{13,17},{1... | collective-permute-start | bytes 786440 | tf_op jit(solution)/shard_map/ppermute | solution.py:25
  7.3 7.4 %collective-permute-start.1 = (bf16[16,64,128]{2,1,0:T(8,128)(2,1)S(1)}, bf16[16,64,128]{2,1,0:T(8,128)(2,1)S(1)}, u32[]{:S(2)}, u32[]{:S(2)}) collective-permute-start(bf16[16,64,128]{2,1,0:T(8,128)(2,1)S(1)} %bitcast.11), channel_id=1, source_target_pairs={{0,4},{4,0},{8,12},{12,8},{16,20},{20,16},{24,28},{28,24},{1,5},{5... | collective-permute-start | bytes 786440 | tf_op jit(solution)/shard_map/ppermute | solution.py:25
  11.3 1.9 %copy-start = (bf16[16,6,64,256]{3,2,1,0:T(8,128)(2,1)S(1)}, bf16[16,6,64,256]{3,2,1,0:T(8,128)(2,1)}, u32[]{:S(2)}) copy-start(bf16[16,6,64,256]{3,2,1,0:T(8,128)(2,1)} %hamiltonian_ref.11) | copy-start | bytes 9437188
  14.1 6.4 %collective-permute-start.4 = (bf16[16,64,128]{2,1,0:T(8,128)(2,1)S(1)}, bf16[16,64,128]{2,1,0:T(8,128)(2,1)S(1)}, u32[]{:S(2)}, u32[]{:S(2)}) collective-permute-start(bf16[16,64,128]{2,1,0:T(8,128)(2,1)S(1)} %collective-permute-done.refs_0_), channel_id=1, source_target_pairs={{0,2},{1,3},{2,0},{3,1},{4,5},{5,4},{6,7},{7,6},{8,10},{9,11},{10,... | collective-permute-start | bytes 786440 | tf_op jit(solution)/shard_map/ppermute | solution.py:43
  16.1 10.0 %copy-start.1 = (f32[1024,128]{1,0:T(8,128)S(1)}, f32[1024,128]{1,0:T(8,128)}, u32[]{:S(2)}) copy-start(f32[1024,128]{1,0:T(8,128)} %refs_2_.1) | copy-start | bytes 1572868
  16.1 10.0 %copy-start.2 = (f32[1024]{0:T(1024)S(1)}, f32[1024]{0:T(1024)}, u32[]{:S(2)}) copy-start(f32[1024]{0:T(1024)} %param.6) | copy-start | bytes 12292
  21.4 7.7 %collective-permute-start.5 = (bf16[16,64,128]{2,1,0:T(8,128)(2,1)S(1)}, bf16[16,64,128]{2,1,0:T(8,128)(2,1)S(1)}, u32[]{:S(2)}, u32[]{:S(2)}) collective-permute-start(bf16[16,64,128]{2,1,0:T(8,128)(2,1)S(1)} %get-tuple-element.12.own_ref), channel_id=1, source_target_pairs={{0,1},{1,0},{2,3},{3,2},{4,6},{5,7},{6,4},{7,5},{8,9},{9,8},{10,11... | collective-permute-start | bytes 786440 | tf_op jit(solution)/shard_map/ppermute | solution.py:43
  22.0 8.6 %collective-permute-start.8 = (bf16[16,64,128]{2,1,0:T(8,128)(2,1)S(1)}, bf16[16,64,128]{2,1,0:T(8,128)(2,1)S(1)}, u32[]{:S(2)}, u32[]{:S(2)}) collective-permute-start(bf16[16,64,128]{2,1,0:T(8,128)(2,1)S(1)} %get-tuple-element.12.own_ref), channel_id=1, source_target_pairs={{0,2},{1,3},{2,0},{3,1},{4,5},{5,4},{6,7},{7,6},{8,10},{9,11},{10,... | collective-permute-start | bytes 786440 | tf_op jit(solution)/shard_map/ppermute | solution.py:43
  22.5 8.1 %collective-permute-start.7 = (bf16[16,64,128]{2,1,0:T(8,128)(2,1)S(1)}, bf16[16,64,128]{2,1,0:T(8,128)(2,1)S(1)}, u32[]{:S(2)}, u32[]{:S(2)}) collective-permute-start(bf16[16,64,128]{2,1,0:T(8,128)(2,1)S(1)} %get-tuple-element.12.own_ref), channel_id=1, source_target_pairs={{4,8},{8,4},{12,16},{16,12},{20,24},{24,20},{5,9},{9,5},{13,17},{1... | collective-permute-start | bytes 786440 | tf_op jit(solution)/shard_map/ppermute | solution.py:25
  23.2 7.5 %collective-permute-start.6 = (bf16[16,64,128]{2,1,0:T(8,128)(2,1)S(1)}, bf16[16,64,128]{2,1,0:T(8,128)(2,1)S(1)}, u32[]{:S(2)}, u32[]{:S(2)}) collective-permute-start(bf16[16,64,128]{2,1,0:T(8,128)(2,1)S(1)} %get-tuple-element.12.own_ref), channel_id=1, source_target_pairs={{0,4},{4,0},{8,12},{12,8},{16,20},{20,16},{24,28},{28,24},{1,5},{5... | collective-permute-start | bytes 786440 | tf_op jit(solution)/shard_map/ppermute | solution.py:25
  29.1 6.4 %collective-permute-start.9 = (bf16[16,64,128]{2,1,0:T(8,128)(2,1)S(1)}, bf16[16,64,128]{2,1,0:T(8,128)(2,1)S(1)}, u32[]{:S(2)}, u32[]{:S(2)}) collective-permute-start(bf16[16,64,128]{2,1,0:T(8,128)(2,1)S(1)} %collective-permute-done.5.refs_0_), channel_id=1, source_target_pairs={{0,2},{1,3},{2,0},{3,1},{4,5},{5,4},{6,7},{7,6},{8,10},{9,11},{10,... | collective-permute-start | bytes 786440 | tf_op jit(solution)/shard_map/ppermute | solution.py:43
  36.7 1.3 %collective-permute-start.10 = (f32[72,128]{1,0:T(8,128)S(1)}, f32[72,128]{1,0:T(8,128)S(1)}, u32[]{:S(2)}, u32[]{:S(2)}) collective-permute-start(f32[72,128]{1,0:T(8,128)S(1)} %get-tuple-element.16), channel_id=1, source_target_pairs={{0,4},{4,0},{8,12},{12,8},{16,20},{20,16},{24,28},{28,24},{1,5},{5... | collective-permute-start | bytes 110600 | tf_op jit(solution)/shard_map/ppermute | solution.py:48
  38.0 5.9 %collective-permute-start.13 = (f32[72,128]{1,0:T(8,128)S(1)}, f32[72,128]{1,0:T(8,128)S(1)}, u32[]{:S(2)}, u32[]{:S(2)}) collective-permute-start(f32[72,128]{1,0:T(8,128)S(1)} %add.28), channel_id=1, source_target_pairs={{0,24},{4,28},{8,16},{12,20},{16,8},{20,12},{24,0},{28,4},{1,25},{... | collective-permute-start | bytes 110600 | tf_op jit(solution)/shard_map/ppermute | solution.py:48
  40.4 5.0 %collective-permute-start.12 = (f32[72,128]{1,0:T(8,128)S(1)}, f32[72,128]{1,0:T(8,128)S(1)}, u32[]{:S(2)}, u32[]{:S(2)}) collective-permute-start(f32[72,128]{1,0:T(8,128)S(1)} %add.28), channel_id=1, source_target_pairs={{0,16},{4,20},{8,24},{12,28},{16,0},{20,4},{24,8},{28,12},{1,17},{... | collective-permute-start | bytes 110600 | tf_op jit(solution)/shard_map/ppermute | solution.py:48
  41.0 4.4 %collective-permute-start.11 = (f32[72,128]{1,0:T(8,128)S(1)}, f32[72,128]{1,0:T(8,128)S(1)}, u32[]{:S(2)}, u32[]{:S(2)}) collective-permute-start(f32[72,128]{1,0:T(8,128)S(1)} %add.28), channel_id=1, source_target_pairs={{0,8},{4,12},{8,0},{12,4},{16,24},{20,28},{24,16},{28,20},{1,9},{5... | collective-permute-start | bytes 110600 | tf_op jit(solution)/shard_map/ppermute | solution.py:48
  45.4 4.9 %collective-permute-start.16 = (f32[72,128]{1,0:T(8,128)S(1)}, f32[72,128]{1,0:T(8,128)S(1)}, u32[]{:S(2)}, u32[]{:S(2)}) collective-permute-start(f32[72,128]{1,0:T(8,128)S(1)} %add_add_fusion.1), channel_id=1, source_target_pairs={{0,3},{1,2},{2,1},{3,0},{4,7},{5,6},{6,5},{7,4},{8,11},{9,10},{10,... | collective-permute-start | bytes 110600 | tf_op jit(solution)/shard_map/ppermute | solution.py:48
  47.0 4.0 %collective-permute-start.15 = (f32[72,128]{1,0:T(8,128)S(1)}, f32[72,128]{1,0:T(8,128)S(1)}, u32[]{:S(2)}, u32[]{:S(2)}) collective-permute-start(f32[72,128]{1,0:T(8,128)S(1)} %add_add_fusion.1), channel_id=1, source_target_pairs={{0,2},{1,3},{2,0},{3,1},{4,6},{5,7},{6,4},{7,5},{8,10},{9,11},{10,... | collective-permute-start | bytes 110600 | tf_op jit(solution)/shard_map/ppermute | solution.py:48
  47.5 4.0 %collective-permute-start.14 = (f32[72,128]{1,0:T(8,128)S(1)}, f32[72,128]{1,0:T(8,128)S(1)}, u32[]{:S(2)}, u32[]{:S(2)}) collective-permute-start(f32[72,128]{1,0:T(8,128)S(1)} %add_add_fusion.1), channel_id=1, source_target_pairs={{0,1},{1,0},{2,3},{3,2},{4,5},{5,4},{6,7},{7,6},{8,9},{9,8},{10,11... | collective-permute-start | bytes 110600 | tf_op jit(solution)/shard_map/ppermute | solution.py:48

commit v10 on v9

--- a/solution.py
+++ b/solution.py
@@ -111,29 +111,25 @@
         )
 
 
-def first_kernel(
-    number, index_ref, hamiltonian_ref, partial_ref, piece_ref, once_ref, round_ref
-):
+def first_kernel(numbers, index_ref, hamiltonian_ref, partial_ref, *refs):
+    pieces, (once_ref, round_ref) = list(zip(numbers, refs)), refs[len(numbers) :]
     shard_blocks, _, block_size, _ = hamiltonian_ref.shape
     for row in range(shard_blocks):
         rows = pl.ds(row * block_size, block_size)
         once = 0.5 * (
-            partial_ref[rows, :]
-            + couple_row(index_ref, hamiltonian_ref, [(number, piece_ref)], row)
+            partial_ref[rows, :] + couple_row(index_ref, hamiltonian_ref, pieces, row)
         )
         once_ref[rows, :] = once
         round_ref[row] = once.astype(jnp.bfloat16)
 
 
-def second_kernel(
-    number, index_ref, hamiltonian_ref, partial_ref, piece_ref,
-    filtered_ref, packed_ref,
-):
+def second_kernel(numbers, index_ref, hamiltonian_ref, partial_ref, *refs):
+    pieces, (filtered_ref, packed_ref) = list(zip(numbers, refs)), refs[len(numbers) :]
     shard_blocks, _, block_size, _ = hamiltonian_ref.shape
     for row in range(shard_blocks):
         rows = pl.ds(row * block_size, block_size)
         filtered_ref[rows, :] = partial_ref[rows, :] + couple_row(
-            index_ref, hamiltonian_ref, [(number, piece_ref)], row
+            index_ref, hamiltonian_ref, pieces, row
         )
     states = filtered_ref.shape[1]
     both = jnp.concatenate(two_parts(filtered_ref[...]), axis=1)
@@ -327,7 +323,8 @@
         [block_columns.reshape(-1)] + [origin.reshape(1).astype(jnp.int32) for origin in origins]
     )
     last = cycle_size - 1
-    middle = [1, cycle_size, cycle_size + 1] + list(range(2, last))
+    ending = [cycle_size, last]
+    middle = [1] + list(range(2, last)) + [cycle_size + 1]
     flat = jax.ShapeDtypeStruct((flat_rows, states), jnp.float32)
     rounded = jax.ShapeDtypeStruct((shard_blocks, block_size, states), jnp.bfloat16)
     packed = jax.ShapeDtypeStruct((states // 2 + SUB, states), jnp.float32)
@@ -338,31 +335,35 @@
             index_array, hamiltonian, value, *terms
         )
 
-    def coupled(value, *terms):
-        pairs = [pair_exchange(value, 0), pair_exchange(value, 1)]
-        pieces = [value, cycle_exchange(value, 0)]
-        partial = own_part(value, *terms)
-        for level in range(1, levels):
-            arrived = pieces[1:]
-            if level == 1:
-                arrived, partial = lax.optimization_barrier((arrived, partial))
-            pieces += [cycle_exchange(piece, level) for piece in [value] + arrived]
-        pieces += pairs
+    def coupled(value, early, *terms):
+        arrived = cycle_exchange(value, 0)
+        outer = pair_exchange(value, 1)
+        others = [cycle_exchange(value, level) for level in range(1, levels)]
+        if early:
+            partial = own_part(value, *terms)
+            arrived, again, partial = lax.optimization_barrier((arrived, value, partial))
+        else:
+            arrived, again = lax.optimization_barrier((arrived, value))
+        pieces = [value, arrived]
+        for level, other in zip(range(1, levels), others):
+            pieces += [other] + [cycle_exchange(piece, level) for piece in pieces[1:]]
+        pieces += [pair_exchange(again, 0), outer]
+        if not early:
+            partial = own_part(value, *terms)
         partial = call(
-            functools.partial(middle_kernel, middle), flat,
-            [smem] + [vmem] * (2 + len(middle)),
+            functools.partial(middle_kernel, middle), flat, [smem] + [vmem] * (2 + len(middle)),
         )(index_array, hamiltonian, partial, *[pieces[number] for number in middle])
-        return partial, pieces[last]
+        return [partial] + [pieces[number] for number in ending]
 
     weighted = (weights.reshape(-1, 1) * trial_slab)
-    partial, piece = coupled(trial_slab.reshape(rounded.shape).astype(jnp.bfloat16), weighted)
+    parts = coupled(trial_slab.reshape(rounded.shape).astype(jnp.bfloat16), False, weighted)
     once, once_round = call(
-        functools.partial(first_kernel, last), (flat, rounded), [smem] + [vmem] * 3
-    )(index_array, hamiltonian, partial, piece)
-    partial, piece = coupled(once_round, weights, once, trial_slab)
+        functools.partial(first_kernel, ending), (flat, rounded), [smem] + [vmem] * 4
+    )(index_array, hamiltonian, *parts)
+    parts = coupled(once_round, True, weights, once, trial_slab)
     filtered, gram = call(
-        functools.partial(second_kernel, last), (flat, packed), [smem] + [vmem] * 3
-    )(index_array, hamiltonian, partial, piece)
+        functools.partial(second_kernel, ending), (flat, packed), [smem] + [vmem] * 4
+    )(index_array, hamiltonian, *parts)
     gram = summed(gram)
     return call(
         functools.partial(factor_kernel, rows_total),

time: 56 us -> 58.3 us (1.041)
  starting transfers between devices: 23.1 us -> 24.9 us
  waiting for transfers between devices: 16.4 us -> 17 us
    ppermute x4, starting transfers between devices: 7.31 us -> 1.42 us  [pair_exchange(): return lax.ppermute(value, 'group', route)]
    ppermute x7, starting transfers between devices: 8.01 us -> 12.8 us  [from_partner(): lax.ppermute(value, axis, [(index, index ^ flip) for index in range(count)])]
    ppermute x6, starting transfers between devices: 7.73 us -> 10.7 us  [cycle_exchange(): return lax.ppermute(value, ('group', 'blk'), route)]
    ppermute x7, waiting for transfers between devices: 6.72 us -> 9.04 us  [from_partner(): lax.ppermute(value, axis, [(index, index ^ flip) for index in range(count)])]
    ppermute x6, waiting for transfers between devices: 9.65 us -> 7.9 us  [cycle_exchange(): return lax.ppermute(value, ('group', 'blk'), route)]
  transfers between devices with their start and end apart: 17 -> 17, of which waited for: 9 -> 10; matrix products, arithmetic and copies ran while one was open for 2% -> 2% of each run, Pallas kernels for 9% -> 8%
where the time goes in v10:
time: 58.3 us; the launch traced here: 58.1 us
  starting transfers between devices  24.9 us (43%)
  waiting for transfers between devices  17 us (29%)
  Pallas kernels  11.1 us (19%)
  local copies, waits for them, and re-layouts  2.92 us (5%)
  other arithmetic  1.46 us (3%)
  between operations  0.77 us (1%)
    ppermute x7, starting transfers between devices, from_partner(): lax.ppermute(value, axis, [(index, index ^ flip) for index in range(count)])  12.8 us
    ppermute x6, starting transfers between devices, cycle_exchange(): return lax.ppermute(value, ('group', 'blk'), route)  10.7 us
    ppermute x7, waiting for transfers between devices, from_partner(): lax.ppermute(value, axis, [(index, index ^ flip) for index in range(count)])  9.04 us
    ppermute x6, waiting for transfers between devices, cycle_exchange(): return lax.ppermute(value, ('group', 'blk'), route)  7.9 us
    pallas_call x1, Pallas kernels, on_device(): call(functools.partial(factor_kernel, rows_total), (flat, square), [vmem,...  4.27 us
    unnamed x7, local copies, waits for them, and re-layouts  2.72 us
    pallas_call x2, Pallas kernels, coupled(): call(functools.partial(middle_kernel, middle), flat, [smem] + [vmem] * (2...  2.53 us
    pallas_call x2, Pallas kernels, own_part(): call(own_kernel, flat, [smem] + [vmem] * (2 + len(terms)))  1.86 us
  transfers between devices with their start and end apart: 17, of which 10 were waited for; matrix products, arithmetic and copies ran while one was open for 2% of the time, Pallas kernels for 8%

profile of v10, /device:TPU:0, one launch (start us, length us, event | category | flops | bytes accessed | tf_op | source)
XLA Modules:
  0.0 58.1 jit_solution(4429092442007658509)
XLA Ops:
  0.6 1.4 %broadcast_multiply_fusion = (f32[1024,128]{1,0:T(8,128)S(1)}, bf16[1024,128]{1,0:T(8,128)(2,1)S(1)}) fusion(f32[1024,128]{1,0:T(8,128)} %refs_2_.1, f32[1024]{0:T(1024)} %param.6), kind=kLoop, calls=%fused_computation | loop fusion | flops 262144 | bytes 1314816 | tf_op jit(solution)/shard_map/mul | solution.py:358
  2.1 3.0 %collective-permute-start = (bf16[16,64,128]{2,1,0:T(8,128)(2,1)S(1)}, bf16[16,64,128]{2,1,0:T(8,128)(2,1)S(1)}, u32[]{:S(2)}, u32[]{:S(2)}) collective-permute-start(bf16[16,64,128]{2,1,0:T(8,128)(2,1)S(1)} %bitcast.8), channel_id=1, source_target_pairs={{0,1},{1,0},{2,3},{3,2},{4,6},{5,7},{6,4},{7,5},{8,9},{9,8},{10,11... | collective-permute-start | bytes 786440 | tf_op jit(solution)/shard_map/ppermute | solution.py:43
  5.1 0.7 %collective-permute-start.2 = (bf16[16,64,128]{2,1,0:T(8,128)(2,1)S(1)}, bf16[16,64,128]{2,1,0:T(8,128)(2,1)S(1)}, u32[]{:S(2)}, u32[]{:S(2)}) collective-permute-start(bf16[16,64,128]{2,1,0:T(8,128)(2,1)S(1)} %bitcast.9), channel_id=1, source_target_pairs={{4,8},{8,4},{12,16},{16,12},{20,24},{24,20},{5,9},{9,5},{13,17},{1... | collective-permute-start | bytes 786440 | tf_op jit(solution)/shard_map/ppermute | solution.py:25
  5.7 1.6 %collective-permute-start.1 = (bf16[16,64,128]{2,1,0:T(8,128)(2,1)S(1)}, bf16[16,64,128]{2,1,0:T(8,128)(2,1)S(1)}, u32[]{:S(2)}, u32[]{:S(2)}) collective-permute-start(bf16[16,64,128]{2,1,0:T(8,128)(2,1)S(1)} %bitcast.10), channel_id=1, source_target_pairs={{0,2},{1,3},{2,0},{3,1},{4,5},{5,4},{6,7},{7,6},{8,10},{9,11},{10,... | collective-permute-start | bytes 786440 | tf_op jit(solution)/shard_map/ppermute | solution.py:43
  7.3 2.1 %collective-permute-done.refs_0_ = bf16[16,64,128]{2,1,0:T(8,128)(2,1)S(1)} collective-permute-done((bf16[16,64,128]{2,1,0:T(8,128)(2,1)S(1)}, bf16[16,64,128]{2,1,0:T(8,128)(2,1)S(1)}, u32[]{:S(2)}, u32[]{:S(2)}) %collective-permute-start) | collective-permute-done | bytes 262176 | tf_op jit(solution)/shard_map/ppermute | solution.py:43
  9.4 0.0 collective-permute-start.3
  9.4 2.0 %collective-permute-start.4 = (bf16[16,64,128]{2,1,0:T(8,128)(2,1)S(1)}, bf16[16,64,128]{2,1,0:T(8,128)(2,1)S(1)}, u32[]{:S(2)}, u32[]{:S(2)}) collective-permute-start(bf16[16,64,128]{2,1,0:T(8,128)(2,1)S(1)} %collective-permute-done.refs_0_), channel_id=1, source_target_pairs={{0,2},{1,3},{2,0},{3,1},{4,5},{5,4},{6,7},{7,6},{8,10},{9,11},{10,... | collective-permute-start | bytes 786440 | tf_op jit(solution)/shard_map/ppermute | solution.py:43
  11.5 0.8 %copy.6 = s32[16,6,4]{2,1,0:T(8,128)S(1)} copy(s32[16,6,4]{0,2,1:T(4,128)} %param.5) | data formatting | bytes 3072 | tf_op args[1]
  12.3 0.1 reshape.31
  12.4 0.1 concatenate.3.index_ref
  12.5 0.0 copy-start
  12.5 1.9 %copy-done = bf16[16,6,64,256]{3,2,1,0:T(8,128)(2,1)S(1)} copy-done((bf16[16,6,64,256]{3,2,1,0:T(8,128)(2,1)S(1)}, bf16[16,6,64,256]{3,2,1,0:T(8,128)(2,1)}, u32[]{:S(2)}) %copy-start) | copy-done | bytes 3145752
  14.4 0.9 %shard_map.59.partial_ref = f32[1024,128]{1,0:T(8,128)S(1)} custom-call(s32[390]{0:T(512)S(1)} %concatenate.3.index_ref, bf16[16,6,64,256]{3,2,1,0:T(8,128)(2,1)S(1)} %copy-done, bf16[16,64,128]{2,1,0:T(8,128)(2,1)S(1)} %bitcast.12, f32[1024,128]{1,0:T(8,128)S(1)} %get-tuple-element.20.refs_0_), custom_call_target="tpu_custom_call" | custom-call | tf_op jit(solution)/shard_map/pallas_call | solution.py:334
  15.3 0.0 collective-permute-done.2.refs_2_
  15.3 0.0 collective-permute-done.1.refs_1_
  15.3 1.3 %shard_map.60.partial_ref = f32[1024,128]{1,0:T(8,128)S(1)} custom-call(s32[390]{0:T(512)S(1)} %concatenate.3.index_ref, bf16[16,6,64,256]{3,2,1,0:T(8,128)(2,1)S(1)} %copy-done, f32[1024,128]{1,0:T(8,128)S(1)} %shard_map.59.partial_ref, bf16[16,64,128]{2,1,0:T(8,128)(2,1)S(1)} %collective-permute-done.refs_0_, ...), custom_call_target="tpu_custom_call" | custom-call | tf_op jit(solution)/shard_map/pallas_call | solution.py:353
  16.6 0.0 copy-start.1
  16.6 0.0 copy-start.2
  16.6 0.0 collective-permute-done.3.refs_0_
  16.6 0.0 collective-permute-done.4.refs_1_
  16.6 1.1 %shard_map.61 = (f32[1024,128]{1,0:T(8,128)S(1)}, bf16[16,64,128]{2,1,0:T(8,128)(2,1)S(1)}) custom-call(s32[390]{0:T(512)S(1)} %concatenate.3.index_ref, bf16[16,6,64,256]{3,2,1,0:T(8,128)(2,1)S(1)} %copy-done, f32[1024,128]{1,0:T(8,128)S(1)} %shard_map.60.partial_ref, bf16[16,64,128]{2,1,0:T(8,128)(2,1)S(1)} %collective-permute-done.3.refs_0_, ...), custom_call_target="tpu_custom_call" | custom-call | tf_op jit(solution)/shard_map/pallas_call | solution.py:360
  17.7 1.6 %collective-permute-start.5 = (bf16[16,64,128]{2,1,0:T(8,128)(2,1)S(1)}, bf16[16,64,128]{2,1,0:T(8,128)(2,1)S(1)}, u32[]{:S(2)}, u32[]{:S(2)}) collective-permute-start(bf16[16,64,128]{2,1,0:T(8,128)(2,1)S(1)} %get-tuple-element.17.own_ref), channel_id=1, source_target_pairs={{0,1},{1,0},{2,3},{3,2},{4,6},{5,7},{6,4},{7,5},{8,9},{9,8},{10,11... | collective-permute-start | bytes 786440 | tf_op jit(solution)/shard_map/ppermute | solution.py:43
  19.2 0.7 %collective-permute-start.7 = (bf16[16,64,128]{2,1,0:T(8,128)(2,1)S(1)}, bf16[16,64,128]{2,1,0:T(8,128)(2,1)S(1)}, u32[]{:S(2)}, u32[]{:S(2)}) collective-permute-start(bf16[16,64,128]{2,1,0:T(8,128)(2,1)S(1)} %get-tuple-element.17.own_ref), channel_id=1, source_target_pairs={{4,8},{8,4},{12,16},{16,12},{20,24},{24,20},{5,9},{9,5},{13,17},{1... | collective-permute-start | bytes 786440 | tf_op jit(solution)/shard_map/ppermute | solution.py:25
  19.9 1.3 %collective-permute-start.6 = (bf16[16,64,128]{2,1,0:T(8,128)(2,1)S(1)}, bf16[16,64,128]{2,1,0:T(8,128)(2,1)S(1)}, u32[]{:S(2)}, u32[]{:S(2)}) collective-permute-start(bf16[16,64,128]{2,1,0:T(8,128)(2,1)S(1)} %get-tuple-element.17.own_ref), channel_id=1, source_target_pairs={{0,2},{1,3},{2,0},{3,1},{4,5},{5,4},{6,7},{7,6},{8,10},{9,11},{10,... | collective-permute-start | bytes 786440 | tf_op jit(solution)/shard_map/ppermute | solution.py:43
  21.2 0.0 copy-done.1
  21.2 0.0 copy-done.2
  21.2 1.0 %shard_map.62.partial_ref = f32[1024,128]{1,0:T(8,128)S(1)} custom-call(s32[390]{0:T(512)S(1)} %concatenate.3.index_ref, bf16[16,6,64,256]{3,2,1,0:T(8,128)(2,1)S(1)} %copy-done, bf16[16,64,128]{2,1,0:T(8,128)(2,1)S(1)} %get-tuple-element.17.own_ref, f32[8,128]{1,0:T(8,128)S(1)} %bitcast.13, f32[1024,128]{1,0:T(8,128)S(1)} %get-tuple-element.14.refs_1_, ...), custom_call_target="tpu_custom_call" | custom-call | tf_op jit(solution)/shard_map/pallas_call | solution.py:334
  22.2 1.9 %collective-permute-done.5.refs_0_ = bf16[16,64,128]{2,1,0:T(8,128)(2,1)S(1)} collective-permute-done((bf16[16,64,128]{2,1,0:T(8,128)(2,1)S(1)}, bf16[16,64,128]{2,1,0:T(8,128)(2,1)S(1)}, u32[]{:S(2)}, u32[]{:S(2)}) %collective-permute-start.5) | collective-permute-done | bytes 262176 | tf_op jit(solution)/shard_map/ppermute | solution.py:43
  24.1 0.1 collective-permute-start.8
  24.2 1.2 %collective-permute-start.9 = (bf16[16,64,128]{2,1,0:T(8,128)(2,1)S(1)}, bf16[16,64,128]{2,1,0:T(8,128)(2,1)S(1)}, u32[]{:S(2)}, u32[]{:S(2)}) collective-permute-start(bf16[16,64,128]{2,1,0:T(8,128)(2,1)S(1)} %collective-permute-done.5.refs_0_), channel_id=1, source_target_pairs={{0,2},{1,3},{2,0},{3,1},{4,5},{5,4},{6,7},{7,6},{8,10},{9,11},{10,... | collective-permute-start | bytes 786440 | tf_op jit(solution)/shard_map/ppermute | solution.py:43
  25.4 0.0 collective-permute-done.7.refs_2_
  25.4 0.9 %collective-permute-done.6.refs_1_ = bf16[16,64,128]{2,1,0:T(8,128)(2,1)S(1)} collective-permute-done((bf16[16,64,128]{2,1,0:T(8,128)(2,1)S(1)}, bf16[16,64,128]{2,1,0:T(8,128)(2,1)S(1)}, u32[]{:S(2)}, u32[]{:S(2)}) %collective-permute-start.6) | collective-permute-done | bytes 262176 | tf_op jit(solution)/shard_map/ppermute | solution.py:43
  26.4 1.3 %shard_map.63.partial_ref = f32[1024,128]{1,0:T(8,128)S(1)} custom-call(s32[390]{0:T(512)S(1)} %concatenate.3.index_ref, bf16[16,6,64,256]{3,2,1,0:T(8,128)(2,1)S(1)} %copy-done, f32[1024,128]{1,0:T(8,128)S(1)} %shard_map.62.partial_ref, bf16[16,64,128]{2,1,0:T(8,128)(2,1)S(1)} %collective-permute-done.5.refs_0_, ...), custom_call_target="tpu_custom_call" | custom-call | tf_op jit(solution)/shard_map/pallas_call | solution.py:353
  27.6 0.0 collective-permute-done.8.refs_0_
  27.6 3.0 %collective-permute-done.9.refs_1_ = bf16[16,64,128]{2,1,0:T(8,128)(2,1)S(1)} collective-permute-done((bf16[16,64,128]{2,1,0:T(8,128)(2,1)S(1)}, bf16[16,64,128]{2,1,0:T(8,128)(2,1)S(1)}, u32[]{:S(2)}, u32[]{:S(2)}) %collective-permute-start.9) | collective-permute-done | bytes 262176 | tf_op jit(solution)/shard_map/ppermute | solution.py:43
  30.6 1.4 %shard_map.64 = (f32[1024,128]{1,0:T(8,128)S(1)}, f32[72,128]{1,0:T(8,128)S(1)}) custom-call(s32[390]{0:T(512)S(1)} %concatenate.3.index_ref, bf16[16,6,64,256]{3,2,1,0:T(8,128)(2,1)S(1)} %copy-done, f32[1024,128]{1,0:T(8,128)S(1)} %shard_map.63.partial_ref, bf16[16,64,128]{2,1,0:T(8,128)(2,1)S(1)} %collective-permute-done.8.refs_0_, ...), custom_call_target="tpu_custom_call" | custom-call | tf_op jit(solution)/shard_map/pallas_call | solution.py:364
  32.0 0.4 collective-permute-start.10
  32.4 0.9 %collective-permute-done.10 = f32[72,128]{1,0:T(8,128)S(1)} collective-permute-done((f32[72,128]{1,0:T(8,128)S(1)}, f32[72,128]{1,0:T(8,128)S(1)}, u32[]{:S(2)}, u32[]{:S(2)}) %collective-permute-start.10) | collective-permute-done | bytes 36896 | tf_op jit(solution)/shard_map/ppermute | solution.py:48
  33.3 7.9 %collective-permute-start.13 = (f32[72,128]{1,0:T(8,128)S(1)}, f32[72,128]{1,0:T(8,128)S(1)}, u32[]{:S(2)}, u32[]{:S(2)}) collective-permute-start(f32[72,128]{1,0:T(8,128)S(1)} %add.28), channel_id=1, source_target_pairs={{0,24},{4,28},{8,16},{12,20},{16,8},{20,12},{24,0},{28,4},{1,25},{... | collective-permute-start | bytes 110600 | tf_op jit(solution)/shard_map/ppermute | solution.py:48
  41.2 0.0 collective-permute-start.12
  41.2 0.6 %collective-permute-start.11 = (f32[72,128]{1,0:T(8,128)S(1)}, f32[72,128]{1,0:T(8,128)S(1)}, u32[]{:S(2)}, u32[]{:S(2)}) collective-permute-start(f32[72,128]{1,0:T(8,128)S(1)} %add.28), channel_id=1, source_target_pairs={{0,8},{4,12},{8,0},{12,4},{16,24},{20,28},{24,16},{28,20},{1,9},{5... | collective-permute-start | bytes 110600 | tf_op jit(solution)/shard_map/ppermute | solution.py:48
  41.8 1.6 %collective-permute-done.13 = f32[72,128]{1,0:T(8,128)S(1)} collective-permute-done((f32[72,128]{1,0:T(8,128)S(1)}, f32[72,128]{1,0:T(8,128)S(1)}, u32[]{:S(2)}, u32[]{:S(2)}) %collective-permute-start.13) | collective-permute-done | bytes 36896 | tf_op jit(solution)/shard_map/ppermute | solution.py:48
  43.4 2.7 %collective-permute-done.12 = f32[72,128]{1,0:T(8,128)S(1)} collective-permute-done((f32[72,128]{1,0:T(8,128)S(1)}, f32[72,128]{1,0:T(8,128)S(1)}, u32[]{:S(2)}, u32[]{:S(2)}) %collective-permute-start.12) | collective-permute-done | bytes 36896 | tf_op jit(solution)/shard_map/ppermute | solution.py:48
  46.0 0.0 collective-permute-done.11
  46.0 2.8 %collective-permute-start.16 = (f32[72,128]{1,0:T(8,128)S(1)}, f32[72,128]{1,0:T(8,128)S(1)}, u32[]{:S(2)}, u32[]{:S(2)}) collective-permute-start(f32[72,128]{1,0:T(8,128)S(1)} %add_add_fusion.1), channel_id=1, source_target_pairs={{0,3},{1,2},{2,1},{3,0},{4,7},{5,6},{6,5},{7,4},{8,11},{9,10},{10,... | collective-permute-start | bytes 110600 | tf_op jit(solution)/shard_map/ppermute | solution.py:48
  48.8 1.1 %collective-permute-start.15 = (f32[72,128]{1,0:T(8,128)S(1)}, f32[72,128]{1,0:T(8,128)S(1)}, u32[]{:S(2)}, u32[]{:S(2)}) collective-permute-start(f32[72,128]{1,0:T(8,128)S(1)} %add_add_fusion.1), channel_id=1, source_target_pairs={{0,2},{1,3},{2,0},{3,1},{4,6},{5,7},{6,4},{7,5},{8,10},{9,11},{10,... | collective-permute-start | bytes 110600 | tf_op jit(solution)/shard_map/ppermute | solution.py:48
  49.9 0.0 collective-permute-start.14
  49.9 1.1 %collective-permute-done.16 = f32[72,128]{1,0:T(8,128)S(1)} collective-permute-done((f32[72,128]{1,0:T(8,128)S(1)}, f32[72,128]{1,0:T(8,128)S(1)}, u32[]{:S(2)}, u32[]{:S(2)}) %collective-permute-start.16) | collective-permute-done | bytes 36896 | tf_op jit(solution)/shard_map/ppermute | solution.py:48
  51.0 1.8 %collective-permute-done.15 = f32[72,128]{1,0:T(8,128)S(1)} collective-permute-done((f32[72,128]{1,0:T(8,128)S(1)}, f32[72,128]{1,0:T(8,128)S(1)}, u32[]{:S(2)}, u32[]{:S(2)}) %collective-permute-start.15) | collective-permute-done | bytes 36896 | tf_op jit(solution)/shard_map/ppermute | solution.py:48
  52.8 1.1 %collective-permute-done.14 = f32[72,128]{1,0:T(8,128)S(1)} collective-permute-done((f32[72,128]{1,0:T(8,128)S(1)}, f32[72,128]{1,0:T(8,128)S(1)}, u32[]{:S(2)}, u32[]{:S(2)}) %collective-permute-start.14) | collective-permute-done | bytes 36896 | tf_op jit(solution)/shard_map/ppermute | solution.py:48
  53.8 4.3 %shard_map.65 = (f32[1024,128]{1,0:T(8,128)}, f32[128,128]{1,0:T(8,128)}) custom-call(f32[72,128]{1,0:T(8,128)S(1)} %add_add_fusion.packed_ref, f32[1024,128]{1,0:T(8,128)S(1)} %get-tuple-element.19.filtered_ref), custom_call_target="tpu_custom_call" | custom-call | tf_op jit(solution)/shard_map/pallas_call | solution.py:368
  (3 shorter events, 0.0 us)
Async XLA Ops:
  2.1 7.4 %collective-permute-start = (bf16[16,64,128]{2,1,0:T(8,128)(2,1)S(1)}, bf16[16,64,128]{2,1,0:T(8,128)(2,1)S(1)}, u32[]{:S(2)}, u32[]{:S(2)}) collective-permute-start(bf16[16,64,128]{2,1,0:T(8,128)(2,1)S(1)} %bitcast.8), channel_id=1, source_target_pairs={{0,1},{1,0},{2,3},{3,2},{4,6},{5,7},{6,4},{7,5},{8,9},{9,8},{10,11... | collective-permute-start | bytes 786440 | tf_op jit(solution)/shard_map/ppermute | solution.py:43
  5.1 10.2 %collective-permute-start.2 = (bf16[16,64,128]{2,1,0:T(8,128)(2,1)S(1)}, bf16[16,64,128]{2,1,0:T(8,128)(2,1)S(1)}, u32[]{:S(2)}, u32[]{:S(2)}) collective-permute-start(bf16[16,64,128]{2,1,0:T(8,128)(2,1)S(1)} %bitcast.9), channel_id=1, source_target_pairs={{4,8},{8,4},{12,16},{16,12},{20,24},{24,20},{5,9},{9,5},{13,17},{1... | collective-permute-start | bytes 786440 | tf_op jit(solution)/shard_map/ppermute | solution.py:25
  5.7 9.6 %collective-permute-start.1 = (bf16[16,64,128]{2,1,0:T(8,128)(2,1)S(1)}, bf16[16,64,128]{2,1,0:T(8,128)(2,1)S(1)}, u32[]{:S(2)}, u32[]{:S(2)}) collective-permute-start(bf16[16,64,128]{2,1,0:T(8,128)(2,1)S(1)} %bitcast.10), channel_id=1, source_target_pairs={{0,2},{1,3},{2,0},{3,1},{4,5},{5,4},{6,7},{7,6},{8,10},{9,11},{10,... | collective-permute-start | bytes 786440 | tf_op jit(solution)/shard_map/ppermute | solution.py:43
  9.4 7.2 %collective-permute-start.3 = (bf16[16,64,128]{2,1,0:T(8,128)(2,1)S(1)}, bf16[16,64,128]{2,1,0:T(8,128)(2,1)S(1)}, u32[]{:S(2)}, u32[]{:S(2)}) collective-permute-start(bf16[16,64,128]{2,1,0:T(8,128)(2,1)S(1)} %bitcast.11), channel_id=1, source_target_pairs={{0,4},{4,0},{8,12},{12,8},{16,20},{20,16},{24,28},{28,24},{1,5},{5... | collective-permute-start | bytes 786440 | tf_op jit(solution)/shard_map/ppermute | solution.py:25
  9.4 7.2 %collective-permute-start.4 = (bf16[16,64,128]{2,1,0:T(8,128)(2,1)S(1)}, bf16[16,64,128]{2,1,0:T(8,128)(2,1)S(1)}, u32[]{:S(2)}, u32[]{:S(2)}) collective-permute-start(bf16[16,64,128]{2,1,0:T(8,128)(2,1)S(1)} %collective-permute-done.refs_0_), channel_id=1, source_target_pairs={{0,2},{1,3},{2,0},{3,1},{4,5},{5,4},{6,7},{7,6},{8,10},{9,11},{10,... | collective-permute-start | bytes 786440 | tf_op jit(solution)/shard_map/ppermute | solution.py:43
  12.5 1.9 %copy-start = (bf16[16,6,64,256]{3,2,1,0:T(8,128)(2,1)S(1)}, bf16[16,6,64,256]{3,2,1,0:T(8,128)(2,1)}, u32[]{:S(2)}) copy-start(bf16[16,6,64,256]{3,2,1,0:T(8,128)(2,1)} %hamiltonian_ref.11) | copy-start | bytes 9437188
  16.6 4.6 %copy-start.1 = (f32[1024,128]{1,0:T(8,128)S(1)}, f32[1024,128]{1,0:T(8,128)}, u32[]{:S(2)}) copy-start(f32[1024,128]{1,0:T(8,128)} %refs_2_.1) | copy-start | bytes 1572868
  16.6 4.6 %copy-start.2 = (f32[1024]{0:T(1024)S(1)}, f32[1024]{0:T(1024)}, u32[]{:S(2)}) copy-start(f32[1024]{0:T(1024)} %param.6) | copy-start | bytes 12292
  17.7 6.4 %collective-permute-start.5 = (bf16[16,64,128]{2,1,0:T(8,128)(2,1)S(1)}, bf16[16,64,128]{2,1,0:T(8,128)(2,1)S(1)}, u32[]{:S(2)}, u32[]{:S(2)}) collective-permute-start(bf16[16,64,128]{2,1,0:T(8,128)(2,1)S(1)} %get-tuple-element.17.own_ref), channel_id=1, source_target_pairs={{0,1},{1,0},{2,3},{3,2},{4,6},{5,7},{6,4},{7,5},{8,9},{9,8},{10,11... | collective-permute-start | bytes 786440 | tf_op jit(solution)/shard_map/ppermute | solution.py:43
  19.2 6.2 %collective-permute-start.7 = (bf16[16,64,128]{2,1,0:T(8,128)(2,1)S(1)}, bf16[16,64,128]{2,1,0:T(8,128)(2,1)S(1)}, u32[]{:S(2)}, u32[]{:S(2)}) collective-permute-start(bf16[16,64,128]{2,1,0:T(8,128)(2,1)S(1)} %get-tuple-element.17.own_ref), channel_id=1, source_target_pairs={{4,8},{8,4},{12,16},{16,12},{20,24},{24,20},{5,9},{9,5},{13,17},{1... | collective-permute-start | bytes 786440 | tf_op jit(solution)/shard_map/ppermute | solution.py:25
  19.9 6.4 %collective-permute-start.6 = (bf16[16,64,128]{2,1,0:T(8,128)(2,1)S(1)}, bf16[16,64,128]{2,1,0:T(8,128)(2,1)S(1)}, u32[]{:S(2)}, u32[]{:S(2)}) collective-permute-start(bf16[16,64,128]{2,1,0:T(8,128)(2,1)S(1)} %get-tuple-element.17.own_ref), channel_id=1, source_target_pairs={{0,2},{1,3},{2,0},{3,1},{4,5},{5,4},{6,7},{7,6},{8,10},{9,11},{10,... | collective-permute-start | bytes 786440 | tf_op jit(solution)/shard_map/ppermute | solution.py:43
  24.1 3.5 %collective-permute-start.8 = (bf16[16,64,128]{2,1,0:T(8,128)(2,1)S(1)}, bf16[16,64,128]{2,1,0:T(8,128)(2,1)S(1)}, u32[]{:S(2)}, u32[]{:S(2)}) collective-permute-start(bf16[16,64,128]{2,1,0:T(8,128)(2,1)S(1)} %get-tuple-element.17.own_ref), channel_id=1, source_target_pairs={{0,4},{4,0},{8,12},{12,8},{16,20},{20,16},{24,28},{28,24},{1,5},{5... | collective-permute-start | bytes 786440 | tf_op jit(solution)/shard_map/ppermute | solution.py:25
  24.2 6.4 %collective-permute-start.9 = (bf16[16,64,128]{2,1,0:T(8,128)(2,1)S(1)}, bf16[16,64,128]{2,1,0:T(8,128)(2,1)S(1)}, u32[]{:S(2)}, u32[]{:S(2)}) collective-permute-start(bf16[16,64,128]{2,1,0:T(8,128)(2,1)S(1)} %collective-permute-done.5.refs_0_), channel_id=1, source_target_pairs={{0,2},{1,3},{2,0},{3,1},{4,5},{5,4},{6,7},{7,6},{8,10},{9,11},{10,... | collective-permute-start | bytes 786440 | tf_op jit(solution)/shard_map/ppermute | solution.py:43
  32.0 1.3 %collective-permute-start.10 = (f32[72,128]{1,0:T(8,128)S(1)}, f32[72,128]{1,0:T(8,128)S(1)}, u32[]{:S(2)}, u32[]{:S(2)}) collective-permute-start(f32[72,128]{1,0:T(8,128)S(1)} %get-tuple-element.18), channel_id=1, source_target_pairs={{0,4},{4,0},{8,12},{12,8},{16,20},{20,16},{24,28},{28,24},{1,5},{5... | collective-permute-start | bytes 110600 | tf_op jit(solution)/shard_map/ppermute | solution.py:48
  33.3 10.1 %collective-permute-start.13 = (f32[72,128]{1,0:T(8,128)S(1)}, f32[72,128]{1,0:T(8,128)S(1)}, u32[]{:S(2)}, u32[]{:S(2)}) collective-permute-start(f32[72,128]{1,0:T(8,128)S(1)} %add.28), channel_id=1, source_target_pairs={{0,24},{4,28},{8,16},{12,20},{16,8},{20,12},{24,0},{28,4},{1,25},{... | collective-permute-start | bytes 110600 | tf_op jit(solution)/shard_map/ppermute | solution.py:48
  41.2 4.9 %collective-permute-start.12 = (f32[72,128]{1,0:T(8,128)S(1)}, f32[72,128]{1,0:T(8,128)S(1)}, u32[]{:S(2)}, u32[]{:S(2)}) collective-permute-start(f32[72,128]{1,0:T(8,128)S(1)} %add.28), channel_id=1, source_target_pairs={{0,16},{4,20},{8,24},{12,28},{16,0},{20,4},{24,8},{28,12},{1,17},{... | collective-permute-start | bytes 110600 | tf_op jit(solution)/shard_map/ppermute | solution.py:48
  41.2 4.9 %collective-permute-start.11 = (f32[72,128]{1,0:T(8,128)S(1)}, f32[72,128]{1,0:T(8,128)S(1)}, u32[]{:S(2)}, u32[]{:S(2)}) collective-permute-start(f32[72,128]{1,0:T(8,128)S(1)} %add.28), channel_id=1, source_target_pairs={{0,8},{4,12},{8,0},{12,4},{16,24},{20,28},{24,16},{28,20},{1,9},{5... | collective-permute-start | bytes 110600 | tf_op jit(solution)/shard_map/ppermute | solution.py:48
  46.0 4.9 %collective-permute-start.16 = (f32[72,128]{1,0:T(8,128)S(1)}, f32[72,128]{1,0:T(8,128)S(1)}, u32[]{:S(2)}, u32[]{:S(2)}) collective-permute-start(f32[72,128]{1,0:T(8,128)S(1)} %add_add_fusion.1), channel_id=1, source_target_pairs={{0,3},{1,2},{2,1},{3,0},{4,7},{5,6},{6,5},{7,4},{8,11},{9,10},{10,... | collective-permute-start | bytes 110600 | tf_op jit(solution)/shard_map/ppermute | solution.py:48
  48.8 4.0 %collective-permute-start.15 = (f32[72,128]{1,0:T(8,128)S(1)}, f32[72,128]{1,0:T(8,128)S(1)}, u32[]{:S(2)}, u32[]{:S(2)}) collective-permute-start(f32[72,128]{1,0:T(8,128)S(1)} %add_add_fusion.1), channel_id=1, source_target_pairs={{0,2},{1,3},{2,0},{3,1},{4,6},{5,7},{6,4},{7,5},{8,10},{9,11},{10,... | collective-permute-start | bytes 110600 | tf_op jit(solution)/shard_map/ppermute | solution.py:48
  49.9 4.0 %collective-permute-start.14 = (f32[72,128]{1,0:T(8,128)S(1)}, f32[72,128]{1,0:T(8,128)S(1)}, u32[]{:S(2)}, u32[]{:S(2)}) collective-permute-start(f32[72,128]{1,0:T(8,128)S(1)} %add_add_fusion.1), channel_id=1, source_target_pairs={{0,1},{1,0},{2,3},{3,2},{4,5},{5,4},{6,7},{7,6},{8,9},{9,8},{10,11... | collective-permute-start | bytes 110600 | tf_op jit(solution)/shard_map/ppermute | solution.py:48

commit v11 on v10

--- a/solution.py
+++ b/solution.py
@@ -330,37 +330,38 @@
     packed = jax.ShapeDtypeStruct((states // 2 + SUB, states), jnp.float32)
     square = jax.ShapeDtypeStruct((states, states), jnp.float32)
 
-    def own_part(value, *terms):
+    def own_part(index_array, value, *terms):
         return call(own_kernel, flat, [smem] + [vmem] * (2 + len(terms)))(
             index_array, hamiltonian, value, *terms
         )
 
-    def coupled(value, early, *terms):
+    def coupled(value, index_array, early, *terms):
         arrived = cycle_exchange(value, 0)
         outer = pair_exchange(value, 1)
-        others = [cycle_exchange(value, level) for level in range(1, levels)]
         if early:
-            partial = own_part(value, *terms)
-            arrived, again, partial = lax.optimization_barrier((arrived, value, partial))
+            partial = own_part(index_array, value, *terms)
+            later, partial = lax.optimization_barrier((value, partial))
         else:
-            arrived, again = lax.optimization_barrier((arrived, value))
+            later, index_array = lax.optimization_barrier((value, index_array))
+        others = [cycle_exchange(later, level) for level in range(1, levels)]
+        arrived, later = lax.optimization_barrier((arrived, later))
         pieces = [value, arrived]
         for level, other in zip(range(1, levels), others):
             pieces += [other] + [cycle_exchange(piece, level) for piece in pieces[1:]]
-        pieces += [pair_exchange(again, 0), outer]
+        pieces += [pair_exchange(later, 0), outer]
         if not early:
-            partial = own_part(value, *terms)
+            partial = own_part(index_array, value, *terms)
         partial = call(
             functools.partial(middle_kernel, middle), flat, [smem] + [vmem] * (2 + len(middle)),
         )(index_array, hamiltonian, partial, *[pieces[number] for number in middle])
         return [partial] + [pieces[number] for number in ending]
 
     weighted = (weights.reshape(-1, 1) * trial_slab)
-    parts = coupled(trial_slab.reshape(rounded.shape).astype(jnp.bfloat16), False, weighted)
+    parts = coupled(trial_slab.reshape(rounded.shape).astype(jnp.bfloat16), index_array, False, weighted)
     once, once_round = call(
         functools.partial(first_kernel, ending), (flat, rounded), [smem] + [vmem] * 4
     )(index_array, hamiltonian, *parts)
-    parts = coupled(once_round, True, weights, once, trial_slab)
+    parts = coupled(once_round, index_array, True, weights, once, trial_slab)
     filtered, gram = call(
         functools.partial(second_kernel, ending), (flat, packed), [smem] + [vmem] * 4
     )(index_array, hamiltonian, *parts)

time: 58.3 us -> 56.8 us (0.974)
  waiting for transfers between devices: 17 us -> 15.5 us
    ppermute x7, starting transfers between devices: 12.8 us -> 11.4 us  [from_partner(): lax.ppermute(value, axis, [(index, index ^ flip) for index in range(count)])]
    ppermute x4, starting transfers between devices: 1.42 us -> 2.79 us  [pair_exchange(): return lax.ppermute(value, 'group', route)]
    ppermute x6, waiting for transfers between devices: 7.9 us -> 7.04 us  [cycle_exchange(): return lax.ppermute(value, ('group', 'blk'), route)]
    ppermute x7, waiting for transfers between devices: 9.04 us -> 8.4 us  [from_partner(): lax.ppermute(value, axis, [(index, index ^ flip) for index in range(count)])]
where the time goes in v11:
time: 56.8 us; the launch traced here: 56.6 us
  starting transfers between devices  24.9 us (44%)
  waiting for transfers between devices  15.5 us (27%)
  Pallas kernels  11.1 us (20%)
  local copies, waits for them, and re-layouts  2.92 us (5%)
  other arithmetic  1.46 us (3%)
  between operations  0.8 us (1%)
    ppermute x7, starting transfers between devices, from_partner(): lax.ppermute(value, axis, [(index, index ^ flip) for index in range(count)])  11.4 us
    ppermute x6, starting transfers between devices, cycle_exchange(): return lax.ppermute(value, ('group', 'blk'), route)  10.7 us
    ppermute x7, waiting for transfers between devices, from_partner(): lax.ppermute(value, axis, [(index, index ^ flip) for index in range(count)])  8.4 us
    ppermute x6, waiting for transfers between devices, cycle_exchange(): return lax.ppermute(value, ('group', 'blk'), route)  7.04 us
    pallas_call x1, Pallas kernels, on_device(): call(functools.partial(factor_kernel, rows_total), (flat, square), [vmem,...  4.27 us
    ppermute x4, starting transfers between devices, pair_exchange(): return lax.ppermute(value, 'group', route)  2.79 us
    unnamed x7, local copies, waits for them, and re-layouts  2.72 us
    pallas_call x2, Pallas kernels, coupled(): call(functools.partial(middle_kernel, middle), flat, [smem] + [vmem] * (2...  2.54 us
  transfers between devices with their start and end apart: 17, of which 10 were waited for; matrix products, arithmetic and copies ran while one was open for 2% of the time, Pallas kernels for 8%

profile of v11, /device:TPU:0, one launch (start us, length us, event | category | flops | bytes accessed | tf_op | source)
XLA Modules:
  0.0 56.6 jit_solution(14990791634680986075)
XLA Ops:
  0.6 1.4 %broadcast_multiply_fusion = (f32[1024,128]{1,0:T(8,128)S(1)}, bf16[1024,128]{1,0:T(8,128)(2,1)S(1)}) fusion(f32[1024,128]{1,0:T(8,128)} %refs_2_.1, f32[1024]{0:T(1024)} %param.6), kind=kLoop, calls=%fused_computation | loop fusion | flops 262144 | bytes 1314816 | tf_op jit(solution)/shard_map/mul | solution.py:359
  2.1 3.0 %collective-permute-start = (bf16[16,64,128]{2,1,0:T(8,128)(2,1)S(1)}, bf16[16,64,128]{2,1,0:T(8,128)(2,1)S(1)}, u32[]{:S(2)}, u32[]{:S(2)}) collective-permute-start(bf16[16,64,128]{2,1,0:T(8,128)(2,1)S(1)} %bitcast.8), channel_id=1, source_target_pairs={{0,1},{1,0},{2,3},{3,2},{4,6},{5,7},{6,4},{7,5},{8,9},{9,8},{10,11... | collective-permute-start | bytes 786440 | tf_op jit(solution)/shard_map/ppermute | solution.py:43
  5.1 0.7 %collective-permute-start.2 = (bf16[16,64,128]{2,1,0:T(8,128)(2,1)S(1)}, bf16[16,64,128]{2,1,0:T(8,128)(2,1)S(1)}, u32[]{:S(2)}, u32[]{:S(2)}) collective-permute-start(bf16[16,64,128]{2,1,0:T(8,128)(2,1)S(1)} %bitcast.9), channel_id=1, source_target_pairs={{4,8},{8,4},{12,16},{16,12},{20,24},{24,20},{5,9},{9,5},{13,17},{1... | collective-permute-start | bytes 786440 | tf_op jit(solution)/shard_map/ppermute | solution.py:25
  5.8 0.8 %copy.6 = s32[16,6,4]{2,1,0:T(8,128)S(1)} copy(s32[16,6,4]{0,2,1:T(4,128)} %param.5) | data formatting | bytes 3072 | tf_op args[1]
  6.6 0.1 reshape.31
  6.7 0.1 concatenate.3.index_ref
  6.8 1.5 %collective-permute-start.1 = (bf16[16,64,128]{2,1,0:T(8,128)(2,1)S(1)}, bf16[16,64,128]{2,1,0:T(8,128)(2,1)S(1)}, u32[]{:S(2)}, u32[]{:S(2)}) collective-permute-start(bf16[16,64,128]{2,1,0:T(8,128)(2,1)S(1)} %bitcast.10), channel_id=1, source_target_pairs={{0,2},{1,3},{2,0},{3,1},{4,5},{5,4},{6,7},{7,6},{8,10},{9,11},{10,... | collective-permute-start | bytes 786440 | tf_op jit(solution)/shard_map/ppermute | solution.py:43
  8.3 1.1 %collective-permute-done.refs_0_ = bf16[16,64,128]{2,1,0:T(8,128)(2,1)S(1)} collective-permute-done((bf16[16,64,128]{2,1,0:T(8,128)(2,1)S(1)}, bf16[16,64,128]{2,1,0:T(8,128)(2,1)S(1)}, u32[]{:S(2)}, u32[]{:S(2)}) %collective-permute-start) | collective-permute-done | bytes 262176 | tf_op jit(solution)/shard_map/ppermute | solution.py:43
  9.4 0.6 collective-permute-start.3
  10.0 1.5 %collective-permute-start.4 = (bf16[16,64,128]{2,1,0:T(8,128)(2,1)S(1)}, bf16[16,64,128]{2,1,0:T(8,128)(2,1)S(1)}, u32[]{:S(2)}, u32[]{:S(2)}) collective-permute-start(bf16[16,64,128]{2,1,0:T(8,128)(2,1)S(1)} %collective-permute-done.refs_0_), channel_id=1, source_target_pairs={{0,2},{1,3},{2,0},{3,1},{4,5},{5,4},{6,7},{7,6},{8,10},{9,11},{10,... | collective-permute-start | bytes 786440 | tf_op jit(solution)/shard_map/ppermute | solution.py:43
  11.5 0.0 copy-start
  11.5 1.9 %copy-done = bf16[16,6,64,256]{3,2,1,0:T(8,128)(2,1)S(1)} copy-done((bf16[16,6,64,256]{3,2,1,0:T(8,128)(2,1)S(1)}, bf16[16,6,64,256]{3,2,1,0:T(8,128)(2,1)}, u32[]{:S(2)}) %copy-start) | copy-done | bytes 3145752
  13.4 0.9 %shard_map.59.partial_ref = f32[1024,128]{1,0:T(8,128)S(1)} custom-call(s32[390]{0:T(512)S(1)} %concatenate.3.index_ref, bf16[16,6,64,256]{3,2,1,0:T(8,128)(2,1)S(1)} %copy-done, bf16[16,64,128]{2,1,0:T(8,128)(2,1)S(1)} %bitcast.12, f32[1024,128]{1,0:T(8,128)S(1)} %get-tuple-element.26.refs_0_), custom_call_target="tpu_custom_call" | custom-call | tf_op jit(solution)/shard_map/pallas_call | solution.py:334
  14.3 0.0 collective-permute-done.1.refs_1_
  14.3 0.0 collective-permute-done.2.refs_2_
  14.3 1.3 %shard_map.60.partial_ref = f32[1024,128]{1,0:T(8,128)S(1)} custom-call(s32[390]{0:T(512)S(1)} %concatenate.3.index_ref, bf16[16,6,64,256]{3,2,1,0:T(8,128)(2,1)S(1)} %copy-done, f32[1024,128]{1,0:T(8,128)S(1)} %shard_map.59.partial_ref, bf16[16,64,128]{2,1,0:T(8,128)(2,1)S(1)} %collective-permute-done.refs_0_, ...), custom_call_target="tpu_custom_call" | custom-call | tf_op jit(solution)/shard_map/pallas_call | solution.py:354
  15.6 0.0 copy-start.1
  15.6 0.0 copy-start.2
  15.6 0.0 collective-permute-done.3.refs_0_
  15.6 0.7 %collective-permute-done.4.refs_1_ = bf16[16,64,128]{2,1,0:T(8,128)(2,1)S(1)} collective-permute-done((bf16[16,64,128]{2,1,0:T(8,128)(2,1)S(1)}, bf16[16,64,128]{2,1,0:T(8,128)(2,1)S(1)}, u32[]{:S(2)}, u32[]{:S(2)}) %collective-permute-start.4) | collective-permute-done | bytes 262176 | tf_op jit(solution)/shard_map/ppermute | solution.py:43
  16.3 1.1 %shard_map.61 = (f32[1024,128]{1,0:T(8,128)S(1)}, bf16[16,64,128]{2,1,0:T(8,128)(2,1)S(1)}) custom-call(s32[390]{0:T(512)S(1)} %concatenate.3.index_ref, bf16[16,6,64,256]{3,2,1,0:T(8,128)(2,1)S(1)} %copy-done, f32[1024,128]{1,0:T(8,128)S(1)} %shard_map.60.partial_ref, bf16[16,64,128]{2,1,0:T(8,128)(2,1)S(1)} %collective-permute-done.3.refs_0_, ...), custom_call_target="tpu_custom_call" | custom-call | tf_op jit(solution)/shard_map/pallas_call | solution.py:361
  17.4 1.6 %collective-permute-start.5 = (bf16[16,64,128]{2,1,0:T(8,128)(2,1)S(1)}, bf16[16,64,128]{2,1,0:T(8,128)(2,1)S(1)}, u32[]{:S(2)}, u32[]{:S(2)}) collective-permute-start(bf16[16,64,128]{2,1,0:T(8,128)(2,1)S(1)} %get-tuple-element.23.own_ref), channel_id=1, source_target_pairs={{0,1},{1,0},{2,3},{3,2},{4,6},{5,7},{6,4},{7,5},{8,9},{9,8},{10,11... | collective-permute-start | bytes 786440 | tf_op jit(solution)/shard_map/ppermute | solution.py:43
  19.0 0.7 %collective-permute-start.7 = (bf16[16,64,128]{2,1,0:T(8,128)(2,1)S(1)}, bf16[16,64,128]{2,1,0:T(8,128)(2,1)S(1)}, u32[]{:S(2)}, u32[]{:S(2)}) collective-permute-start(bf16[16,64,128]{2,1,0:T(8,128)(2,1)S(1)} %get-tuple-element.23.own_ref), channel_id=1, source_target_pairs={{4,8},{8,4},{12,16},{16,12},{20,24},{24,20},{5,9},{9,5},{13,17},{1... | collective-permute-start | bytes 786440 | tf_op jit(solution)/shard_map/ppermute | solution.py:25
  19.6 0.0 copy-done.1
  19.6 0.0 copy-done.2
  19.7 1.0 %shard_map.62.partial_ref = f32[1024,128]{1,0:T(8,128)S(1)} custom-call(s32[390]{0:T(512)S(1)} %concatenate.3.index_ref, bf16[16,6,64,256]{3,2,1,0:T(8,128)(2,1)S(1)} %copy-done, bf16[16,64,128]{2,1,0:T(8,128)(2,1)S(1)} %get-tuple-element.23.own_ref, f32[8,128]{1,0:T(8,128)S(1)} %bitcast.13, f32[1024,128]{1,0:T(8,128)S(1)} %get-tuple-element.19.refs_1_, ...), custom_call_target="tpu_custom_call" | custom-call | tf_op jit(solution)/shard_map/pallas_call | solution.py:334
  20.6 1.6 %collective-permute-start.6 = (bf16[16,64,128]{2,1,0:T(8,128)(2,1)S(1)}, bf16[16,64,128]{2,1,0:T(8,128)(2,1)S(1)}, u32[]{:S(2)}, u32[]{:S(2)}) collective-permute-start(bf16[16,64,128]{2,1,0:T(8,128)(2,1)S(1)} %get-tuple-element.23.own_ref), channel_id=1, source_target_pairs={{0,2},{1,3},{2,0},{3,1},{4,5},{5,4},{6,7},{7,6},{8,10},{9,11},{10,... | collective-permute-start | bytes 786440 | tf_op jit(solution)/shard_map/ppermute | solution.py:43
  22.2 1.6 %collective-permute-done.5.refs_0_ = bf16[16,64,128]{2,1,0:T(8,128)(2,1)S(1)} collective-permute-done((bf16[16,64,128]{2,1,0:T(8,128)(2,1)S(1)}, bf16[16,64,128]{2,1,0:T(8,128)(2,1)S(1)}, u32[]{:S(2)}, u32[]{:S(2)}) %collective-permute-start.5) | collective-permute-done | bytes 262176 | tf_op jit(solution)/shard_map/ppermute | solution.py:43
  23.8 0.9 %collective-permute-start.8 = (bf16[16,64,128]{2,1,0:T(8,128)(2,1)S(1)}, bf16[16,64,128]{2,1,0:T(8,128)(2,1)S(1)}, u32[]{:S(2)}, u32[]{:S(2)}) collective-permute-start(bf16[16,64,128]{2,1,0:T(8,128)(2,1)S(1)} %get-tuple-element.23.own_ref), channel_id=1, source_target_pairs={{0,4},{4,0},{8,12},{12,8},{16,20},{20,16},{24,28},{28,24},{1,5},{5... | collective-permute-start | bytes 786440 | tf_op jit(solution)/shard_map/ppermute | solution.py:25
  24.8 1.5 %collective-permute-start.9 = (bf16[16,64,128]{2,1,0:T(8,128)(2,1)S(1)}, bf16[16,64,128]{2,1,0:T(8,128)(2,1)S(1)}, u32[]{:S(2)}, u32[]{:S(2)}) collective-permute-start(bf16[16,64,128]{2,1,0:T(8,128)(2,1)S(1)} %collective-permute-done.5.refs_0_), channel_id=1, source_target_pairs={{0,2},{1,3},{2,0},{3,1},{4,5},{5,4},{6,7},{7,6},{8,10},{9,11},{10,... | collective-permute-start | bytes 786440 | tf_op jit(solution)/shard_map/ppermute | solution.py:43
  26.3 0.8 %collective-permute-done.6.refs_1_ = bf16[16,64,128]{2,1,0:T(8,128)(2,1)S(1)} collective-permute-done((bf16[16,64,128]{2,1,0:T(8,128)(2,1)S(1)}, bf16[16,64,128]{2,1,0:T(8,128)(2,1)S(1)}, u32[]{:S(2)}, u32[]{:S(2)}) %collective-permute-start.6) | collective-permute-done | bytes 262176 | tf_op jit(solution)/shard_map/ppermute | solution.py:43
  27.1 0.0 collective-permute-done.7.refs_2_
  27.1 1.3 %shard_map.63.partial_ref = f32[1024,128]{1,0:T(8,128)S(1)} custom-call(s32[390]{0:T(512)S(1)} %concatenate.3.index_ref, bf16[16,6,64,256]{3,2,1,0:T(8,128)(2,1)S(1)} %copy-done, f32[1024,128]{1,0:T(8,128)S(1)} %shard_map.62.partial_ref, bf16[16,64,128]{2,1,0:T(8,128)(2,1)S(1)} %collective-permute-done.5.refs_0_, ...), custom_call_target="tpu_custom_call" | custom-call | tf_op jit(solution)/shard_map/pallas_call | solution.py:354
  28.4 0.0 collective-permute-done.8.refs_0_
  28.4 2.8 %collective-permute-done.9.refs_1_ = bf16[16,64,128]{2,1,0:T(8,128)(2,1)S(1)} collective-permute-done((bf16[16,64,128]{2,1,0:T(8,128)(2,1)S(1)}, bf16[16,64,128]{2,1,0:T(8,128)(2,1)S(1)}, u32[]{:S(2)}, u32[]{:S(2)}) %collective-permute-start.9) | collective-permute-done | bytes 262176 | tf_op jit(solution)/shard_map/ppermute | solution.py:43
  31.1 1.4 %shard_map.64 = (f32[1024,128]{1,0:T(8,128)S(1)}, f32[72,128]{1,0:T(8,128)S(1)}) custom-call(s32[390]{0:T(512)S(1)} %concatenate.3.index_ref, bf16[16,6,64,256]{3,2,1,0:T(8,128)(2,1)S(1)} %copy-done, f32[1024,128]{1,0:T(8,128)S(1)} %shard_map.63.partial_ref, bf16[16,64,128]{2,1,0:T(8,128)(2,1)S(1)} %collective-permute-done.8.refs_0_, ...), custom_call_target="tpu_custom_call" | custom-call | tf_op jit(solution)/shard_map/pallas_call | solution.py:365
  32.5 1.1 %collective-permute-start.10 = (f32[72,128]{1,0:T(8,128)S(1)}, f32[72,128]{1,0:T(8,128)S(1)}, u32[]{:S(2)}, u32[]{:S(2)}) collective-permute-start(f32[72,128]{1,0:T(8,128)S(1)} %get-tuple-element.24), channel_id=1, source_target_pairs={{0,4},{4,0},{8,12},{12,8},{16,20},{20,16},{24,28},{28,24},{1,5},{5... | collective-permute-start | bytes 110600 | tf_op jit(solution)/shard_map/ppermute | solution.py:48
  33.6 0.9 %collective-permute-done.10 = f32[72,128]{1,0:T(8,128)S(1)} collective-permute-done((f32[72,128]{1,0:T(8,128)S(1)}, f32[72,128]{1,0:T(8,128)S(1)}, u32[]{:S(2)}, u32[]{:S(2)}) %collective-permute-start.10) | collective-permute-done | bytes 36896 | tf_op jit(solution)/shard_map/ppermute | solution.py:48
  34.5 6.0 %collective-permute-start.13 = (f32[72,128]{1,0:T(8,128)S(1)}, f32[72,128]{1,0:T(8,128)S(1)}, u32[]{:S(2)}, u32[]{:S(2)}) collective-permute-start(f32[72,128]{1,0:T(8,128)S(1)} %add.28), channel_id=1, source_target_pairs={{0,24},{4,28},{8,16},{12,20},{16,8},{20,12},{24,0},{28,4},{1,25},{... | collective-permute-start | bytes 110600 | tf_op jit(solution)/shard_map/ppermute | solution.py:48
  40.5 0.0 collective-permute-start.12
  40.5 0.6 %collective-permute-start.11 = (f32[72,128]{1,0:T(8,128)S(1)}, f32[72,128]{1,0:T(8,128)S(1)}, u32[]{:S(2)}, u32[]{:S(2)}) collective-permute-start(f32[72,128]{1,0:T(8,128)S(1)} %add.28), channel_id=1, source_target_pairs={{0,8},{4,12},{8,0},{12,4},{16,24},{20,28},{24,16},{28,20},{1,9},{5... | collective-permute-start | bytes 110600 | tf_op jit(solution)/shard_map/ppermute | solution.py:48
  41.1 1.6 %collective-permute-done.13 = f32[72,128]{1,0:T(8,128)S(1)} collective-permute-done((f32[72,128]{1,0:T(8,128)S(1)}, f32[72,128]{1,0:T(8,128)S(1)}, u32[]{:S(2)}, u32[]{:S(2)}) %collective-permute-start.13) | collective-permute-done | bytes 36896 | tf_op jit(solution)/shard_map/ppermute | solution.py:48
  42.7 2.7 %collective-permute-done.12 = f32[72,128]{1,0:T(8,128)S(1)} collective-permute-done((f32[72,128]{1,0:T(8,128)S(1)}, f32[72,128]{1,0:T(8,128)S(1)}, u32[]{:S(2)}, u32[]{:S(2)}) %collective-permute-start.12) | collective-permute-done | bytes 36896 | tf_op jit(solution)/shard_map/ppermute | solution.py:48
  45.3 0.0 collective-permute-done.11
  45.3 3.0 %collective-permute-start.16 = (f32[72,128]{1,0:T(8,128)S(1)}, f32[72,128]{1,0:T(8,128)S(1)}, u32[]{:S(2)}, u32[]{:S(2)}) collective-permute-start(f32[72,128]{1,0:T(8,128)S(1)} %add_add_fusion.1), channel_id=1, source_target_pairs={{0,3},{1,2},{2,1},{3,0},{4,7},{5,6},{6,5},{7,4},{8,11},{9,10},{10,... | collective-permute-start | bytes 110600 | tf_op jit(solution)/shard_map/ppermute | solution.py:48
  48.4 0.0 collective-permute-start.15
  48.4 0.6 %collective-permute-start.14 = (f32[72,128]{1,0:T(8,128)S(1)}, f32[72,128]{1,0:T(8,128)S(1)}, u32[]{:S(2)}, u32[]{:S(2)}) collective-permute-start(f32[72,128]{1,0:T(8,128)S(1)} %add_add_fusion.1), channel_id=1, source_target_pairs={{0,1},{1,0},{2,3},{3,2},{4,5},{5,4},{6,7},{7,6},{8,9},{9,8},{10,11... | collective-permute-start | bytes 110600 | tf_op jit(solution)/shard_map/ppermute | solution.py:48
  49.0 1.3 %collective-permute-done.16 = f32[72,128]{1,0:T(8,128)S(1)} collective-permute-done((f32[72,128]{1,0:T(8,128)S(1)}, f32[72,128]{1,0:T(8,128)S(1)}, u32[]{:S(2)}, u32[]{:S(2)}) %collective-permute-start.16) | collective-permute-done | bytes 36896 | tf_op jit(solution)/shard_map/ppermute | solution.py:48
  50.3 2.0 %collective-permute-done.15 = f32[72,128]{1,0:T(8,128)S(1)} collective-permute-done((f32[72,128]{1,0:T(8,128)S(1)}, f32[72,128]{1,0:T(8,128)S(1)}, u32[]{:S(2)}, u32[]{:S(2)}) %collective-permute-start.15) | collective-permute-done | bytes 36896 | tf_op jit(solution)/shard_map/ppermute | solution.py:48
  52.3 0.0 collective-permute-done.14
  52.3 4.3 %shard_map.65 = (f32[1024,128]{1,0:T(8,128)}, f32[128,128]{1,0:T(8,128)}) custom-call(f32[72,128]{1,0:T(8,128)S(1)} %add_add_fusion.packed_ref, f32[1024,128]{1,0:T(8,128)S(1)} %get-tuple-element.25.filtered_ref), custom_call_target="tpu_custom_call" | custom-call | tf_op jit(solution)/shard_map/pallas_call | solution.py:369
  (3 shorter events, 0.0 us)
Async XLA Ops:
  2.1 7.4 %collective-permute-start = (bf16[16,64,128]{2,1,0:T(8,128)(2,1)S(1)}, bf16[16,64,128]{2,1,0:T(8,128)(2,1)S(1)}, u32[]{:S(2)}, u32[]{:S(2)}) collective-permute-start(bf16[16,64,128]{2,1,0:T(8,128)(2,1)S(1)} %bitcast.8), channel_id=1, source_target_pairs={{0,1},{1,0},{2,3},{3,2},{4,6},{5,7},{6,4},{7,5},{8,9},{9,8},{10,11... | collective-permute-start | bytes 786440 | tf_op jit(solution)/shard_map/ppermute | solution.py:43
  5.1 9.2 %collective-permute-start.2 = (bf16[16,64,128]{2,1,0:T(8,128)(2,1)S(1)}, bf16[16,64,128]{2,1,0:T(8,128)(2,1)S(1)}, u32[]{:S(2)}, u32[]{:S(2)}) collective-permute-start(bf16[16,64,128]{2,1,0:T(8,128)(2,1)S(1)} %bitcast.9), channel_id=1, source_target_pairs={{4,8},{8,4},{12,16},{16,12},{20,24},{24,20},{5,9},{9,5},{13,17},{1... | collective-permute-start | bytes 786440 | tf_op jit(solution)/shard_map/ppermute | solution.py:25
  6.8 7.5 %collective-permute-start.1 = (bf16[16,64,128]{2,1,0:T(8,128)(2,1)S(1)}, bf16[16,64,128]{2,1,0:T(8,128)(2,1)S(1)}, u32[]{:S(2)}, u32[]{:S(2)}) collective-permute-start(bf16[16,64,128]{2,1,0:T(8,128)(2,1)S(1)} %bitcast.10), channel_id=1, source_target_pairs={{0,2},{1,3},{2,0},{3,1},{4,5},{5,4},{6,7},{7,6},{8,10},{9,11},{10,... | collective-permute-start | bytes 786440 | tf_op jit(solution)/shard_map/ppermute | solution.py:43
  9.4 6.2 %collective-permute-start.3 = (bf16[16,64,128]{2,1,0:T(8,128)(2,1)S(1)}, bf16[16,64,128]{2,1,0:T(8,128)(2,1)S(1)}, u32[]{:S(2)}, u32[]{:S(2)}) collective-permute-start(bf16[16,64,128]{2,1,0:T(8,128)(2,1)S(1)} %bitcast.11), channel_id=1, source_target_pairs={{0,4},{4,0},{8,12},{12,8},{16,20},{20,16},{24,28},{28,24},{1,5},{5... | collective-permute-start | bytes 786440 | tf_op jit(solution)/shard_map/ppermute | solution.py:25
  10.0 6.4 %collective-permute-start.4 = (bf16[16,64,128]{2,1,0:T(8,128)(2,1)S(1)}, bf16[16,64,128]{2,1,0:T(8,128)(2,1)S(1)}, u32[]{:S(2)}, u32[]{:S(2)}) collective-permute-start(bf16[16,64,128]{2,1,0:T(8,128)(2,1)S(1)} %collective-permute-done.refs_0_), channel_id=1, source_target_pairs={{0,2},{1,3},{2,0},{3,1},{4,5},{5,4},{6,7},{7,6},{8,10},{9,11},{10,... | collective-permute-start | bytes 786440 | tf_op jit(solution)/shard_map/ppermute | solution.py:43
  11.5 1.9 %copy-start = (bf16[16,6,64,256]{3,2,1,0:T(8,128)(2,1)S(1)}, bf16[16,6,64,256]{3,2,1,0:T(8,128)(2,1)}, u32[]{:S(2)}) copy-start(bf16[16,6,64,256]{3,2,1,0:T(8,128)(2,1)} %hamiltonian_ref.11) | copy-start | bytes 9437188
  15.6 4.1 %copy-start.1 = (f32[1024,128]{1,0:T(8,128)S(1)}, f32[1024,128]{1,0:T(8,128)}, u32[]{:S(2)}) copy-start(f32[1024,128]{1,0:T(8,128)} %refs_2_.1) | copy-start | bytes 1572868
  15.6 4.1 %copy-start.2 = (f32[1024]{0:T(1024)S(1)}, f32[1024]{0:T(1024)}, u32[]{:S(2)}) copy-start(f32[1024]{0:T(1024)} %param.6) | copy-start | bytes 12292
  17.4 6.4 %collective-permute-start.5 = (bf16[16,64,128]{2,1,0:T(8,128)(2,1)S(1)}, bf16[16,64,128]{2,1,0:T(8,128)(2,1)S(1)}, u32[]{:S(2)}, u32[]{:S(2)}) collective-permute-start(bf16[16,64,128]{2,1,0:T(8,128)(2,1)S(1)} %get-tuple-element.23.own_ref), channel_id=1, source_target_pairs={{0,1},{1,0},{2,3},{3,2},{4,6},{5,7},{6,4},{7,5},{8,9},{9,8},{10,11... | collective-permute-start | bytes 786440 | tf_op jit(solution)/shard_map/ppermute | solution.py:43
  19.0 8.1 %collective-permute-start.7 = (bf16[16,64,128]{2,1,0:T(8,128)(2,1)S(1)}, bf16[16,64,128]{2,1,0:T(8,128)(2,1)S(1)}, u32[]{:S(2)}, u32[]{:S(2)}) collective-permute-start(bf16[16,64,128]{2,1,0:T(8,128)(2,1)S(1)} %get-tuple-element.23.own_ref), channel_id=1, source_target_pairs={{4,8},{8,4},{12,16},{16,12},{20,24},{24,20},{5,9},{9,5},{13,17},{1... | collective-permute-start | bytes 786440 | tf_op jit(solution)/shard_map/ppermute | solution.py:25
  20.6 6.5 %collective-permute-start.6 = (bf16[16,64,128]{2,1,0:T(8,128)(2,1)S(1)}, bf16[16,64,128]{2,1,0:T(8,128)(2,1)S(1)}, u32[]{:S(2)}, u32[]{:S(2)}) collective-permute-start(bf16[16,64,128]{2,1,0:T(8,128)(2,1)S(1)} %get-tuple-element.23.own_ref), channel_id=1, source_target_pairs={{0,2},{1,3},{2,0},{3,1},{4,5},{5,4},{6,7},{7,6},{8,10},{9,11},{10,... | collective-permute-start | bytes 786440 | tf_op jit(solution)/shard_map/ppermute | solution.py:43
  23.8 4.5 %collective-permute-start.8 = (bf16[16,64,128]{2,1,0:T(8,128)(2,1)S(1)}, bf16[16,64,128]{2,1,0:T(8,128)(2,1)S(1)}, u32[]{:S(2)}, u32[]{:S(2)}) collective-permute-start(bf16[16,64,128]{2,1,0:T(8,128)(2,1)S(1)} %get-tuple-element.23.own_ref), channel_id=1, source_target_pairs={{0,4},{4,0},{8,12},{12,8},{16,20},{20,16},{24,28},{28,24},{1,5},{5... | collective-permute-start | bytes 786440 | tf_op jit(solution)/shard_map/ppermute | solution.py:25
  24.8 6.4 %collective-permute-start.9 = (bf16[16,64,128]{2,1,0:T(8,128)(2,1)S(1)}, bf16[16,64,128]{2,1,0:T(8,128)(2,1)S(1)}, u32[]{:S(2)}, u32[]{:S(2)}) collective-permute-start(bf16[16,64,128]{2,1,0:T(8,128)(2,1)S(1)} %collective-permute-done.5.refs_0_), channel_id=1, source_target_pairs={{0,2},{1,3},{2,0},{3,1},{4,5},{5,4},{6,7},{7,6},{8,10},{9,11},{10,... | collective-permute-start | bytes 786440 | tf_op jit(solution)/shard_map/ppermute | solution.py:43
  32.5 2.0 %collective-permute-start.10 = (f32[72,128]{1,0:T(8,128)S(1)}, f32[72,128]{1,0:T(8,128)S(1)}, u32[]{:S(2)}, u32[]{:S(2)}) collective-permute-start(f32[72,128]{1,0:T(8,128)S(1)} %get-tuple-element.24), channel_id=1, source_target_pairs={{0,4},{4,0},{8,12},{12,8},{16,20},{20,16},{24,28},{28,24},{1,5},{5... | collective-permute-start | bytes 110600 | tf_op jit(solution)/shard_map/ppermute | solution.py:48
  34.5 8.2 %collective-permute-start.13 = (f32[72,128]{1,0:T(8,128)S(1)}, f32[72,128]{1,0:T(8,128)S(1)}, u32[]{:S(2)}, u32[]{:S(2)}) collective-permute-start(f32[72,128]{1,0:T(8,128)S(1)} %add.28), channel_id=1, source_target_pairs={{0,24},{4,28},{8,16},{12,20},{16,8},{20,12},{24,0},{28,4},{1,25},{... | collective-permute-start | bytes 110600 | tf_op jit(solution)/shard_map/ppermute | solution.py:48
  40.5 4.9 %collective-permute-start.12 = (f32[72,128]{1,0:T(8,128)S(1)}, f32[72,128]{1,0:T(8,128)S(1)}, u32[]{:S(2)}, u32[]{:S(2)}) collective-permute-start(f32[72,128]{1,0:T(8,128)S(1)} %add.28), channel_id=1, source_target_pairs={{0,16},{4,20},{8,24},{12,28},{16,0},{20,4},{24,8},{28,12},{1,17},{... | collective-permute-start | bytes 110600 | tf_op jit(solution)/shard_map/ppermute | solution.py:48
  40.5 4.9 %collective-permute-start.11 = (f32[72,128]{1,0:T(8,128)S(1)}, f32[72,128]{1,0:T(8,128)S(1)}, u32[]{:S(2)}, u32[]{:S(2)}) collective-permute-start(f32[72,128]{1,0:T(8,128)S(1)} %add.28), channel_id=1, source_target_pairs={{0,8},{4,12},{8,0},{12,4},{16,24},{20,28},{24,16},{28,20},{1,9},{5... | collective-permute-start | bytes 110600 | tf_op jit(solution)/shard_map/ppermute | solution.py:48
  45.3 5.0 %collective-permute-start.16 = (f32[72,128]{1,0:T(8,128)S(1)}, f32[72,128]{1,0:T(8,128)S(1)}, u32[]{:S(2)}, u32[]{:S(2)}) collective-permute-start(f32[72,128]{1,0:T(8,128)S(1)} %add_add_fusion.1), channel_id=1, source_target_pairs={{0,3},{1,2},{2,1},{3,0},{4,7},{5,6},{6,5},{7,4},{8,11},{9,10},{10,... | collective-permute-start | bytes 110600 | tf_op jit(solution)/shard_map/ppermute | solution.py:48
  48.4 4.0 %collective-permute-start.15 = (f32[72,128]{1,0:T(8,128)S(1)}, f32[72,128]{1,0:T(8,128)S(1)}, u32[]{:S(2)}, u32[]{:S(2)}) collective-permute-start(f32[72,128]{1,0:T(8,128)S(1)} %add_add_fusion.1), channel_id=1, source_target_pairs={{0,2},{1,3},{2,0},{3,1},{4,6},{5,7},{6,4},{7,5},{8,10},{9,11},{10,... | collective-permute-start | bytes 110600 | tf_op jit(solution)/shard_map/ppermute | solution.py:48
  48.4 4.0 %collective-permute-start.14 = (f32[72,128]{1,0:T(8,128)S(1)}, f32[72,128]{1,0:T(8,128)S(1)}, u32[]{:S(2)}, u32[]{:S(2)}) collective-permute-start(f32[72,128]{1,0:T(8,128)S(1)} %add_add_fusion.1), channel_id=1, source_target_pairs={{0,1},{1,0},{2,3},{3,2},{4,5},{5,4},{6,7},{7,6},{8,9},{9,8},{10,11... | collective-permute-start | bytes 110600 | tf_op jit(solution)/shard_map/ppermute | solution.py:48

commit v12 on v11

--- a/solution.py
+++ b/solution.py
@@ -20,8 +20,9 @@
 def pair_exchange(value, offset):
     count = lax.axis_size("group")
     route = []
-    for low in range(offset, count - 1, 2):
-        route += [(low, low + 1), (low + 1, low)]
+    for low in range(offset, count + offset, 2):
+        first, second = low % count, (low + 1) % count
+        route += [(first, second), (second, first)]
     return lax.ppermute(value, "group", route)
 
 
@@ -78,6 +79,9 @@
         product = jnp.dot(
             hamiltonian_ref[row, source], picked, preferred_element_type=jnp.float32
         )
+        if number == sources - 1:
+            absent = index_ref[shard_blocks * sources * per_source + sources] != 0
+            product = jnp.where(absent, 0.0, product)
         total = product if total is None else total + product
     return total
 
@@ -319,12 +323,13 @@
         origins += [jnp.bitwise_xor(origin, flip) for origin in origins]
     odd = group % 2
     origins += [cycle_size + 1 - odd, cycle_size + odd]
+    origins.append((group == 0) | (group == lax.axis_size("group") - 1))
     index_array = jnp.concatenate(
         [block_columns.reshape(-1)] + [origin.reshape(1).astype(jnp.int32) for origin in origins]
     )
     last = cycle_size - 1
     ending = [cycle_size, last]
-    middle = [1] + list(range(2, last)) + [cycle_size + 1]
+    middle = list(range(1, last)) + [cycle_size + 1]
     flat = jax.ShapeDtypeStruct((flat_rows, states), jnp.float32)
     rounded = jax.ShapeDtypeStruct((shard_blocks, block_size, states), jnp.bfloat16)
     packed = jax.ShapeDtypeStruct((states // 2 + SUB, states), jnp.float32)

time: 56.8 us -> 56.9 us (level)
  starting transfers between devices: 24.9 us -> 22 us
  waiting for transfers between devices: 15.5 us -> 18.4 us
    ppermute x6, starting transfers between devices: 10.7 us -> 7.54 us  [cycle_exchange(): return lax.ppermute(value, ('group', 'blk'), route)]
    ppermute x6, waiting for transfers between devices: 7.04 us -> 9.93 us  [cycle_exchange(): return lax.ppermute(value, ('group', 'blk'), route)]
    ppermute x4, starting transfers between devices: 2.79 us -> 5.38 us  [pair_exchange(): return lax.ppermute(value, 'group', route)]
    ppermute x7, starting transfers between devices: 11.4 us -> 9.11 us  [from_partner(): lax.ppermute(value, axis, [(index, index ^ flip) for index in range(count)])]
  transfers between devices with their start and end apart: 17 -> 17, of which waited for: 10 -> 11; matrix products, arithmetic and copies ran while one was open for 2% -> 2% of each run, Pallas kernels for 8% -> 8%
where the time goes in v12:
time: 56.9 us; the launch traced here: 56.7 us
  starting transfers between devices  22 us (39%)
  waiting for transfers between devices  18.4 us (32%)
  Pallas kernels  11.1 us (20%)
  local copies, waits for them, and re-layouts  2.92 us (5%)
  other arithmetic  1.46 us (3%)
  between operations  0.74 us (1%)
    ppermute x6, waiting for transfers between devices, cycle_exchange(): return lax.ppermute(value, ('group', 'blk'), route)  9.93 us
    ppermute x7, starting transfers between devices, from_partner(): lax.ppermute(value, axis, [(index, index ^ flip) for index in range(count)])  9.11 us
    ppermute x7, waiting for transfers between devices, from_partner(): lax.ppermute(value, axis, [(index, index ^ flip) for index in range(count)])  8.33 us
    ppermute x6, starting transfers between devices, cycle_exchange(): return lax.ppermute(value, ('group', 'blk'), route)  7.54 us
    ppermute x4, starting transfers between devices, pair_exchange(): return lax.ppermute(value, 'group', route)  5.38 us
    pallas_call x1, Pallas kernels, on_device(): call(functools.partial(factor_kernel, rows_total), (flat, square), [vmem,...  4.27 us
    unnamed x7, local copies, waits for them, and re-layouts  2.72 us
    pallas_call x2, Pallas kernels, coupled(): call(functools.partial(middle_kernel, middle), flat, [smem] + [vmem] * (2...  2.54 us
  transfers between devices with their start and end apart: 17, of which 11 were waited for; matrix products, arithmetic and copies ran while one was open for 2% of the time, Pallas kernels for 8%

profile of v12, /device:TPU:0, one launch (start us, length us, event | category | flops | bytes accessed | tf_op | source)
XLA Modules:
  0.0 56.7 jit_solution(3265947365180602546)
XLA Ops:
  0.6 1.4 %broadcast_multiply_fusion = (f32[1024,128]{1,0:T(8,128)S(1)}, bf16[1024,128]{1,0:T(8,128)(2,1)S(1)}) fusion(f32[1024,128]{1,0:T(8,128)} %refs_2_.1, f32[1024]{0:T(1024)} %param.6), kind=kLoop, calls=%fused_computation | loop fusion | flops 262144 | bytes 1314816 | tf_op jit(solution)/shard_map/mul | solution.py:364
  2.1 3.0 %collective-permute-start = (bf16[16,64,128]{2,1,0:T(8,128)(2,1)S(1)}, bf16[16,64,128]{2,1,0:T(8,128)(2,1)S(1)}, u32[]{:S(2)}, u32[]{:S(2)}) collective-permute-start(bf16[16,64,128]{2,1,0:T(8,128)(2,1)S(1)} %bitcast.9), channel_id=1, source_target_pairs={{0,1},{1,0},{2,3},{3,2},{4,6},{5,7},{6,4},{7,5},{8,9},{9,8},{10,11... | collective-permute-start | bytes 786440 | tf_op jit(solution)/shard_map/ppermute | solution.py:44
  5.1 2.8 %collective-permute-start.2 = (bf16[16,64,128]{2,1,0:T(8,128)(2,1)S(1)}, bf16[16,64,128]{2,1,0:T(8,128)(2,1)S(1)}, u32[]{:S(2)}, u32[]{:S(2)}) collective-permute-start(bf16[16,64,128]{2,1,0:T(8,128)(2,1)S(1)} %bitcast.10), channel_id=1, source_target_pairs={{4,8},{8,4},{12,16},{16,12},{20,24},{24,20},{28,0},{0,28},{5,9},{9... | collective-permute-start | bytes 786440 | tf_op jit(solution)/shard_map/ppermute | solution.py:26
  7.9 0.8 %copy.6 = s32[16,6,4]{2,1,0:T(8,128)S(1)} copy(s32[16,6,4]{0,2,1:T(4,128)} %param.5) | data formatting | bytes 3072 | tf_op args[1]
  8.7 0.1 reshape.34
  8.8 0.1 concatenate.3.index_ref
  8.9 0.5 collective-permute-start.1
  9.4 0.0 collective-permute-done.refs_0_
  9.4 0.0 collective-permute-start.3
  9.4 2.0 %collective-permute-start.4 = (bf16[16,64,128]{2,1,0:T(8,128)(2,1)S(1)}, bf16[16,64,128]{2,1,0:T(8,128)(2,1)S(1)}, u32[]{:S(2)}, u32[]{:S(2)}) collective-permute-start(bf16[16,64,128]{2,1,0:T(8,128)(2,1)S(1)} %collective-permute-done.refs_0_), channel_id=1, source_target_pairs={{0,2},{1,3},{2,0},{3,1},{4,5},{5,4},{6,7},{7,6},{8,10},{9,11},{10,... | collective-permute-start | bytes 786440 | tf_op jit(solution)/shard_map/ppermute | solution.py:44
  11.5 0.0 copy-start
  11.5 1.9 %copy-done = bf16[16,6,64,256]{3,2,1,0:T(8,128)(2,1)S(1)} copy-done((bf16[16,6,64,256]{3,2,1,0:T(8,128)(2,1)S(1)}, bf16[16,6,64,256]{3,2,1,0:T(8,128)(2,1)}, u32[]{:S(2)}) %copy-start) | copy-done | bytes 3145752
  13.4 0.9 %shard_map.59.partial_ref = f32[1024,128]{1,0:T(8,128)S(1)} custom-call(s32[391]{0:T(512)S(1)} %concatenate.3.index_ref, bf16[16,6,64,256]{3,2,1,0:T(8,128)(2,1)S(1)} %copy-done, bf16[16,64,128]{2,1,0:T(8,128)(2,1)S(1)} %bitcast.13, f32[1024,128]{1,0:T(8,128)S(1)} %get-tuple-element.26.refs_0_), custom_call_target="tpu_custom_call" | custom-call | tf_op jit(solution)/shard_map/pallas_call | solution.py:339
  14.3 1.0 %collective-permute-done.1.refs_1_ = bf16[16,64,128]{2,1,0:T(8,128)(2,1)S(1)} collective-permute-done((bf16[16,64,128]{2,1,0:T(8,128)(2,1)S(1)}, bf16[16,64,128]{2,1,0:T(8,128)(2,1)S(1)}, u32[]{:S(2)}, u32[]{:S(2)}) %collective-permute-start.1) | collective-permute-done | bytes 262176 | tf_op jit(solution)/shard_map/ppermute | solution.py:44
  15.3 0.0 collective-permute-done.2.refs_2_
  15.3 1.3 %shard_map.60.partial_ref = f32[1024,128]{1,0:T(8,128)S(1)} custom-call(s32[391]{0:T(512)S(1)} %concatenate.3.index_ref, bf16[16,6,64,256]{3,2,1,0:T(8,128)(2,1)S(1)} %copy-done, f32[1024,128]{1,0:T(8,128)S(1)} %shard_map.59.partial_ref, bf16[16,64,128]{2,1,0:T(8,128)(2,1)S(1)} %collective-permute-done.refs_0_, ...), custom_call_target="tpu_custom_call" | custom-call | tf_op jit(solution)/shard_map/pallas_call | solution.py:359
  16.5 0.0 copy-start.1
  16.6 0.0 copy-start.2
  16.6 0.0 collective-permute-done.3.refs_0_
  16.6 1.5 %collective-permute-done.4.refs_1_ = bf16[16,64,128]{2,1,0:T(8,128)(2,1)S(1)} collective-permute-done((bf16[16,64,128]{2,1,0:T(8,128)(2,1)S(1)}, bf16[16,64,128]{2,1,0:T(8,128)(2,1)S(1)}, u32[]{:S(2)}, u32[]{:S(2)}) %collective-permute-start.4) | collective-permute-done | bytes 262176 | tf_op jit(solution)/shard_map/ppermute | solution.py:44
  18.1 1.1 %shard_map.61 = (f32[1024,128]{1,0:T(8,128)S(1)}, bf16[16,64,128]{2,1,0:T(8,128)(2,1)S(1)}) custom-call(s32[391]{0:T(512)S(1)} %concatenate.3.index_ref, bf16[16,6,64,256]{3,2,1,0:T(8,128)(2,1)S(1)} %copy-done, f32[1024,128]{1,0:T(8,128)S(1)} %shard_map.60.partial_ref, bf16[16,64,128]{2,1,0:T(8,128)(2,1)S(1)} %collective-permute-done.3.refs_0_, ...), custom_call_target="tpu_custom_call" | custom-call | tf_op jit(solution)/shard_map/pallas_call | solution.py:366
  19.1 1.6 %collective-permute-start.5 = (bf16[16,64,128]{2,1,0:T(8,128)(2,1)S(1)}, bf16[16,64,128]{2,1,0:T(8,128)(2,1)S(1)}, u32[]{:S(2)}, u32[]{:S(2)}) collective-permute-start(bf16[16,64,128]{2,1,0:T(8,128)(2,1)S(1)} %get-tuple-element.23.own_ref), channel_id=1, source_target_pairs={{0,1},{1,0},{2,3},{3,2},{4,6},{5,7},{6,4},{7,5},{8,9},{9,8},{10,11... | collective-permute-start | bytes 786440 | tf_op jit(solution)/shard_map/ppermute | solution.py:44
  20.7 2.6 %collective-permute-start.7 = (bf16[16,64,128]{2,1,0:T(8,128)(2,1)S(1)}, bf16[16,64,128]{2,1,0:T(8,128)(2,1)S(1)}, u32[]{:S(2)}, u32[]{:S(2)}) collective-permute-start(bf16[16,64,128]{2,1,0:T(8,128)(2,1)S(1)} %get-tuple-element.23.own_ref), channel_id=1, source_target_pairs={{4,8},{8,4},{12,16},{16,12},{20,24},{24,20},{28,0},{0,28},{5,9},{9... | collective-permute-start | bytes 786440 | tf_op jit(solution)/shard_map/ppermute | solution.py:26
  23.3 0.0 copy-done.1
  23.3 0.0 copy-done.2
  23.3 1.0 %shard_map.62.partial_ref = f32[1024,128]{1,0:T(8,128)S(1)} custom-call(s32[391]{0:T(512)S(1)} %concatenate.3.index_ref, bf16[16,6,64,256]{3,2,1,0:T(8,128)(2,1)S(1)} %copy-done, bf16[16,64,128]{2,1,0:T(8,128)(2,1)S(1)} %get-tuple-element.23.own_ref, f32[8,128]{1,0:T(8,128)S(1)} %bitcast.14, f32[1024,128]{1,0:T(8,128)S(1)} %get-tuple-element.19.refs_1_, ...), custom_call_target="tpu_custom_call" | custom-call | tf_op jit(solution)/shard_map/pallas_call | solution.py:339
  24.2 0.4 collective-permute-start.6
  24.7 2.0 %collective-permute-done.5.refs_0_ = bf16[16,64,128]{2,1,0:T(8,128)(2,1)S(1)} collective-permute-done((bf16[16,64,128]{2,1,0:T(8,128)(2,1)S(1)}, bf16[16,64,128]{2,1,0:T(8,128)(2,1)S(1)}, u32[]{:S(2)}, u32[]{:S(2)}) %collective-permute-start.5) | collective-permute-done | bytes 262176 | tf_op jit(solution)/shard_map/ppermute | solution.py:44
  26.6 0.0 collective-permute-start.8
  26.6 0.0 collective-permute-start.9
  26.7 4.0 %collective-permute-done.6.refs_1_ = bf16[16,64,128]{2,1,0:T(8,128)(2,1)S(1)} collective-permute-done((bf16[16,64,128]{2,1,0:T(8,128)(2,1)S(1)}, bf16[16,64,128]{2,1,0:T(8,128)(2,1)S(1)}, u32[]{:S(2)}, u32[]{:S(2)}) %collective-permute-start.6) | collective-permute-done | bytes 262176 | tf_op jit(solution)/shard_map/ppermute | solution.py:44
  30.7 0.1 collective-permute-done.7.refs_2_
  30.8 1.3 %shard_map.63.partial_ref = f32[1024,128]{1,0:T(8,128)S(1)} custom-call(s32[391]{0:T(512)S(1)} %concatenate.3.index_ref, bf16[16,6,64,256]{3,2,1,0:T(8,128)(2,1)S(1)} %copy-done, f32[1024,128]{1,0:T(8,128)S(1)} %shard_map.62.partial_ref, bf16[16,64,128]{2,1,0:T(8,128)(2,1)S(1)} %collective-permute-done.5.refs_0_, ...), custom_call_target="tpu_custom_call" | custom-call | tf_op jit(solution)/shard_map/pallas_call | solution.py:359
  32.1 0.0 collective-permute-done.8.refs_0_
  32.1 1.4 %collective-permute-done.9.refs_1_ = bf16[16,64,128]{2,1,0:T(8,128)(2,1)S(1)} collective-permute-done((bf16[16,64,128]{2,1,0:T(8,128)(2,1)S(1)}, bf16[16,64,128]{2,1,0:T(8,128)(2,1)S(1)}, u32[]{:S(2)}, u32[]{:S(2)}) %collective-permute-start.9) | collective-permute-done | bytes 262176 | tf_op jit(solution)/shard_map/ppermute | solution.py:44
  33.5 1.4 %shard_map.64 = (f32[1024,128]{1,0:T(8,128)S(1)}, f32[72,128]{1,0:T(8,128)S(1)}) custom-call(s32[391]{0:T(512)S(1)} %concatenate.3.index_ref, bf16[16,6,64,256]{3,2,1,0:T(8,128)(2,1)S(1)} %copy-done, f32[1024,128]{1,0:T(8,128)S(1)} %shard_map.63.partial_ref, bf16[16,64,128]{2,1,0:T(8,128)(2,1)S(1)} %collective-permute-done.8.refs_0_, ...), custom_call_target="tpu_custom_call" | custom-call | tf_op jit(solution)/shard_map/pallas_call | solution.py:370
  34.9 0.1 collective-permute-start.10
  35.0 1.2 %collective-permute-done.10 = f32[72,128]{1,0:T(8,128)S(1)} collective-permute-done((f32[72,128]{1,0:T(8,128)S(1)}, f32[72,128]{1,0:T(8,128)S(1)}, u32[]{:S(2)}, u32[]{:S(2)}) %collective-permute-start.10) | collective-permute-done | bytes 36896 | tf_op jit(solution)/shard_map/ppermute | solution.py:49
  36.2 3.3 %collective-permute-start.13 = (f32[72,128]{1,0:T(8,128)S(1)}, f32[72,128]{1,0:T(8,128)S(1)}, u32[]{:S(2)}, u32[]{:S(2)}) collective-permute-start(f32[72,128]{1,0:T(8,128)S(1)} %add.28), channel_id=1, source_target_pairs={{0,24},{4,28},{8,16},{12,20},{16,8},{20,12},{24,0},{28,4},{1,25},{... | collective-permute-start | bytes 110600 | tf_op jit(solution)/shard_map/ppermute | solution.py:49
  39.5 0.0 collective-permute-start.12
  39.5 1.0 %collective-permute-start.11 = (f32[72,128]{1,0:T(8,128)S(1)}, f32[72,128]{1,0:T(8,128)S(1)}, u32[]{:S(2)}, u32[]{:S(2)}) collective-permute-start(f32[72,128]{1,0:T(8,128)S(1)} %add.28), channel_id=1, source_target_pairs={{0,8},{4,12},{8,0},{12,4},{16,24},{20,28},{24,16},{28,20},{1,9},{5... | collective-permute-start | bytes 110600 | tf_op jit(solution)/shard_map/ppermute | solution.py:49
  40.6 1.4 %collective-permute-done.13 = f32[72,128]{1,0:T(8,128)S(1)} collective-permute-done((f32[72,128]{1,0:T(8,128)S(1)}, f32[72,128]{1,0:T(8,128)S(1)}, u32[]{:S(2)}, u32[]{:S(2)}) %collective-permute-start.13) | collective-permute-done | bytes 36896 | tf_op jit(solution)/shard_map/ppermute | solution.py:49
  41.9 2.4 %collective-permute-done.12 = f32[72,128]{1,0:T(8,128)S(1)} collective-permute-done((f32[72,128]{1,0:T(8,128)S(1)}, f32[72,128]{1,0:T(8,128)S(1)}, u32[]{:S(2)}, u32[]{:S(2)}) %collective-permute-start.12) | collective-permute-done | bytes 36896 | tf_op jit(solution)/shard_map/ppermute | solution.py:49
  44.4 0.0 collective-permute-done.11
  44.4 4.0 %collective-permute-start.16 = (f32[72,128]{1,0:T(8,128)S(1)}, f32[72,128]{1,0:T(8,128)S(1)}, u32[]{:S(2)}, u32[]{:S(2)}) collective-permute-start(f32[72,128]{1,0:T(8,128)S(1)} %add_add_fusion.1), channel_id=1, source_target_pairs={{0,3},{1,2},{2,1},{3,0},{4,7},{5,6},{6,5},{7,4},{8,11},{9,10},{10,... | collective-permute-start | bytes 110600 | tf_op jit(solution)/shard_map/ppermute | solution.py:49
  48.4 0.0 collective-permute-start.15
  48.4 0.6 %collective-permute-start.14 = (f32[72,128]{1,0:T(8,128)S(1)}, f32[72,128]{1,0:T(8,128)S(1)}, u32[]{:S(2)}, u32[]{:S(2)}) collective-permute-start(f32[72,128]{1,0:T(8,128)S(1)} %add_add_fusion.1), channel_id=1, source_target_pairs={{0,1},{1,0},{2,3},{3,2},{4,5},{5,4},{6,7},{7,6},{8,9},{9,8},{10,11... | collective-permute-start | bytes 110600 | tf_op jit(solution)/shard_map/ppermute | solution.py:49
  49.1 1.3 %collective-permute-done.16 = f32[72,128]{1,0:T(8,128)S(1)} collective-permute-done((f32[72,128]{1,0:T(8,128)S(1)}, f32[72,128]{1,0:T(8,128)S(1)}, u32[]{:S(2)}, u32[]{:S(2)}) %collective-permute-start.16) | collective-permute-done | bytes 36896 | tf_op jit(solution)/shard_map/ppermute | solution.py:49
  50.4 2.0 %collective-permute-done.15 = f32[72,128]{1,0:T(8,128)S(1)} collective-permute-done((f32[72,128]{1,0:T(8,128)S(1)}, f32[72,128]{1,0:T(8,128)S(1)}, u32[]{:S(2)}, u32[]{:S(2)}) %collective-permute-start.15) | collective-permute-done | bytes 36896 | tf_op jit(solution)/shard_map/ppermute | solution.py:49
  52.4 0.0 collective-permute-done.14
  52.4 4.3 %shard_map.65 = (f32[1024,128]{1,0:T(8,128)}, f32[128,128]{1,0:T(8,128)}) custom-call(f32[72,128]{1,0:T(8,128)S(1)} %add_add_fusion.packed_ref, f32[1024,128]{1,0:T(8,128)S(1)} %get-tuple-element.25.filtered_ref), custom_call_target="tpu_custom_call" | custom-call | tf_op jit(solution)/shard_map/pallas_call | solution.py:374
  (3 shorter events, 0.0 us)
Async XLA Ops:
  2.1 7.4 %collective-permute-start = (bf16[16,64,128]{2,1,0:T(8,128)(2,1)S(1)}, bf16[16,64,128]{2,1,0:T(8,128)(2,1)S(1)}, u32[]{:S(2)}, u32[]{:S(2)}) collective-permute-start(bf16[16,64,128]{2,1,0:T(8,128)(2,1)S(1)} %bitcast.9), channel_id=1, source_target_pairs={{0,1},{1,0},{2,3},{3,2},{4,6},{5,7},{6,4},{7,5},{8,9},{9,8},{10,11... | collective-permute-start | bytes 786440 | tf_op jit(solution)/shard_map/ppermute | solution.py:44
  5.1 10.2 %collective-permute-start.2 = (bf16[16,64,128]{2,1,0:T(8,128)(2,1)S(1)}, bf16[16,64,128]{2,1,0:T(8,128)(2,1)S(1)}, u32[]{:S(2)}, u32[]{:S(2)}) collective-permute-start(bf16[16,64,128]{2,1,0:T(8,128)(2,1)S(1)} %bitcast.10), channel_id=1, source_target_pairs={{4,8},{8,4},{12,16},{16,12},{20,24},{24,20},{28,0},{0,28},{5,9},{9... | collective-permute-start | bytes 786440 | tf_op jit(solution)/shard_map/ppermute | solution.py:26
  8.9 6.4 %collective-permute-start.1 = (bf16[16,64,128]{2,1,0:T(8,128)(2,1)S(1)}, bf16[16,64,128]{2,1,0:T(8,128)(2,1)S(1)}, u32[]{:S(2)}, u32[]{:S(2)}) collective-permute-start(bf16[16,64,128]{2,1,0:T(8,128)(2,1)S(1)} %bitcast.11), channel_id=1, source_target_pairs={{0,2},{1,3},{2,0},{3,1},{4,5},{5,4},{6,7},{7,6},{8,10},{9,11},{10,... | collective-permute-start | bytes 786440 | tf_op jit(solution)/shard_map/ppermute | solution.py:44
  9.4 7.1 %collective-permute-start.3 = (bf16[16,64,128]{2,1,0:T(8,128)(2,1)S(1)}, bf16[16,64,128]{2,1,0:T(8,128)(2,1)S(1)}, u32[]{:S(2)}, u32[]{:S(2)}) collective-permute-start(bf16[16,64,128]{2,1,0:T(8,128)(2,1)S(1)} %bitcast.12), channel_id=1, source_target_pairs={{0,4},{4,0},{8,12},{12,8},{16,20},{20,16},{24,28},{28,24},{1,5},{5... | collective-permute-start | bytes 786440 | tf_op jit(solution)/shard_map/ppermute | solution.py:26
  9.4 8.6 %collective-permute-start.4 = (bf16[16,64,128]{2,1,0:T(8,128)(2,1)S(1)}, bf16[16,64,128]{2,1,0:T(8,128)(2,1)S(1)}, u32[]{:S(2)}, u32[]{:S(2)}) collective-permute-start(bf16[16,64,128]{2,1,0:T(8,128)(2,1)S(1)} %collective-permute-done.refs_0_), channel_id=1, source_target_pairs={{0,2},{1,3},{2,0},{3,1},{4,5},{5,4},{6,7},{7,6},{8,10},{9,11},{10,... | collective-permute-start | bytes 786440 | tf_op jit(solution)/shard_map/ppermute | solution.py:44
  11.5 1.9 %copy-start = (bf16[16,6,64,256]{3,2,1,0:T(8,128)(2,1)S(1)}, bf16[16,6,64,256]{3,2,1,0:T(8,128)(2,1)}, u32[]{:S(2)}) copy-start(bf16[16,6,64,256]{3,2,1,0:T(8,128)(2,1)} %hamiltonian_ref.11) | copy-start | bytes 9437188
  16.5 6.7 %copy-start.1 = (f32[1024,128]{1,0:T(8,128)S(1)}, f32[1024,128]{1,0:T(8,128)}, u32[]{:S(2)}) copy-start(f32[1024,128]{1,0:T(8,128)} %refs_2_.1) | copy-start | bytes 1572868
  16.6 6.7 %copy-start.2 = (f32[1024]{0:T(1024)S(1)}, f32[1024]{0:T(1024)}, u32[]{:S(2)}) copy-start(f32[1024]{0:T(1024)} %param.6) | copy-start | bytes 12292
  19.1 7.5 %collective-permute-start.5 = (bf16[16,64,128]{2,1,0:T(8,128)(2,1)S(1)}, bf16[16,64,128]{2,1,0:T(8,128)(2,1)S(1)}, u32[]{:S(2)}, u32[]{:S(2)}) collective-permute-start(bf16[16,64,128]{2,1,0:T(8,128)(2,1)S(1)} %get-tuple-element.23.own_ref), channel_id=1, source_target_pairs={{0,1},{1,0},{2,3},{3,2},{4,6},{5,7},{6,4},{7,5},{8,9},{9,8},{10,11... | collective-permute-start | bytes 786440 | tf_op jit(solution)/shard_map/ppermute | solution.py:44
  20.7 10.1 %collective-permute-start.7 = (bf16[16,64,128]{2,1,0:T(8,128)(2,1)S(1)}, bf16[16,64,128]{2,1,0:T(8,128)(2,1)S(1)}, u32[]{:S(2)}, u32[]{:S(2)}) collective-permute-start(bf16[16,64,128]{2,1,0:T(8,128)(2,1)S(1)} %get-tuple-element.23.own_ref), channel_id=1, source_target_pairs={{4,8},{8,4},{12,16},{16,12},{20,24},{24,20},{28,0},{0,28},{5,9},{9... | collective-permute-start | bytes 786440 | tf_op jit(solution)/shard_map/ppermute | solution.py:26
  24.2 6.4 %collective-permute-start.6 = (bf16[16,64,128]{2,1,0:T(8,128)(2,1)S(1)}, bf16[16,64,128]{2,1,0:T(8,128)(2,1)S(1)}, u32[]{:S(2)}, u32[]{:S(2)}) collective-permute-start(bf16[16,64,128]{2,1,0:T(8,128)(2,1)S(1)} %get-tuple-element.23.own_ref), channel_id=1, source_target_pairs={{0,2},{1,3},{2,0},{3,1},{4,5},{5,4},{6,7},{7,6},{8,10},{9,11},{10,... | collective-permute-start | bytes 786440 | tf_op jit(solution)/shard_map/ppermute | solution.py:44
  26.6 5.4 %collective-permute-start.8 = (bf16[16,64,128]{2,1,0:T(8,128)(2,1)S(1)}, bf16[16,64,128]{2,1,0:T(8,128)(2,1)S(1)}, u32[]{:S(2)}, u32[]{:S(2)}) collective-permute-start(bf16[16,64,128]{2,1,0:T(8,128)(2,1)S(1)} %get-tuple-element.23.own_ref), channel_id=1, source_target_pairs={{0,4},{4,0},{8,12},{12,8},{16,20},{20,16},{24,28},{28,24},{1,5},{5... | collective-permute-start | bytes 786440 | tf_op jit(solution)/shard_map/ppermute | solution.py:26
  26.6 6.8 %collective-permute-start.9 = (bf16[16,64,128]{2,1,0:T(8,128)(2,1)S(1)}, bf16[16,64,128]{2,1,0:T(8,128)(2,1)S(1)}, u32[]{:S(2)}, u32[]{:S(2)}) collective-permute-start(bf16[16,64,128]{2,1,0:T(8,128)(2,1)S(1)} %collective-permute-done.5.refs_0_), channel_id=1, source_target_pairs={{0,2},{1,3},{2,0},{3,1},{4,5},{5,4},{6,7},{7,6},{8,10},{9,11},{10,... | collective-permute-start | bytes 786440 | tf_op jit(solution)/shard_map/ppermute | solution.py:44
  34.9 1.3 %collective-permute-start.10 = (f32[72,128]{1,0:T(8,128)S(1)}, f32[72,128]{1,0:T(8,128)S(1)}, u32[]{:S(2)}, u32[]{:S(2)}) collective-permute-start(f32[72,128]{1,0:T(8,128)S(1)} %get-tuple-element.24), channel_id=1, source_target_pairs={{0,4},{4,0},{8,12},{12,8},{16,20},{20,16},{24,28},{28,24},{1,5},{5... | collective-permute-start | bytes 110600 | tf_op jit(solution)/shard_map/ppermute | solution.py:49
  36.2 5.8 %collective-permute-start.13 = (f32[72,128]{1,0:T(8,128)S(1)}, f32[72,128]{1,0:T(8,128)S(1)}, u32[]{:S(2)}, u32[]{:S(2)}) collective-permute-start(f32[72,128]{1,0:T(8,128)S(1)} %add.28), channel_id=1, source_target_pairs={{0,24},{4,28},{8,16},{12,20},{16,8},{20,12},{24,0},{28,4},{1,25},{... | collective-permute-start | bytes 110600 | tf_op jit(solution)/shard_map/ppermute | solution.py:49
  39.5 4.9 %collective-permute-start.12 = (f32[72,128]{1,0:T(8,128)S(1)}, f32[72,128]{1,0:T(8,128)S(1)}, u32[]{:S(2)}, u32[]{:S(2)}) collective-permute-start(f32[72,128]{1,0:T(8,128)S(1)} %add.28), channel_id=1, source_target_pairs={{0,16},{4,20},{8,24},{12,28},{16,0},{20,4},{24,8},{28,12},{1,17},{... | collective-permute-start | bytes 110600 | tf_op jit(solution)/shard_map/ppermute | solution.py:49
  39.5 4.9 %collective-permute-start.11 = (f32[72,128]{1,0:T(8,128)S(1)}, f32[72,128]{1,0:T(8,128)S(1)}, u32[]{:S(2)}, u32[]{:S(2)}) collective-permute-start(f32[72,128]{1,0:T(8,128)S(1)} %add.28), channel_id=1, source_target_pairs={{0,8},{4,12},{8,0},{12,4},{16,24},{20,28},{24,16},{28,20},{1,9},{5... | collective-permute-start | bytes 110600 | tf_op jit(solution)/shard_map/ppermute | solution.py:49
  44.4 5.9 %collective-permute-start.16 = (f32[72,128]{1,0:T(8,128)S(1)}, f32[72,128]{1,0:T(8,128)S(1)}, u32[]{:S(2)}, u32[]{:S(2)}) collective-permute-start(f32[72,128]{1,0:T(8,128)S(1)} %add_add_fusion.1), channel_id=1, source_target_pairs={{0,3},{1,2},{2,1},{3,0},{4,7},{5,6},{6,5},{7,4},{8,11},{9,10},{10,... | collective-permute-start | bytes 110600 | tf_op jit(solution)/shard_map/ppermute | solution.py:49
  48.4 4.0 %collective-permute-start.15 = (f32[72,128]{1,0:T(8,128)S(1)}, f32[72,128]{1,0:T(8,128)S(1)}, u32[]{:S(2)}, u32[]{:S(2)}) collective-permute-start(f32[72,128]{1,0:T(8,128)S(1)} %add_add_fusion.1), channel_id=1, source_target_pairs={{0,2},{1,3},{2,0},{3,1},{4,6},{5,7},{6,4},{7,5},{8,10},{9,11},{10,... | collective-permute-start | bytes 110600 | tf_op jit(solution)/shard_map/ppermute | solution.py:49
  48.4 4.0 %collective-permute-start.14 = (f32[72,128]{1,0:T(8,128)S(1)}, f32[72,128]{1,0:T(8,128)S(1)}, u32[]{:S(2)}, u32[]{:S(2)}) collective-permute-start(f32[72,128]{1,0:T(8,128)S(1)} %add_add_fusion.1), channel_id=1, source_target_pairs={{0,1},{1,0},{2,3},{3,2},{4,5},{5,4},{6,7},{7,6},{8,9},{9,8},{10,11... | collective-permute-start | bytes 110600 | tf_op jit(solution)/shard_map/ppermute | solution.py:49

commit v13 on v11

--- a/solution.py
+++ b/solution.py
@@ -323,8 +323,8 @@
         [block_columns.reshape(-1)] + [origin.reshape(1).astype(jnp.int32) for origin in origins]
     )
     last = cycle_size - 1
-    ending = [cycle_size, last]
-    middle = [1] + list(range(2, last)) + [cycle_size + 1]
+    ending = [last]
+    middle = [cycle_size, 1] + list(range(2, last)) + [cycle_size + 1]
     flat = jax.ShapeDtypeStruct((flat_rows, states), jnp.float32)
     rounded = jax.ShapeDtypeStruct((shard_blocks, block_size, states), jnp.bfloat16)
     packed = jax.ShapeDtypeStruct((states // 2 + SUB, states), jnp.float32)
@@ -337,18 +337,17 @@
 
     def coupled(value, index_array, early, *terms):
         arrived = cycle_exchange(value, 0)
-        outer = pair_exchange(value, 1)
+        pairs = [pair_exchange(value, 0), pair_exchange(value, 1)]
         if early:
             partial = own_part(index_array, value, *terms)
-            later, partial = lax.optimization_barrier((value, partial))
+            later, pairs[0], partial = lax.optimization_barrier((value, pairs[0], partial))
         else:
-            later, index_array = lax.optimization_barrier((value, index_array))
+            later, pairs[0], index_array = lax.optimization_barrier((value, pairs[0], index_array))
         others = [cycle_exchange(later, level) for level in range(1, levels)]
-        arrived, later = lax.optimization_barrier((arrived, later))
         pieces = [value, arrived]
         for level, other in zip(range(1, levels), others):
             pieces += [other] + [cycle_exchange(piece, level) for piece in pieces[1:]]
-        pieces += [pair_exchange(later, 0), outer]
+        pieces += pairs
         if not early:
             partial = own_part(index_array, value, *terms)
         partial = call(
@@ -359,11 +358,11 @@
     weighted = (weights.reshape(-1, 1) * trial_slab)
     parts = coupled(trial_slab.reshape(rounded.shape).astype(jnp.bfloat16), index_array, False, weighted)
     once, once_round = call(
-        functools.partial(first_kernel, ending), (flat, rounded), [smem] + [vmem] * 4
+        functools.partial(first_kernel, ending), (flat, rounded), [smem] + [vmem] * (2 + len(ending))
     )(index_array, hamiltonian, *parts)
     parts = coupled(once_round, index_array, True, weights, once, trial_slab)
     filtered, gram = call(
-        functools.partial(second_kernel, ending), (flat, packed), [smem] + [vmem] * 4
+        functools.partial(second_kernel, ending), (flat, packed), [smem] + [vmem] * (2 + len(ending))
     )(index_array, hamiltonian, *parts)
     gram = summed(gram)
     return call(

time: 56.8 us -> 57.9 us (1.019)
  waiting for transfers between devices: 15.5 us -> 18.6 us
  starting transfers between devices: 24.9 us -> 22.7 us
    ppermute x7, waiting for transfers between devices: 8.4 us -> 11.3 us  [from_partner(): lax.ppermute(value, axis, [(index, index ^ flip) for index in range(count)])]
    ppermute x7, starting transfers between devices: 11.4 us -> 9.24 us  [from_partner(): lax.ppermute(value, axis, [(index, index ^ flip) for index in range(count)])]
    ppermute x6, starting transfers between devices: 10.7 us -> 9.81 us  [cycle_exchange(): return lax.ppermute(value, ('group', 'blk'), route)]
    ppermute x4, starting transfers between devices: 2.79 us -> 3.69 us  [pair_exchange(): return lax.ppermute(value, 'group', route)]
  transfers between devices with their start and end apart: 17 -> 17, of which waited for: 10 -> 11; matrix products, arithmetic and copies ran while one was open for 2% -> 2% of each run, Pallas kernels for 8% -> 8%
where the time goes in v13:
time: 57.9 us; the launch traced here: 57.6 us
  starting transfers between devices  22.7 us (39%)
  waiting for transfers between devices  18.6 us (32%)
  Pallas kernels  11.2 us (19%)
  local copies, waits for them, and re-layouts  2.92 us (5%)
  other arithmetic  1.46 us (3%)
  between operations  0.79 us (1%)
    ppermute x7, waiting for transfers between devices, from_partner(): lax.ppermute(value, axis, [(index, index ^ flip) for index in range(count)])  11.3 us
    ppermute x6, starting transfers between devices, cycle_exchange(): return lax.ppermute(value, ('group', 'blk'), route)  9.81 us
    ppermute x7, starting transfers between devices, from_partner(): lax.ppermute(value, axis, [(index, index ^ flip) for index in range(count)])  9.24 us
    ppermute x6, waiting for transfers between devices, cycle_exchange(): return lax.ppermute(value, ('group', 'blk'), route)  7.26 us
    pallas_call x1, Pallas kernels, on_device(): call(functools.partial(factor_kernel, rows_total), (flat, square), [vmem,...  4.27 us
    ppermute x4, starting transfers between devices, pair_exchange(): return lax.ppermute(value, 'group', route)  3.69 us
    pallas_call x2, Pallas kernels, coupled(): call(functools.partial(middle_kernel, middle), flat, [smem] + [vmem] * (2...  2.93 us
    unnamed x7, local copies, waits for them, and re-layouts  2.72 us
  transfers between devices with their start and end apart: 17, of which 11 were waited for; matrix products, arithmetic and copies ran while one was open for 2% of the time, Pallas kernels for 8%

profile of v13, /device:TPU:0, one launch (start us, length us, event | category | flops | bytes accessed | tf_op | source)
XLA Modules:
  0.0 57.6 jit_solution(11335424437379149101)
XLA Ops:
  0.6 1.4 %broadcast_multiply_fusion = (f32[1024,128]{1,0:T(8,128)S(1)}, bf16[1024,128]{1,0:T(8,128)(2,1)S(1)}) fusion(f32[1024,128]{1,0:T(8,128)} %refs_2_.1, f32[1024]{0:T(1024)} %param.6), kind=kLoop, calls=%fused_computation | loop fusion | flops 262144 | bytes 1314816 | tf_op jit(solution)/shard_map/mul | solution.py:358
  2.1 0.5 collective-permute-start
  2.6 2.6 %collective-permute-start.1 = (bf16[16,64,128]{2,1,0:T(8,128)(2,1)S(1)}, bf16[16,64,128]{2,1,0:T(8,128)(2,1)S(1)}, u32[]{:S(2)}, u32[]{:S(2)}) collective-permute-start(bf16[16,64,128]{2,1,0:T(8,128)(2,1)S(1)} %bitcast.9), channel_id=1, source_target_pairs={{0,1},{1,0},{2,3},{3,2},{4,6},{5,7},{6,4},{7,5},{8,9},{9,8},{10,11... | collective-permute-start | bytes 786440 | tf_op jit(solution)/shard_map/ppermute | solution.py:43
  5.1 0.7 %collective-permute-start.3 = (bf16[16,64,128]{2,1,0:T(8,128)(2,1)S(1)}, bf16[16,64,128]{2,1,0:T(8,128)(2,1)S(1)}, u32[]{:S(2)}, u32[]{:S(2)}) collective-permute-start(bf16[16,64,128]{2,1,0:T(8,128)(2,1)S(1)} %bitcast.10), channel_id=1, source_target_pairs={{4,8},{8,4},{12,16},{16,12},{20,24},{24,20},{5,9},{9,5},{13,17},{1... | collective-permute-start | bytes 786440 | tf_op jit(solution)/shard_map/ppermute | solution.py:25
  5.8 0.8 %copy.6 = s32[16,6,4]{2,1,0:T(8,128)S(1)} copy(s32[16,6,4]{0,2,1:T(4,128)} %param.5) | data formatting | bytes 3072 | tf_op args[1]
  6.7 0.1 reshape.31
  6.8 0.1 concatenate.3.index_ref
  6.9 0.0 collective-permute-done.refs_0_
  6.9 1.6 %collective-permute-start.2 = (bf16[16,64,128]{2,1,0:T(8,128)(2,1)S(1)}, bf16[16,64,128]{2,1,0:T(8,128)(2,1)S(1)}, u32[]{:S(2)}, u32[]{:S(2)}) collective-permute-start(bf16[16,64,128]{2,1,0:T(8,128)(2,1)S(1)} %bitcast.11), channel_id=1, source_target_pairs={{0,2},{1,3},{2,0},{3,1},{4,5},{5,4},{6,7},{7,6},{8,10},{9,11},{10,... | collective-permute-start | bytes 786440 | tf_op jit(solution)/shard_map/ppermute | solution.py:43
  8.4 1.1 %collective-permute-done.1.refs_1_ = bf16[16,64,128]{2,1,0:T(8,128)(2,1)S(1)} collective-permute-done((bf16[16,64,128]{2,1,0:T(8,128)(2,1)S(1)}, bf16[16,64,128]{2,1,0:T(8,128)(2,1)S(1)}, u32[]{:S(2)}, u32[]{:S(2)}) %collective-permute-start.1) | collective-permute-done | bytes 262176 | tf_op jit(solution)/shard_map/ppermute | solution.py:43
  9.5 2.0 %collective-permute-start.4 = (bf16[16,64,128]{2,1,0:T(8,128)(2,1)S(1)}, bf16[16,64,128]{2,1,0:T(8,128)(2,1)S(1)}, u32[]{:S(2)}, u32[]{:S(2)}) collective-permute-start(bf16[16,64,128]{2,1,0:T(8,128)(2,1)S(1)} %collective-permute-done.1.refs_1_), channel_id=1, source_target_pairs={{0,2},{1,3},{2,0},{3,1},{4,5},{5,4},{6,7},{7,6},{8,10},{9,11},{10,... | collective-permute-start | bytes 786440 | tf_op jit(solution)/shard_map/ppermute | solution.py:43
  11.5 0.0 copy-start
  11.5 1.9 %copy-done = bf16[16,6,64,256]{3,2,1,0:T(8,128)(2,1)S(1)} copy-done((bf16[16,6,64,256]{3,2,1,0:T(8,128)(2,1)S(1)}, bf16[16,6,64,256]{3,2,1,0:T(8,128)(2,1)}, u32[]{:S(2)}) %copy-start) | copy-done | bytes 3145752
  13.4 0.9 %shard_map.59.partial_ref = f32[1024,128]{1,0:T(8,128)S(1)} custom-call(s32[390]{0:T(512)S(1)} %concatenate.3.index_ref, bf16[16,6,64,256]{3,2,1,0:T(8,128)(2,1)S(1)} %copy-done, bf16[16,64,128]{2,1,0:T(8,128)(2,1)S(1)} %bitcast.12, f32[1024,128]{1,0:T(8,128)S(1)} %get-tuple-element.22.refs_0_), custom_call_target="tpu_custom_call" | custom-call | tf_op jit(solution)/shard_map/pallas_call | solution.py:334
  14.3 0.0 collective-permute-done.3.refs_3_
  14.3 0.0 collective-permute-done.2.refs_2_
  14.4 1.5 %shard_map.60.partial_ref = f32[1024,128]{1,0:T(8,128)S(1)} custom-call(s32[390]{0:T(512)S(1)} %concatenate.3.index_ref, bf16[16,6,64,256]{3,2,1,0:T(8,128)(2,1)S(1)} %copy-done, f32[1024,128]{1,0:T(8,128)S(1)} %shard_map.59.partial_ref, bf16[16,64,128]{2,1,0:T(8,128)(2,1)S(1)} %collective-permute-done.refs_0_, ...), custom_call_target="tpu_custom_call" | custom-call | tf_op jit(solution)/shard_map/pallas_call | solution.py:353
  15.8 0.0 copy-start.1
  15.8 0.0 copy-start.2
  15.9 0.2 collective-permute-done.4.refs_0_
  16.1 0.9 %shard_map.61 = (f32[1024,128]{1,0:T(8,128)S(1)}, bf16[16,64,128]{2,1,0:T(8,128)(2,1)S(1)}) custom-call(s32[390]{0:T(512)S(1)} %concatenate.3.index_ref, bf16[16,6,64,256]{3,2,1,0:T(8,128)(2,1)S(1)} %copy-done, f32[1024,128]{1,0:T(8,128)S(1)} %shard_map.60.partial_ref, bf16[16,64,128]{2,1,0:T(8,128)(2,1)S(1)} %collective-permute-done.4.refs_0_), custom_call_target="tpu_custom_call" | custom-call | tf_op jit(solution)/shard_map/pallas_call | solution.py:360
  17.0 1.8 %collective-permute-start.5 = (bf16[16,64,128]{2,1,0:T(8,128)(2,1)S(1)}, bf16[16,64,128]{2,1,0:T(8,128)(2,1)S(1)}, u32[]{:S(2)}, u32[]{:S(2)}) collective-permute-start(bf16[16,64,128]{2,1,0:T(8,128)(2,1)S(1)} %get-tuple-element.19.own_ref), channel_id=1, source_target_pairs={{0,4},{4,0},{8,12},{12,8},{16,20},{20,16},{24,28},{28,24},{1,5},{5... | collective-permute-start | bytes 786440 | tf_op jit(solution)/shard_map/ppermute | solution.py:25
  18.8 0.5 collective-permute-start.6
  19.3 0.7 %collective-permute-start.8 = (bf16[16,64,128]{2,1,0:T(8,128)(2,1)S(1)}, bf16[16,64,128]{2,1,0:T(8,128)(2,1)S(1)}, u32[]{:S(2)}, u32[]{:S(2)}) collective-permute-start(bf16[16,64,128]{2,1,0:T(8,128)(2,1)S(1)} %get-tuple-element.19.own_ref), channel_id=1, source_target_pairs={{4,8},{8,4},{12,16},{16,12},{20,24},{24,20},{5,9},{9,5},{13,17},{1... | collective-permute-start | bytes 786440 | tf_op jit(solution)/shard_map/ppermute | solution.py:25
  20.0 0.0 copy-done.1
  20.0 0.0 copy-done.2
  20.0 1.0 %shard_map.62.partial_ref = f32[1024,128]{1,0:T(8,128)S(1)} custom-call(s32[390]{0:T(512)S(1)} %concatenate.3.index_ref, bf16[16,6,64,256]{3,2,1,0:T(8,128)(2,1)S(1)} %copy-done, bf16[16,64,128]{2,1,0:T(8,128)(2,1)S(1)} %get-tuple-element.19.own_ref, f32[8,128]{1,0:T(8,128)S(1)} %bitcast.13, f32[1024,128]{1,0:T(8,128)S(1)} %get-tuple-element.16.refs_1_, ...), custom_call_target="tpu_custom_call" | custom-call | tf_op jit(solution)/shard_map/pallas_call | solution.py:334
  21.0 0.0 collective-permute-done.5.refs_0_
  21.0 1.6 %collective-permute-start.7 = (bf16[16,64,128]{2,1,0:T(8,128)(2,1)S(1)}, bf16[16,64,128]{2,1,0:T(8,128)(2,1)S(1)}, u32[]{:S(2)}, u32[]{:S(2)}) collective-permute-start(bf16[16,64,128]{2,1,0:T(8,128)(2,1)S(1)} %get-tuple-element.19.own_ref), channel_id=1, source_target_pairs={{0,2},{1,3},{2,0},{3,1},{4,5},{5,4},{6,7},{7,6},{8,10},{9,11},{10,... | collective-permute-start | bytes 786440 | tf_op jit(solution)/shard_map/ppermute | solution.py:43
  22.6 2.6 %collective-permute-done.6.refs_1_ = bf16[16,64,128]{2,1,0:T(8,128)(2,1)S(1)} collective-permute-done((bf16[16,64,128]{2,1,0:T(8,128)(2,1)S(1)}, bf16[16,64,128]{2,1,0:T(8,128)(2,1)S(1)}, u32[]{:S(2)}, u32[]{:S(2)}) %collective-permute-start.6) | collective-permute-done | bytes 262176 | tf_op jit(solution)/shard_map/ppermute | solution.py:43
  25.2 1.5 %collective-permute-start.9 = (bf16[16,64,128]{2,1,0:T(8,128)(2,1)S(1)}, bf16[16,64,128]{2,1,0:T(8,128)(2,1)S(1)}, u32[]{:S(2)}, u32[]{:S(2)}) collective-permute-start(bf16[16,64,128]{2,1,0:T(8,128)(2,1)S(1)} %collective-permute-done.6.refs_1_), channel_id=1, source_target_pairs={{0,2},{1,3},{2,0},{3,1},{4,5},{5,4},{6,7},{7,6},{8,10},{9,11},{10,... | collective-permute-start | bytes 786440 | tf_op jit(solution)/shard_map/ppermute | solution.py:43
  26.7 0.0 collective-permute-done.8.refs_3_
  26.7 0.8 %collective-permute-done.7.refs_2_ = bf16[16,64,128]{2,1,0:T(8,128)(2,1)S(1)} collective-permute-done((bf16[16,64,128]{2,1,0:T(8,128)(2,1)S(1)}, bf16[16,64,128]{2,1,0:T(8,128)(2,1)S(1)}, u32[]{:S(2)}, u32[]{:S(2)}) %collective-permute-start.7) | collective-permute-done | bytes 262176 | tf_op jit(solution)/shard_map/ppermute | solution.py:43
  27.5 1.5 %shard_map.63.partial_ref = f32[1024,128]{1,0:T(8,128)S(1)} custom-call(s32[390]{0:T(512)S(1)} %concatenate.3.index_ref, bf16[16,6,64,256]{3,2,1,0:T(8,128)(2,1)S(1)} %copy-done, f32[1024,128]{1,0:T(8,128)S(1)} %shard_map.62.partial_ref, bf16[16,64,128]{2,1,0:T(8,128)(2,1)S(1)} %collective-permute-done.5.refs_0_, ...), custom_call_target="tpu_custom_call" | custom-call | tf_op jit(solution)/shard_map/pallas_call | solution.py:353
  28.9 2.6 %collective-permute-done.9.refs_0_ = bf16[16,64,128]{2,1,0:T(8,128)(2,1)S(1)} collective-permute-done((bf16[16,64,128]{2,1,0:T(8,128)(2,1)S(1)}, bf16[16,64,128]{2,1,0:T(8,128)(2,1)S(1)}, u32[]{:S(2)}, u32[]{:S(2)}) %collective-permute-start.9) | collective-permute-done | bytes 262176 | tf_op jit(solution)/shard_map/ppermute | solution.py:43
  31.6 1.2 %shard_map.64 = (f32[1024,128]{1,0:T(8,128)S(1)}, f32[72,128]{1,0:T(8,128)S(1)}) custom-call(s32[390]{0:T(512)S(1)} %concatenate.3.index_ref, bf16[16,6,64,256]{3,2,1,0:T(8,128)(2,1)S(1)} %copy-done, f32[1024,128]{1,0:T(8,128)S(1)} %shard_map.63.partial_ref, bf16[16,64,128]{2,1,0:T(8,128)(2,1)S(1)} %collective-permute-done.9.refs_0_), custom_call_target="tpu_custom_call" | custom-call | tf_op jit(solution)/shard_map/pallas_call | solution.py:364
  32.8 1.3 %collective-permute-start.10 = (f32[72,128]{1,0:T(8,128)S(1)}, f32[72,128]{1,0:T(8,128)S(1)}, u32[]{:S(2)}, u32[]{:S(2)}) collective-permute-start(f32[72,128]{1,0:T(8,128)S(1)} %get-tuple-element.20), channel_id=1, source_target_pairs={{0,4},{4,0},{8,12},{12,8},{16,20},{20,16},{24,28},{28,24},{1,5},{5... | collective-permute-start | bytes 110600 | tf_op jit(solution)/shard_map/ppermute | solution.py:48
  34.1 0.9 %collective-permute-done.10 = f32[72,128]{1,0:T(8,128)S(1)} collective-permute-done((f32[72,128]{1,0:T(8,128)S(1)}, f32[72,128]{1,0:T(8,128)S(1)}, u32[]{:S(2)}, u32[]{:S(2)}) %collective-permute-start.10) | collective-permute-done | bytes 36896 | tf_op jit(solution)/shard_map/ppermute | solution.py:48
  34.9 1.6 %collective-permute-start.11 = (f32[72,128]{1,0:T(8,128)S(1)}, f32[72,128]{1,0:T(8,128)S(1)}, u32[]{:S(2)}, u32[]{:S(2)}) collective-permute-start(f32[72,128]{1,0:T(8,128)S(1)} %add.28), channel_id=1, source_target_pairs={{0,8},{4,12},{8,0},{12,4},{16,24},{20,28},{24,16},{28,20},{1,9},{5... | collective-permute-start | bytes 110600 | tf_op jit(solution)/shard_map/ppermute | solution.py:48
  36.5 2.6 %collective-permute-start.12 = (f32[72,128]{1,0:T(8,128)S(1)}, f32[72,128]{1,0:T(8,128)S(1)}, u32[]{:S(2)}, u32[]{:S(2)}) collective-permute-start(f32[72,128]{1,0:T(8,128)S(1)} %add.28), channel_id=1, source_target_pairs={{0,16},{4,20},{8,24},{12,28},{16,0},{20,4},{24,8},{28,12},{1,17},{... | collective-permute-start | bytes 110600 | tf_op jit(solution)/shard_map/ppermute | solution.py:48
  39.2 0.2 collective-permute-start.13
  39.3 0.0 collective-permute-done.11
  39.3 2.7 %collective-permute-done.12 = f32[72,128]{1,0:T(8,128)S(1)} collective-permute-done((f32[72,128]{1,0:T(8,128)S(1)}, f32[72,128]{1,0:T(8,128)S(1)}, u32[]{:S(2)}, u32[]{:S(2)}) %collective-permute-start.12) | collective-permute-done | bytes 36896 | tf_op jit(solution)/shard_map/ppermute | solution.py:48
  42.1 2.9 %collective-permute-done.13 = f32[72,128]{1,0:T(8,128)S(1)} collective-permute-done((f32[72,128]{1,0:T(8,128)S(1)}, f32[72,128]{1,0:T(8,128)S(1)}, u32[]{:S(2)}, u32[]{:S(2)}) %collective-permute-start.13) | collective-permute-done | bytes 36896 | tf_op jit(solution)/shard_map/ppermute | solution.py:48
  44.9 1.6 %collective-permute-start.14 = (f32[72,128]{1,0:T(8,128)S(1)}, f32[72,128]{1,0:T(8,128)S(1)}, u32[]{:S(2)}, u32[]{:S(2)}) collective-permute-start(f32[72,128]{1,0:T(8,128)S(1)} %add_add_fusion.1), channel_id=1, source_target_pairs={{0,1},{1,0},{2,3},{3,2},{4,5},{5,4},{6,7},{7,6},{8,9},{9,8},{10,11... | collective-permute-start | bytes 110600 | tf_op jit(solution)/shard_map/ppermute | solution.py:48
  46.5 2.0 %collective-permute-start.15 = (f32[72,128]{1,0:T(8,128)S(1)}, f32[72,128]{1,0:T(8,128)S(1)}, u32[]{:S(2)}, u32[]{:S(2)}) collective-permute-start(f32[72,128]{1,0:T(8,128)S(1)} %add_add_fusion.1), channel_id=1, source_target_pairs={{0,2},{1,3},{2,0},{3,1},{4,6},{5,7},{6,4},{7,5},{8,10},{9,11},{10,... | collective-permute-start | bytes 110600 | tf_op jit(solution)/shard_map/ppermute | solution.py:48
  48.5 0.0 collective-permute-start.16
  48.5 0.7 %collective-permute-done.14 = f32[72,128]{1,0:T(8,128)S(1)} collective-permute-done((f32[72,128]{1,0:T(8,128)S(1)}, f32[72,128]{1,0:T(8,128)S(1)}, u32[]{:S(2)}, u32[]{:S(2)}) %collective-permute-start.14) | collective-permute-done | bytes 36896 | tf_op jit(solution)/shard_map/ppermute | solution.py:48
  49.2 1.5 %collective-permute-done.15 = f32[72,128]{1,0:T(8,128)S(1)} collective-permute-done((f32[72,128]{1,0:T(8,128)S(1)}, f32[72,128]{1,0:T(8,128)S(1)}, u32[]{:S(2)}, u32[]{:S(2)}) %collective-permute-start.15) | collective-permute-done | bytes 36896 | tf_op jit(solution)/shard_map/ppermute | solution.py:48
  50.7 2.7 %collective-permute-done.16 = f32[72,128]{1,0:T(8,128)S(1)} collective-permute-done((f32[72,128]{1,0:T(8,128)S(1)}, f32[72,128]{1,0:T(8,128)S(1)}, u32[]{:S(2)}, u32[]{:S(2)}) %collective-permute-start.16) | collective-permute-done | bytes 36896 | tf_op jit(solution)/shard_map/ppermute | solution.py:48
  53.4 4.3 %shard_map.65 = (f32[1024,128]{1,0:T(8,128)}, f32[128,128]{1,0:T(8,128)}) custom-call(f32[72,128]{1,0:T(8,128)S(1)} %add_add_fusion.packed_ref, f32[1024,128]{1,0:T(8,128)S(1)} %get-tuple-element.21.filtered_ref), custom_call_target="tpu_custom_call" | custom-call | tf_op jit(solution)/shard_map/pallas_call | solution.py:368
  (3 shorter events, 0.0 us)
Async XLA Ops:
  2.1 4.8 %collective-permute-start = (bf16[16,64,128]{2,1,0:T(8,128)(2,1)S(1)}, bf16[16,64,128]{2,1,0:T(8,128)(2,1)S(1)}, u32[]{:S(2)}, u32[]{:S(2)}) collective-permute-start(bf16[16,64,128]{2,1,0:T(8,128)(2,1)S(1)} %bitcast.8), channel_id=1, source_target_pairs={{0,4},{4,0},{8,12},{12,8},{16,20},{20,16},{24,28},{28,24},{1,5},{5... | collective-permute-start | bytes 786440 | tf_op jit(solution)/shard_map/ppermute | solution.py:25
  2.6 6.9 %collective-permute-start.1 = (bf16[16,64,128]{2,1,0:T(8,128)(2,1)S(1)}, bf16[16,64,128]{2,1,0:T(8,128)(2,1)S(1)}, u32[]{:S(2)}, u32[]{:S(2)}) collective-permute-start(bf16[16,64,128]{2,1,0:T(8,128)(2,1)S(1)} %bitcast.9), channel_id=1, source_target_pairs={{0,1},{1,0},{2,3},{3,2},{4,6},{5,7},{6,4},{7,5},{8,9},{9,8},{10,11... | collective-permute-start | bytes 786440 | tf_op jit(solution)/shard_map/ppermute | solution.py:43
  5.1 9.2 %collective-permute-start.3 = (bf16[16,64,128]{2,1,0:T(8,128)(2,1)S(1)}, bf16[16,64,128]{2,1,0:T(8,128)(2,1)S(1)}, u32[]{:S(2)}, u32[]{:S(2)}) collective-permute-start(bf16[16,64,128]{2,1,0:T(8,128)(2,1)S(1)} %bitcast.10), channel_id=1, source_target_pairs={{4,8},{8,4},{12,16},{16,12},{20,24},{24,20},{5,9},{9,5},{13,17},{1... | collective-permute-start | bytes 786440 | tf_op jit(solution)/shard_map/ppermute | solution.py:25
  6.9 7.5 %collective-permute-start.2 = (bf16[16,64,128]{2,1,0:T(8,128)(2,1)S(1)}, bf16[16,64,128]{2,1,0:T(8,128)(2,1)S(1)}, u32[]{:S(2)}, u32[]{:S(2)}) collective-permute-start(bf16[16,64,128]{2,1,0:T(8,128)(2,1)S(1)} %bitcast.11), channel_id=1, source_target_pairs={{0,2},{1,3},{2,0},{3,1},{4,5},{5,4},{6,7},{7,6},{8,10},{9,11},{10,... | collective-permute-start | bytes 786440 | tf_op jit(solution)/shard_map/ppermute | solution.py:43
  9.5 6.6 %collective-permute-start.4 = (bf16[16,64,128]{2,1,0:T(8,128)(2,1)S(1)}, bf16[16,64,128]{2,1,0:T(8,128)(2,1)S(1)}, u32[]{:S(2)}, u32[]{:S(2)}) collective-permute-start(bf16[16,64,128]{2,1,0:T(8,128)(2,1)S(1)} %collective-permute-done.1.refs_1_), channel_id=1, source_target_pairs={{0,2},{1,3},{2,0},{3,1},{4,5},{5,4},{6,7},{7,6},{8,10},{9,11},{10,... | collective-permute-start | bytes 786440 | tf_op jit(solution)/shard_map/ppermute | solution.py:43
  11.5 1.9 %copy-start = (bf16[16,6,64,256]{3,2,1,0:T(8,128)(2,1)S(1)}, bf16[16,6,64,256]{3,2,1,0:T(8,128)(2,1)}, u32[]{:S(2)}) copy-start(bf16[16,6,64,256]{3,2,1,0:T(8,128)(2,1)} %hamiltonian_ref.11) | copy-start | bytes 9437188
  15.8 4.2 %copy-start.1 = (f32[1024,128]{1,0:T(8,128)S(1)}, f32[1024,128]{1,0:T(8,128)}, u32[]{:S(2)}) copy-start(f32[1024,128]{1,0:T(8,128)} %refs_2_.1) | copy-start | bytes 1572868
  15.8 4.2 %copy-start.2 = (f32[1024]{0:T(1024)S(1)}, f32[1024]{0:T(1024)}, u32[]{:S(2)}) copy-start(f32[1024]{0:T(1024)} %param.6) | copy-start | bytes 12292
  17.0 4.0 %collective-permute-start.5 = (bf16[16,64,128]{2,1,0:T(8,128)(2,1)S(1)}, bf16[16,64,128]{2,1,0:T(8,128)(2,1)S(1)}, u32[]{:S(2)}, u32[]{:S(2)}) collective-permute-start(bf16[16,64,128]{2,1,0:T(8,128)(2,1)S(1)} %get-tuple-element.19.own_ref), channel_id=1, source_target_pairs={{0,4},{4,0},{8,12},{12,8},{16,20},{20,16},{24,28},{28,24},{1,5},{5... | collective-permute-start | bytes 786440 | tf_op jit(solution)/shard_map/ppermute | solution.py:25
  18.8 6.4 %collective-permute-start.6 = (bf16[16,64,128]{2,1,0:T(8,128)(2,1)S(1)}, bf16[16,64,128]{2,1,0:T(8,128)(2,1)S(1)}, u32[]{:S(2)}, u32[]{:S(2)}) collective-permute-start(bf16[16,64,128]{2,1,0:T(8,128)(2,1)S(1)} %get-tuple-element.19.own_ref), channel_id=1, source_target_pairs={{0,1},{1,0},{2,3},{3,2},{4,6},{5,7},{6,4},{7,5},{8,9},{9,8},{10,11... | collective-permute-start | bytes 786440 | tf_op jit(solution)/shard_map/ppermute | solution.py:43
  19.3 7.4 %collective-permute-start.8 = (bf16[16,64,128]{2,1,0:T(8,128)(2,1)S(1)}, bf16[16,64,128]{2,1,0:T(8,128)(2,1)S(1)}, u32[]{:S(2)}, u32[]{:S(2)}) collective-permute-start(bf16[16,64,128]{2,1,0:T(8,128)(2,1)S(1)} %get-tuple-element.19.own_ref), channel_id=1, source_target_pairs={{4,8},{8,4},{12,16},{16,12},{20,24},{24,20},{5,9},{9,5},{13,17},{1... | collective-permute-start | bytes 786440 | tf_op jit(solution)/shard_map/ppermute | solution.py:25
  21.0 6.4 %collective-permute-start.7 = (bf16[16,64,128]{2,1,0:T(8,128)(2,1)S(1)}, bf16[16,64,128]{2,1,0:T(8,128)(2,1)S(1)}, u32[]{:S(2)}, u32[]{:S(2)}) collective-permute-start(bf16[16,64,128]{2,1,0:T(8,128)(2,1)S(1)} %get-tuple-element.19.own_ref), channel_id=1, source_target_pairs={{0,2},{1,3},{2,0},{3,1},{4,5},{5,4},{6,7},{7,6},{8,10},{9,11},{10,... | collective-permute-start | bytes 786440 | tf_op jit(solution)/shard_map/ppermute | solution.py:43
  25.2 6.4 %collective-permute-start.9 = (bf16[16,64,128]{2,1,0:T(8,128)(2,1)S(1)}, bf16[16,64,128]{2,1,0:T(8,128)(2,1)S(1)}, u32[]{:S(2)}, u32[]{:S(2)}) collective-permute-start(bf16[16,64,128]{2,1,0:T(8,128)(2,1)S(1)} %collective-permute-done.6.refs_1_), channel_id=1, source_target_pairs={{0,2},{1,3},{2,0},{3,1},{4,5},{5,4},{6,7},{7,6},{8,10},{9,11},{10,... | collective-permute-start | bytes 786440 | tf_op jit(solution)/shard_map/ppermute | solution.py:43
  32.8 2.1 %collective-permute-start.10 = (f32[72,128]{1,0:T(8,128)S(1)}, f32[72,128]{1,0:T(8,128)S(1)}, u32[]{:S(2)}, u32[]{:S(2)}) collective-permute-start(f32[72,128]{1,0:T(8,128)S(1)} %get-tuple-element.20), channel_id=1, source_target_pairs={{0,4},{4,0},{8,12},{12,8},{16,20},{20,16},{24,28},{28,24},{1,5},{5... | collective-permute-start | bytes 110600 | tf_op jit(solution)/shard_map/ppermute | solution.py:48
  34.9 4.4 %collective-permute-start.11 = (f32[72,128]{1,0:T(8,128)S(1)}, f32[72,128]{1,0:T(8,128)S(1)}, u32[]{:S(2)}, u32[]{:S(2)}) collective-permute-start(f32[72,128]{1,0:T(8,128)S(1)} %add.28), channel_id=1, source_target_pairs={{0,8},{4,12},{8,0},{12,4},{16,24},{20,28},{24,16},{28,20},{1,9},{5... | collective-permute-start | bytes 110600 | tf_op jit(solution)/shard_map/ppermute | solution.py:48
  36.5 5.5 %collective-permute-start.12 = (f32[72,128]{1,0:T(8,128)S(1)}, f32[72,128]{1,0:T(8,128)S(1)}, u32[]{:S(2)}, u32[]{:S(2)}) collective-permute-start(f32[72,128]{1,0:T(8,128)S(1)} %add.28), channel_id=1, source_target_pairs={{0,16},{4,20},{8,24},{12,28},{16,0},{20,4},{24,8},{28,12},{1,17},{... | collective-permute-start | bytes 110600 | tf_op jit(solution)/shard_map/ppermute | solution.py:48
  39.2 5.8 %collective-permute-start.13 = (f32[72,128]{1,0:T(8,128)S(1)}, f32[72,128]{1,0:T(8,128)S(1)}, u32[]{:S(2)}, u32[]{:S(2)}) collective-permute-start(f32[72,128]{1,0:T(8,128)S(1)} %add.28), channel_id=1, source_target_pairs={{0,24},{4,28},{8,16},{12,20},{16,8},{20,12},{24,0},{28,4},{1,25},{... | collective-permute-start | bytes 110600 | tf_op jit(solution)/shard_map/ppermute | solution.py:48
  44.9 4.3 %collective-permute-start.14 = (f32[72,128]{1,0:T(8,128)S(1)}, f32[72,128]{1,0:T(8,128)S(1)}, u32[]{:S(2)}, u32[]{:S(2)}) collective-permute-start(f32[72,128]{1,0:T(8,128)S(1)} %add_add_fusion.1), channel_id=1, source_target_pairs={{0,1},{1,0},{2,3},{3,2},{4,5},{5,4},{6,7},{7,6},{8,9},{9,8},{10,11... | collective-permute-start | bytes 110600 | tf_op jit(solution)/shard_map/ppermute | solution.py:48
  46.5 4.2 %collective-permute-start.15 = (f32[72,128]{1,0:T(8,128)S(1)}, f32[72,128]{1,0:T(8,128)S(1)}, u32[]{:S(2)}, u32[]{:S(2)}) collective-permute-start(f32[72,128]{1,0:T(8,128)S(1)} %add_add_fusion.1), channel_id=1, source_target_pairs={{0,2},{1,3},{2,0},{3,1},{4,6},{5,7},{6,4},{7,5},{8,10},{9,11},{10,... | collective-permute-start | bytes 110600 | tf_op jit(solution)/shard_map/ppermute | solution.py:48
  48.5 4.9 %collective-permute-start.16 = (f32[72,128]{1,0:T(8,128)S(1)}, f32[72,128]{1,0:T(8,128)S(1)}, u32[]{:S(2)}, u32[]{:S(2)}) collective-permute-start(f32[72,128]{1,0:T(8,128)S(1)} %add_add_fusion.1), channel_id=1, source_target_pairs={{0,3},{1,2},{2,1},{3,0},{4,7},{5,6},{6,5},{7,4},{8,11},{9,10},{10,... | collective-permute-start | bytes 110600 | tf_op jit(solution)/shard_map/ppermute | solution.py:48

commit v14 on v13

--- a/solution.py
+++ b/solution.py
@@ -54,9 +54,9 @@
         while step < count:
             flips = [step, 2 * step, 3 * step] if 2 * step < count else [step]
             others = [from_partner(value, axis, flip) for flip in flips]
-            value = value + others[0]
+            value = others[0] + value
             if len(others) == 3:
-                value = value + (others[1] + others[2])
+                value = (others[2] + others[1]) + value
             step *= len(flips) + 1
     return value
 

time: 57.9 us -> 55 us (0.950)
  waiting for transfers between devices: 18.6 us -> 15.6 us
    ppermute x7, waiting for transfers between devices: 11.3 us -> 8.31 us  [from_partner(): lax.ppermute(value, axis, [(index, index ^ flip) for index in range(count)])]
  transfers between devices with their start and end apart: 17 -> 17, of which waited for: 11 -> 10; matrix products, arithmetic and copies ran while one was open for 2% -> 2% of each run, Pallas kernels for 8% -> 9%
where the time goes in v14:
time: 55 us; the launch traced here: 54.7 us
  starting transfers between devices  22.8 us (41%)
  waiting for transfers between devices  15.6 us (28%)
  Pallas kernels  11.2 us (20%)
  local copies, waits for them, and re-layouts  2.92 us (5%)
  other arithmetic  1.46 us (3%)
  between operations  0.79 us (1%)
    ppermute x6, starting transfers between devices, cycle_exchange(): return lax.ppermute(value, ('group', 'blk'), route)  9.81 us
    ppermute x7, starting transfers between devices, from_partner(): lax.ppermute(value, axis, [(index, index ^ flip) for index in range(count)])  9.32 us
    ppermute x7, waiting for transfers between devices, from_partner(): lax.ppermute(value, axis, [(index, index ^ flip) for index in range(count)])  8.31 us
    ppermute x6, waiting for transfers between devices, cycle_exchange(): return lax.ppermute(value, ('group', 'blk'), route)  7.26 us
    pallas_call x1, Pallas kernels, on_device(): call(functools.partial(factor_kernel, rows_total), (flat, square), [vmem,...  4.27 us
    ppermute x4, starting transfers between devices, pair_exchange(): return lax.ppermute(value, 'group', route)  3.69 us
    pallas_call x2, Pallas kernels, coupled(): call(functools.partial(middle_kernel, middle), flat, [smem] + [vmem] * (2...  2.93 us
    unnamed x7, local copies, waits for them, and re-layouts  2.72 us
  transfers between devices with their start and end apart: 17, of which 10 were waited for; matrix products, arithmetic and copies ran while one was open for 2% of the time, Pallas kernels for 9%

profile of v14, /device:TPU:0, one launch (start us, length us, event | category | flops | bytes accessed | tf_op | source)
XLA Modules:
  0.0 54.7 jit_solution(13106973036624062927)
XLA Ops:
  0.6 1.4 %broadcast_multiply_fusion = (f32[1024,128]{1,0:T(8,128)S(1)}, bf16[1024,128]{1,0:T(8,128)(2,1)S(1)}) fusion(f32[1024,128]{1,0:T(8,128)} %refs_2_.1, f32[1024]{0:T(1024)} %param.6), kind=kLoop, calls=%fused_computation | loop fusion | flops 262144 | bytes 1314816 | tf_op jit(solution)/shard_map/mul | solution.py:358
  2.1 0.5 collective-permute-start
  2.6 2.6 %collective-permute-start.1 = (bf16[16,64,128]{2,1,0:T(8,128)(2,1)S(1)}, bf16[16,64,128]{2,1,0:T(8,128)(2,1)S(1)}, u32[]{:S(2)}, u32[]{:S(2)}) collective-permute-start(bf16[16,64,128]{2,1,0:T(8,128)(2,1)S(1)} %bitcast.9), channel_id=1, source_target_pairs={{0,1},{1,0},{2,3},{3,2},{4,6},{5,7},{6,4},{7,5},{8,9},{9,8},{10,11... | collective-permute-start | bytes 786440 | tf_op jit(solution)/shard_map/ppermute | solution.py:43
  5.1 0.7 %collective-permute-start.3 = (bf16[16,64,128]{2,1,0:T(8,128)(2,1)S(1)}, bf16[16,64,128]{2,1,0:T(8,128)(2,1)S(1)}, u32[]{:S(2)}, u32[]{:S(2)}) collective-permute-start(bf16[16,64,128]{2,1,0:T(8,128)(2,1)S(1)} %bitcast.10), channel_id=1, source_target_pairs={{4,8},{8,4},{12,16},{16,12},{20,24},{24,20},{5,9},{9,5},{13,17},{1... | collective-permute-start | bytes 786440 | tf_op jit(solution)/shard_map/ppermute | solution.py:25
  5.8 0.8 %copy.6 = s32[16,6,4]{2,1,0:T(8,128)S(1)} copy(s32[16,6,4]{0,2,1:T(4,128)} %param.5) | data formatting | bytes 3072 | tf_op args[1]
  6.7 0.1 reshape.31
  6.8 0.1 concatenate.3.index_ref
  6.9 0.0 collective-permute-done.refs_0_
  6.9 1.6 %collective-permute-start.2 = (bf16[16,64,128]{2,1,0:T(8,128)(2,1)S(1)}, bf16[16,64,128]{2,1,0:T(8,128)(2,1)S(1)}, u32[]{:S(2)}, u32[]{:S(2)}) collective-permute-start(bf16[16,64,128]{2,1,0:T(8,128)(2,1)S(1)} %bitcast.11), channel_id=1, source_target_pairs={{0,2},{1,3},{2,0},{3,1},{4,5},{5,4},{6,7},{7,6},{8,10},{9,11},{10,... | collective-permute-start | bytes 786440 | tf_op jit(solution)/shard_map/ppermute | solution.py:43
  8.4 1.1 %collective-permute-done.1.refs_1_ = bf16[16,64,128]{2,1,0:T(8,128)(2,1)S(1)} collective-permute-done((bf16[16,64,128]{2,1,0:T(8,128)(2,1)S(1)}, bf16[16,64,128]{2,1,0:T(8,128)(2,1)S(1)}, u32[]{:S(2)}, u32[]{:S(2)}) %collective-permute-start.1) | collective-permute-done | bytes 262176 | tf_op jit(solution)/shard_map/ppermute | solution.py:43
  9.5 2.0 %collective-permute-start.4 = (bf16[16,64,128]{2,1,0:T(8,128)(2,1)S(1)}, bf16[16,64,128]{2,1,0:T(8,128)(2,1)S(1)}, u32[]{:S(2)}, u32[]{:S(2)}) collective-permute-start(bf16[16,64,128]{2,1,0:T(8,128)(2,1)S(1)} %collective-permute-done.1.refs_1_), channel_id=1, source_target_pairs={{0,2},{1,3},{2,0},{3,1},{4,5},{5,4},{6,7},{7,6},{8,10},{9,11},{10,... | collective-permute-start | bytes 786440 | tf_op jit(solution)/shard_map/ppermute | solution.py:43
  11.5 0.0 copy-start
  11.5 1.9 %copy-done = bf16[16,6,64,256]{3,2,1,0:T(8,128)(2,1)S(1)} copy-done((bf16[16,6,64,256]{3,2,1,0:T(8,128)(2,1)S(1)}, bf16[16,6,64,256]{3,2,1,0:T(8,128)(2,1)}, u32[]{:S(2)}) %copy-start) | copy-done | bytes 3145752
  13.4 0.9 %shard_map.59.partial_ref = f32[1024,128]{1,0:T(8,128)S(1)} custom-call(s32[390]{0:T(512)S(1)} %concatenate.3.index_ref, bf16[16,6,64,256]{3,2,1,0:T(8,128)(2,1)S(1)} %copy-done, bf16[16,64,128]{2,1,0:T(8,128)(2,1)S(1)} %bitcast.12, f32[1024,128]{1,0:T(8,128)S(1)} %get-tuple-element.22.refs_0_), custom_call_target="tpu_custom_call" | custom-call | tf_op jit(solution)/shard_map/pallas_call | solution.py:334
  14.3 0.0 collective-permute-done.3.refs_3_
  14.3 0.0 collective-permute-done.2.refs_2_
  14.4 1.5 %shard_map.60.partial_ref = f32[1024,128]{1,0:T(8,128)S(1)} custom-call(s32[390]{0:T(512)S(1)} %concatenate.3.index_ref, bf16[16,6,64,256]{3,2,1,0:T(8,128)(2,1)S(1)} %copy-done, f32[1024,128]{1,0:T(8,128)S(1)} %shard_map.59.partial_ref, bf16[16,64,128]{2,1,0:T(8,128)(2,1)S(1)} %collective-permute-done.refs_0_, ...), custom_call_target="tpu_custom_call" | custom-call | tf_op jit(solution)/shard_map/pallas_call | solution.py:353
  15.8 0.0 copy-start.1
  15.8 0.0 copy-start.2
  15.9 0.2 collective-permute-done.4.refs_0_
  16.1 0.9 %shard_map.61 = (f32[1024,128]{1,0:T(8,128)S(1)}, bf16[16,64,128]{2,1,0:T(8,128)(2,1)S(1)}) custom-call(s32[390]{0:T(512)S(1)} %concatenate.3.index_ref, bf16[16,6,64,256]{3,2,1,0:T(8,128)(2,1)S(1)} %copy-done, f32[1024,128]{1,0:T(8,128)S(1)} %shard_map.60.partial_ref, bf16[16,64,128]{2,1,0:T(8,128)(2,1)S(1)} %collective-permute-done.4.refs_0_), custom_call_target="tpu_custom_call" | custom-call | tf_op jit(solution)/shard_map/pallas_call | solution.py:360
  17.0 1.8 %collective-permute-start.5 = (bf16[16,64,128]{2,1,0:T(8,128)(2,1)S(1)}, bf16[16,64,128]{2,1,0:T(8,128)(2,1)S(1)}, u32[]{:S(2)}, u32[]{:S(2)}) collective-permute-start(bf16[16,64,128]{2,1,0:T(8,128)(2,1)S(1)} %get-tuple-element.19.own_ref), channel_id=1, source_target_pairs={{0,4},{4,0},{8,12},{12,8},{16,20},{20,16},{24,28},{28,24},{1,5},{5... | collective-permute-start | bytes 786440 | tf_op jit(solution)/shard_map/ppermute | solution.py:25
  18.8 0.5 collective-permute-start.6
  19.3 0.7 %collective-permute-start.8 = (bf16[16,64,128]{2,1,0:T(8,128)(2,1)S(1)}, bf16[16,64,128]{2,1,0:T(8,128)(2,1)S(1)}, u32[]{:S(2)}, u32[]{:S(2)}) collective-permute-start(bf16[16,64,128]{2,1,0:T(8,128)(2,1)S(1)} %get-tuple-element.19.own_ref), channel_id=1, source_target_pairs={{4,8},{8,4},{12,16},{16,12},{20,24},{24,20},{5,9},{9,5},{13,17},{1... | collective-permute-start | bytes 786440 | tf_op jit(solution)/shard_map/ppermute | solution.py:25
  20.0 0.0 copy-done.1
  20.0 0.0 copy-done.2
  20.0 1.0 %shard_map.62.partial_ref = f32[1024,128]{1,0:T(8,128)S(1)} custom-call(s32[390]{0:T(512)S(1)} %concatenate.3.index_ref, bf16[16,6,64,256]{3,2,1,0:T(8,128)(2,1)S(1)} %copy-done, bf16[16,64,128]{2,1,0:T(8,128)(2,1)S(1)} %get-tuple-element.19.own_ref, f32[8,128]{1,0:T(8,128)S(1)} %bitcast.13, f32[1024,128]{1,0:T(8,128)S(1)} %get-tuple-element.16.refs_1_, ...), custom_call_target="tpu_custom_call" | custom-call | tf_op jit(solution)/shard_map/pallas_call | solution.py:334
  21.0 0.0 collective-permute-done.5.refs_0_
  21.0 1.6 %collective-permute-start.7 = (bf16[16,64,128]{2,1,0:T(8,128)(2,1)S(1)}, bf16[16,64,128]{2,1,0:T(8,128)(2,1)S(1)}, u32[]{:S(2)}, u32[]{:S(2)}) collective-permute-start(bf16[16,64,128]{2,1,0:T(8,128)(2,1)S(1)} %get-tuple-element.19.own_ref), channel_id=1, source_target_pairs={{0,2},{1,3},{2,0},{3,1},{4,5},{5,4},{6,7},{7,6},{8,10},{9,11},{10,... | collective-permute-start | bytes 786440 | tf_op jit(solution)/shard_map/ppermute | solution.py:43
  22.6 2.6 %collective-permute-done.6.refs_1_ = bf16[16,64,128]{2,1,0:T(8,128)(2,1)S(1)} collective-permute-done((bf16[16,64,128]{2,1,0:T(8,128)(2,1)S(1)}, bf16[16,64,128]{2,1,0:T(8,128)(2,1)S(1)}, u32[]{:S(2)}, u32[]{:S(2)}) %collective-permute-start.6) | collective-permute-done | bytes 262176 | tf_op jit(solution)/shard_map/ppermute | solution.py:43
  25.2 1.5 %collective-permute-start.9 = (bf16[16,64,128]{2,1,0:T(8,128)(2,1)S(1)}, bf16[16,64,128]{2,1,0:T(8,128)(2,1)S(1)}, u32[]{:S(2)}, u32[]{:S(2)}) collective-permute-start(bf16[16,64,128]{2,1,0:T(8,128)(2,1)S(1)} %collective-permute-done.6.refs_1_), channel_id=1, source_target_pairs={{0,2},{1,3},{2,0},{3,1},{4,5},{5,4},{6,7},{7,6},{8,10},{9,11},{10,... | collective-permute-start | bytes 786440 | tf_op jit(solution)/shard_map/ppermute | solution.py:43
  26.7 0.0 collective-permute-done.8.refs_3_
  26.7 0.8 %collective-permute-done.7.refs_2_ = bf16[16,64,128]{2,1,0:T(8,128)(2,1)S(1)} collective-permute-done((bf16[16,64,128]{2,1,0:T(8,128)(2,1)S(1)}, bf16[16,64,128]{2,1,0:T(8,128)(2,1)S(1)}, u32[]{:S(2)}, u32[]{:S(2)}) %collective-permute-start.7) | collective-permute-done | bytes 262176 | tf_op jit(solution)/shard_map/ppermute | solution.py:43
  27.5 1.5 %shard_map.63.partial_ref = f32[1024,128]{1,0:T(8,128)S(1)} custom-call(s32[390]{0:T(512)S(1)} %concatenate.3.index_ref, bf16[16,6,64,256]{3,2,1,0:T(8,128)(2,1)S(1)} %copy-done, f32[1024,128]{1,0:T(8,128)S(1)} %shard_map.62.partial_ref, bf16[16,64,128]{2,1,0:T(8,128)(2,1)S(1)} %collective-permute-done.5.refs_0_, ...), custom_call_target="tpu_custom_call" | custom-call | tf_op jit(solution)/shard_map/pallas_call | solution.py:353
  28.9 2.6 %collective-permute-done.9.refs_0_ = bf16[16,64,128]{2,1,0:T(8,128)(2,1)S(1)} collective-permute-done((bf16[16,64,128]{2,1,0:T(8,128)(2,1)S(1)}, bf16[16,64,128]{2,1,0:T(8,128)(2,1)S(1)}, u32[]{:S(2)}, u32[]{:S(2)}) %collective-permute-start.9) | collective-permute-done | bytes 262176 | tf_op jit(solution)/shard_map/ppermute | solution.py:43
  31.6 1.2 %shard_map.64 = (f32[1024,128]{1,0:T(8,128)S(1)}, f32[72,128]{1,0:T(8,128)S(1)}) custom-call(s32[390]{0:T(512)S(1)} %concatenate.3.index_ref, bf16[16,6,64,256]{3,2,1,0:T(8,128)(2,1)S(1)} %copy-done, f32[1024,128]{1,0:T(8,128)S(1)} %shard_map.63.partial_ref, bf16[16,64,128]{2,1,0:T(8,128)(2,1)S(1)} %collective-permute-done.9.refs_0_), custom_call_target="tpu_custom_call" | custom-call | tf_op jit(solution)/shard_map/pallas_call | solution.py:364
  32.8 1.3 %collective-permute-start.10 = (f32[72,128]{1,0:T(8,128)S(1)}, f32[72,128]{1,0:T(8,128)S(1)}, u32[]{:S(2)}, u32[]{:S(2)}) collective-permute-start(f32[72,128]{1,0:T(8,128)S(1)} %get-tuple-element.20), channel_id=1, source_target_pairs={{0,4},{4,0},{8,12},{12,8},{16,20},{20,16},{24,28},{28,24},{1,5},{5... | collective-permute-start | bytes 110600 | tf_op jit(solution)/shard_map/ppermute | solution.py:48
  34.1 0.9 %collective-permute-done.10 = f32[72,128]{1,0:T(8,128)S(1)} collective-permute-done((f32[72,128]{1,0:T(8,128)S(1)}, f32[72,128]{1,0:T(8,128)S(1)}, u32[]{:S(2)}, u32[]{:S(2)}) %collective-permute-start.10) | collective-permute-done | bytes 36896 | tf_op jit(solution)/shard_map/ppermute | solution.py:48
  34.9 3.7 %collective-permute-start.11 = (f32[72,128]{1,0:T(8,128)S(1)}, f32[72,128]{1,0:T(8,128)S(1)}, u32[]{:S(2)}, u32[]{:S(2)}) collective-permute-start(f32[72,128]{1,0:T(8,128)S(1)} %add.28), channel_id=1, source_target_pairs={{0,24},{4,28},{8,16},{12,20},{16,8},{20,12},{24,0},{28,4},{1,25},{... | collective-permute-start | bytes 110600 | tf_op jit(solution)/shard_map/ppermute | solution.py:48
  38.6 0.0 collective-permute-start.12
  38.6 0.7 %collective-permute-start.13 = (f32[72,128]{1,0:T(8,128)S(1)}, f32[72,128]{1,0:T(8,128)S(1)}, u32[]{:S(2)}, u32[]{:S(2)}) collective-permute-start(f32[72,128]{1,0:T(8,128)S(1)} %add.28), channel_id=1, source_target_pairs={{0,8},{4,12},{8,0},{12,4},{16,24},{20,28},{24,16},{28,20},{1,9},{5... | collective-permute-start | bytes 110600 | tf_op jit(solution)/shard_map/ppermute | solution.py:48
  39.3 1.4 %collective-permute-done.11 = f32[72,128]{1,0:T(8,128)S(1)} collective-permute-done((f32[72,128]{1,0:T(8,128)S(1)}, f32[72,128]{1,0:T(8,128)S(1)}, u32[]{:S(2)}, u32[]{:S(2)}) %collective-permute-start.11) | collective-permute-done | bytes 36896 | tf_op jit(solution)/shard_map/ppermute | solution.py:48
  40.7 2.7 %collective-permute-done.12 = f32[72,128]{1,0:T(8,128)S(1)} collective-permute-done((f32[72,128]{1,0:T(8,128)S(1)}, f32[72,128]{1,0:T(8,128)S(1)}, u32[]{:S(2)}, u32[]{:S(2)}) %collective-permute-start.12) | collective-permute-done | bytes 36896 | tf_op jit(solution)/shard_map/ppermute | solution.py:48
  43.5 0.0 collective-permute-done.13
  43.5 3.0 %collective-permute-start.14 = (f32[72,128]{1,0:T(8,128)S(1)}, f32[72,128]{1,0:T(8,128)S(1)}, u32[]{:S(2)}, u32[]{:S(2)}) collective-permute-start(f32[72,128]{1,0:T(8,128)S(1)} %add_add_fusion.1), channel_id=1, source_target_pairs={{0,3},{1,2},{2,1},{3,0},{4,7},{5,6},{6,5},{7,4},{8,11},{9,10},{10,... | collective-permute-start | bytes 110600 | tf_op jit(solution)/shard_map/ppermute | solution.py:48
  46.5 0.0 collective-permute-start.15
  46.5 0.6 %collective-permute-start.16 = (f32[72,128]{1,0:T(8,128)S(1)}, f32[72,128]{1,0:T(8,128)S(1)}, u32[]{:S(2)}, u32[]{:S(2)}) collective-permute-start(f32[72,128]{1,0:T(8,128)S(1)} %add_add_fusion.1), channel_id=1, source_target_pairs={{0,1},{1,0},{2,3},{3,2},{4,5},{5,4},{6,7},{7,6},{8,9},{9,8},{10,11... | collective-permute-start | bytes 110600 | tf_op jit(solution)/shard_map/ppermute | solution.py:48
  47.1 1.3 %collective-permute-done.14 = f32[72,128]{1,0:T(8,128)S(1)} collective-permute-done((f32[72,128]{1,0:T(8,128)S(1)}, f32[72,128]{1,0:T(8,128)S(1)}, u32[]{:S(2)}, u32[]{:S(2)}) %collective-permute-start.14) | collective-permute-done | bytes 36896 | tf_op jit(solution)/shard_map/ppermute | solution.py:48
  48.4 2.0 %collective-permute-done.15 = f32[72,128]{1,0:T(8,128)S(1)} collective-permute-done((f32[72,128]{1,0:T(8,128)S(1)}, f32[72,128]{1,0:T(8,128)S(1)}, u32[]{:S(2)}, u32[]{:S(2)}) %collective-permute-start.15) | collective-permute-done | bytes 36896 | tf_op jit(solution)/shard_map/ppermute | solution.py:48
  50.4 0.0 collective-permute-done.16
  50.5 4.3 %shard_map.65 = (f32[1024,128]{1,0:T(8,128)}, f32[128,128]{1,0:T(8,128)}) custom-call(f32[72,128]{1,0:T(8,128)S(1)} %add_add_fusion.packed_ref, f32[1024,128]{1,0:T(8,128)S(1)} %get-tuple-element.21.filtered_ref), custom_call_target="tpu_custom_call" | custom-call | tf_op jit(solution)/shard_map/pallas_call | solution.py:368
  (3 shorter events, 0.0 us)
Async XLA Ops:
  2.1 4.8 %collective-permute-start = (bf16[16,64,128]{2,1,0:T(8,128)(2,1)S(1)}, bf16[16,64,128]{2,1,0:T(8,128)(2,1)S(1)}, u32[]{:S(2)}, u32[]{:S(2)}) collective-permute-start(bf16[16,64,128]{2,1,0:T(8,128)(2,1)S(1)} %bitcast.8), channel_id=1, source_target_pairs={{0,4},{4,0},{8,12},{12,8},{16,20},{20,16},{24,28},{28,24},{1,5},{5... | collective-permute-start | bytes 786440 | tf_op jit(solution)/shard_map/ppermute | solution.py:25
  2.6 6.9 %collective-permute-start.1 = (bf16[16,64,128]{2,1,0:T(8,128)(2,1)S(1)}, bf16[16,64,128]{2,1,0:T(8,128)(2,1)S(1)}, u32[]{:S(2)}, u32[]{:S(2)}) collective-permute-start(bf16[16,64,128]{2,1,0:T(8,128)(2,1)S(1)} %bitcast.9), channel_id=1, source_target_pairs={{0,1},{1,0},{2,3},{3,2},{4,6},{5,7},{6,4},{7,5},{8,9},{9,8},{10,11... | collective-permute-start | bytes 786440 | tf_op jit(solution)/shard_map/ppermute | solution.py:43
  5.1 9.2 %collective-permute-start.3 = (bf16[16,64,128]{2,1,0:T(8,128)(2,1)S(1)}, bf16[16,64,128]{2,1,0:T(8,128)(2,1)S(1)}, u32[]{:S(2)}, u32[]{:S(2)}) collective-permute-start(bf16[16,64,128]{2,1,0:T(8,128)(2,1)S(1)} %bitcast.10), channel_id=1, source_target_pairs={{4,8},{8,4},{12,16},{16,12},{20,24},{24,20},{5,9},{9,5},{13,17},{1... | collective-permute-start | bytes 786440 | tf_op jit(solution)/shard_map/ppermute | solution.py:25
  6.9 7.5 %collective-permute-start.2 = (bf16[16,64,128]{2,1,0:T(8,128)(2,1)S(1)}, bf16[16,64,128]{2,1,0:T(8,128)(2,1)S(1)}, u32[]{:S(2)}, u32[]{:S(2)}) collective-permute-start(bf16[16,64,128]{2,1,0:T(8,128)(2,1)S(1)} %bitcast.11), channel_id=1, source_target_pairs={{0,2},{1,3},{2,0},{3,1},{4,5},{5,4},{6,7},{7,6},{8,10},{9,11},{10,... | collective-permute-start | bytes 786440 | tf_op jit(solution)/shard_map/ppermute | solution.py:43
  9.5 6.6 %collective-permute-start.4 = (bf16[16,64,128]{2,1,0:T(8,128)(2,1)S(1)}, bf16[16,64,128]{2,1,0:T(8,128)(2,1)S(1)}, u32[]{:S(2)}, u32[]{:S(2)}) collective-permute-start(bf16[16,64,128]{2,1,0:T(8,128)(2,1)S(1)} %collective-permute-done.1.refs_1_), channel_id=1, source_target_pairs={{0,2},{1,3},{2,0},{3,1},{4,5},{5,4},{6,7},{7,6},{8,10},{9,11},{10,... | collective-permute-start | bytes 786440 | tf_op jit(solution)/shard_map/ppermute | solution.py:43
  11.5 1.9 %copy-start = (bf16[16,6,64,256]{3,2,1,0:T(8,128)(2,1)S(1)}, bf16[16,6,64,256]{3,2,1,0:T(8,128)(2,1)}, u32[]{:S(2)}) copy-start(bf16[16,6,64,256]{3,2,1,0:T(8,128)(2,1)} %hamiltonian_ref.11) | copy-start | bytes 9437188
  15.8 4.2 %copy-start.1 = (f32[1024,128]{1,0:T(8,128)S(1)}, f32[1024,128]{1,0:T(8,128)}, u32[]{:S(2)}) copy-start(f32[1024,128]{1,0:T(8,128)} %refs_2_.1) | copy-start | bytes 1572868
  15.8 4.2 %copy-start.2 = (f32[1024]{0:T(1024)S(1)}, f32[1024]{0:T(1024)}, u32[]{:S(2)}) copy-start(f32[1024]{0:T(1024)} %param.6) | copy-start | bytes 12292
  17.0 4.0 %collective-permute-start.5 = (bf16[16,64,128]{2,1,0:T(8,128)(2,1)S(1)}, bf16[16,64,128]{2,1,0:T(8,128)(2,1)S(1)}, u32[]{:S(2)}, u32[]{:S(2)}) collective-permute-start(bf16[16,64,128]{2,1,0:T(8,128)(2,1)S(1)} %get-tuple-element.19.own_ref), channel_id=1, source_target_pairs={{0,4},{4,0},{8,12},{12,8},{16,20},{20,16},{24,28},{28,24},{1,5},{5... | collective-permute-start | bytes 786440 | tf_op jit(solution)/shard_map/ppermute | solution.py:25
  18.8 6.4 %collective-permute-start.6 = (bf16[16,64,128]{2,1,0:T(8,128)(2,1)S(1)}, bf16[16,64,128]{2,1,0:T(8,128)(2,1)S(1)}, u32[]{:S(2)}, u32[]{:S(2)}) collective-permute-start(bf16[16,64,128]{2,1,0:T(8,128)(2,1)S(1)} %get-tuple-element.19.own_ref), channel_id=1, source_target_pairs={{0,1},{1,0},{2,3},{3,2},{4,6},{5,7},{6,4},{7,5},{8,9},{9,8},{10,11... | collective-permute-start | bytes 786440 | tf_op jit(solution)/shard_map/ppermute | solution.py:43
  19.3 7.4 %collective-permute-start.8 = (bf16[16,64,128]{2,1,0:T(8,128)(2,1)S(1)}, bf16[16,64,128]{2,1,0:T(8,128)(2,1)S(1)}, u32[]{:S(2)}, u32[]{:S(2)}) collective-permute-start(bf16[16,64,128]{2,1,0:T(8,128)(2,1)S(1)} %get-tuple-element.19.own_ref), channel_id=1, source_target_pairs={{4,8},{8,4},{12,16},{16,12},{20,24},{24,20},{5,9},{9,5},{13,17},{1... | collective-permute-start | bytes 786440 | tf_op jit(solution)/shard_map/ppermute | solution.py:25
  21.0 6.4 %collective-permute-start.7 = (bf16[16,64,128]{2,1,0:T(8,128)(2,1)S(1)}, bf16[16,64,128]{2,1,0:T(8,128)(2,1)S(1)}, u32[]{:S(2)}, u32[]{:S(2)}) collective-permute-start(bf16[16,64,128]{2,1,0:T(8,128)(2,1)S(1)} %get-tuple-element.19.own_ref), channel_id=1, source_target_pairs={{0,2},{1,3},{2,0},{3,1},{4,5},{5,4},{6,7},{7,6},{8,10},{9,11},{10,... | collective-permute-start | bytes 786440 | tf_op jit(solution)/shard_map/ppermute | solution.py:43
  25.2 6.4 %collective-permute-start.9 = (bf16[16,64,128]{2,1,0:T(8,128)(2,1)S(1)}, bf16[16,64,128]{2,1,0:T(8,128)(2,1)S(1)}, u32[]{:S(2)}, u32[]{:S(2)}) collective-permute-start(bf16[16,64,128]{2,1,0:T(8,128)(2,1)S(1)} %collective-permute-done.6.refs_1_), channel_id=1, source_target_pairs={{0,2},{1,3},{2,0},{3,1},{4,5},{5,4},{6,7},{7,6},{8,10},{9,11},{10,... | collective-permute-start | bytes 786440 | tf_op jit(solution)/shard_map/ppermute | solution.py:43
  32.8 2.1 %collective-permute-start.10 = (f32[72,128]{1,0:T(8,128)S(1)}, f32[72,128]{1,0:T(8,128)S(1)}, u32[]{:S(2)}, u32[]{:S(2)}) collective-permute-start(f32[72,128]{1,0:T(8,128)S(1)} %get-tuple-element.20), channel_id=1, source_target_pairs={{0,4},{4,0},{8,12},{12,8},{16,20},{20,16},{24,28},{28,24},{1,5},{5... | collective-permute-start | bytes 110600 | tf_op jit(solution)/shard_map/ppermute | solution.py:48
  34.9 5.8 %collective-permute-start.11 = (f32[72,128]{1,0:T(8,128)S(1)}, f32[72,128]{1,0:T(8,128)S(1)}, u32[]{:S(2)}, u32[]{:S(2)}) collective-permute-start(f32[72,128]{1,0:T(8,128)S(1)} %add.28), channel_id=1, source_target_pairs={{0,24},{4,28},{8,16},{12,20},{16,8},{20,12},{24,0},{28,4},{1,25},{... | collective-permute-start | bytes 110600 | tf_op jit(solution)/shard_map/ppermute | solution.py:48
  38.6 4.9 %collective-permute-start.12 = (f32[72,128]{1,0:T(8,128)S(1)}, f32[72,128]{1,0:T(8,128)S(1)}, u32[]{:S(2)}, u32[]{:S(2)}) collective-permute-start(f32[72,128]{1,0:T(8,128)S(1)} %add.28), channel_id=1, source_target_pairs={{0,16},{4,20},{8,24},{12,28},{16,0},{20,4},{24,8},{28,12},{1,17},{... | collective-permute-start | bytes 110600 | tf_op jit(solution)/shard_map/ppermute | solution.py:48
  38.6 4.9 %collective-permute-start.13 = (f32[72,128]{1,0:T(8,128)S(1)}, f32[72,128]{1,0:T(8,128)S(1)}, u32[]{:S(2)}, u32[]{:S(2)}) collective-permute-start(f32[72,128]{1,0:T(8,128)S(1)} %add.28), channel_id=1, source_target_pairs={{0,8},{4,12},{8,0},{12,4},{16,24},{20,28},{24,16},{28,20},{1,9},{5... | collective-permute-start | bytes 110600 | tf_op jit(solution)/shard_map/ppermute | solution.py:48
  43.5 5.0 %collective-permute-start.14 = (f32[72,128]{1,0:T(8,128)S(1)}, f32[72,128]{1,0:T(8,128)S(1)}, u32[]{:S(2)}, u32[]{:S(2)}) collective-permute-start(f32[72,128]{1,0:T(8,128)S(1)} %add_add_fusion.1), channel_id=1, source_target_pairs={{0,3},{1,2},{2,1},{3,0},{4,7},{5,6},{6,5},{7,4},{8,11},{9,10},{10,... | collective-permute-start | bytes 110600 | tf_op jit(solution)/shard_map/ppermute | solution.py:48
  46.5 4.0 %collective-permute-start.15 = (f32[72,128]{1,0:T(8,128)S(1)}, f32[72,128]{1,0:T(8,128)S(1)}, u32[]{:S(2)}, u32[]{:S(2)}) collective-permute-start(f32[72,128]{1,0:T(8,128)S(1)} %add_add_fusion.1), channel_id=1, source_target_pairs={{0,2},{1,3},{2,0},{3,1},{4,6},{5,7},{6,4},{7,5},{8,10},{9,11},{10,... | collective-permute-start | bytes 110600 | tf_op jit(solution)/shard_map/ppermute | solution.py:48
  46.5 4.0 %collective-permute-start.16 = (f32[72,128]{1,0:T(8,128)S(1)}, f32[72,128]{1,0:T(8,128)S(1)}, u32[]{:S(2)}, u32[]{:S(2)}) collective-permute-start(f32[72,128]{1,0:T(8,128)S(1)} %add_add_fusion.1), channel_id=1, source_target_pairs={{0,1},{1,0},{2,3},{3,2},{4,5},{5,4},{6,7},{7,6},{8,9},{9,8},{10,11... | collective-permute-start | bytes 110600 | tf_op jit(solution)/shard_map/ppermute | solution.py:48

commit v15 on v14

--- a/solution.py
+++ b/solution.py
@@ -52,7 +52,9 @@
     for axis, step in (("group", 1), ("group", 2), ("blk", 1)):
         count = 2 if (axis, step) == ("group", 1) else lax.axis_size(axis)
         while step < count:
-            flips = [step, 2 * step, 3 * step] if 2 * step < count else [step]
+            flips = [step, 3 * step, 2 * step] if 2 * step < count else [step]
+            if axis == "blk":
+                flips[1:] = flips[:0:-1]
             others = [from_partner(value, axis, flip) for flip in flips]
             value = others[0] + value
             if len(others) == 3:
@@ -124,15 +126,14 @@
 
 
 def second_kernel(numbers, index_ref, hamiltonian_ref, partial_ref, *refs):
-    pieces, (filtered_ref, packed_ref) = list(zip(numbers, refs)), refs[len(numbers) :]
+    pieces, (both_ref, packed_ref) = list(zip(numbers, refs)), refs[len(numbers) :]
+    states = both_ref.shape[1] // 2
     shard_blocks, _, block_size, _ = hamiltonian_ref.shape
     for row in range(shard_blocks):
         rows = pl.ds(row * block_size, block_size)
-        filtered_ref[rows, :] = partial_ref[rows, :] + couple_row(
-            index_ref, hamiltonian_ref, pieces, row
-        )
-    states = filtered_ref.shape[1]
-    both = jnp.concatenate(two_parts(filtered_ref[...]), axis=1)
+        filtered = partial_ref[rows, :] + couple_row(index_ref, hamiltonian_ref, pieces, row)
+        both_ref[rows, :states], both_ref[rows, states:] = two_parts(filtered)
+    both = both_ref[...]
     products = lax.dot_general(
         both, both, (((0,), (0,)), ((), ())), preferred_element_type=jnp.float32
     )
@@ -269,23 +270,30 @@
 
 
 def factor_kernel(
-    rows_total, packed_ref, filtered_ref, ortho_hbm, upper_hbm,
+    rows_total, packed_ref, both_ref, ortho_hbm, upper_hbm,
     upper_ref, inverse_ref, ortho_ref, sent, upper_sent,
 ):
+    states = upper_ref.shape[0]
     factor(unpack(packed_ref) * (1.0 / rows_total), upper_ref, inverse_ref)
     copies = [pltpu.make_async_copy(upper_ref, upper_hbm, upper_sent)]
     copies[0].start()
     high, low = two_parts(inverse_ref[...])
-    right = jnp.concatenate([high, high, low], axis=1)
+    right = jnp.concatenate(
+        [
+            jnp.concatenate([high, high], axis=1),
+            jnp.concatenate([low, jnp.zeros_like(low)], axis=1),
+        ],
+        axis=0,
+    )
     chunks = sent.shape[0]
-    per_chunk = filtered_ref.shape[0] // chunks
+    per_chunk = both_ref.shape[0] // chunks
     for chunk in range(chunks):
         rows = pl.ds(chunk * per_chunk, per_chunk)
-        high, low = two_parts(filtered_ref[rows, :])
-        ortho_ref[rows, :] = lax.dot_general(
-            jnp.concatenate([high, low, high], axis=1), right, (((1,), (1,)), ((), ())),
+        product = lax.dot_general(
+            both_ref[rows, :], right, (((1,), (1,)), ((), ())),
             preferred_element_type=jnp.float32,
         )
+        ortho_ref[rows, :] = product[:, :states] + product[:, states:]
         copies.append(
             pltpu.make_async_copy(ortho_ref.at[rows, :], ortho_hbm.at[rows, :], sent.at[chunk])
         )
@@ -342,7 +350,10 @@
             partial = own_part(index_array, value, *terms)
             later, pairs[0], partial = lax.optimization_barrier((value, pairs[0], partial))
         else:
-            later, pairs[0], index_array = lax.optimization_barrier((value, pairs[0], index_array))
+            later, pairs[0], index_array, slab = lax.optimization_barrier(
+                (value, pairs[0], index_array, trial_slab)
+            )
+            terms = (weights.reshape(-1, 1) * slab,)
         others = [cycle_exchange(later, level) for level in range(1, levels)]
         pieces = [value, arrived]
         for level, other in zip(range(1, levels), others):
@@ -355,14 +366,14 @@
         )(index_array, hamiltonian, partial, *[pieces[number] for number in middle])
         return [partial] + [pieces[number] for number in ending]
 
-    weighted = (weights.reshape(-1, 1) * trial_slab)
-    parts = coupled(trial_slab.reshape(rounded.shape).astype(jnp.bfloat16), index_array, False, weighted)
+    parts = coupled(trial_slab.reshape(rounded.shape).astype(jnp.bfloat16), index_array, False)
     once, once_round = call(
         functools.partial(first_kernel, ending), (flat, rounded), [smem] + [vmem] * (2 + len(ending))
     )(index_array, hamiltonian, *parts)
     parts = coupled(once_round, index_array, True, weights, once, trial_slab)
+    both = jax.ShapeDtypeStruct((flat_rows, 2 * states), jnp.bfloat16)
     filtered, gram = call(
-        functools.partial(second_kernel, ending), (flat, packed), [smem] + [vmem] * (2 + len(ending))
+        functools.partial(second_kernel, ending), (both, packed), [smem] + [vmem] * (2 + len(ending))
     )(index_array, hamiltonian, *parts)
     gram = summed(gram)
     return call(

time: 55 us -> 54.9 us (level)
  other arithmetic: 1.46 us -> 2.34 us
  starting transfers between devices: 22.8 us -> 22.2 us
  waiting for transfers between devices: 15.6 us -> 15 us
    convert_element_type x0 -> x1, other arithmetic: none -> 1.07 us  [on_device(): trial_slab.reshape(rounded.shape).astype(jnp.bfloat16)]
    ppermute x4, starting transfers between devices: 3.69 us -> 2.65 us  [pair_exchange(): return lax.ppermute(value, 'group', route)]
  transfers between devices with their start and end apart: 17 -> 17, of which waited for: 10 -> 10; matrix products, arithmetic and copies ran while one was open for 2% -> 4% of each run, Pallas kernels for 9% -> 9%
where the time goes in v15:
time: 54.9 us; the launch traced here: 54.6 us
  starting transfers between devices  22.2 us (40%)
  waiting for transfers between devices  15 us (27%)
  Pallas kernels  11.2 us (20%)
  local copies, waits for them, and re-layouts  2.92 us (5%)
  other arithmetic  2.34 us (4%)
  between operations  0.81 us (1%)
    ppermute x6, starting transfers between devices, cycle_exchange(): return lax.ppermute(value, ('group', 'blk'), route)  9.8 us
    ppermute x7, starting transfers between devices, from_partner(): lax.ppermute(value, axis, [(index, index ^ flip) for index in range(count)])  9.78 us
    ppermute x7, waiting for transfers between devices, from_partner(): lax.ppermute(value, axis, [(index, index ^ flip) for index in range(count)])  8 us
    ppermute x6, waiting for transfers between devices, cycle_exchange(): return lax.ppermute(value, ('group', 'blk'), route)  7 us
    pallas_call x1, Pallas kernels, on_device(): call(functools.partial(factor_kernel, rows_total), (flat, square), [vmem,...  4.28 us
    pallas_call x2, Pallas kernels, coupled(): call(functools.partial(middle_kernel, middle), flat, [smem] + [vmem] * (2...  2.96 us
    unnamed x7, local copies, waits for them, and re-layouts  2.72 us
    ppermute x4, starting transfers between devices, pair_exchange(): return lax.ppermute(value, 'group', route)  2.65 us
  transfers between devices with their start and end apart: 17, of which 10 were waited for; matrix products, arithmetic and copies ran while one was open for 4% of the time, Pallas kernels for 9%

profile of v15, /device:TPU:0, one launch (start us, length us, event | category | flops | bytes accessed | tf_op | source)
XLA Modules:
  0.0 54.6 jit_solution(10584600310596990590)
XLA Ops:
  0.6 1.1 %convert_element_type.5 = bf16[1024,128]{1,0:T(8,128)(2,1)S(1)} convert(f32[1024,128]{1,0:T(8,128)} %refs_2_.1) | non-fusion elementwise | flops 131072 | bytes 786432 | tf_op jit(solution)/shard_map/convert_element_type | solution.py:369
  1.7 0.5 collective-permute-start
  2.2 2.6 %collective-permute-start.1 = (bf16[16,64,128]{2,1,0:T(8,128)(2,1)S(1)}, bf16[16,64,128]{2,1,0:T(8,128)(2,1)S(1)}, u32[]{:S(2)}, u32[]{:S(2)}) collective-permute-start(bf16[16,64,128]{2,1,0:T(8,128)(2,1)S(1)} %bitcast.9), channel_id=1, source_target_pairs={{0,1},{1,0},{2,3},{3,2},{4,6},{5,7},{6,4},{7,5},{8,9},{9,8},{10,11... | collective-permute-start | bytes 786440 | tf_op jit(solution)/shard_map/ppermute | solution.py:43
  4.8 0.7 %collective-permute-start.3 = (bf16[16,64,128]{2,1,0:T(8,128)(2,1)S(1)}, bf16[16,64,128]{2,1,0:T(8,128)(2,1)S(1)}, u32[]{:S(2)}, u32[]{:S(2)}) collective-permute-start(bf16[16,64,128]{2,1,0:T(8,128)(2,1)S(1)} %bitcast.10), channel_id=1, source_target_pairs={{4,8},{8,4},{12,16},{16,12},{20,24},{24,20},{5,9},{9,5},{13,17},{1... | collective-permute-start | bytes 786440 | tf_op jit(solution)/shard_map/ppermute | solution.py:25
  5.5 0.8 %copy.6 = s32[16,6,4]{2,1,0:T(8,128)S(1)} copy(s32[16,6,4]{0,2,1:T(4,128)} %param.5) | data formatting | bytes 3072 | tf_op args[1]
  6.3 0.1 reshape.31
  6.4 0.1 concatenate.3.index_ref
  6.5 0.0 collective-permute-done.refs_0_
  6.5 1.6 %collective-permute-start.2 = (bf16[16,64,128]{2,1,0:T(8,128)(2,1)S(1)}, bf16[16,64,128]{2,1,0:T(8,128)(2,1)S(1)}, u32[]{:S(2)}, u32[]{:S(2)}) collective-permute-start(bf16[16,64,128]{2,1,0:T(8,128)(2,1)S(1)} %bitcast.11), channel_id=1, source_target_pairs={{0,2},{1,3},{2,0},{3,1},{4,5},{5,4},{6,7},{7,6},{8,10},{9,11},{10,... | collective-permute-start | bytes 786440 | tf_op jit(solution)/shard_map/ppermute | solution.py:43
  8.1 1.1 %collective-permute-done.1.refs_1_ = bf16[16,64,128]{2,1,0:T(8,128)(2,1)S(1)} collective-permute-done((bf16[16,64,128]{2,1,0:T(8,128)(2,1)S(1)}, bf16[16,64,128]{2,1,0:T(8,128)(2,1)S(1)}, u32[]{:S(2)}, u32[]{:S(2)}) %collective-permute-start.1) | collective-permute-done | bytes 262176 | tf_op jit(solution)/shard_map/ppermute | solution.py:43
  9.1 2.0 %collective-permute-start.4 = (bf16[16,64,128]{2,1,0:T(8,128)(2,1)S(1)}, bf16[16,64,128]{2,1,0:T(8,128)(2,1)S(1)}, u32[]{:S(2)}, u32[]{:S(2)}) collective-permute-start(bf16[16,64,128]{2,1,0:T(8,128)(2,1)S(1)} %collective-permute-done.1.refs_1_), channel_id=1, source_target_pairs={{0,2},{1,3},{2,0},{3,1},{4,5},{5,4},{6,7},{7,6},{8,10},{9,11},{10,... | collective-permute-start | bytes 786440 | tf_op jit(solution)/shard_map/ppermute | solution.py:43
  11.2 1.2 %broadcast_multiply_fusion.refs_0_ = f32[1024,128]{1,0:T(8,128)S(1)} fusion(f32[1024,128]{1,0:T(8,128)} %refs_2_.1, f32[1024]{0:T(1024)} %param.6), kind=kLoop, calls=%fused_computation | loop fusion | flops 131072 | bytes 1052672 | tf_op jit(solution)/shard_map/mul | solution.py:356
  12.4 0.0 copy-start
  12.4 1.9 %copy-done = bf16[16,6,64,256]{3,2,1,0:T(8,128)(2,1)S(1)} copy-done((bf16[16,6,64,256]{3,2,1,0:T(8,128)(2,1)S(1)}, bf16[16,6,64,256]{3,2,1,0:T(8,128)(2,1)}, u32[]{:S(2)}) %copy-start) | copy-done | bytes 3145752
  14.3 0.9 %shard_map.59.partial_ref = f32[1024,128]{1,0:T(8,128)S(1)} custom-call(s32[390]{0:T(512)S(1)} %concatenate.3.index_ref, bf16[16,6,64,256]{3,2,1,0:T(8,128)(2,1)S(1)} %copy-done, bf16[16,64,128]{2,1,0:T(8,128)(2,1)S(1)} %bitcast.12, f32[1024,128]{1,0:T(8,128)S(1)} %broadcast_multiply_fusion.refs_0_), custom_call_target="tpu_custom_call" | custom-call | tf_op jit(solution)/shard_map/pallas_call | solution.py:342
  15.2 0.0 collective-permute-done.3.refs_3_
  15.2 0.0 collective-permute-done.2.refs_2_
  15.2 1.5 %shard_map.60.partial_ref = f32[1024,128]{1,0:T(8,128)S(1)} custom-call(s32[390]{0:T(512)S(1)} %concatenate.3.index_ref, bf16[16,6,64,256]{3,2,1,0:T(8,128)(2,1)S(1)} %copy-done, f32[1024,128]{1,0:T(8,128)S(1)} %shard_map.59.partial_ref, bf16[16,64,128]{2,1,0:T(8,128)(2,1)S(1)} %collective-permute-done.refs_0_, ...), custom_call_target="tpu_custom_call" | custom-call | tf_op jit(solution)/shard_map/pallas_call | solution.py:364
  16.7 0.0 copy-start.1
  16.7 0.0 copy-start.2
  16.7 0.0 collective-permute-done.4.refs_0_
  16.8 0.9 %shard_map.61 = (f32[1024,128]{1,0:T(8,128)S(1)}, bf16[16,64,128]{2,1,0:T(8,128)(2,1)S(1)}) custom-call(s32[390]{0:T(512)S(1)} %concatenate.3.index_ref, bf16[16,6,64,256]{3,2,1,0:T(8,128)(2,1)S(1)} %copy-done, f32[1024,128]{1,0:T(8,128)S(1)} %shard_map.60.partial_ref, bf16[16,64,128]{2,1,0:T(8,128)(2,1)S(1)} %collective-permute-done.4.refs_0_), custom_call_target="tpu_custom_call" | custom-call | tf_op jit(solution)/shard_map/pallas_call | solution.py:370
  17.7 0.8 %collective-permute-start.5 = (bf16[16,64,128]{2,1,0:T(8,128)(2,1)S(1)}, bf16[16,64,128]{2,1,0:T(8,128)(2,1)S(1)}, u32[]{:S(2)}, u32[]{:S(2)}) collective-permute-start(bf16[16,64,128]{2,1,0:T(8,128)(2,1)S(1)} %get-tuple-element.21.own_ref), channel_id=1, source_target_pairs={{0,4},{4,0},{8,12},{12,8},{16,20},{20,16},{24,28},{28,24},{1,5},{5... | collective-permute-start | bytes 786440 | tf_op jit(solution)/shard_map/ppermute | solution.py:25
  18.5 0.8 %collective-permute-start.6 = (bf16[16,64,128]{2,1,0:T(8,128)(2,1)S(1)}, bf16[16,64,128]{2,1,0:T(8,128)(2,1)S(1)}, u32[]{:S(2)}, u32[]{:S(2)}) collective-permute-start(bf16[16,64,128]{2,1,0:T(8,128)(2,1)S(1)} %get-tuple-element.21.own_ref), channel_id=1, source_target_pairs={{0,1},{1,0},{2,3},{3,2},{4,6},{5,7},{6,4},{7,5},{8,9},{9,8},{10,11... | collective-permute-start | bytes 786440 | tf_op jit(solution)/shard_map/ppermute | solution.py:43
  19.3 0.7 %collective-permute-start.8 = (bf16[16,64,128]{2,1,0:T(8,128)(2,1)S(1)}, bf16[16,64,128]{2,1,0:T(8,128)(2,1)S(1)}, u32[]{:S(2)}, u32[]{:S(2)}) collective-permute-start(bf16[16,64,128]{2,1,0:T(8,128)(2,1)S(1)} %get-tuple-element.21.own_ref), channel_id=1, source_target_pairs={{4,8},{8,4},{12,16},{16,12},{20,24},{24,20},{5,9},{9,5},{13,17},{1... | collective-permute-start | bytes 786440 | tf_op jit(solution)/shard_map/ppermute | solution.py:25
  20.0 0.0 copy-done.1
  20.0 0.0 copy-done.2
  20.0 1.0 %shard_map.62.partial_ref = f32[1024,128]{1,0:T(8,128)S(1)} custom-call(s32[390]{0:T(512)S(1)} %concatenate.3.index_ref, bf16[16,6,64,256]{3,2,1,0:T(8,128)(2,1)S(1)} %copy-done, bf16[16,64,128]{2,1,0:T(8,128)(2,1)S(1)} %get-tuple-element.21.own_ref, f32[8,128]{1,0:T(8,128)S(1)} %bitcast.13, f32[1024,128]{1,0:T(8,128)S(1)} %get-tuple-element.18.refs_1_, ...), custom_call_target="tpu_custom_call" | custom-call | tf_op jit(solution)/shard_map/pallas_call | solution.py:342
  21.0 0.0 collective-permute-done.5.refs_0_
  21.0 1.3 %collective-permute-start.7 = (bf16[16,64,128]{2,1,0:T(8,128)(2,1)S(1)}, bf16[16,64,128]{2,1,0:T(8,128)(2,1)S(1)}, u32[]{:S(2)}, u32[]{:S(2)}) collective-permute-start(bf16[16,64,128]{2,1,0:T(8,128)(2,1)S(1)} %get-tuple-element.21.own_ref), channel_id=1, source_target_pairs={{0,2},{1,3},{2,0},{3,1},{4,5},{5,4},{6,7},{7,6},{8,10},{9,11},{10,... | collective-permute-start | bytes 786440 | tf_op jit(solution)/shard_map/ppermute | solution.py:43
  22.3 2.6 %collective-permute-done.6.refs_1_ = bf16[16,64,128]{2,1,0:T(8,128)(2,1)S(1)} collective-permute-done((bf16[16,64,128]{2,1,0:T(8,128)(2,1)S(1)}, bf16[16,64,128]{2,1,0:T(8,128)(2,1)S(1)}, u32[]{:S(2)}, u32[]{:S(2)}) %collective-permute-start.6) | collective-permute-done | bytes 262176 | tf_op jit(solution)/shard_map/ppermute | solution.py:43
  24.8 1.5 %collective-permute-start.9 = (bf16[16,64,128]{2,1,0:T(8,128)(2,1)S(1)}, bf16[16,64,128]{2,1,0:T(8,128)(2,1)S(1)}, u32[]{:S(2)}, u32[]{:S(2)}) collective-permute-start(bf16[16,64,128]{2,1,0:T(8,128)(2,1)S(1)} %collective-permute-done.6.refs_1_), channel_id=1, source_target_pairs={{0,2},{1,3},{2,0},{3,1},{4,5},{5,4},{6,7},{7,6},{8,10},{9,11},{10,... | collective-permute-start | bytes 786440 | tf_op jit(solution)/shard_map/ppermute | solution.py:43
  26.3 0.0 collective-permute-done.8.refs_3_
  26.3 1.1 %collective-permute-done.7.refs_2_ = bf16[16,64,128]{2,1,0:T(8,128)(2,1)S(1)} collective-permute-done((bf16[16,64,128]{2,1,0:T(8,128)(2,1)S(1)}, bf16[16,64,128]{2,1,0:T(8,128)(2,1)S(1)}, u32[]{:S(2)}, u32[]{:S(2)}) %collective-permute-start.7) | collective-permute-done | bytes 262176 | tf_op jit(solution)/shard_map/ppermute | solution.py:43
  27.4 1.5 %shard_map.63.partial_ref = f32[1024,128]{1,0:T(8,128)S(1)} custom-call(s32[390]{0:T(512)S(1)} %concatenate.3.index_ref, bf16[16,6,64,256]{3,2,1,0:T(8,128)(2,1)S(1)} %copy-done, f32[1024,128]{1,0:T(8,128)S(1)} %shard_map.62.partial_ref, bf16[16,64,128]{2,1,0:T(8,128)(2,1)S(1)} %collective-permute-done.5.refs_0_, ...), custom_call_target="tpu_custom_call" | custom-call | tf_op jit(solution)/shard_map/pallas_call | solution.py:364
  28.9 2.3 %collective-permute-done.9.refs_0_ = bf16[16,64,128]{2,1,0:T(8,128)(2,1)S(1)} collective-permute-done((bf16[16,64,128]{2,1,0:T(8,128)(2,1)S(1)}, bf16[16,64,128]{2,1,0:T(8,128)(2,1)S(1)}, u32[]{:S(2)}, u32[]{:S(2)}) %collective-permute-start.9) | collective-permute-done | bytes 262176 | tf_op jit(solution)/shard_map/ppermute | solution.py:43
  31.2 1.3 %shard_map.64 = (bf16[1024,256]{1,0:T(8,128)(2,1)S(1)}, f32[72,128]{1,0:T(8,128)S(1)}) custom-call(s32[390]{0:T(512)S(1)} %concatenate.3.index_ref, bf16[16,6,64,256]{3,2,1,0:T(8,128)(2,1)S(1)} %copy-done, f32[1024,128]{1,0:T(8,128)S(1)} %shard_map.63.partial_ref, bf16[16,64,128]{2,1,0:T(8,128)(2,1)S(1)} %collective-permute-done.9.refs_0_), custom_call_target="tpu_custom_call" | custom-call | tf_op jit(solution)/shard_map/pallas_call | solution.py:375
  32.5 1.3 %collective-permute-start.10 = (f32[72,128]{1,0:T(8,128)S(1)}, f32[72,128]{1,0:T(8,128)S(1)}, u32[]{:S(2)}, u32[]{:S(2)}) collective-permute-start(f32[72,128]{1,0:T(8,128)S(1)} %get-tuple-element.22), channel_id=1, source_target_pairs={{0,4},{4,0},{8,12},{12,8},{16,20},{20,16},{24,28},{28,24},{1,5},{5... | collective-permute-start | bytes 110600 | tf_op jit(solution)/shard_map/ppermute | solution.py:48
  33.8 0.9 %collective-permute-done.10 = f32[72,128]{1,0:T(8,128)S(1)} collective-permute-done((f32[72,128]{1,0:T(8,128)S(1)}, f32[72,128]{1,0:T(8,128)S(1)}, u32[]{:S(2)}, u32[]{:S(2)}) %collective-permute-start.10) | collective-permute-done | bytes 36896 | tf_op jit(solution)/shard_map/ppermute | solution.py:48
  34.6 3.5 %collective-permute-start.11 = (f32[72,128]{1,0:T(8,128)S(1)}, f32[72,128]{1,0:T(8,128)S(1)}, u32[]{:S(2)}, u32[]{:S(2)}) collective-permute-start(f32[72,128]{1,0:T(8,128)S(1)} %add.28), channel_id=1, source_target_pairs={{0,16},{4,20},{8,24},{12,28},{16,0},{20,4},{24,8},{28,12},{1,17},{... | collective-permute-start | bytes 110600 | tf_op jit(solution)/shard_map/ppermute | solution.py:48
  38.1 1.0 %collective-permute-start.12 = (f32[72,128]{1,0:T(8,128)S(1)}, f32[72,128]{1,0:T(8,128)S(1)}, u32[]{:S(2)}, u32[]{:S(2)}) collective-permute-start(f32[72,128]{1,0:T(8,128)S(1)} %add.28), channel_id=1, source_target_pairs={{0,24},{4,28},{8,16},{12,20},{16,8},{20,12},{24,0},{28,4},{1,25},{... | collective-permute-start | bytes 110600 | tf_op jit(solution)/shard_map/ppermute | solution.py:48
  39.1 0.5 collective-permute-start.13
  39.6 0.5 collective-permute-done.11
  40.1 3.8 %collective-permute-done.12 = f32[72,128]{1,0:T(8,128)S(1)} collective-permute-done((f32[72,128]{1,0:T(8,128)S(1)}, f32[72,128]{1,0:T(8,128)S(1)}, u32[]{:S(2)}, u32[]{:S(2)}) %collective-permute-start.12) | collective-permute-done | bytes 36896 | tf_op jit(solution)/shard_map/ppermute | solution.py:48
  43.8 0.0 collective-permute-done.13
  43.9 1.0 %collective-permute-start.14 = (f32[72,128]{1,0:T(8,128)S(1)}, f32[72,128]{1,0:T(8,128)S(1)}, u32[]{:S(2)}, u32[]{:S(2)}) collective-permute-start(f32[72,128]{1,0:T(8,128)S(1)} %add_add_fusion.1), channel_id=1, source_target_pairs={{0,3},{1,2},{2,1},{3,0},{4,7},{5,6},{6,5},{7,4},{8,11},{9,10},{10,... | collective-permute-start | bytes 110600 | tf_op jit(solution)/shard_map/ppermute | solution.py:48
  44.8 1.5 %collective-permute-start.15 = (f32[72,128]{1,0:T(8,128)S(1)}, f32[72,128]{1,0:T(8,128)S(1)}, u32[]{:S(2)}, u32[]{:S(2)}) collective-permute-start(f32[72,128]{1,0:T(8,128)S(1)} %add_add_fusion.1), channel_id=1, source_target_pairs={{0,2},{1,3},{2,0},{3,1},{4,6},{5,7},{6,4},{7,5},{8,10},{9,11},{10,... | collective-permute-start | bytes 110600 | tf_op jit(solution)/shard_map/ppermute | solution.py:48
  46.3 1.1 %collective-permute-start.16 = (f32[72,128]{1,0:T(8,128)S(1)}, f32[72,128]{1,0:T(8,128)S(1)}, u32[]{:S(2)}, u32[]{:S(2)}) collective-permute-start(f32[72,128]{1,0:T(8,128)S(1)} %add_add_fusion.1), channel_id=1, source_target_pairs={{0,1},{1,0},{2,3},{3,2},{4,5},{5,4},{6,7},{7,6},{8,9},{9,8},{10,11... | collective-permute-start | bytes 110600 | tf_op jit(solution)/shard_map/ppermute | solution.py:48
  47.4 1.4 %collective-permute-done.14 = f32[72,128]{1,0:T(8,128)S(1)} collective-permute-done((f32[72,128]{1,0:T(8,128)S(1)}, f32[72,128]{1,0:T(8,128)S(1)}, u32[]{:S(2)}, u32[]{:S(2)}) %collective-permute-start.14) | collective-permute-done | bytes 36896 | tf_op jit(solution)/shard_map/ppermute | solution.py:48
  48.8 0.4 collective-permute-done.15
  49.2 1.1 %collective-permute-done.16 = f32[72,128]{1,0:T(8,128)S(1)} collective-permute-done((f32[72,128]{1,0:T(8,128)S(1)}, f32[72,128]{1,0:T(8,128)S(1)}, u32[]{:S(2)}, u32[]{:S(2)}) %collective-permute-start.16) | collective-permute-done | bytes 36896 | tf_op jit(solution)/shard_map/ppermute | solution.py:48
  50.3 4.3 %shard_map.65 = (f32[1024,128]{1,0:T(8,128)}, f32[128,128]{1,0:T(8,128)}) custom-call(f32[72,128]{1,0:T(8,128)S(1)} %add_add_fusion.packed_ref, bf16[1024,256]{1,0:T(8,128)(2,1)S(1)} %get-tuple-element.23.both_ref), custom_call_target="tpu_custom_call" | custom-call | tf_op jit(solution)/shard_map/pallas_call | solution.py:379
  (3 shorter events, 0.0 us)
Async XLA Ops:
  1.7 4.8 %collective-permute-start = (bf16[16,64,128]{2,1,0:T(8,128)(2,1)S(1)}, bf16[16,64,128]{2,1,0:T(8,128)(2,1)S(1)}, u32[]{:S(2)}, u32[]{:S(2)}) collective-permute-start(bf16[16,64,128]{2,1,0:T(8,128)(2,1)S(1)} %bitcast.8), channel_id=1, source_target_pairs={{0,4},{4,0},{8,12},{12,8},{16,20},{20,16},{24,28},{28,24},{1,5},{5... | collective-permute-start | bytes 786440 | tf_op jit(solution)/shard_map/ppermute | solution.py:25
  2.2 6.9 %collective-permute-start.1 = (bf16[16,64,128]{2,1,0:T(8,128)(2,1)S(1)}, bf16[16,64,128]{2,1,0:T(8,128)(2,1)S(1)}, u32[]{:S(2)}, u32[]{:S(2)}) collective-permute-start(bf16[16,64,128]{2,1,0:T(8,128)(2,1)S(1)} %bitcast.9), channel_id=1, source_target_pairs={{0,1},{1,0},{2,3},{3,2},{4,6},{5,7},{6,4},{7,5},{8,9},{9,8},{10,11... | collective-permute-start | bytes 786440 | tf_op jit(solution)/shard_map/ppermute | solution.py:43
  4.8 10.4 %collective-permute-start.3 = (bf16[16,64,128]{2,1,0:T(8,128)(2,1)S(1)}, bf16[16,64,128]{2,1,0:T(8,128)(2,1)S(1)}, u32[]{:S(2)}, u32[]{:S(2)}) collective-permute-start(bf16[16,64,128]{2,1,0:T(8,128)(2,1)S(1)} %bitcast.10), channel_id=1, source_target_pairs={{4,8},{8,4},{12,16},{16,12},{20,24},{24,20},{5,9},{9,5},{13,17},{1... | collective-permute-start | bytes 786440 | tf_op jit(solution)/shard_map/ppermute | solution.py:25
  6.5 8.7 %collective-permute-start.2 = (bf16[16,64,128]{2,1,0:T(8,128)(2,1)S(1)}, bf16[16,64,128]{2,1,0:T(8,128)(2,1)S(1)}, u32[]{:S(2)}, u32[]{:S(2)}) collective-permute-start(bf16[16,64,128]{2,1,0:T(8,128)(2,1)S(1)} %bitcast.11), channel_id=1, source_target_pairs={{0,2},{1,3},{2,0},{3,1},{4,5},{5,4},{6,7},{7,6},{8,10},{9,11},{10,... | collective-permute-start | bytes 786440 | tf_op jit(solution)/shard_map/ppermute | solution.py:43
  9.1 7.6 %collective-permute-start.4 = (bf16[16,64,128]{2,1,0:T(8,128)(2,1)S(1)}, bf16[16,64,128]{2,1,0:T(8,128)(2,1)S(1)}, u32[]{:S(2)}, u32[]{:S(2)}) collective-permute-start(bf16[16,64,128]{2,1,0:T(8,128)(2,1)S(1)} %collective-permute-done.1.refs_1_), channel_id=1, source_target_pairs={{0,2},{1,3},{2,0},{3,1},{4,5},{5,4},{6,7},{7,6},{8,10},{9,11},{10,... | collective-permute-start | bytes 786440 | tf_op jit(solution)/shard_map/ppermute | solution.py:43
  12.4 1.9 %copy-start = (bf16[16,6,64,256]{3,2,1,0:T(8,128)(2,1)S(1)}, bf16[16,6,64,256]{3,2,1,0:T(8,128)(2,1)}, u32[]{:S(2)}) copy-start(bf16[16,6,64,256]{3,2,1,0:T(8,128)(2,1)} %hamiltonian_ref.11) | copy-start | bytes 9437188
  16.7 3.2 %copy-start.1 = (f32[1024,128]{1,0:T(8,128)S(1)}, f32[1024,128]{1,0:T(8,128)}, u32[]{:S(2)}) copy-start(f32[1024,128]{1,0:T(8,128)} %refs_2_.1) | copy-start | bytes 1572868
  16.7 3.2 %copy-start.2 = (f32[1024]{0:T(1024)S(1)}, f32[1024]{0:T(1024)}, u32[]{:S(2)}) copy-start(f32[1024]{0:T(1024)} %param.6) | copy-start | bytes 12292
  17.7 3.3 %collective-permute-start.5 = (bf16[16,64,128]{2,1,0:T(8,128)(2,1)S(1)}, bf16[16,64,128]{2,1,0:T(8,128)(2,1)S(1)}, u32[]{:S(2)}, u32[]{:S(2)}) collective-permute-start(bf16[16,64,128]{2,1,0:T(8,128)(2,1)S(1)} %get-tuple-element.21.own_ref), channel_id=1, source_target_pairs={{0,4},{4,0},{8,12},{12,8},{16,20},{20,16},{24,28},{28,24},{1,5},{5... | collective-permute-start | bytes 786440 | tf_op jit(solution)/shard_map/ppermute | solution.py:25
  18.5 6.4 %collective-permute-start.6 = (bf16[16,64,128]{2,1,0:T(8,128)(2,1)S(1)}, bf16[16,64,128]{2,1,0:T(8,128)(2,1)S(1)}, u32[]{:S(2)}, u32[]{:S(2)}) collective-permute-start(bf16[16,64,128]{2,1,0:T(8,128)(2,1)S(1)} %get-tuple-element.21.own_ref), channel_id=1, source_target_pairs={{0,1},{1,0},{2,3},{3,2},{4,6},{5,7},{6,4},{7,5},{8,9},{9,8},{10,11... | collective-permute-start | bytes 786440 | tf_op jit(solution)/shard_map/ppermute | solution.py:43
  19.3 7.1 %collective-permute-start.8 = (bf16[16,64,128]{2,1,0:T(8,128)(2,1)S(1)}, bf16[16,64,128]{2,1,0:T(8,128)(2,1)S(1)}, u32[]{:S(2)}, u32[]{:S(2)}) collective-permute-start(bf16[16,64,128]{2,1,0:T(8,128)(2,1)S(1)} %get-tuple-element.21.own_ref), channel_id=1, source_target_pairs={{4,8},{8,4},{12,16},{16,12},{20,24},{24,20},{5,9},{9,5},{13,17},{1... | collective-permute-start | bytes 786440 | tf_op jit(solution)/shard_map/ppermute | solution.py:25
  21.0 6.4 %collective-permute-start.7 = (bf16[16,64,128]{2,1,0:T(8,128)(2,1)S(1)}, bf16[16,64,128]{2,1,0:T(8,128)(2,1)S(1)}, u32[]{:S(2)}, u32[]{:S(2)}) collective-permute-start(bf16[16,64,128]{2,1,0:T(8,128)(2,1)S(1)} %get-tuple-element.21.own_ref), channel_id=1, source_target_pairs={{0,2},{1,3},{2,0},{3,1},{4,5},{5,4},{6,7},{7,6},{8,10},{9,11},{10,... | collective-permute-start | bytes 786440 | tf_op jit(solution)/shard_map/ppermute | solution.py:43
  24.8 6.4 %collective-permute-start.9 = (bf16[16,64,128]{2,1,0:T(8,128)(2,1)S(1)}, bf16[16,64,128]{2,1,0:T(8,128)(2,1)S(1)}, u32[]{:S(2)}, u32[]{:S(2)}) collective-permute-start(bf16[16,64,128]{2,1,0:T(8,128)(2,1)S(1)} %collective-permute-done.6.refs_1_), channel_id=1, source_target_pairs={{0,2},{1,3},{2,0},{3,1},{4,5},{5,4},{6,7},{7,6},{8,10},{9,11},{10,... | collective-permute-start | bytes 786440 | tf_op jit(solution)/shard_map/ppermute | solution.py:43
  32.5 2.2 %collective-permute-start.10 = (f32[72,128]{1,0:T(8,128)S(1)}, f32[72,128]{1,0:T(8,128)S(1)}, u32[]{:S(2)}, u32[]{:S(2)}) collective-permute-start(f32[72,128]{1,0:T(8,128)S(1)} %get-tuple-element.22), channel_id=1, source_target_pairs={{0,4},{4,0},{8,12},{12,8},{16,20},{20,16},{24,28},{28,24},{1,5},{5... | collective-permute-start | bytes 110600 | tf_op jit(solution)/shard_map/ppermute | solution.py:48
  34.6 5.5 %collective-permute-start.11 = (f32[72,128]{1,0:T(8,128)S(1)}, f32[72,128]{1,0:T(8,128)S(1)}, u32[]{:S(2)}, u32[]{:S(2)}) collective-permute-start(f32[72,128]{1,0:T(8,128)S(1)} %add.28), channel_id=1, source_target_pairs={{0,16},{4,20},{8,24},{12,28},{16,0},{20,4},{24,8},{28,12},{1,17},{... | collective-permute-start | bytes 110600 | tf_op jit(solution)/shard_map/ppermute | solution.py:48
  38.1 5.8 %collective-permute-start.12 = (f32[72,128]{1,0:T(8,128)S(1)}, f32[72,128]{1,0:T(8,128)S(1)}, u32[]{:S(2)}, u32[]{:S(2)}) collective-permute-start(f32[72,128]{1,0:T(8,128)S(1)} %add.28), channel_id=1, source_target_pairs={{0,24},{4,28},{8,16},{12,20},{16,8},{20,12},{24,0},{28,4},{1,25},{... | collective-permute-start | bytes 110600 | tf_op jit(solution)/shard_map/ppermute | solution.py:48
  39.1 4.8 %collective-permute-start.13 = (f32[72,128]{1,0:T(8,128)S(1)}, f32[72,128]{1,0:T(8,128)S(1)}, u32[]{:S(2)}, u32[]{:S(2)}) collective-permute-start(f32[72,128]{1,0:T(8,128)S(1)} %add.28), channel_id=1, source_target_pairs={{0,8},{4,12},{8,0},{12,4},{16,24},{20,28},{24,16},{28,20},{1,9},{5... | collective-permute-start | bytes 110600 | tf_op jit(solution)/shard_map/ppermute | solution.py:48
  43.9 5.0 %collective-permute-start.14 = (f32[72,128]{1,0:T(8,128)S(1)}, f32[72,128]{1,0:T(8,128)S(1)}, u32[]{:S(2)}, u32[]{:S(2)}) collective-permute-start(f32[72,128]{1,0:T(8,128)S(1)} %add_add_fusion.1), channel_id=1, source_target_pairs={{0,3},{1,2},{2,1},{3,0},{4,7},{5,6},{6,5},{7,4},{8,11},{9,10},{10,... | collective-permute-start | bytes 110600 | tf_op jit(solution)/shard_map/ppermute | solution.py:48
  44.8 4.4 %collective-permute-start.15 = (f32[72,128]{1,0:T(8,128)S(1)}, f32[72,128]{1,0:T(8,128)S(1)}, u32[]{:S(2)}, u32[]{:S(2)}) collective-permute-start(f32[72,128]{1,0:T(8,128)S(1)} %add_add_fusion.1), channel_id=1, source_target_pairs={{0,2},{1,3},{2,0},{3,1},{4,6},{5,7},{6,4},{7,5},{8,10},{9,11},{10,... | collective-permute-start | bytes 110600 | tf_op jit(solution)/shard_map/ppermute | solution.py:48
  46.3 4.0 %collective-permute-start.16 = (f32[72,128]{1,0:T(8,128)S(1)}, f32[72,128]{1,0:T(8,128)S(1)}, u32[]{:S(2)}, u32[]{:S(2)}) collective-permute-start(f32[72,128]{1,0:T(8,128)S(1)} %add_add_fusion.1), channel_id=1, source_target_pairs={{0,1},{1,0},{2,3},{3,2},{4,5},{5,4},{6,7},{7,6},{8,9},{9,8},{10,11... | collective-permute-start | bytes 110600 | tf_op jit(solution)/shard_map/ppermute | solution.py:48

commit v16 on v15

--- a/solution.py
+++ b/solution.py
@@ -171,12 +171,6 @@
     return off_diagonal + jnp.transpose(off_diagonal) + jnp.where(row == lane, diagonal, 0.0)
 
 
-def inverse_of(value):
-    estimate = pl.reciprocal(value, approx=True)
-    estimate = estimate * (2.0 - value * estimate)
-    return estimate * (2.0 - value * estimate)
-
-
 def factor(gram, upper_ref, inverse_ref):
     size = gram.shape[1]
     panels = size // SUB
@@ -209,37 +203,45 @@
             )
             pivots = jnp.ones(shape, jnp.float32)
             reciprocals = jnp.ones(shape, jnp.float32)
+            columns = [jnp.zeros(shape, jnp.float32)] * SUB
             for j in range(0, SUB, 2):
                 a, b = along_rows(block[j], j), along_rows(block[j], j + 1)
                 c = along_rows(block[j + 1], j + 1)
                 determinant = a * c - b * b
-                over = inverse_of(determinant)
-                over_a = inverse_of(a)
+                over = pltpu.reciprocal(determinant, approx=True)
+                over_a = pltpu.reciprocal(a, approx=True)
+                over_c, shift = a * over, b * over_a
                 pivots = jnp.where(row_index == j, a, pivots)
                 pivots = jnp.where(row_index == j + 1, determinant * over_a, pivots)
                 reciprocals = jnp.where(row_index == j, over_a, reciprocals)
-                reciprocals = jnp.where(row_index == j + 1, a * over, reciprocals)
-                x, y = block[j], block[j + 1]
-                one = jnp.where(row_index == j + 1, b * over_a, 0.0)
-                one = jnp.where(row_index > j + 1, (x * c - y * b) * over, one)
-                two = jnp.where(row_index > j + 1, (y * a - x * b) * over, 0.0)
+                reciprocals = jnp.where(row_index == j + 1, over_c, reciprocals)
+                one, two = block[j] * c - block[j + 1] * b, block[j + 1] * a - block[j] * b
                 upper = {
                     n: (along_rows(block[n], j), along_rows(block[n], j + 1))
                     for n in range(j + 2, SUB)
                 }
                 for n in upper:
-                    block[n] = block[n] - one * upper[n][0] - two * upper[n][1]
+                    block[n] = block[n] - over * (one * upper[n][0] + two * upper[n][1])
                 if following is not None:
                     x, y = after[j], after[j + 1]
-                    next_one, next_two = (x * c - y * b) * over, (y * a - x * b) * over
+                    next_one, next_two = x * c - y * b, y * a - x * b
                     for n in range(SUB):
-                        following[n] = (
-                            following[n] - next_one * along_rows(x, n) - next_two * along_rows(y, n)
+                        following[n] = following[n] - over * (
+                            next_one * along_rows(x, n) + next_two * along_rows(y, n)
                         )
                     for n in upper:
-                        after[n] = after[n] - next_one * upper[n][0] - next_two * upper[n][1]
+                        after[n] = after[n] - over * (
+                            next_one * upper[n][0] + next_two * upper[n][1]
+                        )
+                one = jnp.where(row_index > j + 1, one * over, jnp.where(row_index == j + 1, shift, 0.0))
+                two = jnp.where(row_index > j + 1, two * over, 0.0)
                 right = right - one * along_rows(right, j) - two * along_rows(right, j + 1)
                 left = left - one * along_rows(left, j) - two * along_rows(left, j + 1)
+                columns[j + 1] = jnp.where(row_index == j, shift, columns[j + 1])
+                for n in upper:
+                    unit = (upper[n][1] - shift * upper[n][0]) * over_c
+                    columns[n] = jnp.where(row_index == j, upper[n][0] * over_a, columns[n])
+                    columns[n] = jnp.where(row_index == j + 1, unit, columns[n])
             scale = lax.rsqrt(pivots)
             upper_ref[pl.ds(first, SUB), :] = jnp.where(
                 lane_index >= row_index + first, right * scale, 0.0
@@ -248,8 +250,7 @@
             if k + 1 < panels:
                 reduced = jnp.where(lane_index >= first + SUB, right, left) * reciprocals
                 for n in range(SUB - 1, 0, -1):
-                    column = jnp.where(row_index < n, block[n] * reciprocals, 0.0)
-                    reduced = reduced - column * along_rows(reduced, n)
+                    reduced = reduced - columns[n] * along_rows(reduced, n)
                 rows_then.append(held[k])
                 rows_reduced.append(jnp.where(between(first + SUB, end * SUB), 0.0, reduced))
                 rows = [along_rows(reduced, n) for n in range(SUB)]
@@ -350,10 +351,7 @@
             partial = own_part(index_array, value, *terms)
             later, pairs[0], partial = lax.optimization_barrier((value, pairs[0], partial))
         else:
-            later, pairs[0], index_array, slab = lax.optimization_barrier(
-                (value, pairs[0], index_array, trial_slab)
-            )
-            terms = (weights.reshape(-1, 1) * slab,)
+            later, pairs[0], index_array = lax.optimization_barrier((value, pairs[0], index_array))
         others = [cycle_exchange(later, level) for level in range(1, levels)]
         pieces = [value, arrived]
         for level, other in zip(range(1, levels), others):
@@ -366,7 +364,8 @@
         )(index_array, hamiltonian, partial, *[pieces[number] for number in middle])
         return [partial] + [pieces[number] for number in ending]
 
-    parts = coupled(trial_slab.reshape(rounded.shape).astype(jnp.bfloat16), index_array, False)
+    weighted = weights.reshape(-1, 1) * trial_slab
+    parts = coupled(trial_slab.reshape(rounded.shape).astype(jnp.bfloat16), index_array, False, weighted)
     once, once_round = call(
         functools.partial(first_kernel, ending), (flat, rounded), [smem] + [vmem] * (2 + len(ending))
     )(index_array, hamiltonian, *parts)

time: 54.9 us -> 54.2 us (0.987)
  other arithmetic: 2.34 us -> 1.46 us
    convert_element_type x1 -> x0, other arithmetic: 1.07 us -> none  [on_device(): trial_slab.reshape(rounded.shape).astype(jnp.bfloat16)]
    ppermute x4, starting transfers between devices: 2.65 us -> 3.69 us  [pair_exchange(): return lax.ppermute(value, 'group', route)]
    ppermute x7, starting transfers between devices: 9.78 us -> 9.05 us  [from_partner(): lax.ppermute(value, axis, [(index, index ^ flip) for index in range(count)])]
  transfers between devices with their start and end apart: 17 -> 17, of which waited for: 10 -> 11; matrix products, arithmetic and copies ran while one was open for 4% -> 2% of each run, Pallas kernels for 9% -> 9%
where the time goes in v16:
time: 54.2 us; the launch traced here: 54 us
  starting transfers between devices  22.5 us (42%)
  waiting for transfers between devices  15.2 us (28%)
  Pallas kernels  11.1 us (20%)
  local copies, waits for them, and re-layouts  2.92 us (5%)
  other arithmetic  1.46 us (3%)
  between operations  0.79 us (1%)
    ppermute x6, starting transfers between devices, cycle_exchange(): return lax.ppermute(value, ('group', 'blk'), route)  9.81 us
    ppermute x7, starting transfers between devices, from_partner(): lax.ppermute(value, axis, [(index, index ^ flip) for index in range(count)])  9.05 us
    ppermute x7, waiting for transfers between devices, from_partner(): lax.ppermute(value, axis, [(index, index ^ flip) for index in range(count)])  7.91 us
    ppermute x6, waiting for transfers between devices, cycle_exchange(): return lax.ppermute(value, ('group', 'blk'), route)  7.26 us
    pallas_call x1, Pallas kernels, on_device(): call(functools.partial(factor_kernel, rows_total), (flat, square), [vmem,...  4.17 us
    ppermute x4, starting transfers between devices, pair_exchange(): return lax.ppermute(value, 'group', route)  3.69 us
    pallas_call x2, Pallas kernels, coupled(): call(functools.partial(middle_kernel, middle), flat, [smem] + [vmem] * (2...  2.93 us
    unnamed x7, local copies, waits for them, and re-layouts  2.72 us
  transfers between devices with their start and end apart: 17, of which 11 were waited for; matrix products, arithmetic and copies ran while one was open for 2% of the time, Pallas kernels for 9%

profile of v16, /device:TPU:0, one launch (start us, length us, event | category | flops | bytes accessed | tf_op | source)
XLA Modules:
  0.0 54.0 jit_solution(14925841102820529825)
XLA Ops:
  0.6 1.4 %broadcast_multiply_fusion = (f32[1024,128]{1,0:T(8,128)S(1)}, bf16[1024,128]{1,0:T(8,128)(2,1)S(1)}) fusion(f32[1024,128]{1,0:T(8,128)} %refs_2_.1, f32[1024]{0:T(1024)} %param.6), kind=kLoop, calls=%fused_computation | loop fusion | flops 262144 | bytes 1314816 | tf_op jit(solution)/shard_map/mul | solution.py:367
  2.1 0.5 collective-permute-start
  2.6 2.6 %collective-permute-start.1 = (bf16[16,64,128]{2,1,0:T(8,128)(2,1)S(1)}, bf16[16,64,128]{2,1,0:T(8,128)(2,1)S(1)}, u32[]{:S(2)}, u32[]{:S(2)}) collective-permute-start(bf16[16,64,128]{2,1,0:T(8,128)(2,1)S(1)} %bitcast.9), channel_id=1, source_target_pairs={{0,1},{1,0},{2,3},{3,2},{4,6},{5,7},{6,4},{7,5},{8,9},{9,8},{10,11... | collective-permute-start | bytes 786440 | tf_op jit(solution)/shard_map/ppermute | solution.py:43
  5.1 0.7 %collective-permute-start.3 = (bf16[16,64,128]{2,1,0:T(8,128)(2,1)S(1)}, bf16[16,64,128]{2,1,0:T(8,128)(2,1)S(1)}, u32[]{:S(2)}, u32[]{:S(2)}) collective-permute-start(bf16[16,64,128]{2,1,0:T(8,128)(2,1)S(1)} %bitcast.10), channel_id=1, source_target_pairs={{4,8},{8,4},{12,16},{16,12},{20,24},{24,20},{5,9},{9,5},{13,17},{1... | collective-permute-start | bytes 786440 | tf_op jit(solution)/shard_map/ppermute | solution.py:25
  5.8 0.8 %copy.6 = s32[16,6,4]{2,1,0:T(8,128)S(1)} copy(s32[16,6,4]{0,2,1:T(4,128)} %param.5) | data formatting | bytes 3072 | tf_op args[1]
  6.7 0.1 reshape.31
  6.8 0.1 concatenate.3.index_ref
  6.9 0.0 collective-permute-done.refs_0_
  6.9 1.6 %collective-permute-start.2 = (bf16[16,64,128]{2,1,0:T(8,128)(2,1)S(1)}, bf16[16,64,128]{2,1,0:T(8,128)(2,1)S(1)}, u32[]{:S(2)}, u32[]{:S(2)}) collective-permute-start(bf16[16,64,128]{2,1,0:T(8,128)(2,1)S(1)} %bitcast.11), channel_id=1, source_target_pairs={{0,2},{1,3},{2,0},{3,1},{4,5},{5,4},{6,7},{7,6},{8,10},{9,11},{10,... | collective-permute-start | bytes 786440 | tf_op jit(solution)/shard_map/ppermute | solution.py:43
  8.4 1.1 %collective-permute-done.1.refs_1_ = bf16[16,64,128]{2,1,0:T(8,128)(2,1)S(1)} collective-permute-done((bf16[16,64,128]{2,1,0:T(8,128)(2,1)S(1)}, bf16[16,64,128]{2,1,0:T(8,128)(2,1)S(1)}, u32[]{:S(2)}, u32[]{:S(2)}) %collective-permute-start.1) | collective-permute-done | bytes 262176 | tf_op jit(solution)/shard_map/ppermute | solution.py:43
  9.5 2.0 %collective-permute-start.4 = (bf16[16,64,128]{2,1,0:T(8,128)(2,1)S(1)}, bf16[16,64,128]{2,1,0:T(8,128)(2,1)S(1)}, u32[]{:S(2)}, u32[]{:S(2)}) collective-permute-start(bf16[16,64,128]{2,1,0:T(8,128)(2,1)S(1)} %collective-permute-done.1.refs_1_), channel_id=1, source_target_pairs={{0,2},{1,3},{2,0},{3,1},{4,5},{5,4},{6,7},{7,6},{8,10},{9,11},{10,... | collective-permute-start | bytes 786440 | tf_op jit(solution)/shard_map/ppermute | solution.py:43
  11.5 0.0 copy-start
  11.5 1.9 %copy-done = bf16[16,6,64,256]{3,2,1,0:T(8,128)(2,1)S(1)} copy-done((bf16[16,6,64,256]{3,2,1,0:T(8,128)(2,1)S(1)}, bf16[16,6,64,256]{3,2,1,0:T(8,128)(2,1)}, u32[]{:S(2)}) %copy-start) | copy-done | bytes 3145752
  13.4 0.9 %shard_map.59.partial_ref = f32[1024,128]{1,0:T(8,128)S(1)} custom-call(s32[390]{0:T(512)S(1)} %concatenate.3.index_ref, bf16[16,6,64,256]{3,2,1,0:T(8,128)(2,1)S(1)} %copy-done, bf16[16,64,128]{2,1,0:T(8,128)(2,1)S(1)} %bitcast.12, f32[1024,128]{1,0:T(8,128)S(1)} %get-tuple-element.22.refs_0_), custom_call_target="tpu_custom_call" | custom-call | tf_op jit(solution)/shard_map/pallas_call | solution.py:343
  14.3 0.0 collective-permute-done.3.refs_3_
  14.3 0.0 collective-permute-done.2.refs_2_
  14.4 1.5 %shard_map.60.partial_ref = f32[1024,128]{1,0:T(8,128)S(1)} custom-call(s32[390]{0:T(512)S(1)} %concatenate.3.index_ref, bf16[16,6,64,256]{3,2,1,0:T(8,128)(2,1)S(1)} %copy-done, f32[1024,128]{1,0:T(8,128)S(1)} %shard_map.59.partial_ref, bf16[16,64,128]{2,1,0:T(8,128)(2,1)S(1)} %collective-permute-done.refs_0_, ...), custom_call_target="tpu_custom_call" | custom-call | tf_op jit(solution)/shard_map/pallas_call | solution.py:362
  15.8 0.0 copy-start.1
  15.8 0.0 copy-start.2
  15.9 0.2 collective-permute-done.4.refs_0_
  16.1 0.9 %shard_map.61 = (f32[1024,128]{1,0:T(8,128)S(1)}, bf16[16,64,128]{2,1,0:T(8,128)(2,1)S(1)}) custom-call(s32[390]{0:T(512)S(1)} %concatenate.3.index_ref, bf16[16,6,64,256]{3,2,1,0:T(8,128)(2,1)S(1)} %copy-done, f32[1024,128]{1,0:T(8,128)S(1)} %shard_map.60.partial_ref, bf16[16,64,128]{2,1,0:T(8,128)(2,1)S(1)} %collective-permute-done.4.refs_0_), custom_call_target="tpu_custom_call" | custom-call | tf_op jit(solution)/shard_map/pallas_call | solution.py:369
  17.0 1.8 %collective-permute-start.5 = (bf16[16,64,128]{2,1,0:T(8,128)(2,1)S(1)}, bf16[16,64,128]{2,1,0:T(8,128)(2,1)S(1)}, u32[]{:S(2)}, u32[]{:S(2)}) collective-permute-start(bf16[16,64,128]{2,1,0:T(8,128)(2,1)S(1)} %get-tuple-element.19.own_ref), channel_id=1, source_target_pairs={{0,4},{4,0},{8,12},{12,8},{16,20},{20,16},{24,28},{28,24},{1,5},{5... | collective-permute-start | bytes 786440 | tf_op jit(solution)/shard_map/ppermute | solution.py:25
  18.8 0.5 collective-permute-start.6
  19.3 0.7 %collective-permute-start.8 = (bf16[16,64,128]{2,1,0:T(8,128)(2,1)S(1)}, bf16[16,64,128]{2,1,0:T(8,128)(2,1)S(1)}, u32[]{:S(2)}, u32[]{:S(2)}) collective-permute-start(bf16[16,64,128]{2,1,0:T(8,128)(2,1)S(1)} %get-tuple-element.19.own_ref), channel_id=1, source_target_pairs={{4,8},{8,4},{12,16},{16,12},{20,24},{24,20},{5,9},{9,5},{13,17},{1... | collective-permute-start | bytes 786440 | tf_op jit(solution)/shard_map/ppermute | solution.py:25
  20.0 0.0 copy-done.1
  20.0 0.0 copy-done.2
  20.0 1.0 %shard_map.62.partial_ref = f32[1024,128]{1,0:T(8,128)S(1)} custom-call(s32[390]{0:T(512)S(1)} %concatenate.3.index_ref, bf16[16,6,64,256]{3,2,1,0:T(8,128)(2,1)S(1)} %copy-done, bf16[16,64,128]{2,1,0:T(8,128)(2,1)S(1)} %get-tuple-element.19.own_ref, f32[8,128]{1,0:T(8,128)S(1)} %bitcast.13, f32[1024,128]{1,0:T(8,128)S(1)} %get-tuple-element.16.refs_1_, ...), custom_call_target="tpu_custom_call" | custom-call | tf_op jit(solution)/shard_map/pallas_call | solution.py:343
  21.0 0.0 collective-permute-done.5.refs_0_
  21.0 1.6 %collective-permute-start.7 = (bf16[16,64,128]{2,1,0:T(8,128)(2,1)S(1)}, bf16[16,64,128]{2,1,0:T(8,128)(2,1)S(1)}, u32[]{:S(2)}, u32[]{:S(2)}) collective-permute-start(bf16[16,64,128]{2,1,0:T(8,128)(2,1)S(1)} %get-tuple-element.19.own_ref), channel_id=1, source_target_pairs={{0,2},{1,3},{2,0},{3,1},{4,5},{5,4},{6,7},{7,6},{8,10},{9,11},{10,... | collective-permute-start | bytes 786440 | tf_op jit(solution)/shard_map/ppermute | solution.py:43
  22.6 2.6 %collective-permute-done.6.refs_1_ = bf16[16,64,128]{2,1,0:T(8,128)(2,1)S(1)} collective-permute-done((bf16[16,64,128]{2,1,0:T(8,128)(2,1)S(1)}, bf16[16,64,128]{2,1,0:T(8,128)(2,1)S(1)}, u32[]{:S(2)}, u32[]{:S(2)}) %collective-permute-start.6) | collective-permute-done | bytes 262176 | tf_op jit(solution)/shard_map/ppermute | solution.py:43
  25.2 1.5 %collective-permute-start.9 = (bf16[16,64,128]{2,1,0:T(8,128)(2,1)S(1)}, bf16[16,64,128]{2,1,0:T(8,128)(2,1)S(1)}, u32[]{:S(2)}, u32[]{:S(2)}) collective-permute-start(bf16[16,64,128]{2,1,0:T(8,128)(2,1)S(1)} %collective-permute-done.6.refs_1_), channel_id=1, source_target_pairs={{0,2},{1,3},{2,0},{3,1},{4,5},{5,4},{6,7},{7,6},{8,10},{9,11},{10,... | collective-permute-start | bytes 786440 | tf_op jit(solution)/shard_map/ppermute | solution.py:43
  26.7 0.0 collective-permute-done.8.refs_3_
  26.7 0.8 %collective-permute-done.7.refs_2_ = bf16[16,64,128]{2,1,0:T(8,128)(2,1)S(1)} collective-permute-done((bf16[16,64,128]{2,1,0:T(8,128)(2,1)S(1)}, bf16[16,64,128]{2,1,0:T(8,128)(2,1)S(1)}, u32[]{:S(2)}, u32[]{:S(2)}) %collective-permute-start.7) | collective-permute-done | bytes 262176 | tf_op jit(solution)/shard_map/ppermute | solution.py:43
  27.5 1.5 %shard_map.63.partial_ref = f32[1024,128]{1,0:T(8,128)S(1)} custom-call(s32[390]{0:T(512)S(1)} %concatenate.3.index_ref, bf16[16,6,64,256]{3,2,1,0:T(8,128)(2,1)S(1)} %copy-done, f32[1024,128]{1,0:T(8,128)S(1)} %shard_map.62.partial_ref, bf16[16,64,128]{2,1,0:T(8,128)(2,1)S(1)} %collective-permute-done.5.refs_0_, ...), custom_call_target="tpu_custom_call" | custom-call | tf_op jit(solution)/shard_map/pallas_call | solution.py:362
  28.9 2.6 %collective-permute-done.9.refs_0_ = bf16[16,64,128]{2,1,0:T(8,128)(2,1)S(1)} collective-permute-done((bf16[16,64,128]{2,1,0:T(8,128)(2,1)S(1)}, bf16[16,64,128]{2,1,0:T(8,128)(2,1)S(1)}, u32[]{:S(2)}, u32[]{:S(2)}) %collective-permute-start.9) | collective-permute-done | bytes 262176 | tf_op jit(solution)/shard_map/ppermute | solution.py:43
  31.6 1.3 %shard_map.64 = (bf16[1024,256]{1,0:T(8,128)(2,1)S(1)}, f32[72,128]{1,0:T(8,128)S(1)}) custom-call(s32[390]{0:T(512)S(1)} %concatenate.3.index_ref, bf16[16,6,64,256]{3,2,1,0:T(8,128)(2,1)S(1)} %copy-done, f32[1024,128]{1,0:T(8,128)S(1)} %shard_map.63.partial_ref, bf16[16,64,128]{2,1,0:T(8,128)(2,1)S(1)} %collective-permute-done.9.refs_0_), custom_call_target="tpu_custom_call" | custom-call | tf_op jit(solution)/shard_map/pallas_call | solution.py:374
  32.8 1.3 %collective-permute-start.10 = (f32[72,128]{1,0:T(8,128)S(1)}, f32[72,128]{1,0:T(8,128)S(1)}, u32[]{:S(2)}, u32[]{:S(2)}) collective-permute-start(f32[72,128]{1,0:T(8,128)S(1)} %get-tuple-element.20), channel_id=1, source_target_pairs={{0,4},{4,0},{8,12},{12,8},{16,20},{20,16},{24,28},{28,24},{1,5},{5... | collective-permute-start | bytes 110600 | tf_op jit(solution)/shard_map/ppermute | solution.py:48
  34.1 0.9 %collective-permute-done.10 = f32[72,128]{1,0:T(8,128)S(1)} collective-permute-done((f32[72,128]{1,0:T(8,128)S(1)}, f32[72,128]{1,0:T(8,128)S(1)}, u32[]{:S(2)}, u32[]{:S(2)}) %collective-permute-start.10) | collective-permute-done | bytes 36896 | tf_op jit(solution)/shard_map/ppermute | solution.py:48
  35.0 2.6 %collective-permute-start.11 = (f32[72,128]{1,0:T(8,128)S(1)}, f32[72,128]{1,0:T(8,128)S(1)}, u32[]{:S(2)}, u32[]{:S(2)}) collective-permute-start(f32[72,128]{1,0:T(8,128)S(1)} %add.28), channel_id=1, source_target_pairs={{0,16},{4,20},{8,24},{12,28},{16,0},{20,4},{24,8},{28,12},{1,17},{... | collective-permute-start | bytes 110600 | tf_op jit(solution)/shard_map/ppermute | solution.py:48
  37.6 1.3 %collective-permute-start.12 = (f32[72,128]{1,0:T(8,128)S(1)}, f32[72,128]{1,0:T(8,128)S(1)}, u32[]{:S(2)}, u32[]{:S(2)}) collective-permute-start(f32[72,128]{1,0:T(8,128)S(1)} %add.28), channel_id=1, source_target_pairs={{0,24},{4,28},{8,16},{12,20},{16,8},{20,12},{24,0},{28,4},{1,25},{... | collective-permute-start | bytes 110600 | tf_op jit(solution)/shard_map/ppermute | solution.py:48
  38.9 0.3 collective-permute-start.13
  39.2 0.6 %collective-permute-done.11 = f32[72,128]{1,0:T(8,128)S(1)} collective-permute-done((f32[72,128]{1,0:T(8,128)S(1)}, f32[72,128]{1,0:T(8,128)S(1)}, u32[]{:S(2)}, u32[]{:S(2)}) %collective-permute-start.11) | collective-permute-done | bytes 36896 | tf_op jit(solution)/shard_map/ppermute | solution.py:48
  39.8 3.5 %collective-permute-done.12 = f32[72,128]{1,0:T(8,128)S(1)} collective-permute-done((f32[72,128]{1,0:T(8,128)S(1)}, f32[72,128]{1,0:T(8,128)S(1)}, u32[]{:S(2)}, u32[]{:S(2)}) %collective-permute-start.12) | collective-permute-done | bytes 36896 | tf_op jit(solution)/shard_map/ppermute | solution.py:48
  43.3 0.0 collective-permute-done.13
  43.3 2.3 %collective-permute-start.14 = (f32[72,128]{1,0:T(8,128)S(1)}, f32[72,128]{1,0:T(8,128)S(1)}, u32[]{:S(2)}, u32[]{:S(2)}) collective-permute-start(f32[72,128]{1,0:T(8,128)S(1)} %add_add_fusion.1), channel_id=1, source_target_pairs={{0,3},{1,2},{2,1},{3,0},{4,7},{5,6},{6,5},{7,4},{8,11},{9,10},{10,... | collective-permute-start | bytes 110600 | tf_op jit(solution)/shard_map/ppermute | solution.py:48
  45.7 0.2 collective-permute-start.15
  45.8 1.0 %collective-permute-start.16 = (f32[72,128]{1,0:T(8,128)S(1)}, f32[72,128]{1,0:T(8,128)S(1)}, u32[]{:S(2)}, u32[]{:S(2)}) collective-permute-start(f32[72,128]{1,0:T(8,128)S(1)} %add_add_fusion.1), channel_id=1, source_target_pairs={{0,1},{1,0},{2,3},{3,2},{4,5},{5,4},{6,7},{7,6},{8,9},{9,8},{10,11... | collective-permute-start | bytes 110600 | tf_op jit(solution)/shard_map/ppermute | solution.py:48
  46.9 1.4 %collective-permute-done.14 = f32[72,128]{1,0:T(8,128)S(1)} collective-permute-done((f32[72,128]{1,0:T(8,128)S(1)}, f32[72,128]{1,0:T(8,128)S(1)}, u32[]{:S(2)}, u32[]{:S(2)}) %collective-permute-start.14) | collective-permute-done | bytes 36896 | tf_op jit(solution)/shard_map/ppermute | solution.py:48
  48.3 1.3 %collective-permute-done.15 = f32[72,128]{1,0:T(8,128)S(1)} collective-permute-done((f32[72,128]{1,0:T(8,128)S(1)}, f32[72,128]{1,0:T(8,128)S(1)}, u32[]{:S(2)}, u32[]{:S(2)}) %collective-permute-start.15) | collective-permute-done | bytes 36896 | tf_op jit(solution)/shard_map/ppermute | solution.py:48
  49.6 0.2 collective-permute-done.16
  49.8 4.2 %shard_map.65 = (f32[1024,128]{1,0:T(8,128)}, f32[128,128]{1,0:T(8,128)}) custom-call(f32[72,128]{1,0:T(8,128)S(1)} %add_add_fusion.packed_ref, bf16[1024,256]{1,0:T(8,128)(2,1)S(1)} %get-tuple-element.21.both_ref), custom_call_target="tpu_custom_call" | custom-call | tf_op jit(solution)/shard_map/pallas_call | solution.py:378
  (3 shorter events, 0.0 us)
Async XLA Ops:
  2.1 4.8 %collective-permute-start = (bf16[16,64,128]{2,1,0:T(8,128)(2,1)S(1)}, bf16[16,64,128]{2,1,0:T(8,128)(2,1)S(1)}, u32[]{:S(2)}, u32[]{:S(2)}) collective-permute-start(bf16[16,64,128]{2,1,0:T(8,128)(2,1)S(1)} %bitcast.8), channel_id=1, source_target_pairs={{0,4},{4,0},{8,12},{12,8},{16,20},{20,16},{24,28},{28,24},{1,5},{5... | collective-permute-start | bytes 786440 | tf_op jit(solution)/shard_map/ppermute | solution.py:25
  2.6 6.9 %collective-permute-start.1 = (bf16[16,64,128]{2,1,0:T(8,128)(2,1)S(1)}, bf16[16,64,128]{2,1,0:T(8,128)(2,1)S(1)}, u32[]{:S(2)}, u32[]{:S(2)}) collective-permute-start(bf16[16,64,128]{2,1,0:T(8,128)(2,1)S(1)} %bitcast.9), channel_id=1, source_target_pairs={{0,1},{1,0},{2,3},{3,2},{4,6},{5,7},{6,4},{7,5},{8,9},{9,8},{10,11... | collective-permute-start | bytes 786440 | tf_op jit(solution)/shard_map/ppermute | solution.py:43
  5.1 9.2 %collective-permute-start.3 = (bf16[16,64,128]{2,1,0:T(8,128)(2,1)S(1)}, bf16[16,64,128]{2,1,0:T(8,128)(2,1)S(1)}, u32[]{:S(2)}, u32[]{:S(2)}) collective-permute-start(bf16[16,64,128]{2,1,0:T(8,128)(2,1)S(1)} %bitcast.10), channel_id=1, source_target_pairs={{4,8},{8,4},{12,16},{16,12},{20,24},{24,20},{5,9},{9,5},{13,17},{1... | collective-permute-start | bytes 786440 | tf_op jit(solution)/shard_map/ppermute | solution.py:25
  6.9 7.5 %collective-permute-start.2 = (bf16[16,64,128]{2,1,0:T(8,128)(2,1)S(1)}, bf16[16,64,128]{2,1,0:T(8,128)(2,1)S(1)}, u32[]{:S(2)}, u32[]{:S(2)}) collective-permute-start(bf16[16,64,128]{2,1,0:T(8,128)(2,1)S(1)} %bitcast.11), channel_id=1, source_target_pairs={{0,2},{1,3},{2,0},{3,1},{4,5},{5,4},{6,7},{7,6},{8,10},{9,11},{10,... | collective-permute-start | bytes 786440 | tf_op jit(solution)/shard_map/ppermute | solution.py:43
  9.5 6.6 %collective-permute-start.4 = (bf16[16,64,128]{2,1,0:T(8,128)(2,1)S(1)}, bf16[16,64,128]{2,1,0:T(8,128)(2,1)S(1)}, u32[]{:S(2)}, u32[]{:S(2)}) collective-permute-start(bf16[16,64,128]{2,1,0:T(8,128)(2,1)S(1)} %collective-permute-done.1.refs_1_), channel_id=1, source_target_pairs={{0,2},{1,3},{2,0},{3,1},{4,5},{5,4},{6,7},{7,6},{8,10},{9,11},{10,... | collective-permute-start | bytes 786440 | tf_op jit(solution)/shard_map/ppermute | solution.py:43
  11.5 1.9 %copy-start = (bf16[16,6,64,256]{3,2,1,0:T(8,128)(2,1)S(1)}, bf16[16,6,64,256]{3,2,1,0:T(8,128)(2,1)}, u32[]{:S(2)}) copy-start(bf16[16,6,64,256]{3,2,1,0:T(8,128)(2,1)} %hamiltonian_ref.11) | copy-start | bytes 9437188
  15.8 4.2 %copy-start.1 = (f32[1024,128]{1,0:T(8,128)S(1)}, f32[1024,128]{1,0:T(8,128)}, u32[]{:S(2)}) copy-start(f32[1024,128]{1,0:T(8,128)} %refs_2_.1) | copy-start | bytes 1572868
  15.8 4.2 %copy-start.2 = (f32[1024]{0:T(1024)S(1)}, f32[1024]{0:T(1024)}, u32[]{:S(2)}) copy-start(f32[1024]{0:T(1024)} %param.6) | copy-start | bytes 12292
  17.0 4.0 %collective-permute-start.5 = (bf16[16,64,128]{2,1,0:T(8,128)(2,1)S(1)}, bf16[16,64,128]{2,1,0:T(8,128)(2,1)S(1)}, u32[]{:S(2)}, u32[]{:S(2)}) collective-permute-start(bf16[16,64,128]{2,1,0:T(8,128)(2,1)S(1)} %get-tuple-element.19.own_ref), channel_id=1, source_target_pairs={{0,4},{4,0},{8,12},{12,8},{16,20},{20,16},{24,28},{28,24},{1,5},{5... | collective-permute-start | bytes 786440 | tf_op jit(solution)/shard_map/ppermute | solution.py:25
  18.8 6.4 %collective-permute-start.6 = (bf16[16,64,128]{2,1,0:T(8,128)(2,1)S(1)}, bf16[16,64,128]{2,1,0:T(8,128)(2,1)S(1)}, u32[]{:S(2)}, u32[]{:S(2)}) collective-permute-start(bf16[16,64,128]{2,1,0:T(8,128)(2,1)S(1)} %get-tuple-element.19.own_ref), channel_id=1, source_target_pairs={{0,1},{1,0},{2,3},{3,2},{4,6},{5,7},{6,4},{7,5},{8,9},{9,8},{10,11... | collective-permute-start | bytes 786440 | tf_op jit(solution)/shard_map/ppermute | solution.py:43
  19.3 7.4 %collective-permute-start.8 = (bf16[16,64,128]{2,1,0:T(8,128)(2,1)S(1)}, bf16[16,64,128]{2,1,0:T(8,128)(2,1)S(1)}, u32[]{:S(2)}, u32[]{:S(2)}) collective-permute-start(bf16[16,64,128]{2,1,0:T(8,128)(2,1)S(1)} %get-tuple-element.19.own_ref), channel_id=1, source_target_pairs={{4,8},{8,4},{12,16},{16,12},{20,24},{24,20},{5,9},{9,5},{13,17},{1... | collective-permute-start | bytes 786440 | tf_op jit(solution)/shard_map/ppermute | solution.py:25
  21.0 6.4 %collective-permute-start.7 = (bf16[16,64,128]{2,1,0:T(8,128)(2,1)S(1)}, bf16[16,64,128]{2,1,0:T(8,128)(2,1)S(1)}, u32[]{:S(2)}, u32[]{:S(2)}) collective-permute-start(bf16[16,64,128]{2,1,0:T(8,128)(2,1)S(1)} %get-tuple-element.19.own_ref), channel_id=1, source_target_pairs={{0,2},{1,3},{2,0},{3,1},{4,5},{5,4},{6,7},{7,6},{8,10},{9,11},{10,... | collective-permute-start | bytes 786440 | tf_op jit(solution)/shard_map/ppermute | solution.py:43
  25.2 6.4 %collective-permute-start.9 = (bf16[16,64,128]{2,1,0:T(8,128)(2,1)S(1)}, bf16[16,64,128]{2,1,0:T(8,128)(2,1)S(1)}, u32[]{:S(2)}, u32[]{:S(2)}) collective-permute-start(bf16[16,64,128]{2,1,0:T(8,128)(2,1)S(1)} %collective-permute-done.6.refs_1_), channel_id=1, source_target_pairs={{0,2},{1,3},{2,0},{3,1},{4,5},{5,4},{6,7},{7,6},{8,10},{9,11},{10,... | collective-permute-start | bytes 786440 | tf_op jit(solution)/shard_map/ppermute | solution.py:43
  32.8 2.1 %collective-permute-start.10 = (f32[72,128]{1,0:T(8,128)S(1)}, f32[72,128]{1,0:T(8,128)S(1)}, u32[]{:S(2)}, u32[]{:S(2)}) collective-permute-start(f32[72,128]{1,0:T(8,128)S(1)} %get-tuple-element.20), channel_id=1, source_target_pairs={{0,4},{4,0},{8,12},{12,8},{16,20},{20,16},{24,28},{28,24},{1,5},{5... | collective-permute-start | bytes 110600 | tf_op jit(solution)/shard_map/ppermute | solution.py:48
  35.0 4.9 %collective-permute-start.11 = (f32[72,128]{1,0:T(8,128)S(1)}, f32[72,128]{1,0:T(8,128)S(1)}, u32[]{:S(2)}, u32[]{:S(2)}) collective-permute-start(f32[72,128]{1,0:T(8,128)S(1)} %add.28), channel_id=1, source_target_pairs={{0,16},{4,20},{8,24},{12,28},{16,0},{20,4},{24,8},{28,12},{1,17},{... | collective-permute-start | bytes 110600 | tf_op jit(solution)/shard_map/ppermute | solution.py:48
  37.6 5.8 %collective-permute-start.12 = (f32[72,128]{1,0:T(8,128)S(1)}, f32[72,128]{1,0:T(8,128)S(1)}, u32[]{:S(2)}, u32[]{:S(2)}) collective-permute-start(f32[72,128]{1,0:T(8,128)S(1)} %add.28), channel_id=1, source_target_pairs={{0,24},{4,28},{8,16},{12,20},{16,8},{20,12},{24,0},{28,4},{1,25},{... | collective-permute-start | bytes 110600 | tf_op jit(solution)/shard_map/ppermute | solution.py:48
  38.9 4.4 %collective-permute-start.13 = (f32[72,128]{1,0:T(8,128)S(1)}, f32[72,128]{1,0:T(8,128)S(1)}, u32[]{:S(2)}, u32[]{:S(2)}) collective-permute-start(f32[72,128]{1,0:T(8,128)S(1)} %add.28), channel_id=1, source_target_pairs={{0,8},{4,12},{8,0},{12,4},{16,24},{20,28},{24,16},{28,20},{1,9},{5... | collective-permute-start | bytes 110600 | tf_op jit(solution)/shard_map/ppermute | solution.py:48
  43.3 5.0 %collective-permute-start.14 = (f32[72,128]{1,0:T(8,128)S(1)}, f32[72,128]{1,0:T(8,128)S(1)}, u32[]{:S(2)}, u32[]{:S(2)}) collective-permute-start(f32[72,128]{1,0:T(8,128)S(1)} %add_add_fusion.1), channel_id=1, source_target_pairs={{0,3},{1,2},{2,1},{3,0},{4,7},{5,6},{6,5},{7,4},{8,11},{9,10},{10,... | collective-permute-start | bytes 110600 | tf_op jit(solution)/shard_map/ppermute | solution.py:48
  45.7 4.0 %collective-permute-start.15 = (f32[72,128]{1,0:T(8,128)S(1)}, f32[72,128]{1,0:T(8,128)S(1)}, u32[]{:S(2)}, u32[]{:S(2)}) collective-permute-start(f32[72,128]{1,0:T(8,128)S(1)} %add_add_fusion.1), channel_id=1, source_target_pairs={{0,2},{1,3},{2,0},{3,1},{4,6},{5,7},{6,4},{7,5},{8,10},{9,11},{10,... | collective-permute-start | bytes 110600 | tf_op jit(solution)/shard_map/ppermute | solution.py:48
  45.8 4.0 %collective-permute-start.16 = (f32[72,128]{1,0:T(8,128)S(1)}, f32[72,128]{1,0:T(8,128)S(1)}, u32[]{:S(2)}, u32[]{:S(2)}) collective-permute-start(f32[72,128]{1,0:T(8,128)S(1)} %add_add_fusion.1), channel_id=1, source_target_pairs={{0,1},{1,0},{2,3},{3,2},{4,5},{5,4},{6,7},{7,6},{8,9},{9,8},{10,11... | collective-permute-start | bytes 110600 | tf_op jit(solution)/shard_map/ppermute | solution.py:48

commit v17 on v16

--- a/solution.py
+++ b/solution.py
@@ -171,12 +171,13 @@
     return off_diagonal + jnp.transpose(off_diagonal) + jnp.where(row == lane, diagonal, 0.0)
 
 
-def factor(gram, upper_ref, inverse_ref):
-    size = gram.shape[1]
+def factor(work_ref, upper_ref, inverse_ref):
+    size = work_ref.shape[0]
     panels = size // SUB
     shape = (SUB, size)
     row_index = lax.broadcasted_iota(jnp.int32, shape, 0)
     lane_index = lax.broadcasted_iota(jnp.int32, shape, 1)
+    width = OUTER * SUB
 
     def along_lanes(panel, first):
         return [jnp.broadcast_to(panel[:, first + c : first + c + 1], shape) for c in range(SUB)]
@@ -187,19 +188,20 @@
     def between(low, high):
         return (lane_index >= low) & (lane_index < high)
 
-    held = [gram[k * SUB : (k + 1) * SUB, :] for k in range(panels)]
-    for outer in range(0, panels, OUTER):
-        end = outer + OUTER
+    def outer_block(outer, carry):
+        limit = size - outer * width
+        held = [work_ref[pl.ds(k * SUB, SUB), :] for k in range(panels)]
         rows_then, rows_reduced = [], []
-        block = along_lanes(held[outer], outer * SUB)
-        for k in range(outer, end):
+        block = along_lanes(held[0], 0)
+        for k in range(OUTER):
             first = k * SUB
-            below = {p: along_lanes(held[p], first) for p in range(k + 1, end)}
-            after = list(below[k + 1]) if k + 1 < end else None
-            following = along_lanes(held[k + 1], first + SUB) if k + 1 < end else None
+            below = {p: along_lanes(held[p], first) for p in range(k + 1, OUTER)}
+            after = list(below[k + 1]) if k + 1 < OUTER else None
+            following = along_lanes(held[k + 1], first + SUB) if k + 1 < OUTER else None
             right = held[k]
             left = jnp.where(
-                lane_index < first, held[k], jnp.where(lane_index == row_index + first, 1.0, 0.0)
+                (lane_index < first) | (lane_index >= limit), held[k],
+                jnp.where(lane_index == row_index + first, 1.0, 0.0),
             )
             pivots = jnp.ones(shape, jnp.float32)
             reciprocals = jnp.ones(shape, jnp.float32)
@@ -243,41 +245,45 @@
                     columns[n] = jnp.where(row_index == j, upper[n][0] * over_a, columns[n])
                     columns[n] = jnp.where(row_index == j + 1, unit, columns[n])
             scale = lax.rsqrt(pivots)
-            upper_ref[pl.ds(first, SUB), :] = jnp.where(
-                lane_index >= row_index + first, right * scale, 0.0
+            rows_out = pl.ds(pl.multiple_of(outer * width + first, SUB), SUB)
+            kept = (lane_index >= row_index + first) & (lane_index < limit)
+            upper_ref[rows_out, :] = pltpu.roll(
+                jnp.where(kept, right * scale, 0.0), outer * width, 1
             )
-            inverse_ref[pl.ds(first, SUB), :] = left * scale
-            if k + 1 < panels:
-                reduced = jnp.where(lane_index >= first + SUB, right, left) * reciprocals
-                for n in range(SUB - 1, 0, -1):
-                    reduced = reduced - columns[n] * along_rows(reduced, n)
-                rows_then.append(held[k])
-                rows_reduced.append(jnp.where(between(first + SUB, end * SUB), 0.0, reduced))
-                rows = [along_rows(reduced, n) for n in range(SUB)]
-                for p in below:
-                    total = jnp.where(between(first, first + SUB), 0.0, held[p])
-                    for n in range(SUB):
-                        total = total - below[p][n] * rows[n]
-                    held[p] = total
+            inverse_ref[rows_out, :] = pltpu.roll(left * scale, outer * width, 1)
+            reduced = jnp.where(between(first + SUB, limit), right, left) * reciprocals
+            for n in range(SUB - 1, 0, -1):
+                reduced = reduced - columns[n] * along_rows(reduced, n)
+            rows_then.append(held[k])
+            rows_reduced.append(jnp.where(between(first + SUB, width), 0.0, reduced))
+            rows = [along_rows(reduced, n) for n in range(SUB)]
+            for p in below:
+                total = jnp.where(between(first, first + SUB), 0.0, held[p])
+                for n in range(SUB):
+                    total = total - below[p][n] * rows[n]
+                held[p] = total
             block = following
-        if end < panels:
-            change = lax.dot_general(
-                jnp.concatenate(rows_then, axis=0), jnp.concatenate(rows_reduced, axis=0),
-                (((0,), (0,)), ((), ())), precision=precise, preferred_element_type=jnp.float32,
-            )
-            for p in range(end, panels):
-                kept = jnp.where(between(outer * SUB, end * SUB), 0.0, held[p])
-                held[p] = kept - change[p * SUB : (p + 1) * SUB, :]
+        change = lax.dot_general(
+            jnp.concatenate(rows_then, axis=0), jnp.concatenate(rows_reduced, axis=0),
+            (((0,), (0,)), ((), ())), precision=precise, preferred_element_type=jnp.float32,
+        )
+        for p in range(OUTER, panels):
+            total = jnp.where(between(0, width), 0.0, held[p]) - change[p * SUB : (p + 1) * SUB, :]
+            work_ref[pl.ds((p - OUTER) * SUB, SUB), :] = pltpu.roll(total, size - width, 1)
+        return carry
+
+    lax.fori_loop(0, panels // OUTER, outer_block, 0)
 
 
 def factor_kernel(
     rows_total, packed_ref, both_ref, ortho_hbm, upper_hbm,
-    upper_ref, inverse_ref, ortho_ref, sent, upper_sent,
+    work_ref, upper_ref, inverse_ref, ortho_ref, sent, upper_sent,
 ):
     states = upper_ref.shape[0]
-    factor(unpack(packed_ref) * (1.0 / rows_total), upper_ref, inverse_ref)
-    copies = [pltpu.make_async_copy(upper_ref, upper_hbm, upper_sent)]
-    copies[0].start()
+    work_ref[...] = unpack(packed_ref) * (1.0 / rows_total)
+    factor(work_ref, upper_ref, inverse_ref)
+    upper_copy = pltpu.make_async_copy(upper_ref, upper_hbm, upper_sent)
+    upper_copy.start()
     high, low = two_parts(inverse_ref[...])
     right = jnp.concatenate(
         [
@@ -288,6 +294,7 @@
     )
     chunks = sent.shape[0]
     per_chunk = both_ref.shape[0] // chunks
+    copies = []
     for chunk in range(chunks):
         rows = pl.ds(chunk * per_chunk, per_chunk)
         product = lax.dot_general(
@@ -299,6 +306,7 @@
             pltpu.make_async_copy(ortho_ref.at[rows, :], ortho_hbm.at[rows, :], sent.at[chunk])
         )
         copies[-1].start()
+    upper_copy.wait()
     for copy in copies:
         copy.wait()
 
@@ -382,6 +390,7 @@
         [
             pltpu.VMEM((states, states), jnp.float32),
             pltpu.VMEM((states, states), jnp.float32),
+            pltpu.VMEM((states, states), jnp.float32),
             pltpu.VMEM((flat_rows, states), jnp.float32),
             pltpu.SemaphoreType.DMA((4,)),
             pltpu.SemaphoreType.DMA,

time: 54.2 us -> 54.7 us (level)
  no operation moved by 1% of the time
where the time goes in v17:
time: 54.7 us; the launch traced here: 54.5 us
  starting transfers between devices  22.5 us (41%)
  waiting for transfers between devices  15.2 us (28%)
  Pallas kernels  11.6 us (21%)
  local copies, waits for them, and re-layouts  2.92 us (5%)
  other arithmetic  1.46 us (3%)
  between operations  0.79 us (1%)
    ppermute x6, starting transfers between devices, cycle_exchange(): return lax.ppermute(value, ('group', 'blk'), route)  9.81 us
    ppermute x7, starting transfers between devices, from_partner(): lax.ppermute(value, axis, [(index, index ^ flip) for index in range(count)])  9.05 us
    ppermute x7, waiting for transfers between devices, from_partner(): lax.ppermute(value, axis, [(index, index ^ flip) for index in range(count)])  7.91 us
    ppermute x6, waiting for transfers between devices, cycle_exchange(): return lax.ppermute(value, ('group', 'blk'), route)  7.26 us
    pallas_call x1, Pallas kernels, on_device(): call(functools.partial(factor_kernel, rows_total), (flat, square), [vmem,...  4.64 us
    ppermute x4, starting transfers between devices, pair_exchange(): return lax.ppermute(value, 'group', route)  3.69 us
    pallas_call x2, Pallas kernels, coupled(): call(functools.partial(middle_kernel, middle), flat, [smem] + [vmem] * (2...  2.93 us
    unnamed x7, local copies, waits for them, and re-layouts  2.72 us
  transfers between devices with their start and end apart: 17, of which 11 were waited for; matrix products, arithmetic and copies ran while one was open for 2% of the time, Pallas kernels for 9%

profile of v17, /device:TPU:0, one launch (start us, length us, event | category | flops | bytes accessed | tf_op | source)
XLA Modules:
  0.0 54.5 jit_solution(9734069274908814779)
XLA Ops:
  0.6 1.4 %broadcast_multiply_fusion = (f32[1024,128]{1,0:T(8,128)S(1)}, bf16[1024,128]{1,0:T(8,128)(2,1)S(1)}) fusion(f32[1024,128]{1,0:T(8,128)} %refs_2_.1, f32[1024]{0:T(1024)} %param.6), kind=kLoop, calls=%fused_computation | loop fusion | flops 262144 | bytes 1314816 | tf_op jit(solution)/shard_map/mul | solution.py:375
  2.1 0.5 collective-permute-start
  2.6 2.6 %collective-permute-start.1 = (bf16[16,64,128]{2,1,0:T(8,128)(2,1)S(1)}, bf16[16,64,128]{2,1,0:T(8,128)(2,1)S(1)}, u32[]{:S(2)}, u32[]{:S(2)}) collective-permute-start(bf16[16,64,128]{2,1,0:T(8,128)(2,1)S(1)} %bitcast.9), channel_id=1, source_target_pairs={{0,1},{1,0},{2,3},{3,2},{4,6},{5,7},{6,4},{7,5},{8,9},{9,8},{10,11... | collective-permute-start | bytes 786440 | tf_op jit(solution)/shard_map/ppermute | solution.py:43
  5.1 0.7 %collective-permute-start.3 = (bf16[16,64,128]{2,1,0:T(8,128)(2,1)S(1)}, bf16[16,64,128]{2,1,0:T(8,128)(2,1)S(1)}, u32[]{:S(2)}, u32[]{:S(2)}) collective-permute-start(bf16[16,64,128]{2,1,0:T(8,128)(2,1)S(1)} %bitcast.10), channel_id=1, source_target_pairs={{4,8},{8,4},{12,16},{16,12},{20,24},{24,20},{5,9},{9,5},{13,17},{1... | collective-permute-start | bytes 786440 | tf_op jit(solution)/shard_map/ppermute | solution.py:25
  5.8 0.8 %copy.6 = s32[16,6,4]{2,1,0:T(8,128)S(1)} copy(s32[16,6,4]{0,2,1:T(4,128)} %param.5) | data formatting | bytes 3072 | tf_op args[1]
  6.7 0.1 reshape.31
  6.8 0.1 concatenate.3.index_ref
  6.9 0.0 collective-permute-done.refs_0_
  6.9 1.6 %collective-permute-start.2 = (bf16[16,64,128]{2,1,0:T(8,128)(2,1)S(1)}, bf16[16,64,128]{2,1,0:T(8,128)(2,1)S(1)}, u32[]{:S(2)}, u32[]{:S(2)}) collective-permute-start(bf16[16,64,128]{2,1,0:T(8,128)(2,1)S(1)} %bitcast.11), channel_id=1, source_target_pairs={{0,2},{1,3},{2,0},{3,1},{4,5},{5,4},{6,7},{7,6},{8,10},{9,11},{10,... | collective-permute-start | bytes 786440 | tf_op jit(solution)/shard_map/ppermute | solution.py:43
  8.4 1.1 %collective-permute-done.1.refs_1_ = bf16[16,64,128]{2,1,0:T(8,128)(2,1)S(1)} collective-permute-done((bf16[16,64,128]{2,1,0:T(8,128)(2,1)S(1)}, bf16[16,64,128]{2,1,0:T(8,128)(2,1)S(1)}, u32[]{:S(2)}, u32[]{:S(2)}) %collective-permute-start.1) | collective-permute-done | bytes 262176 | tf_op jit(solution)/shard_map/ppermute | solution.py:43
  9.5 2.0 %collective-permute-start.4 = (bf16[16,64,128]{2,1,0:T(8,128)(2,1)S(1)}, bf16[16,64,128]{2,1,0:T(8,128)(2,1)S(1)}, u32[]{:S(2)}, u32[]{:S(2)}) collective-permute-start(bf16[16,64,128]{2,1,0:T(8,128)(2,1)S(1)} %collective-permute-done.1.refs_1_), channel_id=1, source_target_pairs={{0,2},{1,3},{2,0},{3,1},{4,5},{5,4},{6,7},{7,6},{8,10},{9,11},{10,... | collective-permute-start | bytes 786440 | tf_op jit(solution)/shard_map/ppermute | solution.py:43
  11.5 0.0 copy-start
  11.5 1.9 %copy-done = bf16[16,6,64,256]{3,2,1,0:T(8,128)(2,1)S(1)} copy-done((bf16[16,6,64,256]{3,2,1,0:T(8,128)(2,1)S(1)}, bf16[16,6,64,256]{3,2,1,0:T(8,128)(2,1)}, u32[]{:S(2)}) %copy-start) | copy-done | bytes 3145752
  13.4 0.9 %shard_map.59.partial_ref = f32[1024,128]{1,0:T(8,128)S(1)} custom-call(s32[390]{0:T(512)S(1)} %concatenate.3.index_ref, bf16[16,6,64,256]{3,2,1,0:T(8,128)(2,1)S(1)} %copy-done, bf16[16,64,128]{2,1,0:T(8,128)(2,1)S(1)} %bitcast.12, f32[1024,128]{1,0:T(8,128)S(1)} %get-tuple-element.22.refs_0_), custom_call_target="tpu_custom_call" | custom-call | tf_op jit(solution)/shard_map/pallas_call | solution.py:351
  14.3 0.0 collective-permute-done.3.refs_3_
  14.3 0.0 collective-permute-done.2.refs_2_
  14.4 1.5 %shard_map.60.partial_ref = f32[1024,128]{1,0:T(8,128)S(1)} custom-call(s32[390]{0:T(512)S(1)} %concatenate.3.index_ref, bf16[16,6,64,256]{3,2,1,0:T(8,128)(2,1)S(1)} %copy-done, f32[1024,128]{1,0:T(8,128)S(1)} %shard_map.59.partial_ref, bf16[16,64,128]{2,1,0:T(8,128)(2,1)S(1)} %collective-permute-done.refs_0_, ...), custom_call_target="tpu_custom_call" | custom-call | tf_op jit(solution)/shard_map/pallas_call | solution.py:370
  15.8 0.0 copy-start.1
  15.8 0.0 copy-start.2
  15.9 0.2 collective-permute-done.4.refs_0_
  16.1 0.9 %shard_map.61 = (f32[1024,128]{1,0:T(8,128)S(1)}, bf16[16,64,128]{2,1,0:T(8,128)(2,1)S(1)}) custom-call(s32[390]{0:T(512)S(1)} %concatenate.3.index_ref, bf16[16,6,64,256]{3,2,1,0:T(8,128)(2,1)S(1)} %copy-done, f32[1024,128]{1,0:T(8,128)S(1)} %shard_map.60.partial_ref, bf16[16,64,128]{2,1,0:T(8,128)(2,1)S(1)} %collective-permute-done.4.refs_0_), custom_call_target="tpu_custom_call" | custom-call | tf_op jit(solution)/shard_map/pallas_call | solution.py:377
  17.0 1.8 %collective-permute-start.5 = (bf16[16,64,128]{2,1,0:T(8,128)(2,1)S(1)}, bf16[16,64,128]{2,1,0:T(8,128)(2,1)S(1)}, u32[]{:S(2)}, u32[]{:S(2)}) collective-permute-start(bf16[16,64,128]{2,1,0:T(8,128)(2,1)S(1)} %get-tuple-element.19.own_ref), channel_id=1, source_target_pairs={{0,4},{4,0},{8,12},{12,8},{16,20},{20,16},{24,28},{28,24},{1,5},{5... | collective-permute-start | bytes 786440 | tf_op jit(solution)/shard_map/ppermute | solution.py:25
  18.8 0.5 collective-permute-start.6
  19.3 0.7 %collective-permute-start.8 = (bf16[16,64,128]{2,1,0:T(8,128)(2,1)S(1)}, bf16[16,64,128]{2,1,0:T(8,128)(2,1)S(1)}, u32[]{:S(2)}, u32[]{:S(2)}) collective-permute-start(bf16[16,64,128]{2,1,0:T(8,128)(2,1)S(1)} %get-tuple-element.19.own_ref), channel_id=1, source_target_pairs={{4,8},{8,4},{12,16},{16,12},{20,24},{24,20},{5,9},{9,5},{13,17},{1... | collective-permute-start | bytes 786440 | tf_op jit(solution)/shard_map/ppermute | solution.py:25
  20.0 0.0 copy-done.1
  20.0 0.0 copy-done.2
  20.0 1.0 %shard_map.62.partial_ref = f32[1024,128]{1,0:T(8,128)S(1)} custom-call(s32[390]{0:T(512)S(1)} %concatenate.3.index_ref, bf16[16,6,64,256]{3,2,1,0:T(8,128)(2,1)S(1)} %copy-done, bf16[16,64,128]{2,1,0:T(8,128)(2,1)S(1)} %get-tuple-element.19.own_ref, f32[8,128]{1,0:T(8,128)S(1)} %bitcast.13, f32[1024,128]{1,0:T(8,128)S(1)} %get-tuple-element.16.refs_1_, ...), custom_call_target="tpu_custom_call" | custom-call | tf_op jit(solution)/shard_map/pallas_call | solution.py:351
  21.0 0.0 collective-permute-done.5.refs_0_
  21.0 1.6 %collective-permute-start.7 = (bf16[16,64,128]{2,1,0:T(8,128)(2,1)S(1)}, bf16[16,64,128]{2,1,0:T(8,128)(2,1)S(1)}, u32[]{:S(2)}, u32[]{:S(2)}) collective-permute-start(bf16[16,64,128]{2,1,0:T(8,128)(2,1)S(1)} %get-tuple-element.19.own_ref), channel_id=1, source_target_pairs={{0,2},{1,3},{2,0},{3,1},{4,5},{5,4},{6,7},{7,6},{8,10},{9,11},{10,... | collective-permute-start | bytes 786440 | tf_op jit(solution)/shard_map/ppermute | solution.py:43
  22.6 2.6 %collective-permute-done.6.refs_1_ = bf16[16,64,128]{2,1,0:T(8,128)(2,1)S(1)} collective-permute-done((bf16[16,64,128]{2,1,0:T(8,128)(2,1)S(1)}, bf16[16,64,128]{2,1,0:T(8,128)(2,1)S(1)}, u32[]{:S(2)}, u32[]{:S(2)}) %collective-permute-start.6) | collective-permute-done | bytes 262176 | tf_op jit(solution)/shard_map/ppermute | solution.py:43
  25.2 1.5 %collective-permute-start.9 = (bf16[16,64,128]{2,1,0:T(8,128)(2,1)S(1)}, bf16[16,64,128]{2,1,0:T(8,128)(2,1)S(1)}, u32[]{:S(2)}, u32[]{:S(2)}) collective-permute-start(bf16[16,64,128]{2,1,0:T(8,128)(2,1)S(1)} %collective-permute-done.6.refs_1_), channel_id=1, source_target_pairs={{0,2},{1,3},{2,0},{3,1},{4,5},{5,4},{6,7},{7,6},{8,10},{9,11},{10,... | collective-permute-start | bytes 786440 | tf_op jit(solution)/shard_map/ppermute | solution.py:43
  26.7 0.0 collective-permute-done.8.refs_3_
  26.7 0.8 %collective-permute-done.7.refs_2_ = bf16[16,64,128]{2,1,0:T(8,128)(2,1)S(1)} collective-permute-done((bf16[16,64,128]{2,1,0:T(8,128)(2,1)S(1)}, bf16[16,64,128]{2,1,0:T(8,128)(2,1)S(1)}, u32[]{:S(2)}, u32[]{:S(2)}) %collective-permute-start.7) | collective-permute-done | bytes 262176 | tf_op jit(solution)/shard_map/ppermute | solution.py:43
  27.5 1.5 %shard_map.63.partial_ref = f32[1024,128]{1,0:T(8,128)S(1)} custom-call(s32[390]{0:T(512)S(1)} %concatenate.3.index_ref, bf16[16,6,64,256]{3,2,1,0:T(8,128)(2,1)S(1)} %copy-done, f32[1024,128]{1,0:T(8,128)S(1)} %shard_map.62.partial_ref, bf16[16,64,128]{2,1,0:T(8,128)(2,1)S(1)} %collective-permute-done.5.refs_0_, ...), custom_call_target="tpu_custom_call" | custom-call | tf_op jit(solution)/shard_map/pallas_call | solution.py:370
  28.9 2.6 %collective-permute-done.9.refs_0_ = bf16[16,64,128]{2,1,0:T(8,128)(2,1)S(1)} collective-permute-done((bf16[16,64,128]{2,1,0:T(8,128)(2,1)S(1)}, bf16[16,64,128]{2,1,0:T(8,128)(2,1)S(1)}, u32[]{:S(2)}, u32[]{:S(2)}) %collective-permute-start.9) | collective-permute-done | bytes 262176 | tf_op jit(solution)/shard_map/ppermute | solution.py:43
  31.6 1.3 %shard_map.64 = (bf16[1024,256]{1,0:T(8,128)(2,1)S(1)}, f32[72,128]{1,0:T(8,128)S(1)}) custom-call(s32[390]{0:T(512)S(1)} %concatenate.3.index_ref, bf16[16,6,64,256]{3,2,1,0:T(8,128)(2,1)S(1)} %copy-done, f32[1024,128]{1,0:T(8,128)S(1)} %shard_map.63.partial_ref, bf16[16,64,128]{2,1,0:T(8,128)(2,1)S(1)} %collective-permute-done.9.refs_0_), custom_call_target="tpu_custom_call" | custom-call | tf_op jit(solution)/shard_map/pallas_call | solution.py:382
  32.8 1.3 %collective-permute-start.10 = (f32[72,128]{1,0:T(8,128)S(1)}, f32[72,128]{1,0:T(8,128)S(1)}, u32[]{:S(2)}, u32[]{:S(2)}) collective-permute-start(f32[72,128]{1,0:T(8,128)S(1)} %get-tuple-element.20), channel_id=1, source_target_pairs={{0,4},{4,0},{8,12},{12,8},{16,20},{20,16},{24,28},{28,24},{1,5},{5... | collective-permute-start | bytes 110600 | tf_op jit(solution)/shard_map/ppermute | solution.py:48
  34.1 0.9 %collective-permute-done.10 = f32[72,128]{1,0:T(8,128)S(1)} collective-permute-done((f32[72,128]{1,0:T(8,128)S(1)}, f32[72,128]{1,0:T(8,128)S(1)}, u32[]{:S(2)}, u32[]{:S(2)}) %collective-permute-start.10) | collective-permute-done | bytes 36896 | tf_op jit(solution)/shard_map/ppermute | solution.py:48
  35.0 2.6 %collective-permute-start.11 = (f32[72,128]{1,0:T(8,128)S(1)}, f32[72,128]{1,0:T(8,128)S(1)}, u32[]{:S(2)}, u32[]{:S(2)}) collective-permute-start(f32[72,128]{1,0:T(8,128)S(1)} %add.28), channel_id=1, source_target_pairs={{0,16},{4,20},{8,24},{12,28},{16,0},{20,4},{24,8},{28,12},{1,17},{... | collective-permute-start | bytes 110600 | tf_op jit(solution)/shard_map/ppermute | solution.py:48
  37.6 1.3 %collective-permute-start.12 = (f32[72,128]{1,0:T(8,128)S(1)}, f32[72,128]{1,0:T(8,128)S(1)}, u32[]{:S(2)}, u32[]{:S(2)}) collective-permute-start(f32[72,128]{1,0:T(8,128)S(1)} %add.28), channel_id=1, source_target_pairs={{0,24},{4,28},{8,16},{12,20},{16,8},{20,12},{24,0},{28,4},{1,25},{... | collective-permute-start | bytes 110600 | tf_op jit(solution)/shard_map/ppermute | solution.py:48
  38.9 0.3 collective-permute-start.13
  39.2 0.6 %collective-permute-done.11 = f32[72,128]{1,0:T(8,128)S(1)} collective-permute-done((f32[72,128]{1,0:T(8,128)S(1)}, f32[72,128]{1,0:T(8,128)S(1)}, u32[]{:S(2)}, u32[]{:S(2)}) %collective-permute-start.11) | collective-permute-done | bytes 36896 | tf_op jit(solution)/shard_map/ppermute | solution.py:48
  39.8 3.5 %collective-permute-done.12 = f32[72,128]{1,0:T(8,128)S(1)} collective-permute-done((f32[72,128]{1,0:T(8,128)S(1)}, f32[72,128]{1,0:T(8,128)S(1)}, u32[]{:S(2)}, u32[]{:S(2)}) %collective-permute-start.12) | collective-permute-done | bytes 36896 | tf_op jit(solution)/shard_map/ppermute | solution.py:48
  43.3 0.0 collective-permute-done.13
  43.3 2.3 %collective-permute-start.14 = (f32[72,128]{1,0:T(8,128)S(1)}, f32[72,128]{1,0:T(8,128)S(1)}, u32[]{:S(2)}, u32[]{:S(2)}) collective-permute-start(f32[72,128]{1,0:T(8,128)S(1)} %add_add_fusion.1), channel_id=1, source_target_pairs={{0,3},{1,2},{2,1},{3,0},{4,7},{5,6},{6,5},{7,4},{8,11},{9,10},{10,... | collective-permute-start | bytes 110600 | tf_op jit(solution)/shard_map/ppermute | solution.py:48
  45.7 0.2 collective-permute-start.15
  45.8 1.0 %collective-permute-start.16 = (f32[72,128]{1,0:T(8,128)S(1)}, f32[72,128]{1,0:T(8,128)S(1)}, u32[]{:S(2)}, u32[]{:S(2)}) collective-permute-start(f32[72,128]{1,0:T(8,128)S(1)} %add_add_fusion.1), channel_id=1, source_target_pairs={{0,1},{1,0},{2,3},{3,2},{4,5},{5,4},{6,7},{7,6},{8,9},{9,8},{10,11... | collective-permute-start | bytes 110600 | tf_op jit(solution)/shard_map/ppermute | solution.py:48
  46.9 1.4 %collective-permute-done.14 = f32[72,128]{1,0:T(8,128)S(1)} collective-permute-done((f32[72,128]{1,0:T(8,128)S(1)}, f32[72,128]{1,0:T(8,128)S(1)}, u32[]{:S(2)}, u32[]{:S(2)}) %collective-permute-start.14) | collective-permute-done | bytes 36896 | tf_op jit(solution)/shard_map/ppermute | solution.py:48
  48.3 1.3 %collective-permute-done.15 = f32[72,128]{1,0:T(8,128)S(1)} collective-permute-done((f32[72,128]{1,0:T(8,128)S(1)}, f32[72,128]{1,0:T(8,128)S(1)}, u32[]{:S(2)}, u32[]{:S(2)}) %collective-permute-start.15) | collective-permute-done | bytes 36896 | tf_op jit(solution)/shard_map/ppermute | solution.py:48
  49.6 0.2 collective-permute-done.16
  49.8 4.6 %shard_map.65 = (f32[1024,128]{1,0:T(8,128)}, f32[128,128]{1,0:T(8,128)}) custom-call(f32[72,128]{1,0:T(8,128)S(1)} %add_add_fusion.packed_ref, bf16[1024,256]{1,0:T(8,128)(2,1)S(1)} %get-tuple-element.21.both_ref), custom_call_target="tpu_custom_call" | custom-call | tf_op jit(solution)/shard_map/pallas_call | solution.py:386
  (3 shorter events, 0.0 us)
Async XLA Ops:
  2.1 4.8 %collective-permute-start = (bf16[16,64,128]{2,1,0:T(8,128)(2,1)S(1)}, bf16[16,64,128]{2,1,0:T(8,128)(2,1)S(1)}, u32[]{:S(2)}, u32[]{:S(2)}) collective-permute-start(bf16[16,64,128]{2,1,0:T(8,128)(2,1)S(1)} %bitcast.8), channel_id=1, source_target_pairs={{0,4},{4,0},{8,12},{12,8},{16,20},{20,16},{24,28},{28,24},{1,5},{5... | collective-permute-start | bytes 786440 | tf_op jit(solution)/shard_map/ppermute | solution.py:25
  2.6 6.9 %collective-permute-start.1 = (bf16[16,64,128]{2,1,0:T(8,128)(2,1)S(1)}, bf16[16,64,128]{2,1,0:T(8,128)(2,1)S(1)}, u32[]{:S(2)}, u32[]{:S(2)}) collective-permute-start(bf16[16,64,128]{2,1,0:T(8,128)(2,1)S(1)} %bitcast.9), channel_id=1, source_target_pairs={{0,1},{1,0},{2,3},{3,2},{4,6},{5,7},{6,4},{7,5},{8,9},{9,8},{10,11... | collective-permute-start | bytes 786440 | tf_op jit(solution)/shard_map/ppermute | solution.py:43
  5.1 9.2 %collective-permute-start.3 = (bf16[16,64,128]{2,1,0:T(8,128)(2,1)S(1)}, bf16[16,64,128]{2,1,0:T(8,128)(2,1)S(1)}, u32[]{:S(2)}, u32[]{:S(2)}) collective-permute-start(bf16[16,64,128]{2,1,0:T(8,128)(2,1)S(1)} %bitcast.10), channel_id=1, source_target_pairs={{4,8},{8,4},{12,16},{16,12},{20,24},{24,20},{5,9},{9,5},{13,17},{1... | collective-permute-start | bytes 786440 | tf_op jit(solution)/shard_map/ppermute | solution.py:25
  6.9 7.5 %collective-permute-start.2 = (bf16[16,64,128]{2,1,0:T(8,128)(2,1)S(1)}, bf16[16,64,128]{2,1,0:T(8,128)(2,1)S(1)}, u32[]{:S(2)}, u32[]{:S(2)}) collective-permute-start(bf16[16,64,128]{2,1,0:T(8,128)(2,1)S(1)} %bitcast.11), channel_id=1, source_target_pairs={{0,2},{1,3},{2,0},{3,1},{4,5},{5,4},{6,7},{7,6},{8,10},{9,11},{10,... | collective-permute-start | bytes 786440 | tf_op jit(solution)/shard_map/ppermute | solution.py:43
  9.5 6.6 %collective-permute-start.4 = (bf16[16,64,128]{2,1,0:T(8,128)(2,1)S(1)}, bf16[16,64,128]{2,1,0:T(8,128)(2,1)S(1)}, u32[]{:S(2)}, u32[]{:S(2)}) collective-permute-start(bf16[16,64,128]{2,1,0:T(8,128)(2,1)S(1)} %collective-permute-done.1.refs_1_), channel_id=1, source_target_pairs={{0,2},{1,3},{2,0},{3,1},{4,5},{5,4},{6,7},{7,6},{8,10},{9,11},{10,... | collective-permute-start | bytes 786440 | tf_op jit(solution)/shard_map/ppermute | solution.py:43
  11.5 1.9 %copy-start = (bf16[16,6,64,256]{3,2,1,0:T(8,128)(2,1)S(1)}, bf16[16,6,64,256]{3,2,1,0:T(8,128)(2,1)}, u32[]{:S(2)}) copy-start(bf16[16,6,64,256]{3,2,1,0:T(8,128)(2,1)} %hamiltonian_ref.11) | copy-start | bytes 9437188
  15.8 4.2 %copy-start.1 = (f32[1024,128]{1,0:T(8,128)S(1)}, f32[1024,128]{1,0:T(8,128)}, u32[]{:S(2)}) copy-start(f32[1024,128]{1,0:T(8,128)} %refs_2_.1) | copy-start | bytes 1572868
  15.8 4.2 %copy-start.2 = (f32[1024]{0:T(1024)S(1)}, f32[1024]{0:T(1024)}, u32[]{:S(2)}) copy-start(f32[1024]{0:T(1024)} %param.6) | copy-start | bytes 12292
  17.0 4.0 %collective-permute-start.5 = (bf16[16,64,128]{2,1,0:T(8,128)(2,1)S(1)}, bf16[16,64,128]{2,1,0:T(8,128)(2,1)S(1)}, u32[]{:S(2)}, u32[]{:S(2)}) collective-permute-start(bf16[16,64,128]{2,1,0:T(8,128)(2,1)S(1)} %get-tuple-element.19.own_ref), channel_id=1, source_target_pairs={{0,4},{4,0},{8,12},{12,8},{16,20},{20,16},{24,28},{28,24},{1,5},{5... | collective-permute-start | bytes 786440 | tf_op jit(solution)/shard_map/ppermute | solution.py:25
  18.8 6.4 %collective-permute-start.6 = (bf16[16,64,128]{2,1,0:T(8,128)(2,1)S(1)}, bf16[16,64,128]{2,1,0:T(8,128)(2,1)S(1)}, u32[]{:S(2)}, u32[]{:S(2)}) collective-permute-start(bf16[16,64,128]{2,1,0:T(8,128)(2,1)S(1)} %get-tuple-element.19.own_ref), channel_id=1, source_target_pairs={{0,1},{1,0},{2,3},{3,2},{4,6},{5,7},{6,4},{7,5},{8,9},{9,8},{10,11... | collective-permute-start | bytes 786440 | tf_op jit(solution)/shard_map/ppermute | solution.py:43
  19.3 7.4 %collective-permute-start.8 = (bf16[16,64,128]{2,1,0:T(8,128)(2,1)S(1)}, bf16[16,64,128]{2,1,0:T(8,128)(2,1)S(1)}, u32[]{:S(2)}, u32[]{:S(2)}) collective-permute-start(bf16[16,64,128]{2,1,0:T(8,128)(2,1)S(1)} %get-tuple-element.19.own_ref), channel_id=1, source_target_pairs={{4,8},{8,4},{12,16},{16,12},{20,24},{24,20},{5,9},{9,5},{13,17},{1... | collective-permute-start | bytes 786440 | tf_op jit(solution)/shard_map/ppermute | solution.py:25
  21.0 6.4 %collective-permute-start.7 = (bf16[16,64,128]{2,1,0:T(8,128)(2,1)S(1)}, bf16[16,64,128]{2,1,0:T(8,128)(2,1)S(1)}, u32[]{:S(2)}, u32[]{:S(2)}) collective-permute-start(bf16[16,64,128]{2,1,0:T(8,128)(2,1)S(1)} %get-tuple-element.19.own_ref), channel_id=1, source_target_pairs={{0,2},{1,3},{2,0},{3,1},{4,5},{5,4},{6,7},{7,6},{8,10},{9,11},{10,... | collective-permute-start | bytes 786440 | tf_op jit(solution)/shard_map/ppermute | solution.py:43
  25.2 6.4 %collective-permute-start.9 = (bf16[16,64,128]{2,1,0:T(8,128)(2,1)S(1)}, bf16[16,64,128]{2,1,0:T(8,128)(2,1)S(1)}, u32[]{:S(2)}, u32[]{:S(2)}) collective-permute-start(bf16[16,64,128]{2,1,0:T(8,128)(2,1)S(1)} %collective-permute-done.6.refs_1_), channel_id=1, source_target_pairs={{0,2},{1,3},{2,0},{3,1},{4,5},{5,4},{6,7},{7,6},{8,10},{9,11},{10,... | collective-permute-start | bytes 786440 | tf_op jit(solution)/shard_map/ppermute | solution.py:43
  32.8 2.1 %collective-permute-start.10 = (f32[72,128]{1,0:T(8,128)S(1)}, f32[72,128]{1,0:T(8,128)S(1)}, u32[]{:S(2)}, u32[]{:S(2)}) collective-permute-start(f32[72,128]{1,0:T(8,128)S(1)} %get-tuple-element.20), channel_id=1, source_target_pairs={{0,4},{4,0},{8,12},{12,8},{16,20},{20,16},{24,28},{28,24},{1,5},{5... | collective-permute-start | bytes 110600 | tf_op jit(solution)/shard_map/ppermute | solution.py:48
  35.0 4.9 %collective-permute-start.11 = (f32[72,128]{1,0:T(8,128)S(1)}, f32[72,128]{1,0:T(8,128)S(1)}, u32[]{:S(2)}, u32[]{:S(2)}) collective-permute-start(f32[72,128]{1,0:T(8,128)S(1)} %add.28), channel_id=1, source_target_pairs={{0,16},{4,20},{8,24},{12,28},{16,0},{20,4},{24,8},{28,12},{1,17},{... | collective-permute-start | bytes 110600 | tf_op jit(solution)/shard_map/ppermute | solution.py:48
  37.6 5.8 %collective-permute-start.12 = (f32[72,128]{1,0:T(8,128)S(1)}, f32[72,128]{1,0:T(8,128)S(1)}, u32[]{:S(2)}, u32[]{:S(2)}) collective-permute-start(f32[72,128]{1,0:T(8,128)S(1)} %add.28), channel_id=1, source_target_pairs={{0,24},{4,28},{8,16},{12,20},{16,8},{20,12},{24,0},{28,4},{1,25},{... | collective-permute-start | bytes 110600 | tf_op jit(solution)/shard_map/ppermute | solution.py:48
  38.9 4.4 %collective-permute-start.13 = (f32[72,128]{1,0:T(8,128)S(1)}, f32[72,128]{1,0:T(8,128)S(1)}, u32[]{:S(2)}, u32[]{:S(2)}) collective-permute-start(f32[72,128]{1,0:T(8,128)S(1)} %add.28), channel_id=1, source_target_pairs={{0,8},{4,12},{8,0},{12,4},{16,24},{20,28},{24,16},{28,20},{1,9},{5... | collective-permute-start | bytes 110600 | tf_op jit(solution)/shard_map/ppermute | solution.py:48
  43.3 5.0 %collective-permute-start.14 = (f32[72,128]{1,0:T(8,128)S(1)}, f32[72,128]{1,0:T(8,128)S(1)}, u32[]{:S(2)}, u32[]{:S(2)}) collective-permute-start(f32[72,128]{1,0:T(8,128)S(1)} %add_add_fusion.1), channel_id=1, source_target_pairs={{0,3},{1,2},{2,1},{3,0},{4,7},{5,6},{6,5},{7,4},{8,11},{9,10},{10,... | collective-permute-start | bytes 110600 | tf_op jit(solution)/shard_map/ppermute | solution.py:48
  45.7 4.0 %collective-permute-start.15 = (f32[72,128]{1,0:T(8,128)S(1)}, f32[72,128]{1,0:T(8,128)S(1)}, u32[]{:S(2)}, u32[]{:S(2)}) collective-permute-start(f32[72,128]{1,0:T(8,128)S(1)} %add_add_fusion.1), channel_id=1, source_target_pairs={{0,2},{1,3},{2,0},{3,1},{4,6},{5,7},{6,4},{7,5},{8,10},{9,11},{10,... | collective-permute-start | bytes 110600 | tf_op jit(solution)/shard_map/ppermute | solution.py:48
  45.8 4.0 %collective-permute-start.16 = (f32[72,128]{1,0:T(8,128)S(1)}, f32[72,128]{1,0:T(8,128)S(1)}, u32[]{:S(2)}, u32[]{:S(2)}) collective-permute-start(f32[72,128]{1,0:T(8,128)S(1)} %add_add_fusion.1), channel_id=1, source_target_pairs={{0,1},{1,0},{2,3},{3,2},{4,5},{5,4},{6,7},{7,6},{8,9},{9,8},{10,11... | collective-permute-start | bytes 110600 | tf_op jit(solution)/shard_map/ppermute | solution.py:48

commit v18 on v16

--- a/solution.py
+++ b/solution.py
@@ -187,6 +187,12 @@
     def between(low, high):
         return (lane_index >= low) & (lane_index < high)
 
+    def stacked(rows):
+        panel = rows[0]
+        for n in range(1, SUB):
+            panel = jnp.where(row_index == n, rows[n], panel)
+        return panel
+
     held = [gram[k * SUB : (k + 1) * SUB, :] for k in range(panels)]
     for outer in range(0, panels, OUTER):
         end = outer + OUTER
@@ -197,31 +203,29 @@
             below = {p: along_lanes(held[p], first) for p in range(k + 1, end)}
             after = list(below[k + 1]) if k + 1 < end else None
             following = along_lanes(held[k + 1], first + SUB) if k + 1 < end else None
-            right = held[k]
             left = jnp.where(
                 lane_index < first, held[k], jnp.where(lane_index == row_index + first, 1.0, 0.0)
             )
-            pivots = jnp.ones(shape, jnp.float32)
-            reciprocals = jnp.ones(shape, jnp.float32)
-            columns = [jnp.zeros(shape, jnp.float32)] * SUB
+            rights = [along_rows(held[k], n) for n in range(SUB)]
+            lefts = [along_rows(left, n) for n in range(SUB)]
+            entry = {(n, m): along_rows(block[m], n) for m in range(SUB) for n in range(m + 1)}
+            unit, pivots, reciprocals = {}, [], []
             for j in range(0, SUB, 2):
-                a, b = along_rows(block[j], j), along_rows(block[j], j + 1)
-                c = along_rows(block[j + 1], j + 1)
+                a, b, c = entry[j, j], entry[j, j + 1], entry[j + 1, j + 1]
+                rest = range(j + 2, SUB)
                 determinant = a * c - b * b
                 over = pltpu.reciprocal(determinant, approx=True)
                 over_a = pltpu.reciprocal(a, approx=True)
                 over_c, shift = a * over, b * over_a
-                pivots = jnp.where(row_index == j, a, pivots)
-                pivots = jnp.where(row_index == j + 1, determinant * over_a, pivots)
-                reciprocals = jnp.where(row_index == j, over_a, reciprocals)
-                reciprocals = jnp.where(row_index == j + 1, over_c, reciprocals)
-                one, two = block[j] * c - block[j + 1] * b, block[j + 1] * a - block[j] * b
-                upper = {
-                    n: (along_rows(block[n], j), along_rows(block[n], j + 1))
-                    for n in range(j + 2, SUB)
-                }
-                for n in upper:
-                    block[n] = block[n] - over * (one * upper[n][0] + two * upper[n][1])
+                pivots += [a, determinant * over_a]
+                reciprocals += [over_a, over_c]
+                one = {n: entry[j, n] * c - entry[j + 1, n] * b for n in rest}
+                two = {n: entry[j + 1, n] * a - entry[j, n] * b for n in rest}
+                for n in rest:
+                    for m in range(n, SUB):
+                        entry[n, m] = entry[n, m] - over * (
+                            one[n] * entry[j, m] + two[n] * entry[j + 1, m]
+                        )
                 if following is not None:
                     x, y = after[j], after[j + 1]
                     next_one, next_two = x * c - y * b, y * a - x * b
@@ -229,31 +233,36 @@
                         following[n] = following[n] - over * (
                             next_one * along_rows(x, n) + next_two * along_rows(y, n)
                         )
-                    for n in upper:
+                    for n in rest:
                         after[n] = after[n] - over * (
-                            next_one * upper[n][0] + next_two * upper[n][1]
+                            next_one * entry[j, n] + next_two * entry[j + 1, n]
                         )
-                one = jnp.where(row_index > j + 1, one * over, jnp.where(row_index == j + 1, shift, 0.0))
-                two = jnp.where(row_index > j + 1, two * over, 0.0)
-                right = right - one * along_rows(right, j) - two * along_rows(right, j + 1)
-                left = left - one * along_rows(left, j) - two * along_rows(left, j + 1)
-                columns[j + 1] = jnp.where(row_index == j, shift, columns[j + 1])
-                for n in upper:
-                    unit = (upper[n][1] - shift * upper[n][0]) * over_c
-                    columns[n] = jnp.where(row_index == j, upper[n][0] * over_a, columns[n])
-                    columns[n] = jnp.where(row_index == j + 1, unit, columns[n])
-            scale = lax.rsqrt(pivots)
-            upper_ref[pl.ds(first, SUB), :] = jnp.where(
-                lane_index >= row_index + first, right * scale, 0.0
+                for rows in (rights, lefts):
+                    for n in rest:
+                        rows[n] = rows[n] - over * (one[n] * rows[j] + two[n] * rows[j + 1])
+                    rows[j + 1] = rows[j + 1] - shift * rows[j]
+                unit[j, j + 1] = shift
+                for n in rest:
+                    unit[j, n] = entry[j, n] * over_a
+                    unit[j + 1, n] = (entry[j + 1, n] - shift * entry[j, n]) * over_c
+            scales = [lax.rsqrt(pivot) for pivot in pivots]
+            upper = stacked([row * scale for row, scale in zip(rights, scales)])
+            upper_ref[pl.ds(first, SUB), :] = jnp.where(lane_index >= row_index + first, upper, 0.0)
+            inverse_ref[pl.ds(first, SUB), :] = stacked(
+                [row * scale for row, scale in zip(lefts, scales)]
             )
-            inverse_ref[pl.ds(first, SUB), :] = left * scale
             if k + 1 < panels:
-                reduced = jnp.where(lane_index >= first + SUB, right, left) * reciprocals
-                for n in range(SUB - 1, 0, -1):
-                    reduced = reduced - columns[n] * along_rows(reduced, n)
+                rows = [
+                    jnp.where(lane_index >= first + SUB, rights[n], lefts[n]) * reciprocals[n]
+                    for n in range(SUB)
+                ]
+                for m in range(SUB - 1, 0, -1):
+                    for n in range(m):
+                        rows[n] = rows[n] - unit[n, m] * rows[m]
                 rows_then.append(held[k])
-                rows_reduced.append(jnp.where(between(first + SUB, end * SUB), 0.0, reduced))
-                rows = [along_rows(reduced, n) for n in range(SUB)]
+                rows_reduced.append(
+                    jnp.where(between(first + SUB, end * SUB), 0.0, stacked(rows))
+                )
                 for p in below:
                     total = jnp.where(between(first, first + SUB), 0.0, held[p])
                     for n in range(SUB):

time: 54.2 us -> 54.7 us (level)
  no operation moved by 1% of the time
where the time goes in v18:
time: 54.7 us; the launch traced here: 54.5 us
  starting transfers between devices  22.5 us (41%)
  waiting for transfers between devices  15.2 us (28%)
  Pallas kernels  11.6 us (21%)
  local copies, waits for them, and re-layouts  2.92 us (5%)
  other arithmetic  1.46 us (3%)
  between operations  0.79 us (1%)
    ppermute x6, starting transfers between devices, cycle_exchange(): return lax.ppermute(value, ('group', 'blk'), route)  9.81 us
    ppermute x7, starting transfers between devices, from_partner(): lax.ppermute(value, axis, [(index, index ^ flip) for index in range(count)])  9.05 us
    ppermute x7, waiting for transfers between devices, from_partner(): lax.ppermute(value, axis, [(index, index ^ flip) for index in range(count)])  7.91 us
    ppermute x6, waiting for transfers between devices, cycle_exchange(): return lax.ppermute(value, ('group', 'blk'), route)  7.26 us
    pallas_call x1, Pallas kernels, on_device(): call(functools.partial(factor_kernel, rows_total), (flat, square), [vmem,...  4.64 us
    ppermute x4, starting transfers between devices, pair_exchange(): return lax.ppermute(value, 'group', route)  3.69 us
    pallas_call x2, Pallas kernels, coupled(): call(functools.partial(middle_kernel, middle), flat, [smem] + [vmem] * (2...  2.93 us
    unnamed x7, local copies, waits for them, and re-layouts  2.72 us
  transfers between devices with their start and end apart: 17, of which 11 were waited for; matrix products, arithmetic and copies ran while one was open for 2% of the time, Pallas kernels for 9%

profile of v18, /device:TPU:0, one launch (start us, length us, event | category | flops | bytes accessed | tf_op | source)
XLA Modules:
  0.0 54.5 jit_solution(4171925069653610481)
XLA Ops:
  0.6 1.4 %broadcast_multiply_fusion = (f32[1024,128]{1,0:T(8,128)S(1)}, bf16[1024,128]{1,0:T(8,128)(2,1)S(1)}) fusion(f32[1024,128]{1,0:T(8,128)} %refs_2_.1, f32[1024]{0:T(1024)} %param.6), kind=kLoop, calls=%fused_computation | loop fusion | flops 262144 | bytes 1314816 | tf_op jit(solution)/shard_map/mul | solution.py:376
  2.1 0.5 collective-permute-start
  2.6 2.6 %collective-permute-start.1 = (bf16[16,64,128]{2,1,0:T(8,128)(2,1)S(1)}, bf16[16,64,128]{2,1,0:T(8,128)(2,1)S(1)}, u32[]{:S(2)}, u32[]{:S(2)}) collective-permute-start(bf16[16,64,128]{2,1,0:T(8,128)(2,1)S(1)} %bitcast.9), channel_id=1, source_target_pairs={{0,1},{1,0},{2,3},{3,2},{4,6},{5,7},{6,4},{7,5},{8,9},{9,8},{10,11... | collective-permute-start | bytes 786440 | tf_op jit(solution)/shard_map/ppermute | solution.py:43
  5.1 0.7 %collective-permute-start.3 = (bf16[16,64,128]{2,1,0:T(8,128)(2,1)S(1)}, bf16[16,64,128]{2,1,0:T(8,128)(2,1)S(1)}, u32[]{:S(2)}, u32[]{:S(2)}) collective-permute-start(bf16[16,64,128]{2,1,0:T(8,128)(2,1)S(1)} %bitcast.10), channel_id=1, source_target_pairs={{4,8},{8,4},{12,16},{16,12},{20,24},{24,20},{5,9},{9,5},{13,17},{1... | collective-permute-start | bytes 786440 | tf_op jit(solution)/shard_map/ppermute | solution.py:25
  5.8 0.8 %copy.6 = s32[16,6,4]{2,1,0:T(8,128)S(1)} copy(s32[16,6,4]{0,2,1:T(4,128)} %param.5) | data formatting | bytes 3072 | tf_op args[1]
  6.7 0.1 reshape.31
  6.8 0.1 concatenate.3.index_ref
  6.9 0.0 collective-permute-done.refs_0_
  6.9 1.6 %collective-permute-start.2 = (bf16[16,64,128]{2,1,0:T(8,128)(2,1)S(1)}, bf16[16,64,128]{2,1,0:T(8,128)(2,1)S(1)}, u32[]{:S(2)}, u32[]{:S(2)}) collective-permute-start(bf16[16,64,128]{2,1,0:T(8,128)(2,1)S(1)} %bitcast.11), channel_id=1, source_target_pairs={{0,2},{1,3},{2,0},{3,1},{4,5},{5,4},{6,7},{7,6},{8,10},{9,11},{10,... | collective-permute-start | bytes 786440 | tf_op jit(solution)/shard_map/ppermute | solution.py:43
  8.4 1.1 %collective-permute-done.1.refs_1_ = bf16[16,64,128]{2,1,0:T(8,128)(2,1)S(1)} collective-permute-done((bf16[16,64,128]{2,1,0:T(8,128)(2,1)S(1)}, bf16[16,64,128]{2,1,0:T(8,128)(2,1)S(1)}, u32[]{:S(2)}, u32[]{:S(2)}) %collective-permute-start.1) | collective-permute-done | bytes 262176 | tf_op jit(solution)/shard_map/ppermute | solution.py:43
  9.5 2.0 %collective-permute-start.4 = (bf16[16,64,128]{2,1,0:T(8,128)(2,1)S(1)}, bf16[16,64,128]{2,1,0:T(8,128)(2,1)S(1)}, u32[]{:S(2)}, u32[]{:S(2)}) collective-permute-start(bf16[16,64,128]{2,1,0:T(8,128)(2,1)S(1)} %collective-permute-done.1.refs_1_), channel_id=1, source_target_pairs={{0,2},{1,3},{2,0},{3,1},{4,5},{5,4},{6,7},{7,6},{8,10},{9,11},{10,... | collective-permute-start | bytes 786440 | tf_op jit(solution)/shard_map/ppermute | solution.py:43
  11.5 0.0 copy-start
  11.5 1.9 %copy-done = bf16[16,6,64,256]{3,2,1,0:T(8,128)(2,1)S(1)} copy-done((bf16[16,6,64,256]{3,2,1,0:T(8,128)(2,1)S(1)}, bf16[16,6,64,256]{3,2,1,0:T(8,128)(2,1)}, u32[]{:S(2)}) %copy-start) | copy-done | bytes 3145752
  13.4 0.9 %shard_map.59.partial_ref = f32[1024,128]{1,0:T(8,128)S(1)} custom-call(s32[390]{0:T(512)S(1)} %concatenate.3.index_ref, bf16[16,6,64,256]{3,2,1,0:T(8,128)(2,1)S(1)} %copy-done, bf16[16,64,128]{2,1,0:T(8,128)(2,1)S(1)} %bitcast.12, f32[1024,128]{1,0:T(8,128)S(1)} %get-tuple-element.22.refs_0_), custom_call_target="tpu_custom_call" | custom-call | tf_op jit(solution)/shard_map/pallas_call | solution.py:352
  14.3 0.0 collective-permute-done.3.refs_3_
  14.3 0.0 collective-permute-done.2.refs_2_
  14.4 1.5 %shard_map.60.partial_ref = f32[1024,128]{1,0:T(8,128)S(1)} custom-call(s32[390]{0:T(512)S(1)} %concatenate.3.index_ref, bf16[16,6,64,256]{3,2,1,0:T(8,128)(2,1)S(1)} %copy-done, f32[1024,128]{1,0:T(8,128)S(1)} %shard_map.59.partial_ref, bf16[16,64,128]{2,1,0:T(8,128)(2,1)S(1)} %collective-permute-done.refs_0_, ...), custom_call_target="tpu_custom_call" | custom-call | tf_op jit(solution)/shard_map/pallas_call | solution.py:371
  15.8 0.0 copy-start.1
  15.8 0.0 copy-start.2
  15.9 0.2 collective-permute-done.4.refs_0_
  16.1 0.9 %shard_map.61 = (f32[1024,128]{1,0:T(8,128)S(1)}, bf16[16,64,128]{2,1,0:T(8,128)(2,1)S(1)}) custom-call(s32[390]{0:T(512)S(1)} %concatenate.3.index_ref, bf16[16,6,64,256]{3,2,1,0:T(8,128)(2,1)S(1)} %copy-done, f32[1024,128]{1,0:T(8,128)S(1)} %shard_map.60.partial_ref, bf16[16,64,128]{2,1,0:T(8,128)(2,1)S(1)} %collective-permute-done.4.refs_0_), custom_call_target="tpu_custom_call" | custom-call | tf_op jit(solution)/shard_map/pallas_call | solution.py:378
  17.0 1.8 %collective-permute-start.5 = (bf16[16,64,128]{2,1,0:T(8,128)(2,1)S(1)}, bf16[16,64,128]{2,1,0:T(8,128)(2,1)S(1)}, u32[]{:S(2)}, u32[]{:S(2)}) collective-permute-start(bf16[16,64,128]{2,1,0:T(8,128)(2,1)S(1)} %get-tuple-element.19.own_ref), channel_id=1, source_target_pairs={{0,4},{4,0},{8,12},{12,8},{16,20},{20,16},{24,28},{28,24},{1,5},{5... | collective-permute-start | bytes 786440 | tf_op jit(solution)/shard_map/ppermute | solution.py:25
  18.8 0.5 collective-permute-start.6
  19.3 0.7 %collective-permute-start.8 = (bf16[16,64,128]{2,1,0:T(8,128)(2,1)S(1)}, bf16[16,64,128]{2,1,0:T(8,128)(2,1)S(1)}, u32[]{:S(2)}, u32[]{:S(2)}) collective-permute-start(bf16[16,64,128]{2,1,0:T(8,128)(2,1)S(1)} %get-tuple-element.19.own_ref), channel_id=1, source_target_pairs={{4,8},{8,4},{12,16},{16,12},{20,24},{24,20},{5,9},{9,5},{13,17},{1... | collective-permute-start | bytes 786440 | tf_op jit(solution)/shard_map/ppermute | solution.py:25
  20.0 0.0 copy-done.1
  20.0 0.0 copy-done.2
  20.0 1.0 %shard_map.62.partial_ref = f32[1024,128]{1,0:T(8,128)S(1)} custom-call(s32[390]{0:T(512)S(1)} %concatenate.3.index_ref, bf16[16,6,64,256]{3,2,1,0:T(8,128)(2,1)S(1)} %copy-done, bf16[16,64,128]{2,1,0:T(8,128)(2,1)S(1)} %get-tuple-element.19.own_ref, f32[8,128]{1,0:T(8,128)S(1)} %bitcast.13, f32[1024,128]{1,0:T(8,128)S(1)} %get-tuple-element.16.refs_1_, ...), custom_call_target="tpu_custom_call" | custom-call | tf_op jit(solution)/shard_map/pallas_call | solution.py:352
  21.0 0.0 collective-permute-done.5.refs_0_
  21.0 1.6 %collective-permute-start.7 = (bf16[16,64,128]{2,1,0:T(8,128)(2,1)S(1)}, bf16[16,64,128]{2,1,0:T(8,128)(2,1)S(1)}, u32[]{:S(2)}, u32[]{:S(2)}) collective-permute-start(bf16[16,64,128]{2,1,0:T(8,128)(2,1)S(1)} %get-tuple-element.19.own_ref), channel_id=1, source_target_pairs={{0,2},{1,3},{2,0},{3,1},{4,5},{5,4},{6,7},{7,6},{8,10},{9,11},{10,... | collective-permute-start | bytes 786440 | tf_op jit(solution)/shard_map/ppermute | solution.py:43
  22.6 2.6 %collective-permute-done.6.refs_1_ = bf16[16,64,128]{2,1,0:T(8,128)(2,1)S(1)} collective-permute-done((bf16[16,64,128]{2,1,0:T(8,128)(2,1)S(1)}, bf16[16,64,128]{2,1,0:T(8,128)(2,1)S(1)}, u32[]{:S(2)}, u32[]{:S(2)}) %collective-permute-start.6) | collective-permute-done | bytes 262176 | tf_op jit(solution)/shard_map/ppermute | solution.py:43
  25.2 1.5 %collective-permute-start.9 = (bf16[16,64,128]{2,1,0:T(8,128)(2,1)S(1)}, bf16[16,64,128]{2,1,0:T(8,128)(2,1)S(1)}, u32[]{:S(2)}, u32[]{:S(2)}) collective-permute-start(bf16[16,64,128]{2,1,0:T(8,128)(2,1)S(1)} %collective-permute-done.6.refs_1_), channel_id=1, source_target_pairs={{0,2},{1,3},{2,0},{3,1},{4,5},{5,4},{6,7},{7,6},{8,10},{9,11},{10,... | collective-permute-start | bytes 786440 | tf_op jit(solution)/shard_map/ppermute | solution.py:43
  26.7 0.0 collective-permute-done.8.refs_3_
  26.7 0.8 %collective-permute-done.7.refs_2_ = bf16[16,64,128]{2,1,0:T(8,128)(2,1)S(1)} collective-permute-done((bf16[16,64,128]{2,1,0:T(8,128)(2,1)S(1)}, bf16[16,64,128]{2,1,0:T(8,128)(2,1)S(1)}, u32[]{:S(2)}, u32[]{:S(2)}) %collective-permute-start.7) | collective-permute-done | bytes 262176 | tf_op jit(solution)/shard_map/ppermute | solution.py:43
  27.5 1.5 %shard_map.63.partial_ref = f32[1024,128]{1,0:T(8,128)S(1)} custom-call(s32[390]{0:T(512)S(1)} %concatenate.3.index_ref, bf16[16,6,64,256]{3,2,1,0:T(8,128)(2,1)S(1)} %copy-done, f32[1024,128]{1,0:T(8,128)S(1)} %shard_map.62.partial_ref, bf16[16,64,128]{2,1,0:T(8,128)(2,1)S(1)} %collective-permute-done.5.refs_0_, ...), custom_call_target="tpu_custom_call" | custom-call | tf_op jit(solution)/shard_map/pallas_call | solution.py:371
  28.9 2.6 %collective-permute-done.9.refs_0_ = bf16[16,64,128]{2,1,0:T(8,128)(2,1)S(1)} collective-permute-done((bf16[16,64,128]{2,1,0:T(8,128)(2,1)S(1)}, bf16[16,64,128]{2,1,0:T(8,128)(2,1)S(1)}, u32[]{:S(2)}, u32[]{:S(2)}) %collective-permute-start.9) | collective-permute-done | bytes 262176 | tf_op jit(solution)/shard_map/ppermute | solution.py:43
  31.6 1.3 %shard_map.64 = (bf16[1024,256]{1,0:T(8,128)(2,1)S(1)}, f32[72,128]{1,0:T(8,128)S(1)}) custom-call(s32[390]{0:T(512)S(1)} %concatenate.3.index_ref, bf16[16,6,64,256]{3,2,1,0:T(8,128)(2,1)S(1)} %copy-done, f32[1024,128]{1,0:T(8,128)S(1)} %shard_map.63.partial_ref, bf16[16,64,128]{2,1,0:T(8,128)(2,1)S(1)} %collective-permute-done.9.refs_0_), custom_call_target="tpu_custom_call" | custom-call | tf_op jit(solution)/shard_map/pallas_call | solution.py:383
  32.8 1.3 %collective-permute-start.10 = (f32[72,128]{1,0:T(8,128)S(1)}, f32[72,128]{1,0:T(8,128)S(1)}, u32[]{:S(2)}, u32[]{:S(2)}) collective-permute-start(f32[72,128]{1,0:T(8,128)S(1)} %get-tuple-element.20), channel_id=1, source_target_pairs={{0,4},{4,0},{8,12},{12,8},{16,20},{20,16},{24,28},{28,24},{1,5},{5... | collective-permute-start | bytes 110600 | tf_op jit(solution)/shard_map/ppermute | solution.py:48
  34.1 0.9 %collective-permute-done.10 = f32[72,128]{1,0:T(8,128)S(1)} collective-permute-done((f32[72,128]{1,0:T(8,128)S(1)}, f32[72,128]{1,0:T(8,128)S(1)}, u32[]{:S(2)}, u32[]{:S(2)}) %collective-permute-start.10) | collective-permute-done | bytes 36896 | tf_op jit(solution)/shard_map/ppermute | solution.py:48
  35.0 2.6 %collective-permute-start.11 = (f32[72,128]{1,0:T(8,128)S(1)}, f32[72,128]{1,0:T(8,128)S(1)}, u32[]{:S(2)}, u32[]{:S(2)}) collective-permute-start(f32[72,128]{1,0:T(8,128)S(1)} %add.28), channel_id=1, source_target_pairs={{0,16},{4,20},{8,24},{12,28},{16,0},{20,4},{24,8},{28,12},{1,17},{... | collective-permute-start | bytes 110600 | tf_op jit(solution)/shard_map/ppermute | solution.py:48
  37.6 1.3 %collective-permute-start.12 = (f32[72,128]{1,0:T(8,128)S(1)}, f32[72,128]{1,0:T(8,128)S(1)}, u32[]{:S(2)}, u32[]{:S(2)}) collective-permute-start(f32[72,128]{1,0:T(8,128)S(1)} %add.28), channel_id=1, source_target_pairs={{0,24},{4,28},{8,16},{12,20},{16,8},{20,12},{24,0},{28,4},{1,25},{... | collective-permute-start | bytes 110600 | tf_op jit(solution)/shard_map/ppermute | solution.py:48
  38.9 0.3 collective-permute-start.13
  39.2 0.6 %collective-permute-done.11 = f32[72,128]{1,0:T(8,128)S(1)} collective-permute-done((f32[72,128]{1,0:T(8,128)S(1)}, f32[72,128]{1,0:T(8,128)S(1)}, u32[]{:S(2)}, u32[]{:S(2)}) %collective-permute-start.11) | collective-permute-done | bytes 36896 | tf_op jit(solution)/shard_map/ppermute | solution.py:48
  39.8 3.5 %collective-permute-done.12 = f32[72,128]{1,0:T(8,128)S(1)} collective-permute-done((f32[72,128]{1,0:T(8,128)S(1)}, f32[72,128]{1,0:T(8,128)S(1)}, u32[]{:S(2)}, u32[]{:S(2)}) %collective-permute-start.12) | collective-permute-done | bytes 36896 | tf_op jit(solution)/shard_map/ppermute | solution.py:48
  43.3 0.0 collective-permute-done.13
  43.3 2.3 %collective-permute-start.14 = (f32[72,128]{1,0:T(8,128)S(1)}, f32[72,128]{1,0:T(8,128)S(1)}, u32[]{:S(2)}, u32[]{:S(2)}) collective-permute-start(f32[72,128]{1,0:T(8,128)S(1)} %add_add_fusion.1), channel_id=1, source_target_pairs={{0,3},{1,2},{2,1},{3,0},{4,7},{5,6},{6,5},{7,4},{8,11},{9,10},{10,... | collective-permute-start | bytes 110600 | tf_op jit(solution)/shard_map/ppermute | solution.py:48
  45.7 0.2 collective-permute-start.15
  45.8 1.0 %collective-permute-start.16 = (f32[72,128]{1,0:T(8,128)S(1)}, f32[72,128]{1,0:T(8,128)S(1)}, u32[]{:S(2)}, u32[]{:S(2)}) collective-permute-start(f32[72,128]{1,0:T(8,128)S(1)} %add_add_fusion.1), channel_id=1, source_target_pairs={{0,1},{1,0},{2,3},{3,2},{4,5},{5,4},{6,7},{7,6},{8,9},{9,8},{10,11... | collective-permute-start | bytes 110600 | tf_op jit(solution)/shard_map/ppermute | solution.py:48
  46.9 1.4 %collective-permute-done.14 = f32[72,128]{1,0:T(8,128)S(1)} collective-permute-done((f32[72,128]{1,0:T(8,128)S(1)}, f32[72,128]{1,0:T(8,128)S(1)}, u32[]{:S(2)}, u32[]{:S(2)}) %collective-permute-start.14) | collective-permute-done | bytes 36896 | tf_op jit(solution)/shard_map/ppermute | solution.py:48
  48.3 1.3 %collective-permute-done.15 = f32[72,128]{1,0:T(8,128)S(1)} collective-permute-done((f32[72,128]{1,0:T(8,128)S(1)}, f32[72,128]{1,0:T(8,128)S(1)}, u32[]{:S(2)}, u32[]{:S(2)}) %collective-permute-start.15) | collective-permute-done | bytes 36896 | tf_op jit(solution)/shard_map/ppermute | solution.py:48
  49.6 0.2 collective-permute-done.16
  49.8 4.6 %shard_map.65 = (f32[1024,128]{1,0:T(8,128)}, f32[128,128]{1,0:T(8,128)}) custom-call(f32[72,128]{1,0:T(8,128)S(1)} %add_add_fusion.packed_ref, bf16[1024,256]{1,0:T(8,128)(2,1)S(1)} %get-tuple-element.21.both_ref), custom_call_target="tpu_custom_call" | custom-call | tf_op jit(solution)/shard_map/pallas_call | solution.py:387
  (3 shorter events, 0.0 us)
Async XLA Ops:
  2.1 4.8 %collective-permute-start = (bf16[16,64,128]{2,1,0:T(8,128)(2,1)S(1)}, bf16[16,64,128]{2,1,0:T(8,128)(2,1)S(1)}, u32[]{:S(2)}, u32[]{:S(2)}) collective-permute-start(bf16[16,64,128]{2,1,0:T(8,128)(2,1)S(1)} %bitcast.8), channel_id=1, source_target_pairs={{0,4},{4,0},{8,12},{12,8},{16,20},{20,16},{24,28},{28,24},{1,5},{5... | collective-permute-start | bytes 786440 | tf_op jit(solution)/shard_map/ppermute | solution.py:25
  2.6 6.9 %collective-permute-start.1 = (bf16[16,64,128]{2,1,0:T(8,128)(2,1)S(1)}, bf16[16,64,128]{2,1,0:T(8,128)(2,1)S(1)}, u32[]{:S(2)}, u32[]{:S(2)}) collective-permute-start(bf16[16,64,128]{2,1,0:T(8,128)(2,1)S(1)} %bitcast.9), channel_id=1, source_target_pairs={{0,1},{1,0},{2,3},{3,2},{4,6},{5,7},{6,4},{7,5},{8,9},{9,8},{10,11... | collective-permute-start | bytes 786440 | tf_op jit(solution)/shard_map/ppermute | solution.py:43
  5.1 9.2 %collective-permute-start.3 = (bf16[16,64,128]{2,1,0:T(8,128)(2,1)S(1)}, bf16[16,64,128]{2,1,0:T(8,128)(2,1)S(1)}, u32[]{:S(2)}, u32[]{:S(2)}) collective-permute-start(bf16[16,64,128]{2,1,0:T(8,128)(2,1)S(1)} %bitcast.10), channel_id=1, source_target_pairs={{4,8},{8,4},{12,16},{16,12},{20,24},{24,20},{5,9},{9,5},{13,17},{1... | collective-permute-start | bytes 786440 | tf_op jit(solution)/shard_map/ppermute | solution.py:25
  6.9 7.5 %collective-permute-start.2 = (bf16[16,64,128]{2,1,0:T(8,128)(2,1)S(1)}, bf16[16,64,128]{2,1,0:T(8,128)(2,1)S(1)}, u32[]{:S(2)}, u32[]{:S(2)}) collective-permute-start(bf16[16,64,128]{2,1,0:T(8,128)(2,1)S(1)} %bitcast.11), channel_id=1, source_target_pairs={{0,2},{1,3},{2,0},{3,1},{4,5},{5,4},{6,7},{7,6},{8,10},{9,11},{10,... | collective-permute-start | bytes 786440 | tf_op jit(solution)/shard_map/ppermute | solution.py:43
  9.5 6.6 %collective-permute-start.4 = (bf16[16,64,128]{2,1,0:T(8,128)(2,1)S(1)}, bf16[16,64,128]{2,1,0:T(8,128)(2,1)S(1)}, u32[]{:S(2)}, u32[]{:S(2)}) collective-permute-start(bf16[16,64,128]{2,1,0:T(8,128)(2,1)S(1)} %collective-permute-done.1.refs_1_), channel_id=1, source_target_pairs={{0,2},{1,3},{2,0},{3,1},{4,5},{5,4},{6,7},{7,6},{8,10},{9,11},{10,... | collective-permute-start | bytes 786440 | tf_op jit(solution)/shard_map/ppermute | solution.py:43
  11.5 1.9 %copy-start = (bf16[16,6,64,256]{3,2,1,0:T(8,128)(2,1)S(1)}, bf16[16,6,64,256]{3,2,1,0:T(8,128)(2,1)}, u32[]{:S(2)}) copy-start(bf16[16,6,64,256]{3,2,1,0:T(8,128)(2,1)} %hamiltonian_ref.11) | copy-start | bytes 9437188
  15.8 4.2 %copy-start.1 = (f32[1024,128]{1,0:T(8,128)S(1)}, f32[1024,128]{1,0:T(8,128)}, u32[]{:S(2)}) copy-start(f32[1024,128]{1,0:T(8,128)} %refs_2_.1) | copy-start | bytes 1572868
  15.8 4.2 %copy-start.2 = (f32[1024]{0:T(1024)S(1)}, f32[1024]{0:T(1024)}, u32[]{:S(2)}) copy-start(f32[1024]{0:T(1024)} %param.6) | copy-start | bytes 12292
  17.0 4.0 %collective-permute-start.5 = (bf16[16,64,128]{2,1,0:T(8,128)(2,1)S(1)}, bf16[16,64,128]{2,1,0:T(8,128)(2,1)S(1)}, u32[]{:S(2)}, u32[]{:S(2)}) collective-permute-start(bf16[16,64,128]{2,1,0:T(8,128)(2,1)S(1)} %get-tuple-element.19.own_ref), channel_id=1, source_target_pairs={{0,4},{4,0},{8,12},{12,8},{16,20},{20,16},{24,28},{28,24},{1,5},{5... | collective-permute-start | bytes 786440 | tf_op jit(solution)/shard_map/ppermute | solution.py:25
  18.8 6.4 %collective-permute-start.6 = (bf16[16,64,128]{2,1,0:T(8,128)(2,1)S(1)}, bf16[16,64,128]{2,1,0:T(8,128)(2,1)S(1)}, u32[]{:S(2)}, u32[]{:S(2)}) collective-permute-start(bf16[16,64,128]{2,1,0:T(8,128)(2,1)S(1)} %get-tuple-element.19.own_ref), channel_id=1, source_target_pairs={{0,1},{1,0},{2,3},{3,2},{4,6},{5,7},{6,4},{7,5},{8,9},{9,8},{10,11... | collective-permute-start | bytes 786440 | tf_op jit(solution)/shard_map/ppermute | solution.py:43
  19.3 7.4 %collective-permute-start.8 = (bf16[16,64,128]{2,1,0:T(8,128)(2,1)S(1)}, bf16[16,64,128]{2,1,0:T(8,128)(2,1)S(1)}, u32[]{:S(2)}, u32[]{:S(2)}) collective-permute-start(bf16[16,64,128]{2,1,0:T(8,128)(2,1)S(1)} %get-tuple-element.19.own_ref), channel_id=1, source_target_pairs={{4,8},{8,4},{12,16},{16,12},{20,24},{24,20},{5,9},{9,5},{13,17},{1... | collective-permute-start | bytes 786440 | tf_op jit(solution)/shard_map/ppermute | solution.py:25
  21.0 6.4 %collective-permute-start.7 = (bf16[16,64,128]{2,1,0:T(8,128)(2,1)S(1)}, bf16[16,64,128]{2,1,0:T(8,128)(2,1)S(1)}, u32[]{:S(2)}, u32[]{:S(2)}) collective-permute-start(bf16[16,64,128]{2,1,0:T(8,128)(2,1)S(1)} %get-tuple-element.19.own_ref), channel_id=1, source_target_pairs={{0,2},{1,3},{2,0},{3,1},{4,5},{5,4},{6,7},{7,6},{8,10},{9,11},{10,... | collective-permute-start | bytes 786440 | tf_op jit(solution)/shard_map/ppermute | solution.py:43
  25.2 6.4 %collective-permute-start.9 = (bf16[16,64,128]{2,1,0:T(8,128)(2,1)S(1)}, bf16[16,64,128]{2,1,0:T(8,128)(2,1)S(1)}, u32[]{:S(2)}, u32[]{:S(2)}) collective-permute-start(bf16[16,64,128]{2,1,0:T(8,128)(2,1)S(1)} %collective-permute-done.6.refs_1_), channel_id=1, source_target_pairs={{0,2},{1,3},{2,0},{3,1},{4,5},{5,4},{6,7},{7,6},{8,10},{9,11},{10,... | collective-permute-start | bytes 786440 | tf_op jit(solution)/shard_map/ppermute | solution.py:43
  32.8 2.1 %collective-permute-start.10 = (f32[72,128]{1,0:T(8,128)S(1)}, f32[72,128]{1,0:T(8,128)S(1)}, u32[]{:S(2)}, u32[]{:S(2)}) collective-permute-start(f32[72,128]{1,0:T(8,128)S(1)} %get-tuple-element.20), channel_id=1, source_target_pairs={{0,4},{4,0},{8,12},{12,8},{16,20},{20,16},{24,28},{28,24},{1,5},{5... | collective-permute-start | bytes 110600 | tf_op jit(solution)/shard_map/ppermute | solution.py:48
  35.0 4.9 %collective-permute-start.11 = (f32[72,128]{1,0:T(8,128)S(1)}, f32[72,128]{1,0:T(8,128)S(1)}, u32[]{:S(2)}, u32[]{:S(2)}) collective-permute-start(f32[72,128]{1,0:T(8,128)S(1)} %add.28), channel_id=1, source_target_pairs={{0,16},{4,20},{8,24},{12,28},{16,0},{20,4},{24,8},{28,12},{1,17},{... | collective-permute-start | bytes 110600 | tf_op jit(solution)/shard_map/ppermute | solution.py:48
  37.6 5.8 %collective-permute-start.12 = (f32[72,128]{1,0:T(8,128)S(1)}, f32[72,128]{1,0:T(8,128)S(1)}, u32[]{:S(2)}, u32[]{:S(2)}) collective-permute-start(f32[72,128]{1,0:T(8,128)S(1)} %add.28), channel_id=1, source_target_pairs={{0,24},{4,28},{8,16},{12,20},{16,8},{20,12},{24,0},{28,4},{1,25},{... | collective-permute-start | bytes 110600 | tf_op jit(solution)/shard_map/ppermute | solution.py:48
  38.9 4.4 %collective-permute-start.13 = (f32[72,128]{1,0:T(8,128)S(1)}, f32[72,128]{1,0:T(8,128)S(1)}, u32[]{:S(2)}, u32[]{:S(2)}) collective-permute-start(f32[72,128]{1,0:T(8,128)S(1)} %add.28), channel_id=1, source_target_pairs={{0,8},{4,12},{8,0},{12,4},{16,24},{20,28},{24,16},{28,20},{1,9},{5... | collective-permute-start | bytes 110600 | tf_op jit(solution)/shard_map/ppermute | solution.py:48
  43.3 5.0 %collective-permute-start.14 = (f32[72,128]{1,0:T(8,128)S(1)}, f32[72,128]{1,0:T(8,128)S(1)}, u32[]{:S(2)}, u32[]{:S(2)}) collective-permute-start(f32[72,128]{1,0:T(8,128)S(1)} %add_add_fusion.1), channel_id=1, source_target_pairs={{0,3},{1,2},{2,1},{3,0},{4,7},{5,6},{6,5},{7,4},{8,11},{9,10},{10,... | collective-permute-start | bytes 110600 | tf_op jit(solution)/shard_map/ppermute | solution.py:48
  45.7 4.0 %collective-permute-start.15 = (f32[72,128]{1,0:T(8,128)S(1)}, f32[72,128]{1,0:T(8,128)S(1)}, u32[]{:S(2)}, u32[]{:S(2)}) collective-permute-start(f32[72,128]{1,0:T(8,128)S(1)} %add_add_fusion.1), channel_id=1, source_target_pairs={{0,2},{1,3},{2,0},{3,1},{4,6},{5,7},{6,4},{7,5},{8,10},{9,11},{10,... | collective-permute-start | bytes 110600 | tf_op jit(solution)/shard_map/ppermute | solution.py:48
  45.8 4.0 %collective-permute-start.16 = (f32[72,128]{1,0:T(8,128)S(1)}, f32[72,128]{1,0:T(8,128)S(1)}, u32[]{:S(2)}, u32[]{:S(2)}) collective-permute-start(f32[72,128]{1,0:T(8,128)S(1)} %add_add_fusion.1), channel_id=1, source_target_pairs={{0,1},{1,0},{2,3},{3,2},{4,5},{5,4},{6,7},{7,6},{8,9},{9,8},{10,11... | collective-permute-start | bytes 110600 | tf_op jit(solution)/shard_map/ppermute | solution.py:48

commit v19 on v16

--- a/solution.py
+++ b/solution.py
@@ -84,23 +84,23 @@
     return total
 
 
+def weight_of(weights, block_size, row):
+    column, part = divmod(row, LANES // block_size)
+    return weights[part * block_size : (part + 1) * block_size, column : column + 1]
+
+
 def own_kernel(index_ref, hamiltonian_ref, own_ref, *refs):
     terms, partial_ref = refs[:-1], refs[-1]
     shard_blocks, _, block_size, _ = hamiltonian_ref.shape
-    per_column = LANES // block_size
-    if len(terms) == 3:
+    if terms:
         weights = potential_columns(terms[0])
     for row in range(shard_blocks):
         rows = pl.ds(row * block_size, block_size)
-        if len(terms) == 3:
-            column, part = divmod(row, per_column)
-            weight = weights[part * block_size : (part + 1) * block_size, column : column + 1]
-            total = weight * terms[1][rows, :] - terms[2][rows, :]
-        else:
-            total = terms[0][rows, :]
-        partial_ref[rows, :] = total + couple_row(
-            index_ref, hamiltonian_ref, [(0, own_ref)], row
-        )
+        total = couple_row(index_ref, hamiltonian_ref, [(0, own_ref)], row)
+        if terms:
+            weight = weight_of(weights, block_size, row)
+            total = total + (weight * terms[1][rows, :] - terms[2][rows, :])
+        partial_ref[rows, :] = total
 
 
 def middle_kernel(numbers, index_ref, hamiltonian_ref, partial_ref, *refs):
@@ -113,14 +113,14 @@
         )
 
 
-def first_kernel(numbers, index_ref, hamiltonian_ref, partial_ref, *refs):
+def first_kernel(numbers, index_ref, hamiltonian_ref, potential_ref, trial_ref, partial_ref, *refs):
     pieces, (once_ref, round_ref) = list(zip(numbers, refs)), refs[len(numbers) :]
     shard_blocks, _, block_size, _ = hamiltonian_ref.shape
+    weights = potential_columns(potential_ref)
     for row in range(shard_blocks):
         rows = pl.ds(row * block_size, block_size)
-        once = 0.5 * (
-            partial_ref[rows, :] + couple_row(index_ref, hamiltonian_ref, pieces, row)
-        )
+        partial = partial_ref[rows, :] + weight_of(weights, block_size, row) * trial_ref[rows, :]
+        once = 0.5 * (partial + couple_row(index_ref, hamiltonian_ref, pieces, row))
         once_ref[rows, :] = once
         round_ref[row] = once.astype(jnp.bfloat16)
 
@@ -364,11 +364,10 @@
         )(index_array, hamiltonian, partial, *[pieces[number] for number in middle])
         return [partial] + [pieces[number] for number in ending]
 
-    weighted = weights.reshape(-1, 1) * trial_slab
-    parts = coupled(trial_slab.reshape(rounded.shape).astype(jnp.bfloat16), index_array, False, weighted)
+    parts = coupled(trial_slab.reshape(rounded.shape).astype(jnp.bfloat16), index_array, False)
     once, once_round = call(
-        functools.partial(first_kernel, ending), (flat, rounded), [smem] + [vmem] * (2 + len(ending))
-    )(index_array, hamiltonian, *parts)
+        functools.partial(first_kernel, ending), (flat, rounded), [smem] + [vmem] * (4 + len(ending))
+    )(index_array, hamiltonian, weights, trial_slab, *parts)
     parts = coupled(once_round, index_array, True, weights, once, trial_slab)
     both = jax.ShapeDtypeStruct((flat_rows, 2 * states), jnp.bfloat16)
     filtered, gram = call(

time: 54.2 us -> 54 us (level)
    mul x1 -> x0, other arithmetic: 1.43 us -> none  [on_device(): weighted = weights.reshape(-1, 1) * trial_slab]
    convert_element_type x0 -> x1, other arithmetic: none -> 1.07 us  [on_device(): trial_slab.reshape(rounded.shape).astype(jnp.bfloat16)]
where the time goes in v19:
time: 54 us; the launch traced here: 53.7 us
  starting transfers between devices  22.6 us (42%)
  waiting for transfers between devices  15.1 us (28%)
  Pallas kernels  11.2 us (21%)
  local copies, waits for them, and re-layouts  2.92 us (5%)
  other arithmetic  1.1 us (2%)
  between operations  0.77 us (1%)
    ppermute x6, starting transfers between devices, cycle_exchange(): return lax.ppermute(value, ('group', 'blk'), route)  9.83 us
    ppermute x7, starting transfers between devices, from_partner(): lax.ppermute(value, axis, [(index, index ^ flip) for index in range(count)])  9.06 us
    ppermute x7, waiting for transfers between devices, from_partner(): lax.ppermute(value, axis, [(index, index ^ flip) for index in range(count)])  7.87 us
    ppermute x6, waiting for transfers between devices, cycle_exchange(): return lax.ppermute(value, ('group', 'blk'), route)  7.25 us
    pallas_call x1, Pallas kernels, on_device(): call(functools.partial(factor_kernel, rows_total), (flat, square), [vmem,...  4.17 us
    ppermute x4, starting transfers between devices, pair_exchange(): return lax.ppermute(value, 'group', route)  3.69 us
    pallas_call x2, Pallas kernels, coupled(): call(functools.partial(middle_kernel, middle), flat, [smem] + [vmem] * (2...  2.96 us
    unnamed x7, local copies, waits for them, and re-layouts  2.72 us
  transfers between devices with their start and end apart: 17, of which 11 were waited for; matrix products, arithmetic and copies ran while one was open for 2% of the time, Pallas kernels for 9%

profile of v19, /device:TPU:0, one launch (start us, length us, event | category | flops | bytes accessed | tf_op | source)
XLA Modules:
  0.0 53.7 jit_solution(9442699951012370779)
XLA Ops:
  0.6 1.1 %convert_element_type.5 = bf16[1024,128]{1,0:T(8,128)(2,1)S(1)} convert(f32[1024,128]{1,0:T(8,128)} %refs_2_.1) | non-fusion elementwise | flops 131072 | bytes 786432 | tf_op jit(solution)/shard_map/convert_element_type | solution.py:367
  1.7 0.5 collective-permute-start
  2.2 2.6 %collective-permute-start.1 = (bf16[16,64,128]{2,1,0:T(8,128)(2,1)S(1)}, bf16[16,64,128]{2,1,0:T(8,128)(2,1)S(1)}, u32[]{:S(2)}, u32[]{:S(2)}) collective-permute-start(bf16[16,64,128]{2,1,0:T(8,128)(2,1)S(1)} %bitcast.9), channel_id=1, source_target_pairs={{0,1},{1,0},{2,3},{3,2},{4,6},{5,7},{6,4},{7,5},{8,9},{9,8},{10,11... | collective-permute-start | bytes 786440 | tf_op jit(solution)/shard_map/ppermute | solution.py:43
  4.8 0.7 %collective-permute-start.3 = (bf16[16,64,128]{2,1,0:T(8,128)(2,1)S(1)}, bf16[16,64,128]{2,1,0:T(8,128)(2,1)S(1)}, u32[]{:S(2)}, u32[]{:S(2)}) collective-permute-start(bf16[16,64,128]{2,1,0:T(8,128)(2,1)S(1)} %bitcast.10), channel_id=1, source_target_pairs={{4,8},{8,4},{12,16},{16,12},{20,24},{24,20},{5,9},{9,5},{13,17},{1... | collective-permute-start | bytes 786440 | tf_op jit(solution)/shard_map/ppermute | solution.py:25
  5.5 0.8 %copy.6 = s32[16,6,4]{2,1,0:T(8,128)S(1)} copy(s32[16,6,4]{0,2,1:T(4,128)} %param.5) | data formatting | bytes 3072 | tf_op args[1]
  6.3 0.1 reshape.30
  6.4 0.1 concatenate.3.index_ref
  6.5 0.0 collective-permute-done.refs_0_
  6.5 1.6 %collective-permute-start.2 = (bf16[16,64,128]{2,1,0:T(8,128)(2,1)S(1)}, bf16[16,64,128]{2,1,0:T(8,128)(2,1)S(1)}, u32[]{:S(2)}, u32[]{:S(2)}) collective-permute-start(bf16[16,64,128]{2,1,0:T(8,128)(2,1)S(1)} %bitcast.11), channel_id=1, source_target_pairs={{0,2},{1,3},{2,0},{3,1},{4,5},{5,4},{6,7},{7,6},{8,10},{9,11},{10,... | collective-permute-start | bytes 786440 | tf_op jit(solution)/shard_map/ppermute | solution.py:43
  8.1 1.1 %collective-permute-done.1.refs_1_ = bf16[16,64,128]{2,1,0:T(8,128)(2,1)S(1)} collective-permute-done((bf16[16,64,128]{2,1,0:T(8,128)(2,1)S(1)}, bf16[16,64,128]{2,1,0:T(8,128)(2,1)S(1)}, u32[]{:S(2)}, u32[]{:S(2)}) %collective-permute-start.1) | collective-permute-done | bytes 262176 | tf_op jit(solution)/shard_map/ppermute | solution.py:43
  9.1 2.0 %collective-permute-start.4 = (bf16[16,64,128]{2,1,0:T(8,128)(2,1)S(1)}, bf16[16,64,128]{2,1,0:T(8,128)(2,1)S(1)}, u32[]{:S(2)}, u32[]{:S(2)}) collective-permute-start(bf16[16,64,128]{2,1,0:T(8,128)(2,1)S(1)} %collective-permute-done.1.refs_1_), channel_id=1, source_target_pairs={{0,2},{1,3},{2,0},{3,1},{4,5},{5,4},{6,7},{7,6},{8,10},{9,11},{10,... | collective-permute-start | bytes 786440 | tf_op jit(solution)/shard_map/ppermute | solution.py:43
  11.2 0.0 copy-start
  11.2 1.9 %copy-done = bf16[16,6,64,256]{3,2,1,0:T(8,128)(2,1)S(1)} copy-done((bf16[16,6,64,256]{3,2,1,0:T(8,128)(2,1)S(1)}, bf16[16,6,64,256]{3,2,1,0:T(8,128)(2,1)}, u32[]{:S(2)}) %copy-start) | copy-done | bytes 3145752
  13.1 0.9 %shard_map.59.partial_ref = f32[1024,128]{1,0:T(8,128)S(1)} custom-call(s32[390]{0:T(512)S(1)} %concatenate.3.index_ref, bf16[16,6,64,256]{3,2,1,0:T(8,128)(2,1)S(1)} %copy-done, bf16[16,64,128]{2,1,0:T(8,128)(2,1)S(1)} %bitcast.12), custom_call_target="tpu_custom_call" | custom-call | tf_op jit(solution)/shard_map/pallas_call | solution.py:343
  14.0 0.0 copy-start.1
  14.0 0.0 copy-start.2
  14.0 0.0 collective-permute-done.3.refs_3_
  14.0 0.0 collective-permute-done.2.refs_2_
  14.0 1.5 %shard_map.60.partial_ref = f32[1024,128]{1,0:T(8,128)S(1)} custom-call(s32[390]{0:T(512)S(1)} %concatenate.3.index_ref, bf16[16,6,64,256]{3,2,1,0:T(8,128)(2,1)S(1)} %copy-done, f32[1024,128]{1,0:T(8,128)S(1)} %shard_map.59.partial_ref, bf16[16,64,128]{2,1,0:T(8,128)(2,1)S(1)} %collective-permute-done.refs_0_, ...), custom_call_target="tpu_custom_call" | custom-call | tf_op jit(solution)/shard_map/pallas_call | solution.py:362
  15.5 0.2 collective-permute-done.4.refs_0_
  15.7 0.0 copy-done.1
  15.7 0.0 copy-done.2
  15.7 1.0 %shard_map.61 = (f32[1024,128]{1,0:T(8,128)S(1)}, bf16[16,64,128]{2,1,0:T(8,128)(2,1)S(1)}) custom-call(s32[390]{0:T(512)S(1)} %concatenate.3.index_ref, bf16[16,6,64,256]{3,2,1,0:T(8,128)(2,1)S(1)} %copy-done, f32[8,128]{1,0:T(8,128)S(1)} %bitcast.13, f32[1024,128]{1,0:T(8,128)S(1)} %copy-done.1, f32[1024,128]{1,0:T(8,128)S(1)} %shard_map.60.partial_ref, ...), custom_call_target="tpu_custom_call" | custom-call | tf_op jit(solution)/shard_map/pallas_call | solution.py:368
  16.7 1.8 %collective-permute-start.5 = (bf16[16,64,128]{2,1,0:T(8,128)(2,1)S(1)}, bf16[16,64,128]{2,1,0:T(8,128)(2,1)S(1)}, u32[]{:S(2)}, u32[]{:S(2)}) collective-permute-start(bf16[16,64,128]{2,1,0:T(8,128)(2,1)S(1)} %get-tuple-element.19.own_ref), channel_id=1, source_target_pairs={{0,4},{4,0},{8,12},{12,8},{16,20},{20,16},{24,28},{28,24},{1,5},{5... | collective-permute-start | bytes 786440 | tf_op jit(solution)/shard_map/ppermute | solution.py:25
  18.5 0.5 %collective-permute-start.6 = (bf16[16,64,128]{2,1,0:T(8,128)(2,1)S(1)}, bf16[16,64,128]{2,1,0:T(8,128)(2,1)S(1)}, u32[]{:S(2)}, u32[]{:S(2)}) collective-permute-start(bf16[16,64,128]{2,1,0:T(8,128)(2,1)S(1)} %get-tuple-element.19.own_ref), channel_id=1, source_target_pairs={{0,1},{1,0},{2,3},{3,2},{4,6},{5,7},{6,4},{7,5},{8,9},{9,8},{10,11... | collective-permute-start | bytes 786440 | tf_op jit(solution)/shard_map/ppermute | solution.py:43
  19.1 0.7 %collective-permute-start.8 = (bf16[16,64,128]{2,1,0:T(8,128)(2,1)S(1)}, bf16[16,64,128]{2,1,0:T(8,128)(2,1)S(1)}, u32[]{:S(2)}, u32[]{:S(2)}) collective-permute-start(bf16[16,64,128]{2,1,0:T(8,128)(2,1)S(1)} %get-tuple-element.19.own_ref), channel_id=1, source_target_pairs={{4,8},{8,4},{12,16},{16,12},{20,24},{24,20},{5,9},{9,5},{13,17},{1... | collective-permute-start | bytes 786440 | tf_op jit(solution)/shard_map/ppermute | solution.py:25
  19.8 1.0 %shard_map.62.partial_ref = f32[1024,128]{1,0:T(8,128)S(1)} custom-call(s32[390]{0:T(512)S(1)} %concatenate.3.index_ref, bf16[16,6,64,256]{3,2,1,0:T(8,128)(2,1)S(1)} %copy-done, bf16[16,64,128]{2,1,0:T(8,128)(2,1)S(1)} %get-tuple-element.19.own_ref, f32[8,128]{1,0:T(8,128)S(1)} %bitcast.14, f32[1024,128]{1,0:T(8,128)S(1)} %get-tuple-element.16.refs_1_, ...), custom_call_target="tpu_custom_call" | custom-call | tf_op jit(solution)/shard_map/pallas_call | solution.py:343
  20.7 0.0 collective-permute-done.5.refs_0_
  20.7 1.6 %collective-permute-start.7 = (bf16[16,64,128]{2,1,0:T(8,128)(2,1)S(1)}, bf16[16,64,128]{2,1,0:T(8,128)(2,1)S(1)}, u32[]{:S(2)}, u32[]{:S(2)}) collective-permute-start(bf16[16,64,128]{2,1,0:T(8,128)(2,1)S(1)} %get-tuple-element.19.own_ref), channel_id=1, source_target_pairs={{0,2},{1,3},{2,0},{3,1},{4,5},{5,4},{6,7},{7,6},{8,10},{9,11},{10,... | collective-permute-start | bytes 786440 | tf_op jit(solution)/shard_map/ppermute | solution.py:43
  22.3 2.6 %collective-permute-done.6.refs_1_ = bf16[16,64,128]{2,1,0:T(8,128)(2,1)S(1)} collective-permute-done((bf16[16,64,128]{2,1,0:T(8,128)(2,1)S(1)}, bf16[16,64,128]{2,1,0:T(8,128)(2,1)S(1)}, u32[]{:S(2)}, u32[]{:S(2)}) %collective-permute-start.6) | collective-permute-done | bytes 262176 | tf_op jit(solution)/shard_map/ppermute | solution.py:43
  24.9 1.5 %collective-permute-start.9 = (bf16[16,64,128]{2,1,0:T(8,128)(2,1)S(1)}, bf16[16,64,128]{2,1,0:T(8,128)(2,1)S(1)}, u32[]{:S(2)}, u32[]{:S(2)}) collective-permute-start(bf16[16,64,128]{2,1,0:T(8,128)(2,1)S(1)} %collective-permute-done.6.refs_1_), channel_id=1, source_target_pairs={{0,2},{1,3},{2,0},{3,1},{4,5},{5,4},{6,7},{7,6},{8,10},{9,11},{10,... | collective-permute-start | bytes 786440 | tf_op jit(solution)/shard_map/ppermute | solution.py:43
  26.4 0.0 collective-permute-done.8.refs_3_
  26.4 0.7 %collective-permute-done.7.refs_2_ = bf16[16,64,128]{2,1,0:T(8,128)(2,1)S(1)} collective-permute-done((bf16[16,64,128]{2,1,0:T(8,128)(2,1)S(1)}, bf16[16,64,128]{2,1,0:T(8,128)(2,1)S(1)}, u32[]{:S(2)}, u32[]{:S(2)}) %collective-permute-start.7) | collective-permute-done | bytes 262176 | tf_op jit(solution)/shard_map/ppermute | solution.py:43
  27.2 1.5 %shard_map.63.partial_ref = f32[1024,128]{1,0:T(8,128)S(1)} custom-call(s32[390]{0:T(512)S(1)} %concatenate.3.index_ref, bf16[16,6,64,256]{3,2,1,0:T(8,128)(2,1)S(1)} %copy-done, f32[1024,128]{1,0:T(8,128)S(1)} %shard_map.62.partial_ref, bf16[16,64,128]{2,1,0:T(8,128)(2,1)S(1)} %collective-permute-done.5.refs_0_, ...), custom_call_target="tpu_custom_call" | custom-call | tf_op jit(solution)/shard_map/pallas_call | solution.py:362
  28.7 2.6 %collective-permute-done.9.refs_0_ = bf16[16,64,128]{2,1,0:T(8,128)(2,1)S(1)} collective-permute-done((bf16[16,64,128]{2,1,0:T(8,128)(2,1)S(1)}, bf16[16,64,128]{2,1,0:T(8,128)(2,1)S(1)}, u32[]{:S(2)}, u32[]{:S(2)}) %collective-permute-start.9) | collective-permute-done | bytes 262176 | tf_op jit(solution)/shard_map/ppermute | solution.py:43
  31.3 1.3 %shard_map.64 = (bf16[1024,256]{1,0:T(8,128)(2,1)S(1)}, f32[72,128]{1,0:T(8,128)S(1)}) custom-call(s32[390]{0:T(512)S(1)} %concatenate.3.index_ref, bf16[16,6,64,256]{3,2,1,0:T(8,128)(2,1)S(1)} %copy-done, f32[1024,128]{1,0:T(8,128)S(1)} %shard_map.63.partial_ref, bf16[16,64,128]{2,1,0:T(8,128)(2,1)S(1)} %collective-permute-done.9.refs_0_), custom_call_target="tpu_custom_call" | custom-call | tf_op jit(solution)/shard_map/pallas_call | solution.py:373
  32.5 1.3 %collective-permute-start.10 = (f32[72,128]{1,0:T(8,128)S(1)}, f32[72,128]{1,0:T(8,128)S(1)}, u32[]{:S(2)}, u32[]{:S(2)}) collective-permute-start(f32[72,128]{1,0:T(8,128)S(1)} %get-tuple-element.20), channel_id=1, source_target_pairs={{0,4},{4,0},{8,12},{12,8},{16,20},{20,16},{24,28},{28,24},{1,5},{5... | collective-permute-start | bytes 110600 | tf_op jit(solution)/shard_map/ppermute | solution.py:48
  33.8 0.9 %collective-permute-done.10 = f32[72,128]{1,0:T(8,128)S(1)} collective-permute-done((f32[72,128]{1,0:T(8,128)S(1)}, f32[72,128]{1,0:T(8,128)S(1)}, u32[]{:S(2)}, u32[]{:S(2)}) %collective-permute-start.10) | collective-permute-done | bytes 36896 | tf_op jit(solution)/shard_map/ppermute | solution.py:48
  34.7 2.6 %collective-permute-start.11 = (f32[72,128]{1,0:T(8,128)S(1)}, f32[72,128]{1,0:T(8,128)S(1)}, u32[]{:S(2)}, u32[]{:S(2)}) collective-permute-start(f32[72,128]{1,0:T(8,128)S(1)} %add.28), channel_id=1, source_target_pairs={{0,16},{4,20},{8,24},{12,28},{16,0},{20,4},{24,8},{28,12},{1,17},{... | collective-permute-start | bytes 110600 | tf_op jit(solution)/shard_map/ppermute | solution.py:48
  37.3 1.3 %collective-permute-start.12 = (f32[72,128]{1,0:T(8,128)S(1)}, f32[72,128]{1,0:T(8,128)S(1)}, u32[]{:S(2)}, u32[]{:S(2)}) collective-permute-start(f32[72,128]{1,0:T(8,128)S(1)} %add.28), channel_id=1, source_target_pairs={{0,24},{4,28},{8,16},{12,20},{16,8},{20,12},{24,0},{28,4},{1,25},{... | collective-permute-start | bytes 110600 | tf_op jit(solution)/shard_map/ppermute | solution.py:48
  38.6 0.3 collective-permute-start.13
  38.9 0.6 %collective-permute-done.11 = f32[72,128]{1,0:T(8,128)S(1)} collective-permute-done((f32[72,128]{1,0:T(8,128)S(1)}, f32[72,128]{1,0:T(8,128)S(1)}, u32[]{:S(2)}, u32[]{:S(2)}) %collective-permute-start.11) | collective-permute-done | bytes 36896 | tf_op jit(solution)/shard_map/ppermute | solution.py:48
  39.6 3.5 %collective-permute-done.12 = f32[72,128]{1,0:T(8,128)S(1)} collective-permute-done((f32[72,128]{1,0:T(8,128)S(1)}, f32[72,128]{1,0:T(8,128)S(1)}, u32[]{:S(2)}, u32[]{:S(2)}) %collective-permute-start.12) | collective-permute-done | bytes 36896 | tf_op jit(solution)/shard_map/ppermute | solution.py:48
  43.0 0.0 collective-permute-done.13
  43.1 2.4 %collective-permute-start.14 = (f32[72,128]{1,0:T(8,128)S(1)}, f32[72,128]{1,0:T(8,128)S(1)}, u32[]{:S(2)}, u32[]{:S(2)}) collective-permute-start(f32[72,128]{1,0:T(8,128)S(1)} %add_add_fusion.1), channel_id=1, source_target_pairs={{0,3},{1,2},{2,1},{3,0},{4,7},{5,6},{6,5},{7,4},{8,11},{9,10},{10,... | collective-permute-start | bytes 110600 | tf_op jit(solution)/shard_map/ppermute | solution.py:48
  45.4 0.1 collective-permute-start.15
  45.6 1.1 %collective-permute-start.16 = (f32[72,128]{1,0:T(8,128)S(1)}, f32[72,128]{1,0:T(8,128)S(1)}, u32[]{:S(2)}, u32[]{:S(2)}) collective-permute-start(f32[72,128]{1,0:T(8,128)S(1)} %add_add_fusion.1), channel_id=1, source_target_pairs={{0,1},{1,0},{2,3},{3,2},{4,5},{5,4},{6,7},{7,6},{8,9},{9,8},{10,11... | collective-permute-start | bytes 110600 | tf_op jit(solution)/shard_map/ppermute | solution.py:48
  46.6 1.5 %collective-permute-done.14 = f32[72,128]{1,0:T(8,128)S(1)} collective-permute-done((f32[72,128]{1,0:T(8,128)S(1)}, f32[72,128]{1,0:T(8,128)S(1)}, u32[]{:S(2)}, u32[]{:S(2)}) %collective-permute-start.14) | collective-permute-done | bytes 36896 | tf_op jit(solution)/shard_map/ppermute | solution.py:48
  48.1 1.3 %collective-permute-done.15 = f32[72,128]{1,0:T(8,128)S(1)} collective-permute-done((f32[72,128]{1,0:T(8,128)S(1)}, f32[72,128]{1,0:T(8,128)S(1)}, u32[]{:S(2)}, u32[]{:S(2)}) %collective-permute-start.15) | collective-permute-done | bytes 36896 | tf_op jit(solution)/shard_map/ppermute | solution.py:48
  49.4 0.1 collective-permute-done.16
  49.5 4.2 %shard_map.65 = (f32[1024,128]{1,0:T(8,128)}, f32[128,128]{1,0:T(8,128)}) custom-call(f32[72,128]{1,0:T(8,128)S(1)} %add_add_fusion.packed_ref, bf16[1024,256]{1,0:T(8,128)(2,1)S(1)} %get-tuple-element.21.both_ref), custom_call_target="tpu_custom_call" | custom-call | tf_op jit(solution)/shard_map/pallas_call | solution.py:377
  (3 shorter events, 0.0 us)
Async XLA Ops:
  1.7 4.8 %collective-permute-start = (bf16[16,64,128]{2,1,0:T(8,128)(2,1)S(1)}, bf16[16,64,128]{2,1,0:T(8,128)(2,1)S(1)}, u32[]{:S(2)}, u32[]{:S(2)}) collective-permute-start(bf16[16,64,128]{2,1,0:T(8,128)(2,1)S(1)} %bitcast.8), channel_id=1, source_target_pairs={{0,4},{4,0},{8,12},{12,8},{16,20},{20,16},{24,28},{28,24},{1,5},{5... | collective-permute-start | bytes 786440 | tf_op jit(solution)/shard_map/ppermute | solution.py:25
  2.2 6.9 %collective-permute-start.1 = (bf16[16,64,128]{2,1,0:T(8,128)(2,1)S(1)}, bf16[16,64,128]{2,1,0:T(8,128)(2,1)S(1)}, u32[]{:S(2)}, u32[]{:S(2)}) collective-permute-start(bf16[16,64,128]{2,1,0:T(8,128)(2,1)S(1)} %bitcast.9), channel_id=1, source_target_pairs={{0,1},{1,0},{2,3},{3,2},{4,6},{5,7},{6,4},{7,5},{8,9},{9,8},{10,11... | collective-permute-start | bytes 786440 | tf_op jit(solution)/shard_map/ppermute | solution.py:43
  4.8 9.2 %collective-permute-start.3 = (bf16[16,64,128]{2,1,0:T(8,128)(2,1)S(1)}, bf16[16,64,128]{2,1,0:T(8,128)(2,1)S(1)}, u32[]{:S(2)}, u32[]{:S(2)}) collective-permute-start(bf16[16,64,128]{2,1,0:T(8,128)(2,1)S(1)} %bitcast.10), channel_id=1, source_target_pairs={{4,8},{8,4},{12,16},{16,12},{20,24},{24,20},{5,9},{9,5},{13,17},{1... | collective-permute-start | bytes 786440 | tf_op jit(solution)/shard_map/ppermute | solution.py:25
  6.5 7.5 %collective-permute-start.2 = (bf16[16,64,128]{2,1,0:T(8,128)(2,1)S(1)}, bf16[16,64,128]{2,1,0:T(8,128)(2,1)S(1)}, u32[]{:S(2)}, u32[]{:S(2)}) collective-permute-start(bf16[16,64,128]{2,1,0:T(8,128)(2,1)S(1)} %bitcast.11), channel_id=1, source_target_pairs={{0,2},{1,3},{2,0},{3,1},{4,5},{5,4},{6,7},{7,6},{8,10},{9,11},{10,... | collective-permute-start | bytes 786440 | tf_op jit(solution)/shard_map/ppermute | solution.py:43
  9.1 6.6 %collective-permute-start.4 = (bf16[16,64,128]{2,1,0:T(8,128)(2,1)S(1)}, bf16[16,64,128]{2,1,0:T(8,128)(2,1)S(1)}, u32[]{:S(2)}, u32[]{:S(2)}) collective-permute-start(bf16[16,64,128]{2,1,0:T(8,128)(2,1)S(1)} %collective-permute-done.1.refs_1_), channel_id=1, source_target_pairs={{0,2},{1,3},{2,0},{3,1},{4,5},{5,4},{6,7},{7,6},{8,10},{9,11},{10,... | collective-permute-start | bytes 786440 | tf_op jit(solution)/shard_map/ppermute | solution.py:43
  11.2 1.9 %copy-start = (bf16[16,6,64,256]{3,2,1,0:T(8,128)(2,1)S(1)}, bf16[16,6,64,256]{3,2,1,0:T(8,128)(2,1)}, u32[]{:S(2)}) copy-start(bf16[16,6,64,256]{3,2,1,0:T(8,128)(2,1)} %hamiltonian_ref.11) | copy-start | bytes 9437188
  14.0 1.8 %copy-start.1 = (f32[1024,128]{1,0:T(8,128)S(1)}, f32[1024,128]{1,0:T(8,128)}, u32[]{:S(2)}) copy-start(f32[1024,128]{1,0:T(8,128)} %refs_2_.1) | copy-start | bytes 1572868
  14.0 1.8 %copy-start.2 = (f32[1024]{0:T(1024)S(1)}, f32[1024]{0:T(1024)}, u32[]{:S(2)}) copy-start(f32[1024]{0:T(1024)} %param.6) | copy-start | bytes 12292
  16.7 4.0 %collective-permute-start.5 = (bf16[16,64,128]{2,1,0:T(8,128)(2,1)S(1)}, bf16[16,64,128]{2,1,0:T(8,128)(2,1)S(1)}, u32[]{:S(2)}, u32[]{:S(2)}) collective-permute-start(bf16[16,64,128]{2,1,0:T(8,128)(2,1)S(1)} %get-tuple-element.19.own_ref), channel_id=1, source_target_pairs={{0,4},{4,0},{8,12},{12,8},{16,20},{20,16},{24,28},{28,24},{1,5},{5... | collective-permute-start | bytes 786440 | tf_op jit(solution)/shard_map/ppermute | solution.py:25
  18.5 6.4 %collective-permute-start.6 = (bf16[16,64,128]{2,1,0:T(8,128)(2,1)S(1)}, bf16[16,64,128]{2,1,0:T(8,128)(2,1)S(1)}, u32[]{:S(2)}, u32[]{:S(2)}) collective-permute-start(bf16[16,64,128]{2,1,0:T(8,128)(2,1)S(1)} %get-tuple-element.19.own_ref), channel_id=1, source_target_pairs={{0,1},{1,0},{2,3},{3,2},{4,6},{5,7},{6,4},{7,5},{8,9},{9,8},{10,11... | collective-permute-start | bytes 786440 | tf_op jit(solution)/shard_map/ppermute | solution.py:43
  19.1 7.4 %collective-permute-start.8 = (bf16[16,64,128]{2,1,0:T(8,128)(2,1)S(1)}, bf16[16,64,128]{2,1,0:T(8,128)(2,1)S(1)}, u32[]{:S(2)}, u32[]{:S(2)}) collective-permute-start(bf16[16,64,128]{2,1,0:T(8,128)(2,1)S(1)} %get-tuple-element.19.own_ref), channel_id=1, source_target_pairs={{4,8},{8,4},{12,16},{16,12},{20,24},{24,20},{5,9},{9,5},{13,17},{1... | collective-permute-start | bytes 786440 | tf_op jit(solution)/shard_map/ppermute | solution.py:25
  20.7 6.4 %collective-permute-start.7 = (bf16[16,64,128]{2,1,0:T(8,128)(2,1)S(1)}, bf16[16,64,128]{2,1,0:T(8,128)(2,1)S(1)}, u32[]{:S(2)}, u32[]{:S(2)}) collective-permute-start(bf16[16,64,128]{2,1,0:T(8,128)(2,1)S(1)} %get-tuple-element.19.own_ref), channel_id=1, source_target_pairs={{0,2},{1,3},{2,0},{3,1},{4,5},{5,4},{6,7},{7,6},{8,10},{9,11},{10,... | collective-permute-start | bytes 786440 | tf_op jit(solution)/shard_map/ppermute | solution.py:43
  24.9 6.4 %collective-permute-start.9 = (bf16[16,64,128]{2,1,0:T(8,128)(2,1)S(1)}, bf16[16,64,128]{2,1,0:T(8,128)(2,1)S(1)}, u32[]{:S(2)}, u32[]{:S(2)}) collective-permute-start(bf16[16,64,128]{2,1,0:T(8,128)(2,1)S(1)} %collective-permute-done.6.refs_1_), channel_id=1, source_target_pairs={{0,2},{1,3},{2,0},{3,1},{4,5},{5,4},{6,7},{7,6},{8,10},{9,11},{10,... | collective-permute-start | bytes 786440 | tf_op jit(solution)/shard_map/ppermute | solution.py:43
  32.5 2.1 %collective-permute-start.10 = (f32[72,128]{1,0:T(8,128)S(1)}, f32[72,128]{1,0:T(8,128)S(1)}, u32[]{:S(2)}, u32[]{:S(2)}) collective-permute-start(f32[72,128]{1,0:T(8,128)S(1)} %get-tuple-element.20), channel_id=1, source_target_pairs={{0,4},{4,0},{8,12},{12,8},{16,20},{20,16},{24,28},{28,24},{1,5},{5... | collective-permute-start | bytes 110600 | tf_op jit(solution)/shard_map/ppermute | solution.py:48
  34.7 4.9 %collective-permute-start.11 = (f32[72,128]{1,0:T(8,128)S(1)}, f32[72,128]{1,0:T(8,128)S(1)}, u32[]{:S(2)}, u32[]{:S(2)}) collective-permute-start(f32[72,128]{1,0:T(8,128)S(1)} %add.28), channel_id=1, source_target_pairs={{0,16},{4,20},{8,24},{12,28},{16,0},{20,4},{24,8},{28,12},{1,17},{... | collective-permute-start | bytes 110600 | tf_op jit(solution)/shard_map/ppermute | solution.py:48
  37.3 5.8 %collective-permute-start.12 = (f32[72,128]{1,0:T(8,128)S(1)}, f32[72,128]{1,0:T(8,128)S(1)}, u32[]{:S(2)}, u32[]{:S(2)}) collective-permute-start(f32[72,128]{1,0:T(8,128)S(1)} %add.28), channel_id=1, source_target_pairs={{0,24},{4,28},{8,16},{12,20},{16,8},{20,12},{24,0},{28,4},{1,25},{... | collective-permute-start | bytes 110600 | tf_op jit(solution)/shard_map/ppermute | solution.py:48
  38.6 4.4 %collective-permute-start.13 = (f32[72,128]{1,0:T(8,128)S(1)}, f32[72,128]{1,0:T(8,128)S(1)}, u32[]{:S(2)}, u32[]{:S(2)}) collective-permute-start(f32[72,128]{1,0:T(8,128)S(1)} %add.28), channel_id=1, source_target_pairs={{0,8},{4,12},{8,0},{12,4},{16,24},{20,28},{24,16},{28,20},{1,9},{5... | collective-permute-start | bytes 110600 | tf_op jit(solution)/shard_map/ppermute | solution.py:48
  43.1 5.0 %collective-permute-start.14 = (f32[72,128]{1,0:T(8,128)S(1)}, f32[72,128]{1,0:T(8,128)S(1)}, u32[]{:S(2)}, u32[]{:S(2)}) collective-permute-start(f32[72,128]{1,0:T(8,128)S(1)} %add_add_fusion.1), channel_id=1, source_target_pairs={{0,3},{1,2},{2,1},{3,0},{4,7},{5,6},{6,5},{7,4},{8,11},{9,10},{10,... | collective-permute-start | bytes 110600 | tf_op jit(solution)/shard_map/ppermute | solution.py:48
  45.4 4.0 %collective-permute-start.15 = (f32[72,128]{1,0:T(8,128)S(1)}, f32[72,128]{1,0:T(8,128)S(1)}, u32[]{:S(2)}, u32[]{:S(2)}) collective-permute-start(f32[72,128]{1,0:T(8,128)S(1)} %add_add_fusion.1), channel_id=1, source_target_pairs={{0,2},{1,3},{2,0},{3,1},{4,6},{5,7},{6,4},{7,5},{8,10},{9,11},{10,... | collective-permute-start | bytes 110600 | tf_op jit(solution)/shard_map/ppermute | solution.py:48
  45.6 4.0 %collective-permute-start.16 = (f32[72,128]{1,0:T(8,128)S(1)}, f32[72,128]{1,0:T(8,128)S(1)}, u32[]{:S(2)}, u32[]{:S(2)}) collective-permute-start(f32[72,128]{1,0:T(8,128)S(1)} %add_add_fusion.1), channel_id=1, source_target_pairs={{0,1},{1,0},{2,3},{3,2},{4,5},{5,4},{6,7},{7,6},{8,9},{9,8},{10,11... | collective-permute-start | bytes 110600 | tf_op jit(solution)/shard_map/ppermute | solution.py:48

commit v20 on v19

--- a/solution.py
+++ b/solution.py
@@ -20,8 +20,9 @@
 def pair_exchange(value, offset):
     count = lax.axis_size("group")
     route = []
-    for low in range(offset, count - 1, 2):
-        route += [(low, low + 1), (low + 1, low)]
+    for low in range(offset, count + offset, 2):
+        first, second = low % count, (low + 1) % count
+        route += [(first, second), (second, first)]
     return lax.ppermute(value, "group", route)
 
 
@@ -80,6 +81,9 @@
         product = jnp.dot(
             hamiltonian_ref[row, source], picked, preferred_element_type=jnp.float32
         )
+        if number == sources - 1:
+            absent = index_ref[shard_blocks * sources * per_source + sources] != 0
+            product = jnp.where(absent, 0.0, product)
         total = product if total is None else total + product
     return total
 
@@ -328,6 +332,7 @@
         origins += [jnp.bitwise_xor(origin, flip) for origin in origins]
     odd = group % 2
     origins += [cycle_size + 1 - odd, cycle_size + odd]
+    origins.append((group == 0) | (group == lax.axis_size("group") - 1))
     index_array = jnp.concatenate(
         [block_columns.reshape(-1)] + [origin.reshape(1).astype(jnp.int32) for origin in origins]
     )

time: 54 us -> 55.2 us (1.022)
  waiting for transfers between devices: 15.1 us -> 18.5 us
  starting transfers between devices: 22.6 us -> 20.6 us
    ppermute x4, waiting for transfers between devices: 0.01 us -> 3.95 us  [pair_exchange(): return lax.ppermute(value, 'group', route)]
    ppermute x6, starting transfers between devices: 9.83 us -> 6.73 us  [cycle_exchange(): return lax.ppermute(value, ('group', 'blk'), route)]
    ppermute x4, starting transfers between devices: 3.69 us -> 5.82 us  [pair_exchange(): return lax.ppermute(value, 'group', route)]
    ppermute x7, starting transfers between devices: 9.06 us -> 8.06 us  [from_partner(): lax.ppermute(value, axis, [(index, index ^ flip) for index in range(count)])]
  transfers between devices with their start and end apart: 17 -> 17, of which waited for: 11 -> 12; matrix products, arithmetic and copies ran while one was open for 2% -> 2% of each run, Pallas kernels for 9% -> 9%
where the time goes in v20:
time: 55.2 us; the launch traced here: 54.9 us
  starting transfers between devices  20.6 us (37%)
  waiting for transfers between devices  18.5 us (34%)
  Pallas kernels  11.1 us (20%)
  local copies, waits for them, and re-layouts  2.92 us (5%)
  other arithmetic  1.1 us (2%)
  between operations  0.74 us (1%)
    ppermute x7, starting transfers between devices, from_partner(): lax.ppermute(value, axis, [(index, index ^ flip) for index in range(count)])  8.06 us
    ppermute x7, waiting for transfers between devices, from_partner(): lax.ppermute(value, axis, [(index, index ^ flip) for index in range(count)])  7.6 us
    ppermute x6, waiting for transfers between devices, cycle_exchange(): return lax.ppermute(value, ('group', 'blk'), route)  6.92 us
    ppermute x6, starting transfers between devices, cycle_exchange(): return lax.ppermute(value, ('group', 'blk'), route)  6.73 us
    ppermute x4, starting transfers between devices, pair_exchange(): return lax.ppermute(value, 'group', route)  5.82 us
    pallas_call x1, Pallas kernels, on_device(): call(functools.partial(factor_kernel, rows_total), (flat, square), [vmem,...  4.17 us
    ppermute x4, waiting for transfers between devices, pair_exchange(): return lax.ppermute(value, 'group', route)  3.95 us
    pallas_call x2, Pallas kernels, coupled(): call(functools.partial(middle_kernel, middle), flat, [smem] + [vmem] * (2...  2.85 us
  transfers between devices with their start and end apart: 17, of which 12 were waited for; matrix products, arithmetic and copies ran while one was open for 2% of the time, Pallas kernels for 9%

profile of v20, /device:TPU:0, one launch (start us, length us, event | category | flops | bytes accessed | tf_op | source)
XLA Modules:
  0.0 54.9 jit_solution(10690025928565065110)
XLA Ops:
  0.6 1.1 %convert_element_type.13 = bf16[1024,128]{1,0:T(8,128)(2,1)S(1)} convert(f32[1024,128]{1,0:T(8,128)} %refs_2_.1) | non-fusion elementwise | flops 131072 | bytes 786432 | tf_op jit(solution)/shard_map/convert_element_type | solution.py:372
  1.7 0.5 collective-permute-start
  2.2 2.6 %collective-permute-start.1 = (bf16[16,64,128]{2,1,0:T(8,128)(2,1)S(1)}, bf16[16,64,128]{2,1,0:T(8,128)(2,1)S(1)}, u32[]{:S(2)}, u32[]{:S(2)}) collective-permute-start(bf16[16,64,128]{2,1,0:T(8,128)(2,1)S(1)} %bitcast.10), channel_id=1, source_target_pairs={{0,1},{1,0},{2,3},{3,2},{4,6},{5,7},{6,4},{7,5},{8,9},{9,8},{10,11... | collective-permute-start | bytes 786440 | tf_op jit(solution)/shard_map/ppermute | solution.py:44
  4.8 3.4 %collective-permute-start.3 = (bf16[16,64,128]{2,1,0:T(8,128)(2,1)S(1)}, bf16[16,64,128]{2,1,0:T(8,128)(2,1)S(1)}, u32[]{:S(2)}, u32[]{:S(2)}) collective-permute-start(bf16[16,64,128]{2,1,0:T(8,128)(2,1)S(1)} %bitcast.11), channel_id=1, source_target_pairs={{4,8},{8,4},{12,16},{16,12},{20,24},{24,20},{28,0},{0,28},{5,9},{9... | collective-permute-start | bytes 786440 | tf_op jit(solution)/shard_map/ppermute | solution.py:26
  8.2 0.8 %copy.6 = s32[16,6,4]{2,1,0:T(8,128)S(1)} copy(s32[16,6,4]{0,2,1:T(4,128)} %param.5) | data formatting | bytes 3072 | tf_op args[1]
  9.0 0.1 reshape.33
  9.1 0.1 concatenate.3.index_ref
  9.2 0.0 collective-permute-done.refs_0_
  9.2 0.6 %collective-permute-start.2 = (bf16[16,64,128]{2,1,0:T(8,128)(2,1)S(1)}, bf16[16,64,128]{2,1,0:T(8,128)(2,1)S(1)}, u32[]{:S(2)}, u32[]{:S(2)}) collective-permute-start(bf16[16,64,128]{2,1,0:T(8,128)(2,1)S(1)} %bitcast.12), channel_id=1, source_target_pairs={{0,2},{1,3},{2,0},{3,1},{4,5},{5,4},{6,7},{7,6},{8,10},{9,11},{10,... | collective-permute-start | bytes 786440 | tf_op jit(solution)/shard_map/ppermute | solution.py:44
  9.7 0.0 collective-permute-done.1.refs_1_
  9.8 1.5 %collective-permute-start.4 = (bf16[16,64,128]{2,1,0:T(8,128)(2,1)S(1)}, bf16[16,64,128]{2,1,0:T(8,128)(2,1)S(1)}, u32[]{:S(2)}, u32[]{:S(2)}) collective-permute-start(bf16[16,64,128]{2,1,0:T(8,128)(2,1)S(1)} %collective-permute-done.1.refs_1_), channel_id=1, source_target_pairs={{0,2},{1,3},{2,0},{3,1},{4,5},{5,4},{6,7},{7,6},{8,10},{9,11},{10,... | collective-permute-start | bytes 786440 | tf_op jit(solution)/shard_map/ppermute | solution.py:44
  11.3 0.0 copy-start
  11.3 1.9 %copy-done = bf16[16,6,64,256]{3,2,1,0:T(8,128)(2,1)S(1)} copy-done((bf16[16,6,64,256]{3,2,1,0:T(8,128)(2,1)S(1)}, bf16[16,6,64,256]{3,2,1,0:T(8,128)(2,1)}, u32[]{:S(2)}) %copy-start) | copy-done | bytes 3145752
  13.2 0.9 %shard_map.59.partial_ref = f32[1024,128]{1,0:T(8,128)S(1)} custom-call(s32[391]{0:T(512)S(1)} %concatenate.3.index_ref, bf16[16,6,64,256]{3,2,1,0:T(8,128)(2,1)S(1)} %copy-done, bf16[16,64,128]{2,1,0:T(8,128)(2,1)S(1)} %bitcast.13), custom_call_target="tpu_custom_call" | custom-call | tf_op jit(solution)/shard_map/pallas_call | solution.py:348
  14.0 0.0 copy-start.1
  14.1 0.0 copy-start.2
  14.1 0.6 %collective-permute-done.3.refs_3_ = bf16[16,64,128]{2,1,0:T(8,128)(2,1)S(1)} collective-permute-done((bf16[16,64,128]{2,1,0:T(8,128)(2,1)S(1)}, bf16[16,64,128]{2,1,0:T(8,128)(2,1)S(1)}, u32[]{:S(2)}, u32[]{:S(2)}) %collective-permute-start.3) | collective-permute-done | bytes 262176 | tf_op jit(solution)/shard_map/ppermute | solution.py:26
  14.7 0.9 %collective-permute-done.2.refs_2_ = bf16[16,64,128]{2,1,0:T(8,128)(2,1)S(1)} collective-permute-done((bf16[16,64,128]{2,1,0:T(8,128)(2,1)S(1)}, bf16[16,64,128]{2,1,0:T(8,128)(2,1)S(1)}, u32[]{:S(2)}, u32[]{:S(2)}) %collective-permute-start.2) | collective-permute-done | bytes 262176 | tf_op jit(solution)/shard_map/ppermute | solution.py:44
  15.6 1.4 %shard_map.60.partial_ref = f32[1024,128]{1,0:T(8,128)S(1)} custom-call(s32[391]{0:T(512)S(1)} %concatenate.3.index_ref, bf16[16,6,64,256]{3,2,1,0:T(8,128)(2,1)S(1)} %copy-done, f32[1024,128]{1,0:T(8,128)S(1)} %shard_map.59.partial_ref, bf16[16,64,128]{2,1,0:T(8,128)(2,1)S(1)} %collective-permute-done.refs_0_, ...), custom_call_target="tpu_custom_call" | custom-call | tf_op jit(solution)/shard_map/pallas_call | solution.py:367
  17.0 1.4 %collective-permute-done.4.refs_0_ = bf16[16,64,128]{2,1,0:T(8,128)(2,1)S(1)} collective-permute-done((bf16[16,64,128]{2,1,0:T(8,128)(2,1)S(1)}, bf16[16,64,128]{2,1,0:T(8,128)(2,1)S(1)}, u32[]{:S(2)}, u32[]{:S(2)}) %collective-permute-start.4) | collective-permute-done | bytes 262176 | tf_op jit(solution)/shard_map/ppermute | solution.py:44
  18.4 0.0 copy-done.1
  18.4 0.0 copy-done.2
  18.4 1.0 %shard_map.61 = (f32[1024,128]{1,0:T(8,128)S(1)}, bf16[16,64,128]{2,1,0:T(8,128)(2,1)S(1)}) custom-call(s32[391]{0:T(512)S(1)} %concatenate.3.index_ref, bf16[16,6,64,256]{3,2,1,0:T(8,128)(2,1)S(1)} %copy-done, f32[8,128]{1,0:T(8,128)S(1)} %bitcast.14, f32[1024,128]{1,0:T(8,128)S(1)} %copy-done.1, f32[1024,128]{1,0:T(8,128)S(1)} %shard_map.60.partial_ref, ...), custom_call_target="tpu_custom_call" | custom-call | tf_op jit(solution)/shard_map/pallas_call | solution.py:373
  19.4 0.1 collective-permute-start.5
  19.5 1.6 %collective-permute-start.6 = (bf16[16,64,128]{2,1,0:T(8,128)(2,1)S(1)}, bf16[16,64,128]{2,1,0:T(8,128)(2,1)S(1)}, u32[]{:S(2)}, u32[]{:S(2)}) collective-permute-start(bf16[16,64,128]{2,1,0:T(8,128)(2,1)S(1)} %get-tuple-element.19.own_ref), channel_id=1, source_target_pairs={{0,1},{1,0},{2,3},{3,2},{4,6},{5,7},{6,4},{7,5},{8,9},{9,8},{10,11... | collective-permute-start | bytes 786440 | tf_op jit(solution)/shard_map/ppermute | solution.py:44
  21.0 1.8 %collective-permute-start.8 = (bf16[16,64,128]{2,1,0:T(8,128)(2,1)S(1)}, bf16[16,64,128]{2,1,0:T(8,128)(2,1)S(1)}, u32[]{:S(2)}, u32[]{:S(2)}) collective-permute-start(bf16[16,64,128]{2,1,0:T(8,128)(2,1)S(1)} %get-tuple-element.19.own_ref), channel_id=1, source_target_pairs={{4,8},{8,4},{12,16},{16,12},{20,24},{24,20},{28,0},{0,28},{5,9},{9... | collective-permute-start | bytes 786440 | tf_op jit(solution)/shard_map/ppermute | solution.py:26
  22.9 1.0 %shard_map.62.partial_ref = f32[1024,128]{1,0:T(8,128)S(1)} custom-call(s32[391]{0:T(512)S(1)} %concatenate.3.index_ref, bf16[16,6,64,256]{3,2,1,0:T(8,128)(2,1)S(1)} %copy-done, bf16[16,64,128]{2,1,0:T(8,128)(2,1)S(1)} %get-tuple-element.19.own_ref, f32[8,128]{1,0:T(8,128)S(1)} %bitcast.15, f32[1024,128]{1,0:T(8,128)S(1)} %get-tuple-element.16.refs_1_, ...), custom_call_target="tpu_custom_call" | custom-call | tf_op jit(solution)/shard_map/pallas_call | solution.py:348
  23.9 0.0 collective-permute-done.5.refs_0_
  23.9 0.5 collective-permute-start.7
  24.4 3.0 %collective-permute-done.6.refs_1_ = bf16[16,64,128]{2,1,0:T(8,128)(2,1)S(1)} collective-permute-done((bf16[16,64,128]{2,1,0:T(8,128)(2,1)S(1)}, bf16[16,64,128]{2,1,0:T(8,128)(2,1)S(1)}, u32[]{:S(2)}, u32[]{:S(2)}) %collective-permute-start.6) | collective-permute-done | bytes 262176 | tf_op jit(solution)/shard_map/ppermute | solution.py:44
  27.4 0.0 collective-permute-start.9
  27.4 3.3 %collective-permute-done.8.refs_3_ = bf16[16,64,128]{2,1,0:T(8,128)(2,1)S(1)} collective-permute-done((bf16[16,64,128]{2,1,0:T(8,128)(2,1)S(1)}, bf16[16,64,128]{2,1,0:T(8,128)(2,1)S(1)}, u32[]{:S(2)}, u32[]{:S(2)}) %collective-permute-start.8) | collective-permute-done | bytes 262176 | tf_op jit(solution)/shard_map/ppermute | solution.py:26
  30.7 0.0 collective-permute-done.7.refs_2_
  30.8 1.4 %shard_map.63.partial_ref = f32[1024,128]{1,0:T(8,128)S(1)} custom-call(s32[391]{0:T(512)S(1)} %concatenate.3.index_ref, bf16[16,6,64,256]{3,2,1,0:T(8,128)(2,1)S(1)} %copy-done, f32[1024,128]{1,0:T(8,128)S(1)} %shard_map.62.partial_ref, bf16[16,64,128]{2,1,0:T(8,128)(2,1)S(1)} %collective-permute-done.5.refs_0_, ...), custom_call_target="tpu_custom_call" | custom-call | tf_op jit(solution)/shard_map/pallas_call | solution.py:367
  32.2 1.6 %collective-permute-done.9.refs_0_ = bf16[16,64,128]{2,1,0:T(8,128)(2,1)S(1)} collective-permute-done((bf16[16,64,128]{2,1,0:T(8,128)(2,1)S(1)}, bf16[16,64,128]{2,1,0:T(8,128)(2,1)S(1)}, u32[]{:S(2)}, u32[]{:S(2)}) %collective-permute-start.9) | collective-permute-done | bytes 262176 | tf_op jit(solution)/shard_map/ppermute | solution.py:44
  33.8 1.3 %shard_map.64 = (bf16[1024,256]{1,0:T(8,128)(2,1)S(1)}, f32[72,128]{1,0:T(8,128)S(1)}) custom-call(s32[391]{0:T(512)S(1)} %concatenate.3.index_ref, bf16[16,6,64,256]{3,2,1,0:T(8,128)(2,1)S(1)} %copy-done, f32[1024,128]{1,0:T(8,128)S(1)} %shard_map.63.partial_ref, bf16[16,64,128]{2,1,0:T(8,128)(2,1)S(1)} %collective-permute-done.9.refs_0_), custom_call_target="tpu_custom_call" | custom-call | tf_op jit(solution)/shard_map/pallas_call | solution.py:378
  35.0 0.1 collective-permute-start.10
  35.1 1.2 %collective-permute-done.10 = f32[72,128]{1,0:T(8,128)S(1)} collective-permute-done((f32[72,128]{1,0:T(8,128)S(1)}, f32[72,128]{1,0:T(8,128)S(1)}, u32[]{:S(2)}, u32[]{:S(2)}) %collective-permute-start.10) | collective-permute-done | bytes 36896 | tf_op jit(solution)/shard_map/ppermute | solution.py:49
  36.3 0.0 collective-permute-start.11
  36.3 2.4 %collective-permute-start.12 = (f32[72,128]{1,0:T(8,128)S(1)}, f32[72,128]{1,0:T(8,128)S(1)}, u32[]{:S(2)}, u32[]{:S(2)}) collective-permute-start(f32[72,128]{1,0:T(8,128)S(1)} %add.28), channel_id=1, source_target_pairs={{0,24},{4,28},{8,16},{12,20},{16,8},{20,12},{24,0},{28,4},{1,25},{... | collective-permute-start | bytes 110600 | tf_op jit(solution)/shard_map/ppermute | solution.py:49
  38.7 1.1 %collective-permute-start.13 = (f32[72,128]{1,0:T(8,128)S(1)}, f32[72,128]{1,0:T(8,128)S(1)}, u32[]{:S(2)}, u32[]{:S(2)}) collective-permute-start(f32[72,128]{1,0:T(8,128)S(1)} %add.28), channel_id=1, source_target_pairs={{0,8},{4,12},{8,0},{12,4},{16,24},{20,28},{24,16},{28,20},{1,9},{5... | collective-permute-start | bytes 110600 | tf_op jit(solution)/shard_map/ppermute | solution.py:49
  39.8 2.5 %collective-permute-done.11 = f32[72,128]{1,0:T(8,128)S(1)} collective-permute-done((f32[72,128]{1,0:T(8,128)S(1)}, f32[72,128]{1,0:T(8,128)S(1)}, u32[]{:S(2)}, u32[]{:S(2)}) %collective-permute-start.11) | collective-permute-done | bytes 36896 | tf_op jit(solution)/shard_map/ppermute | solution.py:49
  42.3 0.0 collective-permute-done.12
  42.3 0.5 collective-permute-done.13
  42.8 3.9 %collective-permute-start.14 = (f32[72,128]{1,0:T(8,128)S(1)}, f32[72,128]{1,0:T(8,128)S(1)}, u32[]{:S(2)}, u32[]{:S(2)}) collective-permute-start(f32[72,128]{1,0:T(8,128)S(1)} %add_add_fusion.1), channel_id=1, source_target_pairs={{0,3},{1,2},{2,1},{3,0},{4,7},{5,6},{6,5},{7,4},{8,11},{9,10},{10,... | collective-permute-start | bytes 110600 | tf_op jit(solution)/shard_map/ppermute | solution.py:49
  46.7 0.1 collective-permute-start.15
  46.8 0.6 %collective-permute-start.16 = (f32[72,128]{1,0:T(8,128)S(1)}, f32[72,128]{1,0:T(8,128)S(1)}, u32[]{:S(2)}, u32[]{:S(2)}) collective-permute-start(f32[72,128]{1,0:T(8,128)S(1)} %add_add_fusion.1), channel_id=1, source_target_pairs={{0,1},{1,0},{2,3},{3,2},{4,5},{5,4},{6,7},{7,6},{8,9},{9,8},{10,11... | collective-permute-start | bytes 110600 | tf_op jit(solution)/shard_map/ppermute | solution.py:49
  47.3 1.3 %collective-permute-done.14 = f32[72,128]{1,0:T(8,128)S(1)} collective-permute-done((f32[72,128]{1,0:T(8,128)S(1)}, f32[72,128]{1,0:T(8,128)S(1)}, u32[]{:S(2)}, u32[]{:S(2)}) %collective-permute-start.14) | collective-permute-done | bytes 36896 | tf_op jit(solution)/shard_map/ppermute | solution.py:49
  48.6 2.0 %collective-permute-done.15 = f32[72,128]{1,0:T(8,128)S(1)} collective-permute-done((f32[72,128]{1,0:T(8,128)S(1)}, f32[72,128]{1,0:T(8,128)S(1)}, u32[]{:S(2)}, u32[]{:S(2)}) %collective-permute-start.15) | collective-permute-done | bytes 36896 | tf_op jit(solution)/shard_map/ppermute | solution.py:49
  50.7 0.1 collective-permute-done.16
  50.8 4.2 %shard_map.65 = (f32[1024,128]{1,0:T(8,128)}, f32[128,128]{1,0:T(8,128)}) custom-call(f32[72,128]{1,0:T(8,128)S(1)} %add_add_fusion.packed_ref, bf16[1024,256]{1,0:T(8,128)(2,1)S(1)} %get-tuple-element.21.both_ref), custom_call_target="tpu_custom_call" | custom-call | tf_op jit(solution)/shard_map/pallas_call | solution.py:382
  (3 shorter events, 0.0 us)
Async XLA Ops:
  1.7 7.5 %collective-permute-start = (bf16[16,64,128]{2,1,0:T(8,128)(2,1)S(1)}, bf16[16,64,128]{2,1,0:T(8,128)(2,1)S(1)}, u32[]{:S(2)}, u32[]{:S(2)}) collective-permute-start(bf16[16,64,128]{2,1,0:T(8,128)(2,1)S(1)} %bitcast.9), channel_id=1, source_target_pairs={{0,4},{4,0},{8,12},{12,8},{16,20},{20,16},{24,28},{28,24},{1,5},{5... | collective-permute-start | bytes 786440 | tf_op jit(solution)/shard_map/ppermute | solution.py:26
  2.2 7.5 %collective-permute-start.1 = (bf16[16,64,128]{2,1,0:T(8,128)(2,1)S(1)}, bf16[16,64,128]{2,1,0:T(8,128)(2,1)S(1)}, u32[]{:S(2)}, u32[]{:S(2)}) collective-permute-start(bf16[16,64,128]{2,1,0:T(8,128)(2,1)S(1)} %bitcast.10), channel_id=1, source_target_pairs={{0,1},{1,0},{2,3},{3,2},{4,6},{5,7},{6,4},{7,5},{8,9},{9,8},{10,11... | collective-permute-start | bytes 786440 | tf_op jit(solution)/shard_map/ppermute | solution.py:44
  4.8 9.9 %collective-permute-start.3 = (bf16[16,64,128]{2,1,0:T(8,128)(2,1)S(1)}, bf16[16,64,128]{2,1,0:T(8,128)(2,1)S(1)}, u32[]{:S(2)}, u32[]{:S(2)}) collective-permute-start(bf16[16,64,128]{2,1,0:T(8,128)(2,1)S(1)} %bitcast.11), channel_id=1, source_target_pairs={{4,8},{8,4},{12,16},{16,12},{20,24},{24,20},{28,0},{0,28},{5,9},{9... | collective-permute-start | bytes 786440 | tf_op jit(solution)/shard_map/ppermute | solution.py:26
  9.2 6.4 %collective-permute-start.2 = (bf16[16,64,128]{2,1,0:T(8,128)(2,1)S(1)}, bf16[16,64,128]{2,1,0:T(8,128)(2,1)S(1)}, u32[]{:S(2)}, u32[]{:S(2)}) collective-permute-start(bf16[16,64,128]{2,1,0:T(8,128)(2,1)S(1)} %bitcast.12), channel_id=1, source_target_pairs={{0,2},{1,3},{2,0},{3,1},{4,5},{5,4},{6,7},{7,6},{8,10},{9,11},{10,... | collective-permute-start | bytes 786440 | tf_op jit(solution)/shard_map/ppermute | solution.py:44
  9.8 8.7 %collective-permute-start.4 = (bf16[16,64,128]{2,1,0:T(8,128)(2,1)S(1)}, bf16[16,64,128]{2,1,0:T(8,128)(2,1)S(1)}, u32[]{:S(2)}, u32[]{:S(2)}) collective-permute-start(bf16[16,64,128]{2,1,0:T(8,128)(2,1)S(1)} %collective-permute-done.1.refs_1_), channel_id=1, source_target_pairs={{0,2},{1,3},{2,0},{3,1},{4,5},{5,4},{6,7},{7,6},{8,10},{9,11},{10,... | collective-permute-start | bytes 786440 | tf_op jit(solution)/shard_map/ppermute | solution.py:44
  11.3 1.9 %copy-start = (bf16[16,6,64,256]{3,2,1,0:T(8,128)(2,1)S(1)}, bf16[16,6,64,256]{3,2,1,0:T(8,128)(2,1)}, u32[]{:S(2)}) copy-start(bf16[16,6,64,256]{3,2,1,0:T(8,128)(2,1)} %hamiltonian_ref.11) | copy-start | bytes 9437188
  14.0 4.4 %copy-start.1 = (f32[1024,128]{1,0:T(8,128)S(1)}, f32[1024,128]{1,0:T(8,128)}, u32[]{:S(2)}) copy-start(f32[1024,128]{1,0:T(8,128)} %refs_2_.1) | copy-start | bytes 1572868
  14.1 4.4 %copy-start.2 = (f32[1024]{0:T(1024)S(1)}, f32[1024]{0:T(1024)}, u32[]{:S(2)}) copy-start(f32[1024]{0:T(1024)} %param.6) | copy-start | bytes 12292
  19.4 4.5 %collective-permute-start.5 = (bf16[16,64,128]{2,1,0:T(8,128)(2,1)S(1)}, bf16[16,64,128]{2,1,0:T(8,128)(2,1)S(1)}, u32[]{:S(2)}, u32[]{:S(2)}) collective-permute-start(bf16[16,64,128]{2,1,0:T(8,128)(2,1)S(1)} %get-tuple-element.19.own_ref), channel_id=1, source_target_pairs={{0,4},{4,0},{8,12},{12,8},{16,20},{20,16},{24,28},{28,24},{1,5},{5... | collective-permute-start | bytes 786440 | tf_op jit(solution)/shard_map/ppermute | solution.py:26
  19.5 7.9 %collective-permute-start.6 = (bf16[16,64,128]{2,1,0:T(8,128)(2,1)S(1)}, bf16[16,64,128]{2,1,0:T(8,128)(2,1)S(1)}, u32[]{:S(2)}, u32[]{:S(2)}) collective-permute-start(bf16[16,64,128]{2,1,0:T(8,128)(2,1)S(1)} %get-tuple-element.19.own_ref), channel_id=1, source_target_pairs={{0,1},{1,0},{2,3},{3,2},{4,6},{5,7},{6,4},{7,5},{8,9},{9,8},{10,11... | collective-permute-start | bytes 786440 | tf_op jit(solution)/shard_map/ppermute | solution.py:44
  21.0 9.7 %collective-permute-start.8 = (bf16[16,64,128]{2,1,0:T(8,128)(2,1)S(1)}, bf16[16,64,128]{2,1,0:T(8,128)(2,1)S(1)}, u32[]{:S(2)}, u32[]{:S(2)}) collective-permute-start(bf16[16,64,128]{2,1,0:T(8,128)(2,1)S(1)} %get-tuple-element.19.own_ref), channel_id=1, source_target_pairs={{4,8},{8,4},{12,16},{16,12},{20,24},{24,20},{28,0},{0,28},{5,9},{9... | collective-permute-start | bytes 786440 | tf_op jit(solution)/shard_map/ppermute | solution.py:26
  23.9 6.9 %collective-permute-start.7 = (bf16[16,64,128]{2,1,0:T(8,128)(2,1)S(1)}, bf16[16,64,128]{2,1,0:T(8,128)(2,1)S(1)}, u32[]{:S(2)}, u32[]{:S(2)}) collective-permute-start(bf16[16,64,128]{2,1,0:T(8,128)(2,1)S(1)} %get-tuple-element.19.own_ref), channel_id=1, source_target_pairs={{0,2},{1,3},{2,0},{3,1},{4,5},{5,4},{6,7},{7,6},{8,10},{9,11},{10,... | collective-permute-start | bytes 786440 | tf_op jit(solution)/shard_map/ppermute | solution.py:44
  27.4 6.4 %collective-permute-start.9 = (bf16[16,64,128]{2,1,0:T(8,128)(2,1)S(1)}, bf16[16,64,128]{2,1,0:T(8,128)(2,1)S(1)}, u32[]{:S(2)}, u32[]{:S(2)}) collective-permute-start(bf16[16,64,128]{2,1,0:T(8,128)(2,1)S(1)} %collective-permute-done.6.refs_1_), channel_id=1, source_target_pairs={{0,2},{1,3},{2,0},{3,1},{4,5},{5,4},{6,7},{7,6},{8,10},{9,11},{10,... | collective-permute-start | bytes 786440 | tf_op jit(solution)/shard_map/ppermute | solution.py:44
  35.0 1.3 %collective-permute-start.10 = (f32[72,128]{1,0:T(8,128)S(1)}, f32[72,128]{1,0:T(8,128)S(1)}, u32[]{:S(2)}, u32[]{:S(2)}) collective-permute-start(f32[72,128]{1,0:T(8,128)S(1)} %get-tuple-element.20), channel_id=1, source_target_pairs={{0,4},{4,0},{8,12},{12,8},{16,20},{20,16},{24,28},{28,24},{1,5},{5... | collective-permute-start | bytes 110600 | tf_op jit(solution)/shard_map/ppermute | solution.py:49
  36.3 6.0 %collective-permute-start.11 = (f32[72,128]{1,0:T(8,128)S(1)}, f32[72,128]{1,0:T(8,128)S(1)}, u32[]{:S(2)}, u32[]{:S(2)}) collective-permute-start(f32[72,128]{1,0:T(8,128)S(1)} %add.28), channel_id=1, source_target_pairs={{0,16},{4,20},{8,24},{12,28},{16,0},{20,4},{24,8},{28,12},{1,17},{... | collective-permute-start | bytes 110600 | tf_op jit(solution)/shard_map/ppermute | solution.py:49
  36.3 6.0 %collective-permute-start.12 = (f32[72,128]{1,0:T(8,128)S(1)}, f32[72,128]{1,0:T(8,128)S(1)}, u32[]{:S(2)}, u32[]{:S(2)}) collective-permute-start(f32[72,128]{1,0:T(8,128)S(1)} %add.28), channel_id=1, source_target_pairs={{0,24},{4,28},{8,16},{12,20},{16,8},{20,12},{24,0},{28,4},{1,25},{... | collective-permute-start | bytes 110600 | tf_op jit(solution)/shard_map/ppermute | solution.py:49
  38.7 4.1 %collective-permute-start.13 = (f32[72,128]{1,0:T(8,128)S(1)}, f32[72,128]{1,0:T(8,128)S(1)}, u32[]{:S(2)}, u32[]{:S(2)}) collective-permute-start(f32[72,128]{1,0:T(8,128)S(1)} %add.28), channel_id=1, source_target_pairs={{0,8},{4,12},{8,0},{12,4},{16,24},{20,28},{24,16},{28,20},{1,9},{5... | collective-permute-start | bytes 110600 | tf_op jit(solution)/shard_map/ppermute | solution.py:49
  42.8 5.8 %collective-permute-start.14 = (f32[72,128]{1,0:T(8,128)S(1)}, f32[72,128]{1,0:T(8,128)S(1)}, u32[]{:S(2)}, u32[]{:S(2)}) collective-permute-start(f32[72,128]{1,0:T(8,128)S(1)} %add_add_fusion.1), channel_id=1, source_target_pairs={{0,3},{1,2},{2,1},{3,0},{4,7},{5,6},{6,5},{7,4},{8,11},{9,10},{10,... | collective-permute-start | bytes 110600 | tf_op jit(solution)/shard_map/ppermute | solution.py:49
  46.7 4.0 %collective-permute-start.15 = (f32[72,128]{1,0:T(8,128)S(1)}, f32[72,128]{1,0:T(8,128)S(1)}, u32[]{:S(2)}, u32[]{:S(2)}) collective-permute-start(f32[72,128]{1,0:T(8,128)S(1)} %add_add_fusion.1), channel_id=1, source_target_pairs={{0,2},{1,3},{2,0},{3,1},{4,6},{5,7},{6,4},{7,5},{8,10},{9,11},{10,... | collective-permute-start | bytes 110600 | tf_op jit(solution)/shard_map/ppermute | solution.py:49
  46.8 4.0 %collective-permute-start.16 = (f32[72,128]{1,0:T(8,128)S(1)}, f32[72,128]{1,0:T(8,128)S(1)}, u32[]{:S(2)}, u32[]{:S(2)}) collective-permute-start(f32[72,128]{1,0:T(8,128)S(1)} %add_add_fusion.1), channel_id=1, source_target_pairs={{0,1},{1,0},{2,3},{3,2},{4,5},{5,4},{6,7},{7,6},{8,9},{9,8},{10,11... | collective-permute-start | bytes 110600 | tf_op jit(solution)/shard_map/ppermute | solution.py:49

commit v21 on v19

--- a/solution.py
+++ b/solution.py
@@ -333,7 +333,7 @@
     )
     last = cycle_size - 1
     ending = [last]
-    middle = [cycle_size, 1] + list(range(2, last)) + [cycle_size + 1]
+    middle = [1, cycle_size + 1, cycle_size] + list(range(2, last))
     flat = jax.ShapeDtypeStruct((flat_rows, states), jnp.float32)
     rounded = jax.ShapeDtypeStruct((shard_blocks, block_size, states), jnp.bfloat16)
     packed = jax.ShapeDtypeStruct((states // 2 + SUB, states), jnp.float32)
@@ -347,12 +347,10 @@
     def coupled(value, index_array, early, *terms):
         arrived = cycle_exchange(value, 0)
         pairs = [pair_exchange(value, 0), pair_exchange(value, 1)]
+        others = [cycle_exchange(value, level) for level in range(1, levels)]
         if early:
             partial = own_part(index_array, value, *terms)
-            later, pairs[0], partial = lax.optimization_barrier((value, pairs[0], partial))
-        else:
-            later, pairs[0], index_array = lax.optimization_barrier((value, pairs[0], index_array))
-        others = [cycle_exchange(later, level) for level in range(1, levels)]
+            arrived, partial = lax.optimization_barrier((arrived, partial))
         pieces = [value, arrived]
         for level, other in zip(range(1, levels), others):
             pieces += [other] + [cycle_exchange(piece, level) for piece in pieces[1:]]

time: 54 us -> 54 us (level)
  waiting for transfers between devices: 15.1 us -> 13.8 us
  starting transfers between devices: 22.6 us -> 23.9 us
    ppermute x4, starting transfers between devices: 3.69 us -> 7.31 us  [pair_exchange(): return lax.ppermute(value, 'group', route)]
    ppermute x6, waiting for transfers between devices: 7.25 us -> 5.11 us  [cycle_exchange(): return lax.ppermute(value, ('group', 'blk'), route)]
    ppermute x7, starting transfers between devices: 9.06 us -> 7.56 us  [from_partner(): lax.ppermute(value, axis, [(index, index ^ flip) for index in range(count)])]
    ppermute x7, waiting for transfers between devices: 7.87 us -> 8.68 us  [from_partner(): lax.ppermute(value, axis, [(index, index ^ flip) for index in range(count)])]
    ppermute x6, starting transfers between devices: 9.83 us -> 9.04 us  [cycle_exchange(): return lax.ppermute(value, ('group', 'blk'), route)]
  transfers between devices with their start and end apart: 17 -> 17, of which waited for: 11 -> 9; matrix products, arithmetic and copies ran while one was open for 2% -> 2% of each run, Pallas kernels for 9% -> 9%
where the time goes in v21:
time: 54 us; the launch traced here: 53.7 us
  starting transfers between devices  23.9 us (44%)
  waiting for transfers between devices  13.8 us (26%)
  Pallas kernels  11.2 us (21%)
  local copies, waits for them, and re-layouts  2.92 us (5%)
  other arithmetic  1.1 us (2%)
  between operations  0.76 us (1%)
    ppermute x6, starting transfers between devices, cycle_exchange(): return lax.ppermute(value, ('group', 'blk'), route)  9.04 us
    ppermute x7, waiting for transfers between devices, from_partner(): lax.ppermute(value, axis, [(index, index ^ flip) for index in range(count)])  8.68 us
    ppermute x7, starting transfers between devices, from_partner(): lax.ppermute(value, axis, [(index, index ^ flip) for index in range(count)])  7.56 us
    ppermute x4, starting transfers between devices, pair_exchange(): return lax.ppermute(value, 'group', route)  7.31 us
    ppermute x6, waiting for transfers between devices, cycle_exchange(): return lax.ppermute(value, ('group', 'blk'), route)  5.11 us
    pallas_call x1, Pallas kernels, on_device(): call(functools.partial(factor_kernel, rows_total), (flat, square), [vmem,...  4.17 us
    pallas_call x2, Pallas kernels, coupled(): call(functools.partial(middle_kernel, middle), flat, [smem] + [vmem] * (2...  2.96 us
    unnamed x7, local copies, waits for them, and re-layouts  2.72 us
  transfers between devices with their start and end apart: 17, of which 9 were waited for; matrix products, arithmetic and copies ran while one was open for 2% of the time, Pallas kernels for 9%

profile of v21, /device:TPU:0, one launch (start us, length us, event | category | flops | bytes accessed | tf_op | source)
XLA Modules:
  0.0 53.7 jit_solution(16143570949000241566)
XLA Ops:
  0.6 1.1 %convert_element_type.5 = bf16[1024,128]{1,0:T(8,128)(2,1)S(1)} convert(f32[1024,128]{1,0:T(8,128)} %refs_2_.1) | non-fusion elementwise | flops 131072 | bytes 786432 | tf_op jit(solution)/shard_map/convert_element_type | solution.py:365
  1.7 3.0 %collective-permute-start = (bf16[16,64,128]{2,1,0:T(8,128)(2,1)S(1)}, bf16[16,64,128]{2,1,0:T(8,128)(2,1)S(1)}, u32[]{:S(2)}, u32[]{:S(2)}) collective-permute-start(bf16[16,64,128]{2,1,0:T(8,128)(2,1)S(1)} %bitcast.8), channel_id=1, source_target_pairs={{0,1},{1,0},{2,3},{3,2},{4,6},{5,7},{6,4},{7,5},{8,9},{9,8},{10,11... | collective-permute-start | bytes 786440 | tf_op jit(solution)/shard_map/ppermute | solution.py:43
  4.7 0.7 %collective-permute-start.1 = (bf16[16,64,128]{2,1,0:T(8,128)(2,1)S(1)}, bf16[16,64,128]{2,1,0:T(8,128)(2,1)S(1)}, u32[]{:S(2)}, u32[]{:S(2)}) collective-permute-start(bf16[16,64,128]{2,1,0:T(8,128)(2,1)S(1)} %bitcast.9), channel_id=1, source_target_pairs={{4,8},{8,4},{12,16},{16,12},{20,24},{24,20},{5,9},{9,5},{13,17},{1... | collective-permute-start | bytes 786440 | tf_op jit(solution)/shard_map/ppermute | solution.py:25
  5.4 3.0 %collective-permute-start.2 = (bf16[16,64,128]{2,1,0:T(8,128)(2,1)S(1)}, bf16[16,64,128]{2,1,0:T(8,128)(2,1)S(1)}, u32[]{:S(2)}, u32[]{:S(2)}) collective-permute-start(bf16[16,64,128]{2,1,0:T(8,128)(2,1)S(1)} %bitcast.10), channel_id=1, source_target_pairs={{0,4},{4,0},{8,12},{12,8},{16,20},{20,16},{24,28},{28,24},{1,5},{5... | collective-permute-start | bytes 786440 | tf_op jit(solution)/shard_map/ppermute | solution.py:25
  8.4 1.5 %collective-permute-start.3 = (bf16[16,64,128]{2,1,0:T(8,128)(2,1)S(1)}, bf16[16,64,128]{2,1,0:T(8,128)(2,1)S(1)}, u32[]{:S(2)}, u32[]{:S(2)}) collective-permute-start(bf16[16,64,128]{2,1,0:T(8,128)(2,1)S(1)} %bitcast.11), channel_id=1, source_target_pairs={{0,2},{1,3},{2,0},{3,1},{4,5},{5,4},{6,7},{7,6},{8,10},{9,11},{10,... | collective-permute-start | bytes 786440 | tf_op jit(solution)/shard_map/ppermute | solution.py:43
  9.9 0.0 collective-permute-done.refs_0_
  9.9 1.2 %collective-permute-start.4 = (bf16[16,64,128]{2,1,0:T(8,128)(2,1)S(1)}, bf16[16,64,128]{2,1,0:T(8,128)(2,1)S(1)}, u32[]{:S(2)}, u32[]{:S(2)}) collective-permute-start(bf16[16,64,128]{2,1,0:T(8,128)(2,1)S(1)} %collective-permute-done.refs_0_), channel_id=1, source_target_pairs={{0,2},{1,3},{2,0},{3,1},{4,5},{5,4},{6,7},{7,6},{8,10},{9,11},{10,... | collective-permute-start | bytes 786440 | tf_op jit(solution)/shard_map/ppermute | solution.py:43
  11.1 0.8 %copy.6 = s32[16,6,4]{2,1,0:T(8,128)S(1)} copy(s32[16,6,4]{0,2,1:T(4,128)} %param.5) | data formatting | bytes 3072 | tf_op args[1]
  11.9 0.1 reshape.30
  12.0 0.1 concatenate.3.index_ref
  12.1 0.0 copy-start
  12.1 1.9 %copy-done = bf16[16,6,64,256]{3,2,1,0:T(8,128)(2,1)S(1)} copy-done((bf16[16,6,64,256]{3,2,1,0:T(8,128)(2,1)S(1)}, bf16[16,6,64,256]{3,2,1,0:T(8,128)(2,1)}, u32[]{:S(2)}) %copy-start) | copy-done | bytes 3145752
  14.0 0.9 %shard_map.59.partial_ref = f32[1024,128]{1,0:T(8,128)S(1)} custom-call(s32[390]{0:T(512)S(1)} %concatenate.3.index_ref, bf16[16,6,64,256]{3,2,1,0:T(8,128)(2,1)S(1)} %copy-done, bf16[16,64,128]{2,1,0:T(8,128)(2,1)S(1)} %bitcast.12), custom_call_target="tpu_custom_call" | custom-call | tf_op jit(solution)/shard_map/pallas_call | solution.py:343
  14.9 0.0 copy-start.1
  14.9 0.0 copy-start.2
  14.9 0.0 collective-permute-done.1.refs_1_
  14.9 0.0 collective-permute-done.2.refs_2_
  14.9 0.0 collective-permute-done.3.refs_3_
  15.0 1.5 %shard_map.60.partial_ref = f32[1024,128]{1,0:T(8,128)S(1)} custom-call(s32[390]{0:T(512)S(1)} %concatenate.3.index_ref, bf16[16,6,64,256]{3,2,1,0:T(8,128)(2,1)S(1)} %copy-done, f32[1024,128]{1,0:T(8,128)S(1)} %shard_map.59.partial_ref, bf16[16,64,128]{2,1,0:T(8,128)(2,1)S(1)} %collective-permute-done.refs_0_, ...), custom_call_target="tpu_custom_call" | custom-call | tf_op jit(solution)/shard_map/pallas_call | solution.py:360
  16.4 1.1 %collective-permute-done.4.refs_0_ = bf16[16,64,128]{2,1,0:T(8,128)(2,1)S(1)} collective-permute-done((bf16[16,64,128]{2,1,0:T(8,128)(2,1)S(1)}, bf16[16,64,128]{2,1,0:T(8,128)(2,1)S(1)}, u32[]{:S(2)}, u32[]{:S(2)}) %collective-permute-start.4) | collective-permute-done | bytes 262176 | tf_op jit(solution)/shard_map/ppermute | solution.py:43
  17.6 0.0 copy-done.1
  17.6 0.0 copy-done.2
  17.6 1.0 %shard_map.61 = (f32[1024,128]{1,0:T(8,128)S(1)}, bf16[16,64,128]{2,1,0:T(8,128)(2,1)S(1)}) custom-call(s32[390]{0:T(512)S(1)} %concatenate.3.index_ref, bf16[16,6,64,256]{3,2,1,0:T(8,128)(2,1)S(1)} %copy-done, f32[8,128]{1,0:T(8,128)S(1)} %bitcast.13, f32[1024,128]{1,0:T(8,128)S(1)} %copy-done.1, f32[1024,128]{1,0:T(8,128)S(1)} %shard_map.60.partial_ref, ...), custom_call_target="tpu_custom_call" | custom-call | tf_op jit(solution)/shard_map/pallas_call | solution.py:366
  18.5 0.6 %collective-permute-start.5 = (bf16[16,64,128]{2,1,0:T(8,128)(2,1)S(1)}, bf16[16,64,128]{2,1,0:T(8,128)(2,1)S(1)}, u32[]{:S(2)}, u32[]{:S(2)}) collective-permute-start(bf16[16,64,128]{2,1,0:T(8,128)(2,1)S(1)} %get-tuple-element.8.own_ref), channel_id=1, source_target_pairs={{0,1},{1,0},{2,3},{3,2},{4,6},{5,7},{6,4},{7,5},{8,9},{9,8},{10,11... | collective-permute-start | bytes 786440 | tf_op jit(solution)/shard_map/ppermute | solution.py:43
  19.1 0.7 %collective-permute-start.6 = (bf16[16,64,128]{2,1,0:T(8,128)(2,1)S(1)}, bf16[16,64,128]{2,1,0:T(8,128)(2,1)S(1)}, u32[]{:S(2)}, u32[]{:S(2)}) collective-permute-start(bf16[16,64,128]{2,1,0:T(8,128)(2,1)S(1)} %get-tuple-element.8.own_ref), channel_id=1, source_target_pairs={{4,8},{8,4},{12,16},{16,12},{20,24},{24,20},{5,9},{9,5},{13,17},{1... | collective-permute-start | bytes 786440 | tf_op jit(solution)/shard_map/ppermute | solution.py:25
  19.8 3.0 %collective-permute-start.7 = (bf16[16,64,128]{2,1,0:T(8,128)(2,1)S(1)}, bf16[16,64,128]{2,1,0:T(8,128)(2,1)S(1)}, u32[]{:S(2)}, u32[]{:S(2)}) collective-permute-start(bf16[16,64,128]{2,1,0:T(8,128)(2,1)S(1)} %get-tuple-element.8.own_ref), channel_id=1, source_target_pairs={{0,4},{4,0},{8,12},{12,8},{16,20},{20,16},{24,28},{28,24},{1,5},{5... | collective-permute-start | bytes 786440 | tf_op jit(solution)/shard_map/ppermute | solution.py:25
  22.8 1.5 %collective-permute-start.8 = (bf16[16,64,128]{2,1,0:T(8,128)(2,1)S(1)}, bf16[16,64,128]{2,1,0:T(8,128)(2,1)S(1)}, u32[]{:S(2)}, u32[]{:S(2)}) collective-permute-start(bf16[16,64,128]{2,1,0:T(8,128)(2,1)S(1)} %get-tuple-element.8.own_ref), channel_id=1, source_target_pairs={{0,2},{1,3},{2,0},{3,1},{4,5},{5,4},{6,7},{7,6},{8,10},{9,11},{10,... | collective-permute-start | bytes 786440 | tf_op jit(solution)/shard_map/ppermute | solution.py:43
  24.3 1.0 %shard_map.62.partial_ref = f32[1024,128]{1,0:T(8,128)S(1)} custom-call(s32[390]{0:T(512)S(1)} %concatenate.3.index_ref, bf16[16,6,64,256]{3,2,1,0:T(8,128)(2,1)S(1)} %copy-done, bf16[16,64,128]{2,1,0:T(8,128)(2,1)S(1)} %get-tuple-element.8.own_ref, f32[8,128]{1,0:T(8,128)S(1)} %bitcast.14, f32[1024,128]{1,0:T(8,128)S(1)} %get-tuple-element.9.refs_1_, ...), custom_call_target="tpu_custom_call" | custom-call | tf_op jit(solution)/shard_map/pallas_call | solution.py:343
  25.3 0.0 collective-permute-done.5.refs_0_
  25.3 1.2 %collective-permute-start.9 = (bf16[16,64,128]{2,1,0:T(8,128)(2,1)S(1)}, bf16[16,64,128]{2,1,0:T(8,128)(2,1)S(1)}, u32[]{:S(2)}, u32[]{:S(2)}) collective-permute-start(bf16[16,64,128]{2,1,0:T(8,128)(2,1)S(1)} %collective-permute-done.5.refs_0_), channel_id=1, source_target_pairs={{0,2},{1,3},{2,0},{3,1},{4,5},{5,4},{6,7},{7,6},{8,10},{9,11},{10,... | collective-permute-start | bytes 786440 | tf_op jit(solution)/shard_map/ppermute | solution.py:43
  26.5 0.0 collective-permute-done.6.refs_1_
  26.5 0.0 collective-permute-done.7.refs_2_
  26.5 2.7 %collective-permute-done.8.refs_3_ = bf16[16,64,128]{2,1,0:T(8,128)(2,1)S(1)} collective-permute-done((bf16[16,64,128]{2,1,0:T(8,128)(2,1)S(1)}, bf16[16,64,128]{2,1,0:T(8,128)(2,1)S(1)}, u32[]{:S(2)}, u32[]{:S(2)}) %collective-permute-start.8) | collective-permute-done | bytes 262176 | tf_op jit(solution)/shard_map/ppermute | solution.py:43
  29.2 1.5 %shard_map.63.partial_ref = f32[1024,128]{1,0:T(8,128)S(1)} custom-call(s32[390]{0:T(512)S(1)} %concatenate.3.index_ref, bf16[16,6,64,256]{3,2,1,0:T(8,128)(2,1)S(1)} %copy-done, f32[1024,128]{1,0:T(8,128)S(1)} %shard_map.62.partial_ref, bf16[16,64,128]{2,1,0:T(8,128)(2,1)S(1)} %collective-permute-done.5.refs_0_, ...), custom_call_target="tpu_custom_call" | custom-call | tf_op jit(solution)/shard_map/pallas_call | solution.py:360
  30.7 1.3 %collective-permute-done.9.refs_0_ = bf16[16,64,128]{2,1,0:T(8,128)(2,1)S(1)} collective-permute-done((bf16[16,64,128]{2,1,0:T(8,128)(2,1)S(1)}, bf16[16,64,128]{2,1,0:T(8,128)(2,1)S(1)}, u32[]{:S(2)}, u32[]{:S(2)}) %collective-permute-start.9) | collective-permute-done | bytes 262176 | tf_op jit(solution)/shard_map/ppermute | solution.py:43
  32.0 1.3 %shard_map.64 = (bf16[1024,256]{1,0:T(8,128)(2,1)S(1)}, f32[72,128]{1,0:T(8,128)S(1)}) custom-call(s32[390]{0:T(512)S(1)} %concatenate.3.index_ref, bf16[16,6,64,256]{3,2,1,0:T(8,128)(2,1)S(1)} %copy-done, f32[1024,128]{1,0:T(8,128)S(1)} %shard_map.63.partial_ref, bf16[16,64,128]{2,1,0:T(8,128)(2,1)S(1)} %collective-permute-done.9.refs_0_), custom_call_target="tpu_custom_call" | custom-call | tf_op jit(solution)/shard_map/pallas_call | solution.py:371
  33.2 0.1 collective-permute-start.10
  33.3 1.2 %collective-permute-done.10 = f32[72,128]{1,0:T(8,128)S(1)} collective-permute-done((f32[72,128]{1,0:T(8,128)S(1)}, f32[72,128]{1,0:T(8,128)S(1)}, u32[]{:S(2)}, u32[]{:S(2)}) %collective-permute-start.10) | collective-permute-done | bytes 36896 | tf_op jit(solution)/shard_map/ppermute | solution.py:48
  34.5 3.1 %collective-permute-start.11 = (f32[72,128]{1,0:T(8,128)S(1)}, f32[72,128]{1,0:T(8,128)S(1)}, u32[]{:S(2)}, u32[]{:S(2)}) collective-permute-start(f32[72,128]{1,0:T(8,128)S(1)} %add.28), channel_id=1, source_target_pairs={{0,16},{4,20},{8,24},{12,28},{16,0},{20,4},{24,8},{28,12},{1,17},{... | collective-permute-start | bytes 110600 | tf_op jit(solution)/shard_map/ppermute | solution.py:48
  37.7 0.8 %collective-permute-start.12 = (f32[72,128]{1,0:T(8,128)S(1)}, f32[72,128]{1,0:T(8,128)S(1)}, u32[]{:S(2)}, u32[]{:S(2)}) collective-permute-start(f32[72,128]{1,0:T(8,128)S(1)} %add.28), channel_id=1, source_target_pairs={{0,24},{4,28},{8,16},{12,20},{16,8},{20,12},{24,0},{28,4},{1,25},{... | collective-permute-start | bytes 110600 | tf_op jit(solution)/shard_map/ppermute | solution.py:48
  38.5 0.0 collective-permute-start.13
  38.5 2.3 %collective-permute-done.11 = f32[72,128]{1,0:T(8,128)S(1)} collective-permute-done((f32[72,128]{1,0:T(8,128)S(1)}, f32[72,128]{1,0:T(8,128)S(1)}, u32[]{:S(2)}, u32[]{:S(2)}) %collective-permute-start.11) | collective-permute-done | bytes 36896 | tf_op jit(solution)/shard_map/ppermute | solution.py:48
  40.7 2.7 %collective-permute-done.12 = f32[72,128]{1,0:T(8,128)S(1)} collective-permute-done((f32[72,128]{1,0:T(8,128)S(1)}, f32[72,128]{1,0:T(8,128)S(1)}, u32[]{:S(2)}, u32[]{:S(2)}) %collective-permute-start.12) | collective-permute-done | bytes 36896 | tf_op jit(solution)/shard_map/ppermute | solution.py:48
  43.4 0.0 collective-permute-done.13
  43.5 1.5 %collective-permute-start.14 = (f32[72,128]{1,0:T(8,128)S(1)}, f32[72,128]{1,0:T(8,128)S(1)}, u32[]{:S(2)}, u32[]{:S(2)}) collective-permute-start(f32[72,128]{1,0:T(8,128)S(1)} %add_add_fusion.1), channel_id=1, source_target_pairs={{0,3},{1,2},{2,1},{3,0},{4,7},{5,6},{6,5},{7,4},{8,11},{9,10},{10,... | collective-permute-start | bytes 110600 | tf_op jit(solution)/shard_map/ppermute | solution.py:48
  45.0 0.6 %collective-permute-start.15 = (f32[72,128]{1,0:T(8,128)S(1)}, f32[72,128]{1,0:T(8,128)S(1)}, u32[]{:S(2)}, u32[]{:S(2)}) collective-permute-start(f32[72,128]{1,0:T(8,128)S(1)} %add_add_fusion.1), channel_id=1, source_target_pairs={{0,2},{1,3},{2,0},{3,1},{4,6},{5,7},{6,4},{7,5},{8,10},{9,11},{10,... | collective-permute-start | bytes 110600 | tf_op jit(solution)/shard_map/ppermute | solution.py:48
  45.6 1.4 %collective-permute-start.16 = (f32[72,128]{1,0:T(8,128)S(1)}, f32[72,128]{1,0:T(8,128)S(1)}, u32[]{:S(2)}, u32[]{:S(2)}) collective-permute-start(f32[72,128]{1,0:T(8,128)S(1)} %add_add_fusion.1), channel_id=1, source_target_pairs={{0,1},{1,0},{2,3},{3,2},{4,5},{5,4},{6,7},{7,6},{8,9},{9,8},{10,11... | collective-permute-start | bytes 110600 | tf_op jit(solution)/shard_map/ppermute | solution.py:48
  47.0 1.4 %collective-permute-done.14 = f32[72,128]{1,0:T(8,128)S(1)} collective-permute-done((f32[72,128]{1,0:T(8,128)S(1)}, f32[72,128]{1,0:T(8,128)S(1)}, u32[]{:S(2)}, u32[]{:S(2)}) %collective-permute-start.14) | collective-permute-done | bytes 36896 | tf_op jit(solution)/shard_map/ppermute | solution.py:48
  48.4 0.5 %collective-permute-done.15 = f32[72,128]{1,0:T(8,128)S(1)} collective-permute-done((f32[72,128]{1,0:T(8,128)S(1)}, f32[72,128]{1,0:T(8,128)S(1)}, u32[]{:S(2)}, u32[]{:S(2)}) %collective-permute-start.15) | collective-permute-done | bytes 36896 | tf_op jit(solution)/shard_map/ppermute | solution.py:48
  48.9 0.6 %collective-permute-done.16 = f32[72,128]{1,0:T(8,128)S(1)} collective-permute-done((f32[72,128]{1,0:T(8,128)S(1)}, f32[72,128]{1,0:T(8,128)S(1)}, u32[]{:S(2)}, u32[]{:S(2)}) %collective-permute-start.16) | collective-permute-done | bytes 36896 | tf_op jit(solution)/shard_map/ppermute | solution.py:48
  49.5 4.2 %shard_map.65 = (f32[1024,128]{1,0:T(8,128)}, f32[128,128]{1,0:T(8,128)}) custom-call(f32[72,128]{1,0:T(8,128)S(1)} %add_add_fusion.packed_ref, bf16[1024,256]{1,0:T(8,128)(2,1)S(1)} %get-tuple-element.13.both_ref), custom_call_target="tpu_custom_call" | custom-call | tf_op jit(solution)/shard_map/pallas_call | solution.py:375
  (3 shorter events, 0.0 us)
Async XLA Ops:
  1.7 8.2 %collective-permute-start = (bf16[16,64,128]{2,1,0:T(8,128)(2,1)S(1)}, bf16[16,64,128]{2,1,0:T(8,128)(2,1)S(1)}, u32[]{:S(2)}, u32[]{:S(2)}) collective-permute-start(bf16[16,64,128]{2,1,0:T(8,128)(2,1)S(1)} %bitcast.8), channel_id=1, source_target_pairs={{0,1},{1,0},{2,3},{3,2},{4,6},{5,7},{6,4},{7,5},{8,9},{9,8},{10,11... | collective-permute-start | bytes 786440 | tf_op jit(solution)/shard_map/ppermute | solution.py:43
  4.7 10.2 %collective-permute-start.1 = (bf16[16,64,128]{2,1,0:T(8,128)(2,1)S(1)}, bf16[16,64,128]{2,1,0:T(8,128)(2,1)S(1)}, u32[]{:S(2)}, u32[]{:S(2)}) collective-permute-start(bf16[16,64,128]{2,1,0:T(8,128)(2,1)S(1)} %bitcast.9), channel_id=1, source_target_pairs={{4,8},{8,4},{12,16},{16,12},{20,24},{24,20},{5,9},{9,5},{13,17},{1... | collective-permute-start | bytes 786440 | tf_op jit(solution)/shard_map/ppermute | solution.py:25
  5.4 9.6 %collective-permute-start.2 = (bf16[16,64,128]{2,1,0:T(8,128)(2,1)S(1)}, bf16[16,64,128]{2,1,0:T(8,128)(2,1)S(1)}, u32[]{:S(2)}, u32[]{:S(2)}) collective-permute-start(bf16[16,64,128]{2,1,0:T(8,128)(2,1)S(1)} %bitcast.10), channel_id=1, source_target_pairs={{0,4},{4,0},{8,12},{12,8},{16,20},{20,16},{24,28},{28,24},{1,5},{5... | collective-permute-start | bytes 786440 | tf_op jit(solution)/shard_map/ppermute | solution.py:25
  8.4 6.6 %collective-permute-start.3 = (bf16[16,64,128]{2,1,0:T(8,128)(2,1)S(1)}, bf16[16,64,128]{2,1,0:T(8,128)(2,1)S(1)}, u32[]{:S(2)}, u32[]{:S(2)}) collective-permute-start(bf16[16,64,128]{2,1,0:T(8,128)(2,1)S(1)} %bitcast.11), channel_id=1, source_target_pairs={{0,2},{1,3},{2,0},{3,1},{4,5},{5,4},{6,7},{7,6},{8,10},{9,11},{10,... | collective-permute-start | bytes 786440 | tf_op jit(solution)/shard_map/ppermute | solution.py:43
  9.9 7.7 %collective-permute-start.4 = (bf16[16,64,128]{2,1,0:T(8,128)(2,1)S(1)}, bf16[16,64,128]{2,1,0:T(8,128)(2,1)S(1)}, u32[]{:S(2)}, u32[]{:S(2)}) collective-permute-start(bf16[16,64,128]{2,1,0:T(8,128)(2,1)S(1)} %collective-permute-done.refs_0_), channel_id=1, source_target_pairs={{0,2},{1,3},{2,0},{3,1},{4,5},{5,4},{6,7},{7,6},{8,10},{9,11},{10,... | collective-permute-start | bytes 786440 | tf_op jit(solution)/shard_map/ppermute | solution.py:43
  12.1 1.9 %copy-start = (bf16[16,6,64,256]{3,2,1,0:T(8,128)(2,1)S(1)}, bf16[16,6,64,256]{3,2,1,0:T(8,128)(2,1)}, u32[]{:S(2)}) copy-start(bf16[16,6,64,256]{3,2,1,0:T(8,128)(2,1)} %hamiltonian_ref.11) | copy-start | bytes 9437188
  14.9 2.7 %copy-start.1 = (f32[1024,128]{1,0:T(8,128)S(1)}, f32[1024,128]{1,0:T(8,128)}, u32[]{:S(2)}) copy-start(f32[1024,128]{1,0:T(8,128)} %refs_2_.1) | copy-start | bytes 1572868
  14.9 2.6 %copy-start.2 = (f32[1024]{0:T(1024)S(1)}, f32[1024]{0:T(1024)}, u32[]{:S(2)}) copy-start(f32[1024]{0:T(1024)} %param.6) | copy-start | bytes 12292
  18.5 6.8 %collective-permute-start.5 = (bf16[16,64,128]{2,1,0:T(8,128)(2,1)S(1)}, bf16[16,64,128]{2,1,0:T(8,128)(2,1)S(1)}, u32[]{:S(2)}, u32[]{:S(2)}) collective-permute-start(bf16[16,64,128]{2,1,0:T(8,128)(2,1)S(1)} %get-tuple-element.8.own_ref), channel_id=1, source_target_pairs={{0,1},{1,0},{2,3},{3,2},{4,6},{5,7},{6,4},{7,5},{8,9},{9,8},{10,11... | collective-permute-start | bytes 786440 | tf_op jit(solution)/shard_map/ppermute | solution.py:43
  19.1 7.4 %collective-permute-start.6 = (bf16[16,64,128]{2,1,0:T(8,128)(2,1)S(1)}, bf16[16,64,128]{2,1,0:T(8,128)(2,1)S(1)}, u32[]{:S(2)}, u32[]{:S(2)}) collective-permute-start(bf16[16,64,128]{2,1,0:T(8,128)(2,1)S(1)} %get-tuple-element.8.own_ref), channel_id=1, source_target_pairs={{4,8},{8,4},{12,16},{16,12},{20,24},{24,20},{5,9},{9,5},{13,17},{1... | collective-permute-start | bytes 786440 | tf_op jit(solution)/shard_map/ppermute | solution.py:25
  19.8 6.7 %collective-permute-start.7 = (bf16[16,64,128]{2,1,0:T(8,128)(2,1)S(1)}, bf16[16,64,128]{2,1,0:T(8,128)(2,1)S(1)}, u32[]{:S(2)}, u32[]{:S(2)}) collective-permute-start(bf16[16,64,128]{2,1,0:T(8,128)(2,1)S(1)} %get-tuple-element.8.own_ref), channel_id=1, source_target_pairs={{0,4},{4,0},{8,12},{12,8},{16,20},{20,16},{24,28},{28,24},{1,5},{5... | collective-permute-start | bytes 786440 | tf_op jit(solution)/shard_map/ppermute | solution.py:25
  22.8 6.4 %collective-permute-start.8 = (bf16[16,64,128]{2,1,0:T(8,128)(2,1)S(1)}, bf16[16,64,128]{2,1,0:T(8,128)(2,1)S(1)}, u32[]{:S(2)}, u32[]{:S(2)}) collective-permute-start(bf16[16,64,128]{2,1,0:T(8,128)(2,1)S(1)} %get-tuple-element.8.own_ref), channel_id=1, source_target_pairs={{0,2},{1,3},{2,0},{3,1},{4,5},{5,4},{6,7},{7,6},{8,10},{9,11},{10,... | collective-permute-start | bytes 786440 | tf_op jit(solution)/shard_map/ppermute | solution.py:43
  25.3 6.7 %collective-permute-start.9 = (bf16[16,64,128]{2,1,0:T(8,128)(2,1)S(1)}, bf16[16,64,128]{2,1,0:T(8,128)(2,1)S(1)}, u32[]{:S(2)}, u32[]{:S(2)}) collective-permute-start(bf16[16,64,128]{2,1,0:T(8,128)(2,1)S(1)} %collective-permute-done.5.refs_0_), channel_id=1, source_target_pairs={{0,2},{1,3},{2,0},{3,1},{4,5},{5,4},{6,7},{7,6},{8,10},{9,11},{10,... | collective-permute-start | bytes 786440 | tf_op jit(solution)/shard_map/ppermute | solution.py:43
  33.2 1.3 %collective-permute-start.10 = (f32[72,128]{1,0:T(8,128)S(1)}, f32[72,128]{1,0:T(8,128)S(1)}, u32[]{:S(2)}, u32[]{:S(2)}) collective-permute-start(f32[72,128]{1,0:T(8,128)S(1)} %get-tuple-element.12), channel_id=1, source_target_pairs={{0,4},{4,0},{8,12},{12,8},{16,20},{20,16},{24,28},{28,24},{1,5},{5... | collective-permute-start | bytes 110600 | tf_op jit(solution)/shard_map/ppermute | solution.py:48
  34.5 6.2 %collective-permute-start.11 = (f32[72,128]{1,0:T(8,128)S(1)}, f32[72,128]{1,0:T(8,128)S(1)}, u32[]{:S(2)}, u32[]{:S(2)}) collective-permute-start(f32[72,128]{1,0:T(8,128)S(1)} %add.28), channel_id=1, source_target_pairs={{0,16},{4,20},{8,24},{12,28},{16,0},{20,4},{24,8},{28,12},{1,17},{... | collective-permute-start | bytes 110600 | tf_op jit(solution)/shard_map/ppermute | solution.py:48
  37.7 5.8 %collective-permute-start.12 = (f32[72,128]{1,0:T(8,128)S(1)}, f32[72,128]{1,0:T(8,128)S(1)}, u32[]{:S(2)}, u32[]{:S(2)}) collective-permute-start(f32[72,128]{1,0:T(8,128)S(1)} %add.28), channel_id=1, source_target_pairs={{0,24},{4,28},{8,16},{12,20},{16,8},{20,12},{24,0},{28,4},{1,25},{... | collective-permute-start | bytes 110600 | tf_op jit(solution)/shard_map/ppermute | solution.py:48
  38.5 5.0 %collective-permute-start.13 = (f32[72,128]{1,0:T(8,128)S(1)}, f32[72,128]{1,0:T(8,128)S(1)}, u32[]{:S(2)}, u32[]{:S(2)}) collective-permute-start(f32[72,128]{1,0:T(8,128)S(1)} %add.28), channel_id=1, source_target_pairs={{0,8},{4,12},{8,0},{12,4},{16,24},{20,28},{24,16},{28,20},{1,9},{5... | collective-permute-start | bytes 110600 | tf_op jit(solution)/shard_map/ppermute | solution.py:48
  43.5 4.9 %collective-permute-start.14 = (f32[72,128]{1,0:T(8,128)S(1)}, f32[72,128]{1,0:T(8,128)S(1)}, u32[]{:S(2)}, u32[]{:S(2)}) collective-permute-start(f32[72,128]{1,0:T(8,128)S(1)} %add_add_fusion.1), channel_id=1, source_target_pairs={{0,3},{1,2},{2,1},{3,0},{4,7},{5,6},{6,5},{7,4},{8,11},{9,10},{10,... | collective-permute-start | bytes 110600 | tf_op jit(solution)/shard_map/ppermute | solution.py:48
  45.0 4.0 %collective-permute-start.15 = (f32[72,128]{1,0:T(8,128)S(1)}, f32[72,128]{1,0:T(8,128)S(1)}, u32[]{:S(2)}, u32[]{:S(2)}) collective-permute-start(f32[72,128]{1,0:T(8,128)S(1)} %add_add_fusion.1), channel_id=1, source_target_pairs={{0,2},{1,3},{2,0},{3,1},{4,6},{5,7},{6,4},{7,5},{8,10},{9,11},{10,... | collective-permute-start | bytes 110600 | tf_op jit(solution)/shard_map/ppermute | solution.py:48
  45.6 4.0 %collective-permute-start.16 = (f32[72,128]{1,0:T(8,128)S(1)}, f32[72,128]{1,0:T(8,128)S(1)}, u32[]{:S(2)}, u32[]{:S(2)}) collective-permute-start(f32[72,128]{1,0:T(8,128)S(1)} %add_add_fusion.1), channel_id=1, source_target_pairs={{0,1},{1,0},{2,3},{3,2},{4,5},{5,4},{6,7},{7,6},{8,9},{9,8},{10,11... | collective-permute-start | bytes 110600 | tf_op jit(solution)/shard_map/ppermute | solution.py:48
